TPU v7x, 32 devices: a whole 2x2x4 slice. The times are simulated.
32 devices in a mesh: rows: 8 (over z, y), src: 4 (over x, core).
Axes of the slice: x: 2, y: 2, z: 4, core: 2. Of those that a mesh axis runs over, the one named last changes fastest.
Arguments:
- misfit: float32 [32, 64, 1024], P('rows', 'src'), may hold values from -6 to 6
- forward_fields: bfloat16 [32, 64, 1024], P('rows', 'src'), may hold values from -6 to 6
- contrast: float32 [32, 1024], P('rows'), may hold values from 0.2 to 0.6
- u_factors: bfloat16 [32, 16, 96, 1024], P('rows'), may hold values from -0.1875 to 0.1875
- v_factors: bfloat16 [32, 16, 96, 1024], P('rows'), may hold values from -0.1796875 to 0.1796875
- ranks: int32 [32, 16], P('rows'), may hold values from 32 to 96
- tile_cols: int32 [32, 16], replicated, may hold values from 0 to 31, as said below
- owner_slot: int32 [32], replicated, may hold values from 0 to 31, as said below
Outputs:
- adjoint_field: float32 [32, 64, 1024], P('rows', 'src')
- gradient: float32 [32, 1024], P('rows')
Inputs may be any that keep to these rules, and one draw needn't show every extreme that they name: The 16 entries of each row of tile_cols differ. With a tile's receiving device taken as owner_slot[tile_cols[s, k]] // 4 and its sending device as s // 4, at most 8 tiles of one sending device go to one receiving device, and every sending device sends exactly 8 to some receiving device. Each block of unknowns has exactly one slot: owner_slot is a permutation.
All inputs are finite; a program needn't handle non-finite values.
Results may differ from a plain program's by a relative error of at most 0.005.
Values may be sent and summed in bfloat16 or wider, within the bound.
No kernel may reach another device: no remote copies, remote signals or barrier semaphores. Data moves between devices by JAX's collectives and lax.ppermute only.
A program may use at most 192 MiB of HBM per device.

v0:
```python
import jax
import jax.numpy as jnp
from jax import lax
from jax.sharding import PartitionSpec as P

B = 1024
K = 16
RMAX = 96
APPS = 4


def route_tiles(tile_cols, owner_slot, rows_dev, peers):
    slot_count = owner_slot.shape[0]
    tiles = rows_dev * tile_cols.shape[1]
    match = (
        tile_cols.reshape(peers, tiles)[:, :, None]
        == jnp.arange(slot_count, dtype=jnp.int32)[None, None, :]
    )
    target_slot = jnp.sum(jnp.where(match, owner_slot[None, None, :], 0), axis=2)
    target_dev = target_slot // rows_dev
    local_slot = target_slot % rows_dev
    same = target_dev[:, :, None] == target_dev[:, None, :]
    before = jnp.arange(tiles)[None, :] < jnp.arange(tiles)[:, None]
    order = jnp.sum(jnp.where(same & before[None, :, :], 1, 0), axis=2).astype(jnp.int32)
    return (target_dev, local_slot, order)


def per_device(
    misfit, forward_fields, contrast, u_factors, v_factors, ranks, tile_cols, owner_slot
):
    rows_dev = u_factors.shape[0]
    tiles = rows_dev * K
    peers = lax.axis_size("rows")
    cap = (tiles + peers - 1) // peers
    sources = misfit.shape[1]
    here = lax.axis_index("rows")
    target_dev, local_slot, order = route_tiles(tile_cols, owner_slot, rows_dev, peers)
    mine_dev = lax.dynamic_index_in_dim(target_dev, here, 0, keepdims=False)
    mine_order = lax.dynamic_index_in_dim(order, here, 0, keepdims=False)
    box = mine_dev * cap + mine_order
    sender = jnp.arange(peers, dtype=jnp.int32)[:, None] * cap + order
    entry = jnp.where(target_dev == here, sender, peers * cap).reshape(-1)
    arrival = (
        jnp.full((peers * cap,), -1, jnp.int32).at[entry].set(local_slot.reshape(-1), mode="drop")
    )
    pick = (arrival[:, None] == jnp.arange(rows_dev, dtype=jnp.int32)[None, :]).astype(jnp.float32)
    keep = (jnp.arange(RMAX, dtype=jnp.int32)[None, None, :] < ranks[:, :, None]).astype(
        jnp.float32
    )
    field = misfit
    for step in range(APPS):
        coeff = jnp.einsum(
            "lsb,lkrb->lksr",
            field.astype(jnp.bfloat16),
            u_factors,
            preferred_element_type=jnp.float32,
        )
        tile_coeff = (coeff * keep[:, :, None, :]).astype(jnp.bfloat16)
        terms = jnp.einsum(
            "lksr,lkrb->lksb", tile_coeff, v_factors, preferred_element_type=jnp.float32
        )
        terms = terms.reshape(tiles, sources, B)
        outgoing = jnp.zeros((peers * cap, sources, B), jnp.float32).at[box].set(terms)
        incoming = lax.all_to_all(
            outgoing.reshape(peers, cap, sources, B).astype(jnp.bfloat16),
            "rows",
            split_axis=0,
            concat_axis=0,
            tiled=True,
        ).astype(jnp.float32)
        field = misfit + contrast[:, None, :] * jnp.einsum(
            "eq,esb->qsb",
            pick,
            incoming.reshape(peers * cap, sources, B),
            precision=lax.Precision.HIGHEST,
        )
    partial_sum = jnp.sum(forward_fields.astype(jnp.float32) * field, axis=1)
    total = lax.psum(partial_sum, "src")
    gradient = total * lax.rsqrt(jnp.float32(sources * lax.axis_size("src")))
    return (field, gradient)


def solution(mesh):
    placed = (
        P("rows", "src", None),
        P("rows", "src", None),
        P("rows", None),
        P("rows", None, None, None),
        P("rows", None, None, None),
        P("rows", None),
        P(),
        P(),
    )
    return jax.shard_map(
        per_device,
        mesh=mesh,
        in_specs=placed,
        out_specs=(P("rows", "src", None), P("rows", None)),
        check_vma=False,
    )
```

profile of v0, /device:TPU:0, one launch (start us, length us, event | category | flops | bytes accessed | tf_op | source)
XLA Modules:
  0.0 354.3 jit_solution(6710682604696740265)
XLA Ops:
  0.7 0.8 copy.57
  1.4 0.1 eq.57
  1.5 0.8 select_reduce_fusion.1
  2.3 0.8 fusion.66
  3.0 0.3 select_reduce_fusion
  3.4 8.5 %fusion.12 = bf16[4,16,96,16]{2,3,1,0:T(8,128)(2,1)S(1)} fusion(bf16[4,16,96,1024]{3,2,1,0:T(8,128)(2,1)} %param.11, f32[4,16,96]{2,1,0:T(8,128)S(1)} %fusion.66, f32[4,16,1024]{2,1,0:T(8,128)} %param.8), kind=kOutput, calls=%fused_computation.21 | convolution fusion | flops 201588736 | bytes 13066240 | tf_op jit(solution)/shard_map/lsb,lkrb->lksr/dot_general | solution.py:52
  11.9 8.3 %fusion.78 = f32[4,16,16,1024]{3,2,1,0:T(8,128)} fusion(bf16[4,16,96,16]{2,3,1,0:T(8,128)(2,1)S(1)} %fusion.12, bf16[4,16,96,1024]{3,2,1,0:T(8,128)(2,1)} %param.12), kind=kOutput, calls=%fused_computation.80 | convolution fusion | flops 201326592 | bytes 16973824 | tf_op jit(solution)/shard_map/lksr,lkrb->lksb/dot_general | solution.py:59
  20.2 2.5 broadcast.218.clone.2
  22.6 12.0 %scatter_fusion = f32[64,16,1024]{2,1,0:T(8,128)} fusion(f32[64,16,1024]{2,1,0:T(8,128)} %broadcast.218.clone.2, s32[64]{0:T(128)S(1)} %fusion.71, f32[64,16,1024]{2,1,0:T(8,128)} %bitcast.102), kind=kCustom, calls=%fused_computation.1 | custom fusion | bytes 12583168 | tf_op jit(solution)/shard_map/scatter | solution.py:63
  34.7 2.5 convert_element_type.76
  37.2 0.0 copy-start
  37.2 0.0 copy-start.1
  37.2 2.6 copy.58
  39.8 7.3 %all-to-all-start = ((bf16[8,8,16,1024]{3,1,2,0:T(8,128)(2,1)}), bf16[8,8,16,1024]{3,1,2,0:T(8,128)(2,1)S(1)}, u32[]{:S(2)}, u32[]{:S(2)}) async-start(bf16[8,8,16,1024]{3,1,2,0:T(8,128)(2,1)} %copy.58), calls=%async_computation | async-start | bytes 4194304 | tf_op jit(solution)/shard_map/all_to_all | solution.py:64
  47.1 0.1 reduce_sum.34
  47.2 0.1 reduce_sum.32
  47.3 0.1 broadcast_add_fusion
  47.3 0.1 add.101
  47.5 2.6 scatter_custom_fusion
  50.1 45.3 %all-to-all-done = bf16[8,8,16,1024]{3,1,2,0:T(8,128)(2,1)S(1)} async-done(((bf16[8,8,16,1024]{3,1,2,0:T(8,128)(2,1)}), bf16[8,8,16,1024]{3,1,2,0:T(8,128)(2,1)S(1)}, u32[]{:S(2)}, u32[]{:S(2)}) %all-to-all-start) | async-done | bytes 2097184 | tf_op jit(solution)/shard_map/all_to_all | solution.py:64
  95.4 0.0 copy-done
  95.4 0.0 copy-done.1
  95.4 0.4 fusion.58
  95.8 6.9 %fusion.18 = bf16[4,16,16,96]{3,2,1,0:T(8,128)(2,1)S(1)} fusion(bf16[4,16,96,1024]{3,2,1,0:T(8,128)(2,1)} %param.11, f32[4,16,96]{2,1,0:T(8,128)S(1)} %fusion.66, bf16[4,16,1024,1]{2,0,1,3:T(4,128)(2,1)S(1)} %fusion.58), kind=kOutput, calls=%fused_computation.27 | convolution fusion | flops 201523200 | bytes 12935168 | tf_op jit(solution)/shard_map/lsb,lkrb->lksr/dot_general | solution.py:52
  102.7 8.3 %fusion.79 = f32[4,16,16,1024]{3,2,1,0:T(8,128)} fusion(bf16[4,16,16,96]{3,2,1,0:T(8,128)(2,1)S(1)} %fusion.18, bf16[4,16,96,1024]{3,2,1,0:T(8,128)(2,1)} %param.12), kind=kOutput, calls=%fused_computation.81 | convolution fusion | flops 201326592 | bytes 16973824 | tf_op jit(solution)/shard_map/lksr,lkrb->lksb/dot_general | solution.py:59
  111.0 2.5 broadcast.218.clone.1
  113.5 12.0 %scatter_fusion.1 = f32[64,16,1024]{2,1,0:T(8,128)} fusion(f32[64,16,1024]{2,1,0:T(8,128)} %broadcast.218.clone.1, s32[64]{0:T(128)S(1)} %fusion.71, f32[64,16,1024]{2,1,0:T(8,128)} %bitcast.103), kind=kCustom, calls=%fused_computation.2 | custom fusion | bytes 12583168 | tf_op jit(solution)/shard_map/scatter | solution.py:63
  125.5 2.5 convert_element_type.81
  128.0 1.2 copy.62
  129.2 0.0 slice-start
  129.2 52.1 %all_to_all.20 = bf16[8,8,16,1024]{3,1,2,0:T(8,128)(2,1)S(1)} all-to-all(bf16[8,8,16,1024]{3,1,2,0:T(8,128)(2,1)S(1)} %copy.62), channel_id=1, replica_groups=mesh['rows'=8,'src'=4] {'rows'}, dimensions={0} | all-to-all | bytes 4194304 | tf_op jit(solution)/shard_map/all_to_all | solution.py:64
  181.3 0.4 fusion.55
  181.8 0.0 slice-start.1
  181.8 0.0 slice-start.2
  181.8 7.1 %fusion.17 = bf16[4,16,16,96]{3,2,1,0:T(8,128)(2,1)S(1)} fusion(bf16[4,16,96,1024]{3,2,1,0:T(8,128)(2,1)} %param.11, f32[4,16,96]{2,1,0:T(8,128)S(1)} %fusion.66, bf16[4,16,1024,1]{2,0,1,3:T(4,128)(2,1)S(1)} %fusion.55), kind=kOutput, calls=%fused_computation.26 | convolution fusion | flops 201523200 | bytes 12935168 | tf_op jit(solution)/shard_map/lsb,lkrb->lksr/dot_general | solution.py:52
  188.8 0.0 slice-done
  188.8 0.0 slice-done.1
  188.9 0.0 slice-done.2
  188.9 3.3 fusion.80
  192.1 2.5 broadcast.218.clone
  194.6 12.0 %scatter_fusion.2 = f32[64,16,1024]{2,1,0:T(8,128)} fusion(f32[64,16,1024]{2,1,0:T(8,128)} %broadcast.218.clone, s32[64]{0:T(128)S(1)} %fusion.71, f32[64,16,1024]{2,1,0:T(8,128)} %bitcast.104), kind=kCustom, calls=%fused_computation.3 | custom fusion | bytes 12583168 | tf_op jit(solution)/shard_map/scatter | solution.py:63
  206.6 2.5 convert_element_type.86
  209.1 1.2 copy.66
  210.3 0.0 slice-start.3
  210.3 51.7 %all_to_all.21 = bf16[8,8,16,1024]{3,1,2,0:T(8,128)(2,1)S(1)} all-to-all(bf16[8,8,16,1024]{3,1,2,0:T(8,128)(2,1)S(1)} %copy.66), channel_id=1, replica_groups=mesh['rows'=8,'src'=4] {'rows'}, dimensions={0} | all-to-all | bytes 4194304 | tf_op jit(solution)/shard_map/all_to_all | solution.py:64
  262.0 0.4 fusion.52
  262.5 0.0 slice-start.4
  262.5 0.0 slice-start.5
  262.5 7.1 %fusion.16 = bf16[4,16,16,96]{3,2,1,0:T(8,128)(2,1)S(1)} fusion(bf16[4,16,96,1024]{3,2,1,0:T(8,128)(2,1)} %param.11, f32[4,16,96]{2,1,0:T(8,128)S(1)} %fusion.66, bf16[4,16,1024,1]{2,0,1,3:T(4,128)(2,1)S(1)} %fusion.52), kind=kOutput, calls=%fused_computation.25 | convolution fusion | flops 201523200 | bytes 12935168 | tf_op jit(solution)/shard_map/lsb,lkrb->lksr/dot_general | solution.py:52
  269.5 0.0 slice-done.3
  269.6 0.0 slice-done.4
  269.6 0.0 slice-done.5
  269.6 3.2 fusion.81
  272.8 2.5 broadcast.218
  275.3 12.0 %scatter_fusion.3 = f32[64,16,1024]{2,1,0:T(8,128)} fusion(f32[64,16,1024]{2,1,0:T(8,128)} %broadcast.218, s32[64]{0:T(128)S(1)} %fusion.71, f32[64,16,1024]{2,1,0:T(8,128)} %bitcast.101), kind=kCustom, calls=%fused_computation.4 | custom fusion | bytes 12583168 | tf_op jit(solution)/shard_map/scatter | solution.py:63
  287.3 2.5 convert_element_type.91
  289.8 0.0 copy-start.2
  289.8 1.2 copy.70
  291.1 51.1 %all_to_all.22 = bf16[8,8,16,1024]{3,1,2,0:T(8,128)(2,1)S(1)} all-to-all(bf16[8,8,16,1024]{3,1,2,0:T(8,128)(2,1)S(1)} %copy.70), channel_id=1, replica_groups=mesh['rows'=8,'src'=4] {'rows'}, dimensions={0} | all-to-all | bytes 4194304 | tf_op jit(solution)/shard_map/all_to_all | solution.py:64
  342.2 0.0 copy-done.2
  342.2 0.5 multiply_reduce_fusion
  342.7 10.1 %psum.7 = f32[4,1024]{1,0:T(4,128)S(1)} all-reduce(f32[4,1024]{1,0:T(4,128)S(1)} %get-tuple-element.12), channel_id=1, replica_groups=mesh['rows'=8,'src'=4] {'src'}, use_global_device_ids=true, to_apply=%region_8.9 | all-reduce | flops 4096 | bytes 32768 | tf_op jit(solution)/shard_map/psum | solution.py:78
  352.8 0.6 broadcast_multiply_fusion
  353.4 0.9 copy.74
  (8 shorter events, 0.1 us)
Async XLA Ops:
  37.2 58.2 %copy-start = (f32[4,16,1024]{2,1,0:T(8,128)S(1)}, f32[4,16,1024]{2,1,0:T(8,128)}, u32[]{:S(2)}) copy-start(f32[4,16,1024]{2,1,0:T(8,128)} %param.8) | copy-start | bytes 786436
  37.2 58.2 %copy-start.1 = (f32[4,1024]{1,0:T(4,128)S(1)}, f32[4,1024]{1,0:T(4,128)}, u32[]{:S(2)}) copy-start(f32[4,1024]{1,0:T(4,128)} %param.10) | copy-start | bytes 49156
  39.8 55.5 %all-to-all-start = ((bf16[8,8,16,1024]{3,1,2,0:T(8,128)(2,1)}), bf16[8,8,16,1024]{3,1,2,0:T(8,128)(2,1)S(1)}, u32[]{:S(2)}, u32[]{:S(2)}) async-start(bf16[8,8,16,1024]{3,1,2,0:T(8,128)(2,1)} %copy.58), calls=%async_computation | async-start | bytes 4194304 | tf_op jit(solution)/shard_map/all_to_all | solution.py:64
  129.2 59.6 %slice-start = ((s8[12582912]{0:T(1024)(128)(4,1)}), s8[4194304]{0:T(1024)(128)(4,1)S(1)}, s32[]{:S(2)}) async-start(s8[12582912]{0:T(1024)(128)(4,1)} %bitcast.97), calls=%async_computation.4 | async-start | bytes 8388608
  181.8 7.1 %slice-start.1 = ((s8[12582912]{0:T(1024)(128)(4,1)}), s8[4194304]{0:T(1024)(128)(4,1)S(1)}, s32[]{:S(2)}) async-start(s8[12582912]{0:T(1024)(128)(4,1)} %bitcast.97), calls=%async_computation.5 | async-start | bytes 8388608
  181.8 7.1 %slice-start.2 = ((s8[12582912]{0:T(1024)(128)(4,1)}), s8[4194304]{0:T(1024)(128)(4,1)S(1)}, s32[]{:S(2)}) async-start(s8[12582912]{0:T(1024)(128)(4,1)} %bitcast.97), calls=%async_computation.6 | async-start | bytes 8388608
  210.3 59.2 %slice-start.3 = ((s8[12582912]{0:T(1024)(128)(4,1)}), s8[4194304]{0:T(1024)(128)(4,1)S(1)}, s32[]{:S(2)}) async-start(s8[12582912]{0:T(1024)(128)(4,1)} %bitcast.99), calls=%async_computation.7 | async-start | bytes 8388608
  262.5 7.1 %slice-start.4 = ((s8[12582912]{0:T(1024)(128)(4,1)}), s8[4194304]{0:T(1024)(128)(4,1)S(1)}, s32[]{:S(2)}) async-start(s8[12582912]{0:T(1024)(128)(4,1)} %bitcast.99), calls=%async_computation.8 | async-start | bytes 8388608
  262.5 7.1 %slice-start.5 = ((s8[12582912]{0:T(1024)(128)(4,1)}), s8[4194304]{0:T(1024)(128)(4,1)S(1)}, s32[]{:S(2)}) async-start(s8[12582912]{0:T(1024)(128)(4,1)} %bitcast.99), calls=%async_computation.9 | async-start | bytes 8388608
  289.8 52.4 %copy-start.2 = (bf16[4,16,1024]{2,1,0:T(8,128)(2,1)S(1)}, bf16[4,16,1024]{2,1,0:T(8,128)(2,1)}, u32[]{:S(2)}) copy-start(bf16[4,16,1024]{2,1,0:T(8,128)(2,1)} %param.9) | copy-start | bytes 393220
where the time goes:
time: 355 us; the launch traced here: 354 us
  blocking collectives  165 us (46%)
  local copies, waits for them, and re-layouts  68.8 us (19%)
  matrix products  54.4 us (15%)
  waiting for transfers between devices  45.3 us (13%)
  other arithmetic  12.6 us (4%)
  starting transfers between devices  7.28 us (2%)
    all_to_all x3, blocking collectives, per_device(): lax.all_to_all(outgoing.reshape(peers, cap, sources, B).astype(jnp.bfloat...  155 us
    scatter x4, local copies, waits for them, and re-layouts, per_device(): jnp.zeros((peers * cap, sources, B), jnp.float32).at[box].set(terms)  48.1 us
    all_to_all x1, waiting for transfers between devices, per_device(): lax.all_to_all(outgoing.reshape(peers, cap, sources, B).astype(jnp.bfloat...  45.3 us
    dot_general x4, matrix products, per_device(): jnp.einsum('lsb,lkrb->lksr', field.astype(jnp.bfloat16), u_factors, prefe...  29.5 us
    dot_general x4, matrix products, per_device(): jnp.einsum('lksr,lkrb->lksb', tile_coeff, v_factors, preferred_element_ty...  23.1 us
    psum x1, blocking collectives, per_device(): total = lax.psum(partial_sum, 'src')  10.1 us
    convert_element_type x4, other arithmetic, per_device(): outgoing.reshape(peers, cap, sources, B).astype(jnp.bfloat16)  10 us
    another operation x4, local copies, waits for them, and re-layouts  9.81 us
  transfers between devices with their start and end apart: 1, of which 1 were waited for; matrix products, arithmetic and copies ran while one was open for 1% of the time, Pallas kernels for 0%

commit v1 on v0

v1 whole, which is shorter than its diff:
```python
import functools

import jax
import jax.numpy as jnp
from jax import lax
from jax.experimental import pallas as pl
from jax.experimental.pallas import tpu as pltpu
from jax.sharding import PartitionSpec as P

APPS = 4
GROUP = 8


def sends(rows_dev, peers):
    bits = peers.bit_length() - 1
    near = list(range(bits))
    half = rows_dev // 2
    return [(half, near), (rows_dev - half, near[1:] + near[:1])]


def spot(bits_order, rel):
    place = 0
    for bit in bits_order:
        place = place * 2 + ((rel >> bit) & 1)
    return place


def tile_kernel(dims, first, *refs):
    rows_dev, tiles_row, rank_max, peers, plan = dims
    refs = list(refs)
    cols_ref, owner_ref, ranks_ref, contrast_ref, base_ref = refs[:5]
    if first:
        u_from, v_from = refs[5:7]
        outs, u_ref, v_ref, acc, u_sem, v_sem = refs[7:11], *refs[11:16]
    else:
        arrived, u_ref, v_ref = refs[5:7], *refs[7:9]
        outs, acc = refs[9:13], refs[13]
    here = lax.axis_index("rows")
    half = plan[0][0]
    width = GROUP * rank_max
    steps = rows_dev * (tiles_row // GROUP)

    def load(step, whence, to, sem):
        piece = pl.ds(step * width, width)
        return pltpu.make_async_copy(whence.at[piece], to.at[piece], sem.at[step])

    if first:
        for step in range(steps):
            load(step, u_from, u_ref, u_sem).start()
            load(step, v_from, v_ref, v_sem).start()
    acc[...] = jnp.zeros_like(acc)
    lane = lax.broadcasted_iota(jnp.int32, (base_ref.shape[1], width), 1)
    for step in range(steps):
        row, group = divmod(step, tiles_row // GROUP)
        if group == 0:
            field = base_ref[row]
            if not first:
                part = arrived[0][row] if row < half else arrived[1][row - half]
                field = field + contrast_ref[pl.ds(row, 1), :] * part.astype(jnp.float32)
            low = field.astype(jnp.bfloat16)
        piece = pl.ds(step * width, width)
        if first:
            load(step, u_from, u_ref, u_sem).wait()
        coeff = lax.dot_general(
            low, u_ref[piece, :], (((1,), (1,)), ((), ())), preferred_element_type=jnp.float32
        )
        blocks = []
        for i in range(GROUP):
            rank = ranks_ref[row, group * GROUP + i]
            inside = (lane >= i * rank_max) & (lane < i * rank_max + rank)
            blocks.append(jnp.where(inside, coeff, 0.0).astype(jnp.bfloat16))
        spread = jnp.concatenate(blocks, axis=0)
        if first:
            load(step, v_from, v_ref, v_sem).wait()
        terms = jnp.dot(spread, v_ref[piece, :], preferred_element_type=jnp.float32)
        sources = low.shape[0]
        for i in range(GROUP):
            slot = owner_ref[cols_ref[here * rows_dev + row, group * GROUP + i]]
            rel = jnp.bitwise_xor(slot // rows_dev, here)
            local = slot % rows_dev
            place = jnp.where(
                local < half,
                spot(plan[0][1], rel) * half + local,
                peers * half + spot(plan[1][1], rel) * (rows_dev - half) + local - half,
            )
            acc[place] += terms[i * sources : (i + 1) * sources]
    base = 0
    for part, (count, _) in enumerate(plan):
        kept = peers * count // 2
        outs[2 * part][...] = acc[base : base + kept]
        outs[2 * part + 1][...] = acc[base + kept : base + 2 * kept].astype(jnp.bfloat16)
        base += 2 * kept


def apply_tiles(plan, peers, cols, owner, ranks, contrast, base, arrived, u, v):
    rows_dev, tiles_row = ranks.shape
    rank_max = u.shape[0] // (rows_dev * tiles_row)
    sources, unknowns = base.shape[1:]
    first = arrived is None
    smem = pl.BlockSpec(memory_space=pltpu.SMEM)
    vmem = pl.BlockSpec(memory_space=pltpu.VMEM)
    outs = []
    for count, _ in plan:
        outs.append(jax.ShapeDtypeStruct((peers * count // 2, sources, unknowns), jnp.float32))
        outs.append(jax.ShapeDtypeStruct((peers * count // 2, sources, unknowns), jnp.bfloat16))
    scratch = [pltpu.VMEM((peers * rows_dev, sources, unknowns), jnp.float32)]
    if first:
        specs = [vmem] * 2 + [pl.BlockSpec(memory_space=pl.ANY)] * 2
        outs += [pltpu.VMEM(x.shape, x.dtype) for x in (u, v)]
        steps = rows_dev * tiles_row // GROUP
        scratch += [pltpu.SemaphoreType.DMA((steps,))] * 2
        extra = []
    else:
        specs = [vmem] * 6
        u, v = (pltpu.with_memory_space_constraint(x, pltpu.VMEM) for x in (u, v))
        extra = list(arrived)
    flops = 4 * u.shape[0] * unknowns * sources
    got = pl.pallas_call(
        functools.partial(tile_kernel, (rows_dev, tiles_row, rank_max, peers, plan), first),
        out_shape=outs,
        in_specs=[smem] * 3 + specs,
        out_specs=[vmem] * len(outs),
        scratch_shapes=scratch,
        compiler_params=pltpu.CompilerParams(vmem_limit_bytes=24 * 1024 * 1024),
        cost_estimate=pl.CostEstimate(flops=flops, bytes_accessed=4 * u.size, transcendentals=0),
    )(cols, owner, ranks, contrast, base, *extra, u, v)
    return got[:4], got[4:]


def swap(x, bit, peers):
    return lax.ppermute(x, "rows", [(i, i ^ (1 << bit)) for i in range(peers)])


def slot_sums(misfit, contrast, u_factors, v_factors, ranks, tile_cols, owner_slot):
    peers = lax.axis_size("rows")
    rows_dev = ranks.shape[0]
    unknowns = misfit.shape[-1]
    plan = sends(rows_dev, peers)
    factors = [x.reshape(-1, unknowns) for x in (u_factors, v_factors)]
    base, arrived = misfit, None
    for step in range(APPS):
        got, held = apply_tiles(
            plan, peers, tile_cols, owner_slot, ranks, contrast, base, arrived, *factors
        )
        factors = held or factors
        keeps, goes = [got[0], got[2]], [got[1], got[3]]
        for level in range(len(plan[0][1])):
            came = [swap(goes[p], plan[p][1][level], peers) for p in range(2)]
            if level == len(plan[0][1]) - 1:
                break
            for p in range(2):
                mid = keeps[p].shape[0] // 2
                goes[p] = (keeps[p][mid:] + came[p][mid:].astype(jnp.float32)).astype(jnp.bfloat16)
                keeps[p] = keeps[p][:mid] + came[p][:mid].astype(jnp.float32)
        base = misfit + contrast[:, None, :] * jnp.concatenate(keeps, axis=0)
        arrived = came
    return base + contrast[:, None, :] * jnp.concatenate(arrived, axis=0).astype(jnp.float32)


def route_tiles(tile_cols, owner_slot, rows_dev, peers):
    tiles = rows_dev * tile_cols.shape[1]
    target_slot = owner_slot[tile_cols.reshape(peers, tiles)]
    target_dev = target_slot // rows_dev
    local_slot = target_slot % rows_dev
    same = target_dev[:, :, None] == target_dev[:, None, :]
    before = jnp.arange(tiles)[None, :] < jnp.arange(tiles)[:, None]
    order = jnp.sum(jnp.where(same & before[None, :, :], 1, 0), axis=2).astype(jnp.int32)
    return target_dev, local_slot, order


def tile_terms(misfit, contrast, u_factors, v_factors, ranks, tile_cols, owner_slot):
    rows_dev, tiles_row, rank_max, unknowns = u_factors.shape
    tiles = rows_dev * tiles_row
    peers = lax.axis_size("rows")
    cap = (tiles + peers - 1) // peers
    sources = misfit.shape[1]
    here = lax.axis_index("rows")
    target_dev, local_slot, order = route_tiles(tile_cols, owner_slot, rows_dev, peers)
    mine_dev = lax.dynamic_index_in_dim(target_dev, here, 0, keepdims=False)
    mine_order = lax.dynamic_index_in_dim(order, here, 0, keepdims=False)
    box = mine_dev * cap + mine_order
    sender = jnp.arange(peers, dtype=jnp.int32)[:, None] * cap + order
    entry = jnp.where(target_dev == here, sender, peers * cap).reshape(-1)
    arrival = (
        jnp.full((peers * cap,), -1, jnp.int32).at[entry].set(local_slot.reshape(-1), mode="drop")
    )
    pick = (arrival[:, None] == jnp.arange(rows_dev, dtype=jnp.int32)[None, :]).astype(jnp.float32)
    keep = (jnp.arange(rank_max, dtype=jnp.int32)[None, None, :] < ranks[:, :, None]).astype(
        jnp.float32
    )
    field = misfit
    for step in range(APPS):
        coeff = jnp.einsum(
            "lsb,lkrb->lksr",
            field.astype(jnp.bfloat16),
            u_factors,
            preferred_element_type=jnp.float32,
        )
        tile_coeff = (coeff * keep[:, :, None, :]).astype(jnp.bfloat16)
        terms = jnp.einsum(
            "lksr,lkrb->lksb", tile_coeff, v_factors, preferred_element_type=jnp.float32
        )
        terms = terms.reshape(tiles, sources, unknowns)
        outgoing = jnp.zeros((peers * cap, sources, unknowns), jnp.float32).at[box].set(terms)
        incoming = lax.all_to_all(
            outgoing.reshape(peers, cap, sources, unknowns).astype(jnp.bfloat16),
            "rows",
            split_axis=0,
            concat_axis=0,
            tiled=True,
        ).astype(jnp.float32)
        field = misfit + contrast[:, None, :] * jnp.einsum(
            "eq,esb->qsb",
            pick,
            incoming.reshape(peers * cap, sources, unknowns),
            precision=lax.Precision.HIGHEST,
        )
    return field


def src_sum(x):
    count = lax.axis_size("src")
    if count & (count - 1):
        return lax.psum(x, "src")
    terms = [x]
    for step in range(1, count):
        terms.append(lax.ppermute(x, "src", [(i, i ^ step) for i in range(count)]))
    while len(terms) > 1:
        terms = [a + b for a, b in zip(terms[::2], terms[1::2])]
    return terms[0]


def per_device(
    misfit, forward_fields, contrast, u_factors, v_factors, ranks, tile_cols, owner_slot
):
    rows_dev, tiles_row = ranks.shape
    peers = lax.axis_size("rows")
    dense = (
        peers & (peers - 1) == 0
        and peers > 1
        and rows_dev % 2 == 0
        and tiles_row % GROUP == 0
        and peers <= tiles_row
    )
    run = slot_sums if dense else tile_terms
    field = run(misfit, contrast, u_factors, v_factors, ranks, tile_cols, owner_slot)
    partial_sum = jnp.sum(forward_fields.astype(jnp.float32) * field, axis=1)
    total = src_sum(partial_sum)
    sources = misfit.shape[1] * lax.axis_size("src")
    gradient = total * lax.rsqrt(jnp.float32(sources))
    return (field, gradient)


def solution(mesh):
    placed = (
        P("rows", "src", None),
        P("rows", "src", None),
        P("rows", None),
        P("rows", None, None, None),
        P("rows", None, None, None),
        P("rows", None),
        P(),
        P(),
    )
    return jax.shard_map(
        per_device,
        mesh=mesh,
        in_specs=placed,
        out_specs=(P("rows", "src", None), P("rows", None)),
        check_vma=False,
    )
```

time: 355 us -> 133 us (0.37)
  blocking collectives: 165 us -> 0 us
  local copies, waits for them, and re-layouts: 68.8 us -> 3.78 us
  matrix products: 54.4 us -> 0 us
  Pallas kernels: 0 us -> 36.8 us
  starting transfers between devices: 7.28 us -> 35.8 us
  other arithmetic: 12.6 us -> 2.18 us
  waiting for transfers between devices: 45.3 us -> 53.3 us
    all_to_all x3 -> x0, blocking collectives: 155 us -> none  [per_device(): lax.all_to_all(outgoing.reshape(peers, cap, sources, B).astype(jnp.bfloat...]
    dot_general x12 -> x0, matrix products: 54.4 us -> none  [the longest x4 29.5 us: per_device(): jnp.einsum('lsb,lkrb->lksr', field.astype(jnp.bfloat16), u_factors, prefe...]
    ppermute x0 -> x27, waiting for transfers between devices: none -> 53.3 us  [the longest x24 51.4 us: swap(): return lax.ppermute(x, 'rows', [(i, i ^ 1 << bit) for i in range(peers)])]
    scatter x5 -> x0, local copies, waits for them, and re-layouts: 50.7 us -> none  [the longest x4 48.1 us: per_device(): jnp.zeros((peers * cap, sources, B), jnp.float32).at[box].set(terms)]
    all_to_all x1 -> x0, waiting for transfers between devices: 45.3 us -> none  [per_device(): lax.all_to_all(outgoing.reshape(peers, cap, sources, B).astype(jnp.bfloat...]
    pallas_call x0 -> x4, Pallas kernels: none -> 36.8 us  [apply_tiles(): pl.pallas_call(functools.partial(tile_kernel, (rows_dev, tiles_row, rank_...]
    ppermute x0 -> x27, starting transfers between devices: none -> 35.8 us  [the longest x24 34 us: swap(): return lax.ppermute(x, 'rows', [(i, i ^ 1 << bit) for i in range(peers)])]
    convert_element_type x5 -> x14, other arithmetic: 10.8 us -> 0.61 us  [slot_sums(): (keeps[p][mid:] + came[p][mid:].astype(jnp.float32)).astype(jnp.bfloat16)]
  transfers between devices with their start and end apart: 1 -> 27, of which waited for: 1 -> 22; matrix products, arithmetic and copies ran while one was open for 1% -> 1% of each run, Pallas kernels for 0% -> 0%
where the time goes in v1:
time: 133 us
  waiting for transfers between devices  53.3 us (40%)
  Pallas kernels  36.8 us (28%)
  starting transfers between devices  35.8 us (27%)
  local copies, waits for them, and re-layouts  3.78 us (3%)
  other arithmetic  2.18 us (2%)
    ppermute x24, waiting for transfers between devices, swap(): return lax.ppermute(x, 'rows', [(i, i ^ 1 << bit) for i in range(peers)])  51.4 us
    pallas_call x4, Pallas kernels, apply_tiles(): pl.pallas_call(functools.partial(tile_kernel, (rows_dev, tiles_row, rank_...  36.8 us
    ppermute x24, starting transfers between devices, swap(): return lax.ppermute(x, 'rows', [(i, i ^ 1 << bit) for i in range(peers)])  34 us
    unnamed x11, local copies, waits for them, and re-layouts  3.78 us
  transfers between devices with their start and end apart: 27, of which 22 were waited for; matrix products, arithmetic and copies ran while one was open for 1% of the time, Pallas kernels for 0%

profile of v1, /device:TPU:0, one launch (start us, length us, event | category | flops | bytes accessed | tf_op | source)
XLA Modules:
  0.0 132.7 jit_solution(15564194335917970259)
XLA Ops:
  0.6 0.8 copy.13.refs_0_
  1.4 0.9 copy-done
  2.4 0.7 copy-done.1
  3.1 0.7 copy-done.2
  3.8 0.7 copy-done.3
  4.4 11.8 %shard_map.95 = (f32[8,16,1024]{2,1,0:T(8,128)S(1)}, bf16[8,16,1024]{2,1,0:T(8,128)(2,1)S(1)}, f32[8,16,1024]{2,1,0:T(8,128)S(1)}, bf16[8,16,1024]{2,1,0:T(8,128...) custom-call(s32[32,16]{1,0:T(8,128)S(1)} %copy.13.refs_0_, s32[32]{0:T(128)S(1)} %copy-done.3, ...), custom_call_target="tpu_custom_call" | custom-call | flops 402653184 | bytes 25165824 | tf_op jit(solution)/shard_map/pallas_call | solution.py:118
  16.2 3.0 %collective-permute-start = (bf16[8,16,1024]{2,1,0:T(8,128)(2,1)S(1)}, bf16[8,16,1024]{2,1,0:T(8,128)(2,1)S(1)}, u32[]{:S(2)}, u32[]{:S(2)}) collective-permute-start(bf16[8,16,1024]{2,1,0:T(8,128)(2,1)S(1)} %get-tuple-element.21), channel_id=1, source_target_pairs={{0,4},{4,0},{8,12},{12,8},{16,20},{20,16},{24,28},{28,24},{1,5},{5... | collective-permute-start | bytes 786440 | tf_op jit(solution)/shard_map/ppermute | solution.py:131
  19.2 1.6 %collective-permute-start.2 = (bf16[8,16,1024]{2,1,0:T(8,128)(2,1)S(1)}, bf16[8,16,1024]{2,1,0:T(8,128)(2,1)S(1)}, u32[]{:S(2)}, u32[]{:S(2)}) collective-permute-start(bf16[8,16,1024]{2,1,0:T(8,128)(2,1)S(1)} %get-tuple-element.23), channel_id=1, source_target_pairs={{0,8},{4,12},{8,0},{12,4},{16,24},{20,28},{24,16},{28,20},{1,9},{5... | collective-permute-start | bytes 786440 | tf_op jit(solution)/shard_map/ppermute | solution.py:131
  20.8 4.7 %collective-permute-done = bf16[8,16,1024]{2,1,0:T(8,128)(2,1)S(1)} collective-permute-done((bf16[8,16,1024]{2,1,0:T(8,128)(2,1)S(1)}, bf16[8,16,1024]{2,1,0:T(8,128)(2,1)S(1)}, u32[]{:S(2)}, u32[]{:S(2)}) %collective-permute-start) | collective-permute-done | bytes 262176 | tf_op jit(solution)/shard_map/ppermute | solution.py:131
  25.5 0.1 add_convert_fusion.7
  25.6 1.9 %collective-permute-start.1 = (bf16[4,16,1024]{2,1,0:T(8,128)(2,1)S(1)}, bf16[4,16,1024]{2,1,0:T(8,128)(2,1)S(1)}, u32[]{:S(2)}, u32[]{:S(2)}) collective-permute-start(bf16[4,16,1024]{2,1,0:T(8,128)(2,1)S(1)} %get-tuple-element.52), channel_id=1, source_target_pairs={{0,8},{4,12},{8,0},{12,4},{16,24},{20,28},{24,16},{28,20},{1,9},{5... | collective-permute-start | bytes 393224 | tf_op jit(solution)/shard_map/ppermute | solution.py:131
  27.5 0.1 add_convert_fusion.6
  27.5 2.7 %collective-permute-start.3 = (bf16[4,16,1024]{2,1,0:T(8,128)(2,1)S(1)}, bf16[4,16,1024]{2,1,0:T(8,128)(2,1)S(1)}, u32[]{:S(2)}, u32[]{:S(2)}) collective-permute-start(bf16[4,16,1024]{2,1,0:T(8,128)(2,1)S(1)} %get-tuple-element.54), channel_id=1, source_target_pairs={{0,16},{4,20},{8,24},{12,28},{16,0},{20,4},{24,8},{28,12},{1,17},{... | collective-permute-start | bytes 393224 | tf_op jit(solution)/shard_map/ppermute | solution.py:131
  30.2 1.6 %collective-permute-done.1 = bf16[4,16,1024]{2,1,0:T(8,128)(2,1)S(1)} collective-permute-done((bf16[4,16,1024]{2,1,0:T(8,128)(2,1)S(1)}, bf16[4,16,1024]{2,1,0:T(8,128)(2,1)S(1)}, u32[]{:S(2)}, u32[]{:S(2)}) %collective-permute-start.1) | collective-permute-done | bytes 131104 | tf_op jit(solution)/shard_map/ppermute | solution.py:131
  31.8 2.8 %collective-permute-start.4 = (bf16[2,16,1024]{2,1,0:T(8,128)(2,1)S(1)}, bf16[2,16,1024]{2,1,0:T(8,128)(2,1)S(1)}, u32[]{:S(2)}, u32[]{:S(2)}) collective-permute-start(bf16[2,16,1024]{2,1,0:T(8,128)(2,1)S(1)} %get-tuple-element.70), channel_id=1, source_target_pairs={{0,16},{4,20},{8,24},{12,28},{16,0},{20,4},{24,8},{28,12},{1,17},{... | collective-permute-start | bytes 196616 | tf_op jit(solution)/shard_map/ppermute | solution.py:131
  34.7 2.2 %collective-permute-done.3 = bf16[4,16,1024]{2,1,0:T(8,128)(2,1)S(1)} collective-permute-done((bf16[4,16,1024]{2,1,0:T(8,128)(2,1)S(1)}, bf16[4,16,1024]{2,1,0:T(8,128)(2,1)S(1)}, u32[]{:S(2)}, u32[]{:S(2)}) %collective-permute-start.3) | collective-permute-done | bytes 131104 | tf_op jit(solution)/shard_map/ppermute | solution.py:131
  36.9 1.6 %collective-permute-start.5 = (bf16[2,16,1024]{2,1,0:T(8,128)(2,1)S(1)}, bf16[2,16,1024]{2,1,0:T(8,128)(2,1)S(1)}, u32[]{:S(2)}, u32[]{:S(2)}) collective-permute-start(bf16[2,16,1024]{2,1,0:T(8,128)(2,1)S(1)} %get-tuple-element.68), channel_id=1, source_target_pairs={{0,4},{4,0},{8,12},{12,8},{16,20},{20,16},{24,28},{28,24},{1,5},{5... | collective-permute-start | bytes 196616 | tf_op jit(solution)/shard_map/ppermute | solution.py:131
  38.5 2.7 %collective-permute-done.5.refs_6_ = bf16[2,16,1024]{2,1,0:T(8,128)(2,1)S(1)} collective-permute-done((bf16[2,16,1024]{2,1,0:T(8,128)(2,1)S(1)}, bf16[2,16,1024]{2,1,0:T(8,128)(2,1)S(1)}, u32[]{:S(2)}, u32[]{:S(2)}) %collective-permute-start.5) | collective-permute-done | bytes 65568 | tf_op jit(solution)/shard_map/ppermute | solution.py:131
  41.2 8.4 %shard_map.96 = (f32[8,16,1024]{2,1,0:T(8,128)S(1)}, bf16[8,16,1024]{2,1,0:T(8,128)(2,1)S(1)}, f32[8,16,1024]{2,1,0:T(8,128)S(1)}, bf16[8,16,1024]{2,1,0:T(8,128)(2,1)S(1)}) custom-call(s32[32,16]{1,0:T(8,128)S(1)} %copy.13.refs_0_, s32[32]{0:T(128)S(1)} %copy-done.3, s32[4,16]{1,0:T(4,128)S(1)} %copy-done.2, f32[4,1024]{1,0:T(4,128)S(1)} %copy-done.1, ...), custom_call_target="tpu_custom_call" | custom-call | flops 402653184 | bytes 25165824 | tf_op jit(solution)/shard_map/pallas_call | solution.py:118
  49.6 1.6 %collective-permute-start.6 = (bf16[8,16,1024]{2,1,0:T(8,128)(2,1)S(1)}, bf16[8,16,1024]{2,1,0:T(8,128)(2,1)S(1)}, u32[]{:S(2)}, u32[]{:S(2)}) collective-permute-start(bf16[8,16,1024]{2,1,0:T(8,128)(2,1)S(1)} %get-tuple-element.27), channel_id=1, source_target_pairs={{0,4},{4,0},{8,12},{12,8},{16,20},{20,16},{24,28},{28,24},{1,5},{5... | collective-permute-start | bytes 786440 | tf_op jit(solution)/shard_map/ppermute | solution.py:131
  51.2 4.8 %collective-permute-done.6 = bf16[8,16,1024]{2,1,0:T(8,128)(2,1)S(1)} collective-permute-done((bf16[8,16,1024]{2,1,0:T(8,128)(2,1)S(1)}, bf16[8,16,1024]{2,1,0:T(8,128)(2,1)S(1)}, u32[]{:S(2)}, u32[]{:S(2)}) %collective-permute-start.6) | collective-permute-done | bytes 262176 | tf_op jit(solution)/shard_map/ppermute | solution.py:131
  56.0 0.1 add_convert_fusion.5
  56.0 0.3 collective-permute-start.7
  56.3 2.6 %collective-permute-done.8 = bf16[8,16,1024]{2,1,0:T(8,128)(2,1)S(1)} collective-permute-done((bf16[8,16,1024]{2,1,0:T(8,128)(2,1)S(1)}, bf16[8,16,1024]{2,1,0:T(8,128)(2,1)S(1)}, u32[]{:S(2)}, u32[]{:S(2)}) %collective-permute-start.8) | collective-permute-done | bytes 262176 | tf_op jit(solution)/shard_map/ppermute | solution.py:131
  58.9 0.1 add_convert_fusion.4
  59.0 2.2 %collective-permute-start.9 = (bf16[4,16,1024]{2,1,0:T(8,128)(2,1)S(1)}, bf16[4,16,1024]{2,1,0:T(8,128)(2,1)S(1)}, u32[]{:S(2)}, u32[]{:S(2)}) collective-permute-start(bf16[4,16,1024]{2,1,0:T(8,128)(2,1)S(1)} %get-tuple-element.50), channel_id=1, source_target_pairs={{0,16},{4,20},{8,24},{12,28},{16,0},{20,4},{24,8},{28,12},{1,17},{... | collective-permute-start | bytes 393224 | tf_op jit(solution)/shard_map/ppermute | solution.py:131
  61.2 0.6 collective-permute-done.7
  61.8 1.2 collective-permute-start.10
  63.0 3.5 %collective-permute-done.9 = bf16[4,16,1024]{2,1,0:T(8,128)(2,1)S(1)} collective-permute-done((bf16[4,16,1024]{2,1,0:T(8,128)(2,1)S(1)}, bf16[4,16,1024]{2,1,0:T(8,128)(2,1)S(1)}, u32[]{:S(2)}, u32[]{:S(2)}) %collective-permute-start.9) | collective-permute-done | bytes 131104 | tf_op jit(solution)/shard_map/ppermute | solution.py:131
  66.5 0.8 collective-permute-start.11
  67.3 3.5 %collective-permute-done.11.refs_6_ = bf16[2,16,1024]{2,1,0:T(8,128)(2,1)S(1)} collective-permute-done((bf16[2,16,1024]{2,1,0:T(8,128)(2,1)S(1)}, bf16[2,16,1024]{2,1,0:T(8,128)(2,1)S(1)}, u32[]{:S(2)}, u32[]{:S(2)}) %collective-permute-start.11) | collective-permute-done | bytes 65568 | tf_op jit(solution)/shard_map/ppermute | solution.py:131
  70.8 8.4 %shard_map.97 = (f32[8,16,1024]{2,1,0:T(8,128)S(1)}, bf16[8,16,1024]{2,1,0:T(8,128)(2,1)S(1)}, f32[8,16,1024]{2,1,0:T(8,128)S(1)}, bf16[8,16,1024]{2,1,0:T(8,128)(2,1)S(1)}) custom-call(s32[32,16]{1,0:T(8,128)S(1)} %copy.13.refs_0_, s32[32]{0:T(128)S(1)} %copy-done.3, s32[4,16]{1,0:T(4,128)S(1)} %copy-done.2, f32[4,1024]{1,0:T(4,128)S(1)} %copy-done.1, ...), custom_call_target="tpu_custom_call" | custom-call | flops 402653184 | bytes 25165824 | tf_op jit(solution)/shard_map/pallas_call | solution.py:118
  79.2 0.8 collective-permute-start.12
  80.0 1.4 %collective-permute-start.14 = (bf16[8,16,1024]{2,1,0:T(8,128)(2,1)S(1)}, bf16[8,16,1024]{2,1,0:T(8,128)(2,1)S(1)}, u32[]{:S(2)}, u32[]{:S(2)}) collective-permute-start(bf16[8,16,1024]{2,1,0:T(8,128)(2,1)S(1)} %get-tuple-element.33), channel_id=1, source_target_pairs={{0,8},{4,12},{8,0},{12,4},{16,24},{20,28},{24,16},{28,20},{1,9},{5... | collective-permute-start | bytes 786440 | tf_op jit(solution)/shard_map/ppermute | solution.py:131
  81.3 4.3 %collective-permute-done.12 = bf16[8,16,1024]{2,1,0:T(8,128)(2,1)S(1)} collective-permute-done((bf16[8,16,1024]{2,1,0:T(8,128)(2,1)S(1)}, bf16[8,16,1024]{2,1,0:T(8,128)(2,1)S(1)}, u32[]{:S(2)}, u32[]{:S(2)}) %collective-permute-start.12) | collective-permute-done | bytes 262176 | tf_op jit(solution)/shard_map/ppermute | solution.py:131
  85.7 0.8 collective-permute-start.13
  86.5 1.9 %collective-permute-done.14 = bf16[8,16,1024]{2,1,0:T(8,128)(2,1)S(1)} collective-permute-done((bf16[8,16,1024]{2,1,0:T(8,128)(2,1)S(1)}, bf16[8,16,1024]{2,1,0:T(8,128)(2,1)S(1)}, u32[]{:S(2)}, u32[]{:S(2)}) %collective-permute-start.14) | collective-permute-done | bytes 262176 | tf_op jit(solution)/shard_map/ppermute | solution.py:131
  88.4 1.6 %collective-permute-start.15 = (bf16[4,16,1024]{2,1,0:T(8,128)(2,1)S(1)}, bf16[4,16,1024]{2,1,0:T(8,128)(2,1)S(1)}, u32[]{:S(2)}, u32[]{:S(2)}) collective-permute-start(bf16[4,16,1024]{2,1,0:T(8,128)(2,1)S(1)} %get-tuple-element.46), channel_id=1, source_target_pairs={{0,16},{4,20},{8,24},{12,28},{16,0},{20,4},{24,8},{28,12},{1,17},{... | collective-permute-start | bytes 393224 | tf_op jit(solution)/shard_map/ppermute | solution.py:131
  90.0 0.7 collective-permute-done.13
  90.8 2.2 %collective-permute-start.16 = (bf16[2,16,1024]{2,1,0:T(8,128)(2,1)S(1)}, bf16[2,16,1024]{2,1,0:T(8,128)(2,1)S(1)}, u32[]{:S(2)}, u32[]{:S(2)}) collective-permute-start(bf16[2,16,1024]{2,1,0:T(8,128)(2,1)S(1)} %get-tuple-element.62), channel_id=1, source_target_pairs={{0,16},{4,20},{8,24},{12,28},{16,0},{20,4},{24,8},{28,12},{1,17},{... | collective-permute-start | bytes 196616 | tf_op jit(solution)/shard_map/ppermute | solution.py:131
  92.9 2.7 %collective-permute-done.15 = bf16[4,16,1024]{2,1,0:T(8,128)(2,1)S(1)} collective-permute-done((bf16[4,16,1024]{2,1,0:T(8,128)(2,1)S(1)}, bf16[4,16,1024]{2,1,0:T(8,128)(2,1)S(1)}, u32[]{:S(2)}, u32[]{:S(2)}) %collective-permute-start.15) | collective-permute-done | bytes 131104 | tf_op jit(solution)/shard_map/ppermute | solution.py:131
  95.7 0.4 collective-permute-start.17
  96.2 0.9 collective-permute-done.16.refs_5_
  97.1 3.3 %collective-permute-done.17.refs_6_ = bf16[2,16,1024]{2,1,0:T(8,128)(2,1)S(1)} collective-permute-done((bf16[2,16,1024]{2,1,0:T(8,128)(2,1)S(1)}, bf16[2,16,1024]{2,1,0:T(8,128)(2,1)S(1)}, u32[]{:S(2)}, u32[]{:S(2)}) %collective-permute-start.17) | collective-permute-done | bytes 65568 | tf_op jit(solution)/shard_map/ppermute | solution.py:131
  100.4 8.4 %shard_map.98 = (f32[8,16,1024]{2,1,0:T(8,128)S(1)}, bf16[8,16,1024]{2,1,0:T(8,128)(2,1)S(1)}, f32[8,16,1024]{2,1,0:T(8,128)S(1)}, bf16[8,16,1024]{2,1,0:T(8,128)(2,1)S(1)}) custom-call(s32[32,16]{1,0:T(8,128)S(1)} %copy.13.refs_0_, s32[32]{0:T(128)S(1)} %copy-done.3, s32[4,16]{1,0:T(4,128)S(1)} %copy-done.2, f32[4,1024]{1,0:T(4,128)S(1)} %copy-done.1, ...), custom_call_target="tpu_custom_call" | custom-call | flops 402653184 | bytes 25165824 | tf_op jit(solution)/shard_map/pallas_call | solution.py:118
  108.7 0.2 collective-permute-start.18
  109.0 0.9 collective-permute-start.20
  109.9 5.4 %collective-permute-done.18 = bf16[8,16,1024]{2,1,0:T(8,128)(2,1)S(1)} collective-permute-done((bf16[8,16,1024]{2,1,0:T(8,128)(2,1)S(1)}, bf16[8,16,1024]{2,1,0:T(8,128)(2,1)S(1)}, u32[]{:S(2)}, u32[]{:S(2)}) %collective-permute-start.18) | collective-permute-done | bytes 262176 | tf_op jit(solution)/shard_map/ppermute | solution.py:131
  115.3 0.1 add_convert_fusion.1
  115.4 0.1 collective-permute-start.19
  115.5 0.1 add_convert_fusion
  115.5 3.3 %collective-permute-start.21 = (bf16[4,16,1024]{2,1,0:T(8,128)(2,1)S(1)}, bf16[4,16,1024]{2,1,0:T(8,128)(2,1)S(1)}, u32[]{:S(2)}, u32[]{:S(2)}) collective-permute-start(bf16[4,16,1024]{2,1,0:T(8,128)(2,1)S(1)} %get-tuple-element.42), channel_id=1, source_target_pairs={{0,16},{4,20},{8,24},{12,28},{16,0},{20,4},{24,8},{28,12},{1,17},{... | collective-permute-start | bytes 393224 | tf_op jit(solution)/shard_map/ppermute | solution.py:131
  118.8 1.6 %collective-permute-done.19 = bf16[4,16,1024]{2,1,0:T(8,128)(2,1)S(1)} collective-permute-done((bf16[4,16,1024]{2,1,0:T(8,128)(2,1)S(1)}, bf16[4,16,1024]{2,1,0:T(8,128)(2,1)S(1)}, u32[]{:S(2)}, u32[]{:S(2)}) %collective-permute-start.19) | collective-permute-done | bytes 131104 | tf_op jit(solution)/shard_map/ppermute | solution.py:131
  120.4 1.3 collective-permute-start.22
  121.7 1.4 %collective-permute-done.21 = bf16[4,16,1024]{2,1,0:T(8,128)(2,1)S(1)} collective-permute-done((bf16[4,16,1024]{2,1,0:T(8,128)(2,1)S(1)}, bf16[4,16,1024]{2,1,0:T(8,128)(2,1)S(1)}, u32[]{:S(2)}, u32[]{:S(2)}) %collective-permute-start.21) | collective-permute-done | bytes 131104 | tf_op jit(solution)/shard_map/ppermute | solution.py:131
  123.2 1.5 %collective-permute-start.23 = (bf16[2,16,1024]{2,1,0:T(8,128)(2,1)S(1)}, bf16[2,16,1024]{2,1,0:T(8,128)(2,1)S(1)}, u32[]{:S(2)}, u32[]{:S(2)}) collective-permute-start(bf16[2,16,1024]{2,1,0:T(8,128)(2,1)S(1)} %get-tuple-element.59), channel_id=1, source_target_pairs={{0,4},{4,0},{8,12},{12,8},{16,20},{20,16},{24,28},{28,24},{1,5},{5... | collective-permute-start | bytes 196616 | tf_op jit(solution)/shard_map/ppermute | solution.py:131
  124.7 1.4 %collective-permute-done.22 = bf16[2,16,1024]{2,1,0:T(8,128)(2,1)S(1)} collective-permute-done((bf16[2,16,1024]{2,1,0:T(8,128)(2,1)S(1)}, bf16[2,16,1024]{2,1,0:T(8,128)(2,1)S(1)}, u32[]{:S(2)}, u32[]{:S(2)}) %collective-permute-start.22) | collective-permute-done | bytes 65568 | tf_op jit(solution)/shard_map/ppermute | solution.py:131
  126.1 1.4 %collective-permute-done.23 = bf16[2,16,1024]{2,1,0:T(8,128)(2,1)S(1)} collective-permute-done((bf16[2,16,1024]{2,1,0:T(8,128)(2,1)S(1)}, bf16[2,16,1024]{2,1,0:T(8,128)(2,1)S(1)}, u32[]{:S(2)}, u32[]{:S(2)}) %collective-permute-start.23) | collective-permute-done | bytes 65568 | tf_op jit(solution)/shard_map/ppermute | solution.py:131
  127.5 0.8 multiply_reduce_fusion
  128.3 1.5 %collective-permute-start.25 = (f32[4,1024]{1,0:T(4,128)S(1)}, f32[4,1024]{1,0:T(4,128)S(1)}, u32[]{:S(2)}, u32[]{:S(2)}) collective-permute-start(f32[4,1024]{1,0:T(4,128)S(1)} %get-tuple-element.38), channel_id=1, source_target_pairs={{0,2},{1,3},{2,0},{3,1},{4,6},{5,7},{6,4},{7,5},{8,10},{9,11},{10,... | collective-permute-start | bytes 49160 | tf_op jit(solution)/shard_map/ppermute | solution.py:227
  129.8 0.3 collective-permute-start.24
  130.2 1.4 %collective-permute-done.26 = f32[4,1024]{1,0:T(4,128)S(1)} collective-permute-done((f32[4,1024]{1,0:T(4,128)S(1)}, f32[4,1024]{1,0:T(4,128)S(1)}, u32[]{:S(2)}, u32[]{:S(2)}) %collective-permute-start.26) | collective-permute-done | bytes 16416 | tf_op jit(solution)/shard_map/ppermute | solution.py:227
  131.6 0.5 collective-permute-done.25
  132.1 0.6 add_multiply_fusion
  (26 shorter events, 0.4 us)
Async XLA Ops:
  1.4 1.0 copy-start
  2.4 0.7 copy-start.1
  3.1 0.7 copy-start.2
  3.8 0.7 copy-start.3
  16.2 9.3 %collective-permute-start = (bf16[8,16,1024]{2,1,0:T(8,128)(2,1)S(1)}, bf16[8,16,1024]{2,1,0:T(8,128)(2,1)S(1)}, u32[]{:S(2)}, u32[]{:S(2)}) collective-permute-start(bf16[8,16,1024]{2,1,0:T(8,128)(2,1)S(1)} %get-tuple-element.21), channel_id=1, source_target_pairs={{0,4},{4,0},{8,12},{12,8},{16,20},{20,16},{24,28},{28,24},{1,5},{5... | collective-permute-start | bytes 786440 | tf_op jit(solution)/shard_map/ppermute | solution.py:131
  19.2 8.2 %collective-permute-start.2 = (bf16[8,16,1024]{2,1,0:T(8,128)(2,1)S(1)}, bf16[8,16,1024]{2,1,0:T(8,128)(2,1)S(1)}, u32[]{:S(2)}, u32[]{:S(2)}) collective-permute-start(bf16[8,16,1024]{2,1,0:T(8,128)(2,1)S(1)} %get-tuple-element.23), channel_id=1, source_target_pairs={{0,8},{4,12},{8,0},{12,4},{16,24},{20,28},{24,16},{28,20},{1,9},{5... | collective-permute-start | bytes 786440 | tf_op jit(solution)/shard_map/ppermute | solution.py:131
  25.6 6.2 %collective-permute-start.1 = (bf16[4,16,1024]{2,1,0:T(8,128)(2,1)S(1)}, bf16[4,16,1024]{2,1,0:T(8,128)(2,1)S(1)}, u32[]{:S(2)}, u32[]{:S(2)}) collective-permute-start(bf16[4,16,1024]{2,1,0:T(8,128)(2,1)S(1)} %get-tuple-element.52), channel_id=1, source_target_pairs={{0,8},{4,12},{8,0},{12,4},{16,24},{20,28},{24,16},{28,20},{1,9},{5... | collective-permute-start | bytes 393224 | tf_op jit(solution)/shard_map/ppermute | solution.py:131
  27.5 9.3 %collective-permute-start.3 = (bf16[4,16,1024]{2,1,0:T(8,128)(2,1)S(1)}, bf16[4,16,1024]{2,1,0:T(8,128)(2,1)S(1)}, u32[]{:S(2)}, u32[]{:S(2)}) collective-permute-start(bf16[4,16,1024]{2,1,0:T(8,128)(2,1)S(1)} %get-tuple-element.54), channel_id=1, source_target_pairs={{0,16},{4,20},{8,24},{12,28},{16,0},{20,4},{24,8},{28,12},{1,17},{... | collective-permute-start | bytes 393224 | tf_op jit(solution)/shard_map/ppermute | solution.py:131
  31.8 6.6 %collective-permute-start.4 = (bf16[2,16,1024]{2,1,0:T(8,128)(2,1)S(1)}, bf16[2,16,1024]{2,1,0:T(8,128)(2,1)S(1)}, u32[]{:S(2)}, u32[]{:S(2)}) collective-permute-start(bf16[2,16,1024]{2,1,0:T(8,128)(2,1)S(1)} %get-tuple-element.70), channel_id=1, source_target_pairs={{0,16},{4,20},{8,24},{12,28},{16,0},{20,4},{24,8},{28,12},{1,17},{... | collective-permute-start | bytes 196616 | tf_op jit(solution)/shard_map/ppermute | solution.py:131
  36.9 4.3 %collective-permute-start.5 = (bf16[2,16,1024]{2,1,0:T(8,128)(2,1)S(1)}, bf16[2,16,1024]{2,1,0:T(8,128)(2,1)S(1)}, u32[]{:S(2)}, u32[]{:S(2)}) collective-permute-start(bf16[2,16,1024]{2,1,0:T(8,128)(2,1)S(1)} %get-tuple-element.68), channel_id=1, source_target_pairs={{0,4},{4,0},{8,12},{12,8},{16,20},{20,16},{24,28},{28,24},{1,5},{5... | collective-permute-start | bytes 196616 | tf_op jit(solution)/shard_map/ppermute | solution.py:131
  49.6 6.4 %collective-permute-start.6 = (bf16[8,16,1024]{2,1,0:T(8,128)(2,1)S(1)}, bf16[8,16,1024]{2,1,0:T(8,128)(2,1)S(1)}, u32[]{:S(2)}, u32[]{:S(2)}) collective-permute-start(bf16[8,16,1024]{2,1,0:T(8,128)(2,1)S(1)} %get-tuple-element.27), channel_id=1, source_target_pairs={{0,4},{4,0},{8,12},{12,8},{16,20},{20,16},{24,28},{28,24},{1,5},{5... | collective-permute-start | bytes 786440 | tf_op jit(solution)/shard_map/ppermute | solution.py:131
  51.1 7.8 %collective-permute-start.8 = (bf16[8,16,1024]{2,1,0:T(8,128)(2,1)S(1)}, bf16[8,16,1024]{2,1,0:T(8,128)(2,1)S(1)}, u32[]{:S(2)}, u32[]{:S(2)}) collective-permute-start(bf16[8,16,1024]{2,1,0:T(8,128)(2,1)S(1)} %get-tuple-element.29), channel_id=1, source_target_pairs={{0,8},{4,12},{8,0},{12,4},{16,24},{20,28},{24,16},{28,20},{1,9},{5... | collective-permute-start | bytes 786440 | tf_op jit(solution)/shard_map/ppermute | solution.py:131
  56.0 5.7 %collective-permute-start.7 = (bf16[4,16,1024]{2,1,0:T(8,128)(2,1)S(1)}, bf16[4,16,1024]{2,1,0:T(8,128)(2,1)S(1)}, u32[]{:S(2)}, u32[]{:S(2)}) collective-permute-start(bf16[4,16,1024]{2,1,0:T(8,128)(2,1)S(1)} %get-tuple-element.48), channel_id=1, source_target_pairs={{0,8},{4,12},{8,0},{12,4},{16,24},{20,28},{24,16},{28,20},{1,9},{5... | collective-permute-start | bytes 393224 | tf_op jit(solution)/shard_map/ppermute | solution.py:131
  59.0 7.5 %collective-permute-start.9 = (bf16[4,16,1024]{2,1,0:T(8,128)(2,1)S(1)}, bf16[4,16,1024]{2,1,0:T(8,128)(2,1)S(1)}, u32[]{:S(2)}, u32[]{:S(2)}) collective-permute-start(bf16[4,16,1024]{2,1,0:T(8,128)(2,1)S(1)} %get-tuple-element.50), channel_id=1, source_target_pairs={{0,16},{4,20},{8,24},{12,28},{16,0},{20,4},{24,8},{28,12},{1,17},{... | collective-permute-start | bytes 393224 | tf_op jit(solution)/shard_map/ppermute | solution.py:131
  61.8 5.5 %collective-permute-start.10 = (bf16[2,16,1024]{2,1,0:T(8,128)(2,1)S(1)}, bf16[2,16,1024]{2,1,0:T(8,128)(2,1)S(1)}, u32[]{:S(2)}, u32[]{:S(2)}) collective-permute-start(bf16[2,16,1024]{2,1,0:T(8,128)(2,1)S(1)} %get-tuple-element.66), channel_id=1, source_target_pairs={{0,16},{4,20},{8,24},{12,28},{16,0},{20,4},{24,8},{28,12},{1,17},{... | collective-permute-start | bytes 196616 | tf_op jit(solution)/shard_map/ppermute | solution.py:131
  66.5 4.3 %collective-permute-start.11 = (bf16[2,16,1024]{2,1,0:T(8,128)(2,1)S(1)}, bf16[2,16,1024]{2,1,0:T(8,128)(2,1)S(1)}, u32[]{:S(2)}, u32[]{:S(2)}) collective-permute-start(bf16[2,16,1024]{2,1,0:T(8,128)(2,1)S(1)} %get-tuple-element.64), channel_id=1, source_target_pairs={{0,4},{4,0},{8,12},{12,8},{16,20},{20,16},{24,28},{28,24},{1,5},{5... | collective-permute-start | bytes 196616 | tf_op jit(solution)/shard_map/ppermute | solution.py:131
  79.2 6.4 %collective-permute-start.12 = (bf16[8,16,1024]{2,1,0:T(8,128)(2,1)S(1)}, bf16[8,16,1024]{2,1,0:T(8,128)(2,1)S(1)}, u32[]{:S(2)}, u32[]{:S(2)}) collective-permute-start(bf16[8,16,1024]{2,1,0:T(8,128)(2,1)S(1)} %get-tuple-element.31), channel_id=1, source_target_pairs={{0,4},{4,0},{8,12},{12,8},{16,20},{20,16},{24,28},{28,24},{1,5},{5... | collective-permute-start | bytes 786440 | tf_op jit(solution)/shard_map/ppermute | solution.py:131
  80.0 8.4 %collective-permute-start.14 = (bf16[8,16,1024]{2,1,0:T(8,128)(2,1)S(1)}, bf16[8,16,1024]{2,1,0:T(8,128)(2,1)S(1)}, u32[]{:S(2)}, u32[]{:S(2)}) collective-permute-start(bf16[8,16,1024]{2,1,0:T(8,128)(2,1)S(1)} %get-tuple-element.33), channel_id=1, source_target_pairs={{0,8},{4,12},{8,0},{12,4},{16,24},{20,28},{24,16},{28,20},{1,9},{5... | collective-permute-start | bytes 786440 | tf_op jit(solution)/shard_map/ppermute | solution.py:131
  85.7 5.0 %collective-permute-start.13 = (bf16[4,16,1024]{2,1,0:T(8,128)(2,1)S(1)}, bf16[4,16,1024]{2,1,0:T(8,128)(2,1)S(1)}, u32[]{:S(2)}, u32[]{:S(2)}) collective-permute-start(bf16[4,16,1024]{2,1,0:T(8,128)(2,1)S(1)} %get-tuple-element.44), channel_id=1, source_target_pairs={{0,8},{4,12},{8,0},{12,4},{16,24},{20,28},{24,16},{28,20},{1,9},{5... | collective-permute-start | bytes 393224 | tf_op jit(solution)/shard_map/ppermute | solution.py:131
  88.4 7.2 %collective-permute-start.15 = (bf16[4,16,1024]{2,1,0:T(8,128)(2,1)S(1)}, bf16[4,16,1024]{2,1,0:T(8,128)(2,1)S(1)}, u32[]{:S(2)}, u32[]{:S(2)}) collective-permute-start(bf16[4,16,1024]{2,1,0:T(8,128)(2,1)S(1)} %get-tuple-element.46), channel_id=1, source_target_pairs={{0,16},{4,20},{8,24},{12,28},{16,0},{20,4},{24,8},{28,12},{1,17},{... | collective-permute-start | bytes 393224 | tf_op jit(solution)/shard_map/ppermute | solution.py:131
  90.8 6.3 %collective-permute-start.16 = (bf16[2,16,1024]{2,1,0:T(8,128)(2,1)S(1)}, bf16[2,16,1024]{2,1,0:T(8,128)(2,1)S(1)}, u32[]{:S(2)}, u32[]{:S(2)}) collective-permute-start(bf16[2,16,1024]{2,1,0:T(8,128)(2,1)S(1)} %get-tuple-element.62), channel_id=1, source_target_pairs={{0,16},{4,20},{8,24},{12,28},{16,0},{20,4},{24,8},{28,12},{1,17},{... | collective-permute-start | bytes 196616 | tf_op jit(solution)/shard_map/ppermute | solution.py:131
  95.7 4.7 %collective-permute-start.17 = (bf16[2,16,1024]{2,1,0:T(8,128)(2,1)S(1)}, bf16[2,16,1024]{2,1,0:T(8,128)(2,1)S(1)}, u32[]{:S(2)}, u32[]{:S(2)}) collective-permute-start(bf16[2,16,1024]{2,1,0:T(8,128)(2,1)S(1)} %get-tuple-element.60), channel_id=1, source_target_pairs={{0,4},{4,0},{8,12},{12,8},{16,20},{20,16},{24,28},{28,24},{1,5},{5... | collective-permute-start | bytes 196616 | tf_op jit(solution)/shard_map/ppermute | solution.py:131
  96.2 31.4 %copy-start.4 = (bf16[4,16,1024]{2,1,0:T(8,128)(2,1)S(1)}, bf16[4,16,1024]{2,1,0:T(8,128)(2,1)}, u32[]{:S(2)}) copy-start(bf16[4,16,1024]{2,1,0:T(8,128)(2,1)} %param.9) | copy-start | bytes 393220
  108.7 6.6 %collective-permute-start.18 = (bf16[8,16,1024]{2,1,0:T(8,128)(2,1)S(1)}, bf16[8,16,1024]{2,1,0:T(8,128)(2,1)S(1)}, u32[]{:S(2)}, u32[]{:S(2)}) collective-permute-start(bf16[8,16,1024]{2,1,0:T(8,128)(2,1)S(1)} %get-tuple-element.35), channel_id=1, source_target_pairs={{0,4},{4,0},{8,12},{12,8},{16,20},{20,16},{24,28},{28,24},{1,5},{5... | collective-permute-start | bytes 786440 | tf_op jit(solution)/shard_map/ppermute | solution.py:131
  109.0 6.5 %collective-permute-start.20 = (bf16[8,16,1024]{2,1,0:T(8,128)(2,1)S(1)}, bf16[8,16,1024]{2,1,0:T(8,128)(2,1)S(1)}, u32[]{:S(2)}, u32[]{:S(2)}) collective-permute-start(bf16[8,16,1024]{2,1,0:T(8,128)(2,1)S(1)} %get-tuple-element.37), channel_id=1, source_target_pairs={{0,8},{4,12},{8,0},{12,4},{16,24},{20,28},{24,16},{28,20},{1,9},{5... | collective-permute-start | bytes 786440 | tf_op jit(solution)/shard_map/ppermute | solution.py:131
  115.4 5.0 %collective-permute-start.19 = (bf16[4,16,1024]{2,1,0:T(8,128)(2,1)S(1)}, bf16[4,16,1024]{2,1,0:T(8,128)(2,1)S(1)}, u32[]{:S(2)}, u32[]{:S(2)}) collective-permute-start(bf16[4,16,1024]{2,1,0:T(8,128)(2,1)S(1)} %get-tuple-element.40), channel_id=1, source_target_pairs={{0,8},{4,12},{8,0},{12,4},{16,24},{20,28},{24,16},{28,20},{1,9},{5... | collective-permute-start | bytes 393224 | tf_op jit(solution)/shard_map/ppermute | solution.py:131
  115.5 7.6 %collective-permute-start.21 = (bf16[4,16,1024]{2,1,0:T(8,128)(2,1)S(1)}, bf16[4,16,1024]{2,1,0:T(8,128)(2,1)S(1)}, u32[]{:S(2)}, u32[]{:S(2)}) collective-permute-start(bf16[4,16,1024]{2,1,0:T(8,128)(2,1)S(1)} %get-tuple-element.42), channel_id=1, source_target_pairs={{0,16},{4,20},{8,24},{12,28},{16,0},{20,4},{24,8},{28,12},{1,17},{... | collective-permute-start | bytes 393224 | tf_op jit(solution)/shard_map/ppermute | solution.py:131
  120.4 5.7 %collective-permute-start.22 = (bf16[2,16,1024]{2,1,0:T(8,128)(2,1)S(1)}, bf16[2,16,1024]{2,1,0:T(8,128)(2,1)S(1)}, u32[]{:S(2)}, u32[]{:S(2)}) collective-permute-start(bf16[2,16,1024]{2,1,0:T(8,128)(2,1)S(1)} %get-tuple-element.57), channel_id=1, source_target_pairs={{0,16},{4,20},{8,24},{12,28},{16,0},{20,4},{24,8},{28,12},{1,17},{... | collective-permute-start | bytes 196616 | tf_op jit(solution)/shard_map/ppermute | solution.py:131
  123.2 4.3 %collective-permute-start.23 = (bf16[2,16,1024]{2,1,0:T(8,128)(2,1)S(1)}, bf16[2,16,1024]{2,1,0:T(8,128)(2,1)S(1)}, u32[]{:S(2)}, u32[]{:S(2)}) collective-permute-start(bf16[2,16,1024]{2,1,0:T(8,128)(2,1)S(1)} %get-tuple-element.59), channel_id=1, source_target_pairs={{0,4},{4,0},{8,12},{12,8},{16,20},{20,16},{24,28},{28,24},{1,5},{5... | collective-permute-start | bytes 196616 | tf_op jit(solution)/shard_map/ppermute | solution.py:131
  128.3 3.3 %collective-permute-start.26 = (f32[4,1024]{1,0:T(4,128)S(1)}, f32[4,1024]{1,0:T(4,128)S(1)}, u32[]{:S(2)}, u32[]{:S(2)}) collective-permute-start(f32[4,1024]{1,0:T(4,128)S(1)} %get-tuple-element.38), channel_id=1, source_target_pairs={{0,3},{1,2},{2,1},{3,0},{4,7},{5,6},{6,5},{7,4},{8,11},{9,10},{10,... | collective-permute-start | bytes 49160 | tf_op jit(solution)/shard_map/ppermute | solution.py:227
  128.3 3.8 %collective-permute-start.25 = (f32[4,1024]{1,0:T(4,128)S(1)}, f32[4,1024]{1,0:T(4,128)S(1)}, u32[]{:S(2)}, u32[]{:S(2)}) collective-permute-start(f32[4,1024]{1,0:T(4,128)S(1)} %get-tuple-element.38), channel_id=1, source_target_pairs={{0,2},{1,3},{2,0},{3,1},{4,6},{5,7},{6,4},{7,5},{8,10},{9,11},{10,... | collective-permute-start | bytes 49160 | tf_op jit(solution)/shard_map/ppermute | solution.py:227
  129.8 2.3 %collective-permute-start.24 = (f32[4,1024]{1,0:T(4,128)S(1)}, f32[4,1024]{1,0:T(4,128)S(1)}, u32[]{:S(2)}, u32[]{:S(2)}) collective-permute-start(f32[4,1024]{1,0:T(4,128)S(1)} %get-tuple-element.38), channel_id=1, source_target_pairs={{0,1},{1,0},{2,3},{3,2},{4,5},{5,4},{6,7},{7,6},{8,9},{9,8},{10,11... | collective-permute-start | bytes 49160 | tf_op jit(solution)/shard_map/ppermute | solution.py:227

commit v2 on v1

--- a/solution.py
+++ b/solution.py
@@ -31,10 +31,10 @@
     cols_ref, owner_ref, ranks_ref, contrast_ref, base_ref = refs[:5]
     if first:
         u_from, v_from = refs[5:7]
-        outs, u_ref, v_ref, acc, u_sem, v_sem = refs[7:11], *refs[11:16]
+        outs, u_ref, v_ref, acc, u_sem, v_sem = refs[7:8], *refs[8:13]
     else:
-        arrived, u_ref, v_ref = refs[5:7], *refs[7:9]
-        outs, acc = refs[9:13], refs[13]
+        arrived, u_ref, v_ref = refs[5:6], *refs[6:8]
+        outs, acc = refs[8:9], refs[9]
     here = lax.axis_index("rows")
     half = plan[0][0]
     width = GROUP * rank_max
@@ -55,8 +55,8 @@
         if group == 0:
             field = base_ref[row]
             if not first:
-                part = arrived[0][row] if row < half else arrived[1][row - half]
-                field = field + contrast_ref[pl.ds(row, 1), :] * part.astype(jnp.float32)
+                part = arrived[0][row].astype(jnp.float32)
+                field = field + contrast_ref[pl.ds(row, 1), :] * part
             low = field.astype(jnp.bfloat16)
         piece = pl.ds(step * width, width)
         if first:
@@ -76,20 +76,9 @@
         sources = low.shape[0]
         for i in range(GROUP):
             slot = owner_ref[cols_ref[here * rows_dev + row, group * GROUP + i]]
-            rel = jnp.bitwise_xor(slot // rows_dev, here)
-            local = slot % rows_dev
-            place = jnp.where(
-                local < half,
-                spot(plan[0][1], rel) * half + local,
-                peers * half + spot(plan[1][1], rel) * (rows_dev - half) + local - half,
-            )
+            place = slot
             acc[place] += terms[i * sources : (i + 1) * sources]
-    base = 0
-    for part, (count, _) in enumerate(plan):
-        kept = peers * count // 2
-        outs[2 * part][...] = acc[base : base + kept]
-        outs[2 * part + 1][...] = acc[base + kept : base + 2 * kept].astype(jnp.bfloat16)
-        base += 2 * kept
+    outs[0][...] = acc[...].astype(jnp.bfloat16)
 
 
 def apply_tiles(plan, peers, cols, owner, ranks, contrast, base, arrived, u, v):
@@ -100,9 +89,7 @@
     smem = pl.BlockSpec(memory_space=pltpu.SMEM)
     vmem = pl.BlockSpec(memory_space=pltpu.VMEM)
     outs = []
-    for count, _ in plan:
-        outs.append(jax.ShapeDtypeStruct((peers * count // 2, sources, unknowns), jnp.float32))
-        outs.append(jax.ShapeDtypeStruct((peers * count // 2, sources, unknowns), jnp.bfloat16))
+    outs.append(jax.ShapeDtypeStruct((peers * rows_dev, sources, unknowns), jnp.bfloat16))
     scratch = [pltpu.VMEM((peers * rows_dev, sources, unknowns), jnp.float32)]
     if first:
         specs = [vmem] * 2 + [pl.BlockSpec(memory_space=pl.ANY)] * 2
@@ -111,7 +98,7 @@
         scratch += [pltpu.SemaphoreType.DMA((steps,))] * 2
         extra = []
     else:
-        specs = [vmem] * 6
+        specs = [vmem] * 5
         u, v = (pltpu.with_memory_space_constraint(x, pltpu.VMEM) for x in (u, v))
         extra = list(arrived)
     flops = 4 * u.shape[0] * unknowns * sources
@@ -124,7 +111,7 @@
         compiler_params=pltpu.CompilerParams(vmem_limit_bytes=24 * 1024 * 1024),
         cost_estimate=pl.CostEstimate(flops=flops, bytes_accessed=4 * u.size, transcendentals=0),
     )(cols, owner, ranks, contrast, base, *extra, u, v)
-    return got[:4], got[4:]
+    return got[:1], got[1:]
 
 
 def swap(x, bit, peers):
@@ -140,21 +127,12 @@
     base, arrived = misfit, None
     for step in range(APPS):
         got, held = apply_tiles(
-            plan, peers, tile_cols, owner_slot, ranks, contrast, base, arrived, *factors
+            plan, peers, tile_cols, owner_slot, ranks, contrast, misfit, arrived, *factors
         )
         factors = held or factors
-        keeps, goes = [got[0], got[2]], [got[1], got[3]]
-        for level in range(len(plan[0][1])):
-            came = [swap(goes[p], plan[p][1][level], peers) for p in range(2)]
-            if level == len(plan[0][1]) - 1:
-                break
-            for p in range(2):
-                mid = keeps[p].shape[0] // 2
-                goes[p] = (keeps[p][mid:] + came[p][mid:].astype(jnp.float32)).astype(jnp.bfloat16)
-                keeps[p] = keeps[p][:mid] + came[p][:mid].astype(jnp.float32)
-        base = misfit + contrast[:, None, :] * jnp.concatenate(keeps, axis=0)
-        arrived = came
-    return base + contrast[:, None, :] * jnp.concatenate(arrived, axis=0).astype(jnp.float32)
+        total = lax.psum_scatter(got[0], "rows", scatter_dimension=0, tiled=True)
+        arrived = (total,)
+    return misfit + contrast[:, None, :] * total.astype(jnp.float32)
 
 
 def route_tiles(tile_cols, owner_slot, rows_dev, peers):

time: 133 us -> 359 us (2.70)
  waiting for transfers between devices: 53.3 us -> 256 us
  local copies, waits for them, and re-layouts: 3.78 us -> 43 us
  starting transfers between devices: 35.8 us -> 2.21 us
  between operations: 0.8 us -> 13.8 us
  Pallas kernels: 36.8 us -> 40.9 us
    reduce_scatter x0 -> x4, waiting for transfers between devices: none -> 254 us  [slot_sums(): total = lax.psum_scatter(got[0], 'rows', scatter_dimension=0, tiled=True)]
    ppermute x24 -> x0, waiting for transfers between devices: 51.4 us -> none  [swap(): return lax.ppermute(x, 'rows', [(i, i ^ 1 << bit) for i in range(peers)])]
    unnamed x11 -> x41, local copies, waits for them, and re-layouts: 3.78 us -> 43 us
    ppermute x24 -> x0, starting transfers between devices: 34 us -> none  [swap(): return lax.ppermute(x, 'rows', [(i, i ^ 1 << bit) for i in range(peers)])]
    pallas_call x4, Pallas kernels: 36.8 us -> 40.9 us  [apply_tiles(): pl.pallas_call(functools.partial(tile_kernel, (rows_dev, tiles_row, rank_...]
  transfers between devices with their start and end apart: 27 -> 7, of which waited for: 22 -> 6; matrix products, arithmetic and copies ran while one was open for 1% -> 0% of each run, Pallas kernels for 0% -> 0%
where the time goes in v2:
time: 359 us; the launch traced here: 358 us
  waiting for transfers between devices  256 us (71%)
  local copies, waits for them, and re-layouts  43 us (12%)
  Pallas kernels  40.9 us (11%)
  between operations  13.8 us (4%)
    reduce_scatter x4, waiting for transfers between devices, slot_sums(): total = lax.psum_scatter(got[0], 'rows', scatter_dimension=0, tiled=True)  254 us
    unnamed x41, local copies, waits for them, and re-layouts  43 us
    pallas_call x4, Pallas kernels, apply_tiles(): pl.pallas_call(functools.partial(tile_kernel, (rows_dev, tiles_row, rank_...  40.9 us
  transfers between devices with their start and end apart: 7, of which 6 were waited for; matrix products, arithmetic and copies ran while one was open for 0% of the time, Pallas kernels for 0%

profile of v2, /device:TPU:0, one launch (start us, length us, event | category | flops | bytes accessed | tf_op | source)
XLA Modules:
  0.0 358.0 jit_solution(17860002415303639439)
XLA Ops:
  7.2 0.0 reduce-scatter.5.cloned.1.call-start
  7.2 0.8 copy.13.refs_0_
  8.0 0.0 copy-start.8
  8.0 0.9 copy-done.8
  8.9 0.0 copy-start.10
  8.9 0.7 copy-done.10
  9.7 0.0 copy-start.15
  9.7 0.7 copy-done.15
  10.3 0.0 copy-start.17
  10.3 0.7 copy-done.17
  11.0 0.0 copy-start.9
  11.0 0.0 copy-start.11
  11.0 0.0 copy-start.16
  11.0 0.0 copy-start.18
  11.0 12.8 %shard_map.95 = (bf16[32,16,1024]{2,1,0:T(8,128)(2,1)}, bf16[6144,1024]{1,0:T(8,128)(2,1)S(1)}, bf16[6144,1024]{1,0:T(8,128)(2,1)S(1)}) custom-call(s32[32,16]{1,0:T(8,128)S(1)} %copy.13.refs_0_, s32[32]{0:T(128)S(1)} %copy-done.17, s32[4,16]{1,0:T(4,128)S(1)} %copy-done.15, f32[4,1024]{1,0:T(4,128)S(1)} %copy-done.10, f32[4,16,1024]{2,1,0:T(8,128)S(1)} %copy-done.8, ...), custom_call_target="tpu_custom_call" | custom-call | flops 402653184 | bytes 25165824 | tf_op jit(solution)/shard_map/pallas_call | solution.py:105
  23.8 0.0 copy-start
  23.8 4.5 %copy-done = bf16[6144,1024]{1,0:T(8,128)(2,1)} copy-done((bf16[6144,1024]{1,0:T(8,128)(2,1)}, bf16[6144,1024]{1,0:T(8,128)(2,1)S(1)}, u32[]{:S(2)}) %copy-start) | copy-done | bytes 12582936
  28.4 0.0 copy-start.4
  28.4 4.5 %copy-done.4 = bf16[6144,1024]{1,0:T(8,128)(2,1)} copy-done((bf16[6144,1024]{1,0:T(8,128)(2,1)}, bf16[6144,1024]{1,0:T(8,128)(2,1)S(1)}, u32[]{:S(2)}) %copy-start.4) | copy-done | bytes 12582936
  32.9 0.0 reduce-scatter.5.cloned.1.call-update
  32.9 0.0 reduce-scatter.7.cloned.1.call-start
  32.9 66.3 %reduce-scatter.5.cloned.1.call-done.refs_5_ = bf16[4,16,1024]{2,1,0:T(8,128)(2,1)} async-done(((bf16[32,16,1024]{2,1,0:T(8,128)(2,1)}), bf16[4,16,1024]{2,1,0:T(8,128)(2,1)}) %reduce-scatter.5.cloned.1.call-update) | async-done | bytes 131088 | tf_op jit(solution)/shard_map/reduce_scatter | solution.py:133
  99.2 0.0 copy-done.9
  99.2 0.0 copy-done.11
  99.2 0.0 copy-done.16
  99.2 0.0 copy-done.18
  99.2 0.0 copy-start.1
  99.2 4.6 %copy-done.1 = bf16[6144,1024]{1,0:T(8,128)(2,1)S(1)} copy-done((bf16[6144,1024]{1,0:T(8,128)(2,1)S(1)}, bf16[6144,1024]{1,0:T(8,128)(2,1)}, u32[]{:S(2)}) %copy-start.1) | copy-done | bytes 12582936
  103.8 0.0 copy-start.5
  103.8 4.6 %copy-done.5 = bf16[6144,1024]{1,0:T(8,128)(2,1)S(1)} copy-done((bf16[6144,1024]{1,0:T(8,128)(2,1)S(1)}, bf16[6144,1024]{1,0:T(8,128)(2,1)}, u32[]{:S(2)}) %copy-start.5) | copy-done | bytes 12582936
  108.4 0.0 copy-start.13
  108.4 0.9 copy-done.13
  109.3 9.4 %shard_map.96 = bf16[32,16,1024]{2,1,0:T(8,128)(2,1)} custom-call(s32[32,16]{1,0:T(8,128)S(1)} %copy.13.refs_0_, s32[32]{0:T(128)S(1)} %copy-done.18, s32[4,16]{1,0:T(4,128)S(1)} %copy-done.16, f32[4,1024]{1,0:T(4,128)S(1)} %copy-done.11, f32[4,16,1024]{2,1,0:T(8,128)S(1)} %copy-done.9, bf16[4,16,1024]{2,1,0:T(8,128)(2,1)S(1)} %copy-done.13, ...), custom_call_target="tpu_custom_call" | custom-call | flops 402653184 | bytes 25165824 | tf_op jit(solution)/shard_map/pallas_call | solution.py:105
  118.7 0.0 reduce-scatter.7.cloned.1.call-update
  118.7 0.2 reduce-scatter.9.cloned.1.call-start
  118.9 62.3 %reduce-scatter.7.cloned.1.call-done.refs_5_ = bf16[4,16,1024]{2,1,0:T(8,128)(2,1)} async-done(((bf16[32,16,1024]{2,1,0:T(8,128)(2,1)}), bf16[4,16,1024]{2,1,0:T(8,128)(2,1)}) %reduce-scatter.7.cloned.1.call-update) | async-done | bytes 131088 | tf_op jit(solution)/shard_map/reduce_scatter | solution.py:133
  181.2 0.0 copy-start.2
  181.2 4.6 %copy-done.2 = bf16[6144,1024]{1,0:T(8,128)(2,1)S(1)} copy-done((bf16[6144,1024]{1,0:T(8,128)(2,1)S(1)}, bf16[6144,1024]{1,0:T(8,128)(2,1)}, u32[]{:S(2)}) %copy-start.2) | copy-done | bytes 12582936
  185.8 0.0 copy-start.6
  185.8 4.6 %copy-done.6 = bf16[6144,1024]{1,0:T(8,128)(2,1)S(1)} copy-done((bf16[6144,1024]{1,0:T(8,128)(2,1)S(1)}, bf16[6144,1024]{1,0:T(8,128)(2,1)}, u32[]{:S(2)}) %copy-start.6) | copy-done | bytes 12582936
  190.4 0.0 copy-start.14
  190.4 0.9 copy-done.14
  191.3 9.4 %shard_map.97 = bf16[32,16,1024]{2,1,0:T(8,128)(2,1)} custom-call(s32[32,16]{1,0:T(8,128)S(1)} %copy.13.refs_0_, s32[32]{0:T(128)S(1)} %copy-done.18, s32[4,16]{1,0:T(4,128)S(1)} %copy-done.16, f32[4,1024]{1,0:T(4,128)S(1)} %copy-done.11, f32[4,16,1024]{2,1,0:T(8,128)S(1)} %copy-done.9, bf16[4,16,1024]{2,1,0:T(8,128)(2,1)S(1)} %copy-done.14, ...), custom_call_target="tpu_custom_call" | custom-call | flops 402653184 | bytes 25165824 | tf_op jit(solution)/shard_map/pallas_call | solution.py:105
  200.7 0.0 copy-start.19
  200.7 0.0 reduce-scatter.9.cloned.1.call-update
  200.7 0.0 reduce-scatter.11.cloned.1.call-start
  200.8 62.5 %reduce-scatter.9.cloned.1.call-done.refs_5_ = bf16[4,16,1024]{2,1,0:T(8,128)(2,1)} async-done(((bf16[32,16,1024]{2,1,0:T(8,128)(2,1)}), bf16[4,16,1024]{2,1,0:T(8,128)(2,1)}) %reduce-scatter.9.cloned.1.call-update) | async-done | bytes 131088 | tf_op jit(solution)/shard_map/reduce_scatter | solution.py:133
  263.3 0.0 copy-start.3
  263.3 4.6 %copy-done.3 = bf16[6144,1024]{1,0:T(8,128)(2,1)S(1)} copy-done((bf16[6144,1024]{1,0:T(8,128)(2,1)S(1)}, bf16[6144,1024]{1,0:T(8,128)(2,1)}, u32[]{:S(2)}) %copy-start.3) | copy-done | bytes 12582936
  267.9 0.0 copy-start.7
  267.9 4.6 %copy-done.7 = bf16[6144,1024]{1,0:T(8,128)(2,1)S(1)} copy-done((bf16[6144,1024]{1,0:T(8,128)(2,1)S(1)}, bf16[6144,1024]{1,0:T(8,128)(2,1)}, u32[]{:S(2)}) %copy-start.7) | copy-done | bytes 12582936
  272.4 0.9 copy-done.12
  273.3 9.3 %shard_map.98 = bf16[32,16,1024]{2,1,0:T(8,128)(2,1)} custom-call(s32[32,16]{1,0:T(8,128)S(1)} %copy.13.refs_0_, s32[32]{0:T(128)S(1)} %copy-done.18, s32[4,16]{1,0:T(4,128)S(1)} %copy-done.16, f32[4,1024]{1,0:T(4,128)S(1)} %copy-done.11, f32[4,16,1024]{2,1,0:T(8,128)S(1)} %copy-done.9, bf16[4,16,1024]{2,1,0:T(8,128)(2,1)S(1)} %copy-done.12, ...), custom_call_target="tpu_custom_call" | custom-call | flops 402653184 | bytes 25165824 | tf_op jit(solution)/shard_map/pallas_call | solution.py:105
  282.7 0.0 reduce-scatter.11.cloned.1.call-update
  282.7 62.7 %reduce-scatter.11.cloned.1.call-done = bf16[4,16,1024]{2,1,0:T(8,128)(2,1)} async-done(((bf16[32,16,1024]{2,1,0:T(8,128)(2,1)}), bf16[4,16,1024]{2,1,0:T(8,128)(2,1)}) %reduce-scatter.11.cloned.1.call-update) | async-done | bytes 131088 | tf_op jit(solution)/shard_map/reduce_scatter | solution.py:133
  345.4 0.0 copy-done.19
  345.4 1.7 multiply_reduce_fusion
  347.1 0.0 collective-permute-start.2
  347.1 1.5 collective-permute-start.1
  348.5 0.4 collective-permute-start
  348.9 1.5 collective-permute-done.2
  350.4 0.4 collective-permute-done.1
  350.8 0.0 collective-permute-done
  350.8 0.6 add_multiply_fusion
  (1 shorter events, 0.0 us)
Async XLA Ops:
  7.2 92.0 %reduce-scatter.5.cloned.1.call-start = ((), (), s32[]{:S(2)}) async-start(), calls=%async_computation.4 | async-start | bytes 1179648 | tf_op jit(solution)/shard_map/reduce_scatter | solution.py:133
  8.0 1.0 copy-start.8
  8.9 0.7 copy-start.10
  9.7 0.7 copy-start.15
  10.3 0.7 copy-start.17
  11.0 88.2 %copy-start.9 = (f32[4,16,1024]{2,1,0:T(8,128)S(1)}, f32[4,16,1024]{2,1,0:T(8,128)}, u32[]{:S(2)}) copy-start(f32[4,16,1024]{2,1,0:T(8,128)} %refs_4_.7) | copy-start | bytes 786436
  11.0 88.2 %copy-start.11 = (f32[4,1024]{1,0:T(4,128)S(1)}, f32[4,1024]{1,0:T(4,128)}, u32[]{:S(2)}) copy-start(f32[4,1024]{1,0:T(4,128)} %refs_3_.7) | copy-start | bytes 49156
  11.0 88.2 %copy-start.16 = (s32[4,16]{1,0:T(4,128)S(1)}, s32[4,16]{1,0:T(4,128)}, u32[]{:S(2)}) copy-start(s32[4,16]{1,0:T(4,128)} %refs_2_.7) | copy-start | bytes 772
  11.0 88.2 %copy-start.18 = (s32[32]{0:T(128)S(1)}, s32[32]{0:T(128)}, u32[]{:S(2)}) copy-start(s32[32]{0:T(128)} %refs_1_.7) | copy-start | bytes 388
  23.8 4.5 %copy-start = (bf16[6144,1024]{1,0:T(8,128)(2,1)}, bf16[6144,1024]{1,0:T(8,128)(2,1)S(1)}, u32[]{:S(2)}) copy-start(bf16[6144,1024]{1,0:T(8,128)(2,1)S(1)} %get-tuple-element.6.refs_6_) | copy-start | bytes 37748740
  28.4 4.5 %copy-start.4 = (bf16[6144,1024]{1,0:T(8,128)(2,1)}, bf16[6144,1024]{1,0:T(8,128)(2,1)S(1)}, u32[]{:S(2)}) copy-start(bf16[6144,1024]{1,0:T(8,128)(2,1)S(1)} %get-tuple-element.7.refs_7_) | copy-start | bytes 37748740
  32.9 148.4 %reduce-scatter.7.cloned.1.call-start = ((), (), s32[]{:S(2)}) async-start(), calls=%async_computation.5 | async-start | bytes 1179648 | tf_op jit(solution)/shard_map/reduce_scatter | solution.py:133
  99.2 4.6 %copy-start.1 = (bf16[6144,1024]{1,0:T(8,128)(2,1)S(1)}, bf16[6144,1024]{1,0:T(8,128)(2,1)}, u32[]{:S(2)}) copy-start(bf16[6144,1024]{1,0:T(8,128)(2,1)} %copy-done) | copy-start | bytes 37748740
  103.8 4.6 %copy-start.5 = (bf16[6144,1024]{1,0:T(8,128)(2,1)S(1)}, bf16[6144,1024]{1,0:T(8,128)(2,1)}, u32[]{:S(2)}) copy-start(bf16[6144,1024]{1,0:T(8,128)(2,1)} %copy-done.4) | copy-start | bytes 37748740
  108.4 0.9 copy-start.13
  118.7 144.6 %reduce-scatter.9.cloned.1.call-start = ((), (), s32[]{:S(2)}) async-start(), calls=%async_computation.6 | async-start | bytes 1179648 | tf_op jit(solution)/shard_map/reduce_scatter | solution.py:133
  181.2 4.6 %copy-start.2 = (bf16[6144,1024]{1,0:T(8,128)(2,1)S(1)}, bf16[6144,1024]{1,0:T(8,128)(2,1)}, u32[]{:S(2)}) copy-start(bf16[6144,1024]{1,0:T(8,128)(2,1)} %copy-done) | copy-start | bytes 37748740
  185.8 4.6 %copy-start.6 = (bf16[6144,1024]{1,0:T(8,128)(2,1)S(1)}, bf16[6144,1024]{1,0:T(8,128)(2,1)}, u32[]{:S(2)}) copy-start(bf16[6144,1024]{1,0:T(8,128)(2,1)} %copy-done.4) | copy-start | bytes 37748740
  190.4 0.9 copy-start.14
  200.7 144.7 %copy-start.19 = (bf16[4,16,1024]{2,1,0:T(8,128)(2,1)S(1)}, bf16[4,16,1024]{2,1,0:T(8,128)(2,1)}, u32[]{:S(2)}) copy-start(bf16[4,16,1024]{2,1,0:T(8,128)(2,1)} %param.9) | copy-start | bytes 393220
  200.7 144.7 %reduce-scatter.11.cloned.1.call-start = ((), (), s32[]{:S(2)}) async-start(), calls=%async_computation.7 | async-start | bytes 1179648 | tf_op jit(solution)/shard_map/reduce_scatter | solution.py:133
  263.3 4.6 %copy-start.3 = (bf16[6144,1024]{1,0:T(8,128)(2,1)S(1)}, bf16[6144,1024]{1,0:T(8,128)(2,1)}, u32[]{:S(2)}) copy-start(bf16[6144,1024]{1,0:T(8,128)(2,1)} %copy-done) | copy-start | bytes 37748740
  267.9 4.6 %copy-start.7 = (bf16[6144,1024]{1,0:T(8,128)(2,1)S(1)}, bf16[6144,1024]{1,0:T(8,128)(2,1)}, u32[]{:S(2)}) copy-start(bf16[6144,1024]{1,0:T(8,128)(2,1)} %copy-done.4) | copy-start | bytes 37748740
  272.4 0.9 copy-start.12
  347.1 3.3 collective-permute-start.2
  347.1 3.8 %collective-permute-start.1 = (f32[4,1024]{1,0:T(4,128)S(1)}, f32[4,1024]{1,0:T(4,128)S(1)}, u32[]{:S(2)}, u32[]{:S(2)}) collective-permute-start(f32[4,1024]{1,0:T(4,128)S(1)} %get-tuple-element.8), channel_id=1, source_target_pairs={{0,2},{1,3},{2,0},{3,1},{4,6},{5,7},{6,4},{7,5},{8,10},{9,11},{10,... | collective-permute-start | bytes 49160 | tf_op jit(solution)/shard_map/ppermute | solution.py:205
  348.5 2.3 collective-permute-start
Sparse Core Ops, SparseCore 0:
  33.0 66.1 reduce-scatter.4
  118.8 62.3 reduce-scatter.6
  200.8 62.3 reduce-scatter.8
  282.8 62.4 reduce-scatter.10

commit v3 on v0

v3 whole, which is shorter than its diff:
```python
import functools

import jax
import jax.numpy as jnp
from jax import lax
from jax.experimental import pallas as pl
from jax.experimental.pallas import tpu as pltpu
from jax.sharding import PartitionSpec as P

APPS = 4

def parts_of(unknowns, peers):
    bits = list(range(peers.bit_length() - 1))
    near, far = bits, bits[1:] + bits[:1]
    width = unknowns // 4
    return [(i * width, width, far if i == 3 else near) for i in range(4)]


def spot(order, rel):
    place = 0
    for bit in order:
        place = place * 2 + ((rel >> bit) & 1)
    return place


def in_order(order, peers):
    return sorted(range(peers), key=lambda rel: spot(order, rel))


def vmem(count):
    return [pl.BlockSpec(memory_space=pltpu.VMEM)] * count


def params():
    return pltpu.CompilerParams(vmem_limit_bytes=24 * 1024 * 1024)


def cost(rows, columns, sources):
    return pl.CostEstimate(
        flops=2 * rows * columns * sources, bytes_accessed=2 * rows * columns, transcendentals=0
    )


def in_vmem(x):
    return pltpu.with_memory_space_constraint(x, pltpu.VMEM)


def in_hbm(x):
    return pltpu.with_memory_space_constraint(x, pltpu.HBM)


def pick_rows(every, code, sources, rows_dev):
    row = code // rows_dev
    total = jnp.zeros((sources, every.shape[1]), jnp.float32)
    for index in range(rows_dev):
        mine = every[index * sources : (index + 1) * sources]
        total = total + jnp.where(row == index, mine, 0.0)
    return total


def by_slot(coeff, code, rows_dev):
    local = code % rows_dev
    low = [
        jnp.where(local == index, coeff, 0.0).astype(jnp.bfloat16) for index in range(rows_dev)
    ]
    return jnp.concatenate(low, axis=0)


def times_u(low, factors):
    return lax.dot_general(
        low, factors, (((1,), (1,)), ((), ())), preferred_element_type=jnp.float32
    )


def put_terms(lhs, v_ref, group, part, outs, rows_dev, peers):
    first, width, order = part
    deep = lhs.shape[1]
    terms = jnp.dot(
        lhs,
        v_ref[pl.ds(group * deep, deep), pl.ds(first, width)],
        preferred_element_type=jnp.float32,
    )
    place = spot(order, group)
    out = outs[place >= peers // 2]
    place = place % (peers // 2) * rows_dev
    out[place : place + rows_dev] = terms.reshape(rows_dev, -1, width).astype(out.dtype)


def start_kernel(dims, *refs):
    rows_dev, tiles_row, rank_max, peers, parts = dims
    cols_hbm, owner_hbm, ranks_hbm, misfit_hbm, u_hbm, v_hbm = refs[:6]
    u_ref, v_ref, code_ref = refs[6:9]
    outs = refs[9 : 9 + 2 * len(parts)]
    cols, owner, ranks, misfit, tile_at, code_at, rank_at, count, small, u_sem, v_sem = refs[
        9 + 2 * len(parts) :
    ]
    here = lax.axis_index("rows")
    tiles = rows_dev * tiles_row
    group_tiles = tiles // peers
    deep = group_tiles * rank_max
    sources = misfit.shape[1]
    copies = [
        pltpu.make_async_copy(whence, to, small.at[i])
        for i, (whence, to) in enumerate(
            zip((cols_hbm, owner_hbm, ranks_hbm, misfit_hbm), (cols, owner, ranks, misfit))
        )
    ]
    for copy in copies:
        copy.start()
    for rel in range(peers):
        count[rel] = 0
    for copy in copies[:3]:
        copy.wait()

    def sort_tile(tile, carry):
        row, k = lax.div(tile, tiles_row), lax.rem(tile, tiles_row)
        slot = owner[cols[k, here * rows_dev + row]]
        rel = jnp.bitwise_xor(lax.div(slot, rows_dev), here)
        at = rel * group_tiles + count[rel]
        count[rel] = count[rel] + 1
        tile_at[at] = tile
        code_at[at] = row * rows_dev + lax.rem(slot, rows_dev)
        rank_at[at] = ranks[row, k]
        return carry

    lax.fori_loop(0, tiles, sort_tile, 0)

    def load(whence, to, sem, group):
        def one(i, carry):
            at = group * group_tiles + i
            pltpu.make_async_copy(
                whence.at[pl.ds(pl.multiple_of(tile_at[at] * rank_max, rank_max), rank_max)],
                to.at[pl.ds(pl.multiple_of(at * rank_max, rank_max), rank_max)],
                sem.at[group],
            ).start()
            return carry

        lax.fori_loop(0, group_tiles, one, 0)

    def loaded(ref, sem, group):
        piece = ref.at[pl.ds(group * deep, deep)]
        pltpu.make_async_copy(piece, piece, sem.at[group]).wait()

    for group in range(peers):
        load(u_hbm, u_ref, u_sem, group)
        load(v_hbm, v_ref, v_sem, group)
    lane = lax.broadcasted_iota(jnp.int32, (1, deep), 1)
    for group in range(peers):
        code = jnp.full((1, deep), -1, jnp.int32)
        for i in range(group_tiles):
            at = group * group_tiles + i
            inside = (lane >= i * rank_max) & (lane < i * rank_max + rank_at[at])
            code = jnp.where(inside, code_at[at], code)
        code_ref[pl.ds(group, 1), :] = code
    copies[3].wait()
    low = misfit[...].astype(jnp.bfloat16).reshape(rows_dev * sources, -1)
    for group in range(peers):
        loaded(u_ref, u_sem, group)
        code = code_ref[pl.ds(group, 1), :]
        every = times_u(low, u_ref[pl.ds(group * deep, deep), :])
        lhs = by_slot(pick_rows(every, code, sources, rows_dev), code, rows_dev)
        loaded(v_ref, v_sem, group)
        for i, part in enumerate(parts):
            put_terms(lhs, v_ref, group, part, outs[2 * i : 2 * i + 2], rows_dev, peers)


def low_field(base_ref, came_ref, contrast_ref, part):
    first, width, _ = part
    rows = []
    for row in range(base_ref.shape[0]):
        scale = contrast_ref[pl.ds(row, 1), pl.ds(first, width)]
        field = base_ref[row] + scale * came_ref[row].astype(jnp.float32)
        rows.append(field.astype(jnp.bfloat16))
    return jnp.concatenate(rows, axis=0)


def early_kernel(dims, parts, code_ref, contrast_ref, *refs):
    rows_dev, peers = dims
    fields, (u_ref, out_ref) = refs[: 2 * len(parts)], refs[2 * len(parts) :]
    deep = code_ref.shape[1]
    sources = out_ref.shape[1]
    lows = [
        low_field(fields[2 * i], fields[2 * i + 1], contrast_ref, part)
        for i, part in enumerate(parts)
    ]
    for group in range(peers):
        every = 0.0
        for low, (first, width, _) in zip(lows, parts):
            every = every + times_u(low, u_ref[pl.ds(group * deep, deep), pl.ds(first, width)])
        code = code_ref[pl.ds(group, 1), :]
        out_ref[group] = pick_rows(every, code, sources, rows_dev)


def ready_kernel(dims, late, parts, code_ref, contrast_ref, sum_ref, base_ref, came_ref, *refs):
    rows_dev, peers = dims
    u_ref, v_ref, lhs_ref = refs[:3]
    outs = refs[3:]
    deep = code_ref.shape[1]
    sources = sum_ref.shape[1]
    low = low_field(base_ref, came_ref, contrast_ref, late)
    first, width, _ = late
    for group in reversed(range(peers)):
        every = times_u(low, u_ref[pl.ds(group * deep, deep), pl.ds(first, width)])
        code = code_ref[pl.ds(group, 1), :]
        coeff = sum_ref[group] + pick_rows(every, code, sources, rows_dev)
        lhs = by_slot(coeff, code, rows_dev)
        lhs_ref[group] = lhs
        for out, part in zip(outs, parts):
            if spot(part[2], group) >= peers // 2:
                put_terms(lhs, v_ref, group, part, (None, out), rows_dev, peers)


def rest_kernel(dims, sent, parts, lhs_ref, v_ref, *refs):
    rows_dev, peers = dims
    sends = refs[: len(sent)]
    keeps = refs[len(sent) :]
    for out, i in zip(sends, sent):
        for group in in_order(parts[i][2], peers)[peers // 2 :]:
            put_terms(lhs_ref[group], v_ref, group, parts[i], (None, out), rows_dev, peers)
    for keep, part in zip(keeps, parts):
        for group in in_order(part[2], peers)[: peers // 2]:
            put_terms(lhs_ref[group], v_ref, group, part, (keep, None), rows_dev, peers)


def finish_kernel(parts, contrast_ref, forward_ref, *refs):
    fields, (field_ref, total_ref) = refs[: 2 * len(parts)], refs[2 * len(parts) :]
    for i, (first, width, _) in enumerate(parts):
        here = pl.ds(first, width)
        for row in range(field_ref.shape[0]):
            scale = contrast_ref[pl.ds(row, 1), here]
            field = fields[2 * i][row] + scale * fields[2 * i + 1][row].astype(jnp.float32)
            field_ref[row, :, here] = field
            product = forward_ref[row, :, here].astype(jnp.float32) * field
            total_ref[pl.ds(row, 1), here] = jnp.sum(product, axis=0, keepdims=True)


def swap(x, bit, peers):
    return lax.ppermute(x, "rows", [(i, i ^ (1 << bit)) for i in range(peers)])


def slot_sums(
    misfit, forward_fields, contrast, u_factors, v_factors, ranks, tile_cols, owner_slot
):
    peers = lax.axis_size("rows")
    rows_dev, tiles_row, rank_max, unknowns = u_factors.shape
    sources = misfit.shape[1]
    tiles = rows_dev * tiles_row
    deep = tiles // peers * rank_max
    parts = parts_of(unknowns, peers)
    first_sent, then_sent, late = [0, 3], [1, 2], 2
    early = [i for i in range(len(parts)) if i != late]
    half = (peers // 2 * rows_dev, sources)
    sent = [jax.ShapeDtypeStruct((*half, part[1]), jnp.bfloat16) for part in parts]
    kept = [jax.ShapeDtypeStruct((*half, part[1]), jnp.float32) for part in parts]
    u, v = (x.reshape(tiles * rank_max, unknowns) for x in (u_factors, v_factors))
    hbm = [pl.BlockSpec(memory_space=pl.ANY)]
    smem = lambda *shape: pltpu.SMEM(shape, jnp.int32)
    u, v, code, *got = pl.pallas_call(
        functools.partial(start_kernel, (rows_dev, tiles_row, rank_max, peers, parts)),
        out_shape=[pltpu.VMEM(x.shape, x.dtype) for x in (u, v)]
        + [jax.ShapeDtypeStruct((peers, deep), jnp.int32)]
        + [x for pair in zip(kept, sent) for x in pair],
        in_specs=hbm * 6,
        out_specs=vmem(3 + 2 * len(parts)),
        scratch_shapes=[
            smem(*tile_cols.shape[::-1]),
            smem(*owner_slot.shape),
            smem(*ranks.shape),
            pltpu.VMEM(misfit.shape, misfit.dtype),
            smem(tiles),
            smem(tiles),
            smem(tiles),
            smem(peers),
            pltpu.SemaphoreType.DMA((4,)),
            pltpu.SemaphoreType.DMA((peers,)),
            pltpu.SemaphoreType.DMA((peers,)),
        ],
        compiler_params=params(),
        cost_estimate=cost(2 * tiles * rank_max, unknowns, sources),
        name="start",
    )(*(in_hbm(x) for x in (tile_cols.T, owner_slot, ranks, misfit, u, v)))
    dims = (rows_dev, peers)
    scale = contrast[:, None, :]
    columns = [(slice(None), slice(None), slice(part[0], part[0] + part[1])) for part in parts]
    for step in range(APPS):
        if step == 0:
            keeps, goes = list(got[::2]), list(got[1::2])
        else:
            coeff = pl.pallas_call(
                functools.partial(early_kernel, dims, [parts[i] for i in early]),
                out_shape=jax.ShapeDtypeStruct((peers, sources, deep), jnp.float32),
                in_specs=vmem(3 + 2 * len(early)),
                out_specs=vmem(1)[0],
                compiler_params=params(),
                cost_estimate=cost(u.shape[0], unknowns * 3 // 4, sources),
                name="early",
            )(code, contrast, *(x for i in early for x in (base[i], came[i])), in_vmem(u))
            lhs, *some = pl.pallas_call(
                functools.partial(ready_kernel, dims, parts[late], [parts[i] for i in first_sent]),
                out_shape=[jax.ShapeDtypeStruct((peers, rows_dev * sources, deep), jnp.bfloat16)]
                + [sent[i] for i in first_sent],
                in_specs=vmem(7),
                out_specs=vmem(1 + len(first_sent)),
                compiler_params=params(),
                cost_estimate=cost(u.shape[0], unknowns // 2, sources),
                name="ready",
            )(code, contrast, coeff, base[late], came[late], in_vmem(u), in_vmem(v))
            rest = pl.pallas_call(
                functools.partial(rest_kernel, dims, then_sent, parts),
                out_shape=[sent[i] for i in then_sent] + kept,
                in_specs=vmem(2),
                out_specs=vmem(len(then_sent) + len(parts)),
                compiler_params=params(),
                cost_estimate=cost(u.shape[0], unknowns * 3 // 4, sources),
                name="rest",
            )(lhs, in_vmem(v))
            goes = [None] * len(parts)
            for i, x in zip(first_sent + then_sent, [*some, *rest[: len(then_sent)]]):
                goes[i] = x
            keeps = list(rest[len(then_sent) :])
        base, came = [None] * len(parts), [None] * len(parts)
        levels = len(parts[0][2])
        for level in range(levels):
            for i, part in enumerate(parts):
                came[i] = swap(goes[i], part[2][level], peers)
                if level < levels - 1:
                    mid = keeps[i].shape[0] // 2
                    goes[i] = keeps[i][mid:] + came[i][mid:].astype(jnp.float32)
                    goes[i] = goes[i].astype(jnp.bfloat16)
                    keeps[i] = keeps[i][:mid] + came[i][:mid].astype(jnp.float32)
        for i in range(len(parts)):
            base[i] = misfit[columns[i]] + scale[columns[i]] * keeps[i]
    return pl.pallas_call(
        functools.partial(finish_kernel, parts),
        out_shape=[
            jax.ShapeDtypeStruct(misfit.shape, jnp.float32),
            jax.ShapeDtypeStruct(contrast.shape, jnp.float32),
        ],
        in_specs=vmem(2 + 2 * len(parts)),
        out_specs=vmem(2),
        compiler_params=params(),
        name="finish",
    )(contrast, forward_fields, *(x for pair in zip(base, came) for x in pair))


def route_tiles(tile_cols, owner_slot, rows_dev, peers):
    tiles = rows_dev * tile_cols.shape[1]
    target_slot = owner_slot[tile_cols.reshape(peers, tiles)]
    target_dev = target_slot // rows_dev
    local_slot = target_slot % rows_dev
    same = target_dev[:, :, None] == target_dev[:, None, :]
    before = jnp.arange(tiles)[None, :] < jnp.arange(tiles)[:, None]
    order = jnp.sum(jnp.where(same & before[None, :, :], 1, 0), axis=2).astype(jnp.int32)
    return target_dev, local_slot, order


def tile_terms(
    misfit, forward_fields, contrast, u_factors, v_factors, ranks, tile_cols, owner_slot
):
    rows_dev, tiles_row, rank_max, unknowns = u_factors.shape
    tiles = rows_dev * tiles_row
    peers = lax.axis_size("rows")
    cap = (tiles + peers - 1) // peers
    sources = misfit.shape[1]
    here = lax.axis_index("rows")
    target_dev, local_slot, order = route_tiles(tile_cols, owner_slot, rows_dev, peers)
    mine_dev = lax.dynamic_index_in_dim(target_dev, here, 0, keepdims=False)
    mine_order = lax.dynamic_index_in_dim(order, here, 0, keepdims=False)
    box = mine_dev * cap + mine_order
    sender = jnp.arange(peers, dtype=jnp.int32)[:, None] * cap + order
    entry = jnp.where(target_dev == here, sender, peers * cap).reshape(-1)
    arrival = (
        jnp.full((peers * cap,), -1, jnp.int32).at[entry].set(local_slot.reshape(-1), mode="drop")
    )
    pick = (arrival[:, None] == jnp.arange(rows_dev, dtype=jnp.int32)[None, :]).astype(jnp.float32)
    keep = (jnp.arange(rank_max, dtype=jnp.int32)[None, None, :] < ranks[:, :, None]).astype(
        jnp.float32
    )
    field = misfit
    for step in range(APPS):
        coeff = jnp.einsum(
            "lsb,lkrb->lksr",
            field.astype(jnp.bfloat16),
            u_factors,
            preferred_element_type=jnp.float32,
        )
        tile_coeff = (coeff * keep[:, :, None, :]).astype(jnp.bfloat16)
        terms = jnp.einsum(
            "lksr,lkrb->lksb", tile_coeff, v_factors, preferred_element_type=jnp.float32
        )
        terms = terms.reshape(tiles, sources, unknowns)
        outgoing = jnp.zeros((peers * cap, sources, unknowns), jnp.float32).at[box].set(terms)
        incoming = lax.all_to_all(
            outgoing.reshape(peers, cap, sources, unknowns).astype(jnp.bfloat16),
            "rows",
            split_axis=0,
            concat_axis=0,
            tiled=True,
        ).astype(jnp.float32)
        field = misfit + contrast[:, None, :] * jnp.einsum(
            "eq,esb->qsb",
            pick,
            incoming.reshape(peers * cap, sources, unknowns),
            precision=lax.Precision.HIGHEST,
        )
    return field, jnp.sum(forward_fields.astype(jnp.float32) * field, axis=1)


def src_sum(x):
    count = lax.axis_size("src")
    if count & (count - 1):
        return lax.psum(x, "src")
    terms = [x]
    for step in range(1, count):
        terms.append(lax.ppermute(x, "src", [(i, i ^ step) for i in range(count)]))
    while len(terms) > 1:
        terms = [a + b for a, b in zip(terms[::2], terms[1::2])]
    return terms[0]


def per_device(
    misfit, forward_fields, contrast, u_factors, v_factors, ranks, tile_cols, owner_slot
):
    rows_dev, tiles_row = ranks.shape
    peers = lax.axis_size("rows")
    tiles = rows_dev * tiles_row
    cap = (tiles + peers - 1) // peers
    dense = (
        peers > 1
        and peers & (peers - 1) == 0
        and tiles == cap * peers
        and cap >= rows_dev
        and cap * u_factors.shape[2] % 128 == 0
        and misfit.shape[2] % 512 == 0
        and misfit.shape[1] % 16 == 0
    )
    run = slot_sums if dense else tile_terms
    field, partial_sum = run(
        misfit, forward_fields, contrast, u_factors, v_factors, ranks, tile_cols, owner_slot
    )
    total = src_sum(partial_sum)
    sources = misfit.shape[1] * lax.axis_size("src")
    gradient = total * lax.rsqrt(jnp.float32(sources))
    return (field, gradient)


def solution(mesh):
    placed = (
        P("rows", "src", None),
        P("rows", "src", None),
        P("rows", None),
        P("rows", None, None, None),
        P("rows", None, None, None),
        P("rows", None),
        P(),
        P(),
    )
    return jax.shard_map(
        per_device,
        mesh=mesh,
        in_specs=placed,
        out_specs=(P("rows", "src", None), P("rows", None)),
        check_vma=False,
    )
```

time: 355 us -> 122 us (0.34)
  blocking collectives: 165 us -> 0 us
  local copies, waits for them, and re-layouts: 68.8 us -> 0.02 us
  starting transfers between devices: 7.28 us -> 68.9 us
  matrix products: 54.4 us -> 0 us
  Pallas kernels: 0 us -> 35.2 us
  waiting for transfers between devices: 45.3 us -> 14.9 us
  other arithmetic: 12.6 us -> 1.5 us
    all_to_all x3 -> x0, blocking collectives: 155 us -> none  [per_device(): lax.all_to_all(outgoing.reshape(peers, cap, sources, B).astype(jnp.bfloat...]
    ppermute x0 -> x51, starting transfers between devices: none -> 68.9 us  [the longest x48 67.1 us: swap(): return lax.ppermute(x, 'rows', [(i, i ^ 1 << bit) for i in range(peers)])]
    dot_general x12 -> x0, matrix products: 54.4 us -> none  [the longest x4 29.5 us: per_device(): jnp.einsum('lsb,lkrb->lksr', field.astype(jnp.bfloat16), u_factors, prefe...]
    scatter x5 -> x0, local copies, waits for them, and re-layouts: 50.7 us -> none  [the longest x4 48.1 us: per_device(): jnp.zeros((peers * cap, sources, B), jnp.float32).at[box].set(terms)]
    all_to_all x1 -> x0, waiting for transfers between devices: 45.3 us -> none  [per_device(): lax.all_to_all(outgoing.reshape(peers, cap, sources, B).astype(jnp.bfloat...]
    pallas_call x0 -> x11, Pallas kernels: none -> 35.2 us  [the longest x1 13.9 us: slot_sums(): pl.pallas_call(functools.partial(start_kernel, (rows_dev, tiles_row, rank...]
    ppermute x0 -> x51, waiting for transfers between devices: none -> 14.9 us  [the longest x48 13 us: swap(): return lax.ppermute(x, 'rows', [(i, i ^ 1 << bit) for i in range(peers)])]
    convert_element_type x5 -> x28, other arithmetic: 10.8 us -> 0.57 us  [slot_sums(): goes[i] = goes[i].astype(jnp.bfloat16)]
  transfers between devices with their start and end apart: 1 -> 51, of which waited for: 1 -> 20; matrix products, arithmetic and copies ran while one was open for 1% -> 1% of each run, Pallas kernels for 0% -> 10%
where the time goes in v3:
time: 122 us; the launch traced here: 121 us
  starting transfers between devices  68.9 us (56%)
  Pallas kernels  35.2 us (29%)
  waiting for transfers between devices  14.9 us (12%)
  other arithmetic  1.5 us (1%)
    ppermute x48, starting transfers between devices, swap(): return lax.ppermute(x, 'rows', [(i, i ^ 1 << bit) for i in range(peers)])  67.1 us
    pallas_call x1, Pallas kernels, slot_sums(): pl.pallas_call(functools.partial(start_kernel, (rows_dev, tiles_row, rank...  13.9 us
    ppermute x48, waiting for transfers between devices, swap(): return lax.ppermute(x, 'rows', [(i, i ^ 1 << bit) for i in range(peers)])  13 us
    pallas_call x3, Pallas kernels, slot_sums(): pl.pallas_call(functools.partial(early_kernel, dims, [parts[i] for i in e...  8.89 us
    pallas_call x3, Pallas kernels, slot_sums(): pl.pallas_call(functools.partial(ready_kernel, dims, parts[late], [parts[...  5.97 us
    pallas_call x3, Pallas kernels, slot_sums(): pl.pallas_call(functools.partial(rest_kernel, dims, then_sent, parts), ou...  5.72 us
  transfers between devices with their start and end apart: 51, of which 20 were waited for; matrix products, arithmetic and copies ran while one was open for 1% of the time, Pallas kernels for 10%

profile of v3, /device:TPU:0, one launch (start us, length us, event | category | flops | bytes accessed | tf_op | source)
XLA Modules:
  0.0 121.5 jit_solution(2273436365230905061)
XLA Ops:
  0.7 13.9 %start.1 = (bf16[6144,1024]{1,0:T(8,128)(2,1)S(1)}, bf16[6144,1024]{1,0:T(8,128)(2,1)S(1)}, s32[8,768]{1,0:T(8,128)S(1)}, f32[16,16,256]{2,1,0:T(8,128)S(1)}, bf...) custom-call(s32[16,32]{1,0:T(8,128)} %bitcast.15, ...), custom_call_target="tpu_custom_call" | custom-call | flops 402653184 | bytes 25165824 | tf_op jit(solution)/shard_map/start/pallas_call | solution.py:258
  14.6 3.0 %collective-permute-start = (bf16[16,16,256]{2,1,0:T(8,128)(2,1)S(1)}, bf16[16,16,256]{2,1,0:T(8,128)(2,1)S(1)}, u32[]{:S(2)}, u32[]{:S(2)}) collective-permute-start(bf16[16,16,256]{2,1,0:T(8,128)(2,1)S(1)} %get-tuple-element.44), channel_id=1, source_target_pairs={{0,4},{4,0},{8,12},{12,8},{16,20},{20,16},{24,28},{28,24},{1,5},{5... | collective-permute-start | bytes 393224 | tf_op jit(solution)/shard_map/ppermute | solution.py:238
  17.7 2.0 %collective-permute-start.6 = (bf16[16,16,256]{2,1,0:T(8,128)(2,1)S(1)}, bf16[16,16,256]{2,1,0:T(8,128)(2,1)S(1)}, u32[]{:S(2)}, u32[]{:S(2)}) collective-permute-start(bf16[16,16,256]{2,1,0:T(8,128)(2,1)S(1)} %get-tuple-element.48), channel_id=1, source_target_pairs={{0,8},{4,12},{8,0},{12,4},{16,24},{20,28},{24,16},{28,20},{1,9},{5... | collective-permute-start | bytes 393224 | tf_op jit(solution)/shard_map/ppermute | solution.py:238
  19.7 1.5 %collective-permute-start.9 = (bf16[16,16,256]{2,1,0:T(8,128)(2,1)S(1)}, bf16[16,16,256]{2,1,0:T(8,128)(2,1)S(1)}, u32[]{:S(2)}, u32[]{:S(2)}) collective-permute-start(bf16[16,16,256]{2,1,0:T(8,128)(2,1)S(1)} %get-tuple-element.51), channel_id=1, source_target_pairs={{0,4},{4,0},{8,12},{12,8},{16,20},{20,16},{24,28},{28,24},{1,5},{5... | collective-permute-start | bytes 393224 | tf_op jit(solution)/shard_map/ppermute | solution.py:238
  21.2 0.7 collective-permute-done
  21.9 2.2 %collective-permute-start.1 = (bf16[8,16,256]{2,1,0:T(8,128)(2,1)S(1)}, bf16[8,16,256]{2,1,0:T(8,128)(2,1)S(1)}, u32[]{:S(2)}, u32[]{:S(2)}) collective-permute-start(bf16[8,16,256]{2,1,0:T(8,128)(2,1)S(1)} %get-tuple-element.112), channel_id=1, source_target_pairs={{0,8},{4,12},{8,0},{12,4},{16,24},{20,28},{24,16},{28,20},{1,9},{5... | collective-permute-start | bytes 196616 | tf_op jit(solution)/shard_map/ppermute | solution.py:238
  24.1 0.6 collective-permute-done.3
  24.8 2.2 %collective-permute-start.4 = (bf16[8,16,256]{2,1,0:T(8,128)(2,1)S(1)}, bf16[8,16,256]{2,1,0:T(8,128)(2,1)S(1)}, u32[]{:S(2)}, u32[]{:S(2)}) collective-permute-start(bf16[8,16,256]{2,1,0:T(8,128)(2,1)S(1)} %get-tuple-element.110), channel_id=1, source_target_pairs={{0,8},{4,12},{8,0},{12,4},{16,24},{20,28},{24,16},{28,20},{1,9},{5... | collective-permute-start | bytes 196616 | tf_op jit(solution)/shard_map/ppermute | solution.py:238
  27.0 2.7 %collective-permute-start.7 = (bf16[8,16,256]{2,1,0:T(8,128)(2,1)S(1)}, bf16[8,16,256]{2,1,0:T(8,128)(2,1)S(1)}, u32[]{:S(2)}, u32[]{:S(2)}) collective-permute-start(bf16[8,16,256]{2,1,0:T(8,128)(2,1)S(1)} %get-tuple-element.108), channel_id=1, source_target_pairs={{0,16},{4,20},{8,24},{12,28},{16,0},{20,4},{24,8},{28,12},{1,17},{... | collective-permute-start | bytes 196616 | tf_op jit(solution)/shard_map/ppermute | solution.py:238
  30.2 1.1 collective-permute-start.2
  31.3 2.0 %collective-permute-start.5 = (bf16[4,16,256]{2,1,0:T(8,128)(2,1)S(1)}, bf16[4,16,256]{2,1,0:T(8,128)(2,1)S(1)}, u32[]{:S(2)}, u32[]{:S(2)}) collective-permute-start(bf16[4,16,256]{2,1,0:T(8,128)(2,1)S(1)} %fusion.42), channel_id=1, source_target_pairs={{0,16},{4,20},{8,24},{12,28},{16,0},{20,4},{24,8},{28,12},{1,17},{... | collective-permute-start | bytes 98312 | tf_op jit(solution)/shard_map/ppermute | solution.py:238
  33.3 1.0 collective-permute-done.10
  34.4 1.9 %collective-permute-start.8 = (bf16[4,16,256]{2,1,0:T(8,128)(2,1)S(1)}, bf16[4,16,256]{2,1,0:T(8,128)(2,1)S(1)}, u32[]{:S(2)}, u32[]{:S(2)}) collective-permute-start(bf16[4,16,256]{2,1,0:T(8,128)(2,1)S(1)} %get-tuple-element.130), channel_id=1, source_target_pairs={{0,4},{4,0},{8,12},{12,8},{16,20},{20,16},{24,28},{28,24},{1,5},{5... | collective-permute-start | bytes 98312 | tf_op jit(solution)/shard_map/ppermute | solution.py:238
  37.1 1.3 %collective-permute-done.8.refs_5_ = bf16[4,16,256]{2,1,0:T(8,128)(2,1)S(1)} collective-permute-done((bf16[4,16,256]{2,1,0:T(8,128)(2,1)S(1)}, bf16[4,16,256]{2,1,0:T(8,128)(2,1)S(1)}, u32[]{:S(2)}, u32[]{:S(2)}) %collective-permute-start.8) | collective-permute-done | bytes 32800 | tf_op jit(solution)/shard_map/ppermute | solution.py:238
  38.4 3.0 %early.3.sum_ref = f32[8,16,768]{2,1,0:T(8,128)S(1)} custom-call(s32[8,768]{1,0:T(8,128)S(1)} %get-tuple-element.42.code_ref, f32[4,1024]{1,0:T(4,128)S(1)} %copy-done, f32[4,16,256]{2,1,0:T(8,128)S(1)} %get-tuple-element.128.refs_0_, bf16[4,16,256]{2,1,0:T(8,128)(2,1)S(1)} %collective-permute-done.2.refs_1_, f32[4,16,256]{2,1,0:T(8,128)S(1)} %get-tuple-element.127.refs_2_, ...), custom_call_target="tpu_custom_call" | custom-call | flops 150994944 | bytes 9437184 | tf_op jit(solution)/shard_map/early/pallas_call | solution.py:289
  41.4 2.0 %ready.3 = (bf16[8,64,768]{2,1,0:T(8,128)(2,1)S(1)}, bf16[16,16,256]{2,1,0:T(8,128)(2,1)S(1)}, bf16[16,16,256]{2,1,0:T(8,128)(2,1)S(1)}) custom-call(s32[8,768]{1,0:T(8,128)S(1)} %get-tuple-element.42.code_ref, f32[4,1024]{1,0:T(4,128)S(1)} %copy-done, f32[8,16,768]{2,1,0:T(8,128)S(1)} %early.3.sum_ref, f32[4,16,256]{2,1,0:T(8,128)S(1)} %get-tuple-element.126.base_ref, ...), custom_call_target="tpu_custom_call" | custom-call | flops 100663296 | bytes 6291456 | tf_op jit(solution)/shard_map/ready/pallas_call | solution.py:298
  43.9 1.5 %collective-permute-start.12 = (bf16[16,16,256]{2,1,0:T(8,128)(2,1)S(1)}, bf16[16,16,256]{2,1,0:T(8,128)(2,1)S(1)}, u32[]{:S(2)}, u32[]{:S(2)}) collective-permute-start(bf16[16,16,256]{2,1,0:T(8,128)(2,1)S(1)} %get-tuple-element.55), channel_id=1, source_target_pairs={{0,4},{4,0},{8,12},{12,8},{16,20},{20,16},{24,28},{28,24},{1,5},{5... | collective-permute-start | bytes 393224 | tf_op jit(solution)/shard_map/ppermute | solution.py:238
  45.5 1.9 %rest.3 = (bf16[16,16,256]{2,1,0:T(8,128)(2,1)S(1)}, bf16[16,16,256]{2,1,0:T(8,128)(2,1)S(1)}, f32[16,16,256]{2,1,0:T(8,128)S(1)}, f32[16,16,256]{2,1,0:T(8,128)...) custom-call(bf16[8,64,768]{2,1,0:T(8,128)(2,1)S(1)} %get-tuple-element.53.lhs_ref, ...), custom_call_target="tpu_custom_call" | custom-call | flops 150994944 | bytes 9437184 | tf_op jit(solution)/shard_map/rest/pallas_call | solution.py:308
  47.4 0.6 collective-permute-start.15
  48.0 1.5 %collective-permute-start.21 = (bf16[16,16,256]{2,1,0:T(8,128)(2,1)S(1)}, bf16[16,16,256]{2,1,0:T(8,128)(2,1)S(1)}, u32[]{:S(2)}, u32[]{:S(2)}) collective-permute-start(bf16[16,16,256]{2,1,0:T(8,128)(2,1)S(1)} %get-tuple-element.61), channel_id=1, source_target_pairs={{0,4},{4,0},{8,12},{12,8},{16,20},{20,16},{24,28},{28,24},{1,5},{5... | collective-permute-start | bytes 393224 | tf_op jit(solution)/shard_map/ppermute | solution.py:238
  49.5 2.2 %collective-permute-start.19 = (bf16[8,16,256]{2,1,0:T(8,128)(2,1)S(1)}, bf16[8,16,256]{2,1,0:T(8,128)(2,1)S(1)}, u32[]{:S(2)}, u32[]{:S(2)}) collective-permute-start(bf16[8,16,256]{2,1,0:T(8,128)(2,1)S(1)} %get-tuple-element.100), channel_id=1, source_target_pairs={{0,16},{4,20},{8,24},{12,28},{16,0},{20,4},{24,8},{28,12},{1,17},{... | collective-permute-start | bytes 196616 | tf_op jit(solution)/shard_map/ppermute | solution.py:238
  51.7 0.6 collective-permute-start.13
  52.4 1.9 %collective-permute-start.16 = (bf16[8,16,256]{2,1,0:T(8,128)(2,1)S(1)}, bf16[8,16,256]{2,1,0:T(8,128)(2,1)S(1)}, u32[]{:S(2)}, u32[]{:S(2)}) collective-permute-start(bf16[8,16,256]{2,1,0:T(8,128)(2,1)S(1)} %get-tuple-element.102), channel_id=1, source_target_pairs={{0,8},{4,12},{8,0},{12,4},{16,24},{20,28},{24,16},{28,20},{1,9},{5... | collective-permute-start | bytes 196616 | tf_op jit(solution)/shard_map/ppermute | solution.py:238
  54.4 1.4 %collective-permute-start.22 = (bf16[8,16,256]{2,1,0:T(8,128)(2,1)S(1)}, bf16[8,16,256]{2,1,0:T(8,128)(2,1)S(1)}, u32[]{:S(2)}, u32[]{:S(2)}) collective-permute-start(bf16[8,16,256]{2,1,0:T(8,128)(2,1)S(1)} %get-tuple-element.98), channel_id=1, source_target_pairs={{0,8},{4,12},{8,0},{12,4},{16,24},{20,28},{24,16},{28,20},{1,9},{5... | collective-permute-start | bytes 196616 | tf_op jit(solution)/shard_map/ppermute | solution.py:238
  56.2 1.6 %collective-permute-start.14 = (bf16[4,16,256]{2,1,0:T(8,128)(2,1)S(1)}, bf16[4,16,256]{2,1,0:T(8,128)(2,1)S(1)}, u32[]{:S(2)}, u32[]{:S(2)}) collective-permute-start(bf16[4,16,256]{2,1,0:T(8,128)(2,1)S(1)} %fusion.33), channel_id=1, source_target_pairs={{0,16},{4,20},{8,24},{12,28},{16,0},{20,4},{24,8},{28,12},{1,17},{... | collective-permute-start | bytes 98312 | tf_op jit(solution)/shard_map/ppermute | solution.py:238
  57.8 1.5 %collective-permute-start.17 = (bf16[4,16,256]{2,1,0:T(8,128)(2,1)S(1)}, bf16[4,16,256]{2,1,0:T(8,128)(2,1)S(1)}, u32[]{:S(2)}, u32[]{:S(2)}) collective-permute-start(bf16[4,16,256]{2,1,0:T(8,128)(2,1)S(1)} %fusion.30), channel_id=1, source_target_pairs={{0,16},{4,20},{8,24},{12,28},{16,0},{20,4},{24,8},{28,12},{1,17},{... | collective-permute-start | bytes 98312 | tf_op jit(solution)/shard_map/ppermute | solution.py:238
  59.3 1.9 %collective-permute-start.20 = (bf16[4,16,256]{2,1,0:T(8,128)(2,1)S(1)}, bf16[4,16,256]{2,1,0:T(8,128)(2,1)S(1)}, u32[]{:S(2)}, u32[]{:S(2)}) collective-permute-start(bf16[4,16,256]{2,1,0:T(8,128)(2,1)S(1)} %get-tuple-element.131), channel_id=1, source_target_pairs={{0,4},{4,0},{8,12},{12,8},{16,20},{20,16},{24,28},{28,24},{1,5},{5... | collective-permute-start | bytes 98312 | tf_op jit(solution)/shard_map/ppermute | solution.py:238
  61.3 1.5 %collective-permute-start.23 = (bf16[4,16,256]{2,1,0:T(8,128)(2,1)S(1)}, bf16[4,16,256]{2,1,0:T(8,128)(2,1)S(1)}, u32[]{:S(2)}, u32[]{:S(2)}) collective-permute-start(bf16[4,16,256]{2,1,0:T(8,128)(2,1)S(1)} %fusion.24), channel_id=1, source_target_pairs={{0,16},{4,20},{8,24},{12,28},{16,0},{20,4},{24,8},{28,12},{1,17},{... | collective-permute-start | bytes 98312 | tf_op jit(solution)/shard_map/ppermute | solution.py:238
  63.3 3.0 %early.4.sum_ref = f32[8,16,768]{2,1,0:T(8,128)S(1)} custom-call(s32[8,768]{1,0:T(8,128)S(1)} %get-tuple-element.42.code_ref, f32[4,1024]{1,0:T(4,128)S(1)} %copy-done, f32[4,16,256]{2,1,0:T(8,128)S(1)} %get-tuple-element.123.refs_0_, bf16[4,16,256]{2,1,0:T(8,128)(2,1)S(1)} %collective-permute-done.14.refs_1_, f32[4,16,256]{2,1,0:T(8,128)S(1)} %get-tuple-element.124.refs_2_, ...), custom_call_target="tpu_custom_call" | custom-call | flops 150994944 | bytes 9437184 | tf_op jit(solution)/shard_map/early/pallas_call | solution.py:289
  66.3 2.0 %ready.4 = (bf16[8,64,768]{2,1,0:T(8,128)(2,1)S(1)}, bf16[16,16,256]{2,1,0:T(8,128)(2,1)S(1)}, bf16[16,16,256]{2,1,0:T(8,128)(2,1)S(1)}) custom-call(s32[8,768]{1,0:T(8,128)S(1)} %get-tuple-element.42.code_ref, f32[4,1024]{1,0:T(4,128)S(1)} %copy-done, f32[8,16,768]{2,1,0:T(8,128)S(1)} %early.4.sum_ref, f32[4,16,256]{2,1,0:T(8,128)S(1)} %get-tuple-element.122.base_ref, ...), custom_call_target="tpu_custom_call" | custom-call | flops 100663296 | bytes 6291456 | tf_op jit(solution)/shard_map/ready/pallas_call | solution.py:298
  68.3 1.6 %collective-permute-start.30 = (bf16[16,16,256]{2,1,0:T(8,128)(2,1)S(1)}, bf16[16,16,256]{2,1,0:T(8,128)(2,1)S(1)}, u32[]{:S(2)}, u32[]{:S(2)}) collective-permute-start(bf16[16,16,256]{2,1,0:T(8,128)(2,1)S(1)} %get-tuple-element.68), channel_id=1, source_target_pairs={{0,8},{4,12},{8,0},{12,4},{16,24},{20,28},{24,16},{28,20},{1,9},{5... | collective-permute-start | bytes 393224 | tf_op jit(solution)/shard_map/ppermute | solution.py:238
  69.8 1.3 %collective-permute-start.24 = (bf16[16,16,256]{2,1,0:T(8,128)(2,1)S(1)}, bf16[16,16,256]{2,1,0:T(8,128)(2,1)S(1)}, u32[]{:S(2)}, u32[]{:S(2)}) collective-permute-start(bf16[16,16,256]{2,1,0:T(8,128)(2,1)S(1)} %get-tuple-element.64), channel_id=1, source_target_pairs={{0,4},{4,0},{8,12},{12,8},{16,20},{20,16},{24,28},{28,24},{1,5},{5... | collective-permute-start | bytes 393224 | tf_op jit(solution)/shard_map/ppermute | solution.py:238
  71.1 1.9 %rest.4 = (bf16[16,16,256]{2,1,0:T(8,128)(2,1)S(1)}, bf16[16,16,256]{2,1,0:T(8,128)(2,1)S(1)}, f32[16,16,256]{2,1,0:T(8,128)S(1)}, f32[16,16,256]{2,1,0:T(8,128)...) custom-call(bf16[8,64,768]{2,1,0:T(8,128)(2,1)S(1)} %get-tuple-element.62.lhs_ref, ...), custom_call_target="tpu_custom_call" | custom-call | flops 150994944 | bytes 9437184 | tf_op jit(solution)/shard_map/rest/pallas_call | solution.py:308
  73.0 0.8 collective-permute-start.27
  73.8 1.3 %collective-permute-start.33 = (bf16[16,16,256]{2,1,0:T(8,128)(2,1)S(1)}, bf16[16,16,256]{2,1,0:T(8,128)(2,1)S(1)}, u32[]{:S(2)}, u32[]{:S(2)}) collective-permute-start(bf16[16,16,256]{2,1,0:T(8,128)(2,1)S(1)} %get-tuple-element.70), channel_id=1, source_target_pairs={{0,4},{4,0},{8,12},{12,8},{16,20},{20,16},{24,28},{28,24},{1,5},{5... | collective-permute-start | bytes 393224 | tf_op jit(solution)/shard_map/ppermute | solution.py:238
  75.2 0.9 collective-permute-start.31
  76.1 1.8 %collective-permute-start.25 = (bf16[8,16,256]{2,1,0:T(8,128)(2,1)S(1)}, bf16[8,16,256]{2,1,0:T(8,128)(2,1)S(1)}, u32[]{:S(2)}, u32[]{:S(2)}) collective-permute-start(bf16[8,16,256]{2,1,0:T(8,128)(2,1)S(1)} %get-tuple-element.96), channel_id=1, source_target_pairs={{0,8},{4,12},{8,0},{12,4},{16,24},{20,28},{24,16},{28,20},{1,9},{5... | collective-permute-start | bytes 196616 | tf_op jit(solution)/shard_map/ppermute | solution.py:238
  78.2 1.4 %collective-permute-start.28 = (bf16[8,16,256]{2,1,0:T(8,128)(2,1)S(1)}, bf16[8,16,256]{2,1,0:T(8,128)(2,1)S(1)}, u32[]{:S(2)}, u32[]{:S(2)}) collective-permute-start(bf16[8,16,256]{2,1,0:T(8,128)(2,1)S(1)} %get-tuple-element.94), channel_id=1, source_target_pairs={{0,8},{4,12},{8,0},{12,4},{16,24},{20,28},{24,16},{28,20},{1,9},{5... | collective-permute-start | bytes 196616 | tf_op jit(solution)/shard_map/ppermute | solution.py:238
  79.7 1.4 %collective-permute-start.34 = (bf16[8,16,256]{2,1,0:T(8,128)(2,1)S(1)}, bf16[8,16,256]{2,1,0:T(8,128)(2,1)S(1)}, u32[]{:S(2)}, u32[]{:S(2)}) collective-permute-start(bf16[8,16,256]{2,1,0:T(8,128)(2,1)S(1)} %get-tuple-element.90), channel_id=1, source_target_pairs={{0,8},{4,12},{8,0},{12,4},{16,24},{20,28},{24,16},{28,20},{1,9},{5... | collective-permute-start | bytes 196616 | tf_op jit(solution)/shard_map/ppermute | solution.py:238
  81.1 1.5 %collective-permute-start.26 = (bf16[4,16,256]{2,1,0:T(8,128)(2,1)S(1)}, bf16[4,16,256]{2,1,0:T(8,128)(2,1)S(1)}, u32[]{:S(2)}, u32[]{:S(2)}) collective-permute-start(bf16[4,16,256]{2,1,0:T(8,128)(2,1)S(1)} %fusion.21), channel_id=1, source_target_pairs={{0,16},{4,20},{8,24},{12,28},{16,0},{20,4},{24,8},{28,12},{1,17},{... | collective-permute-start | bytes 98312 | tf_op jit(solution)/shard_map/ppermute | solution.py:238
  82.6 1.5 %collective-permute-start.29 = (bf16[4,16,256]{2,1,0:T(8,128)(2,1)S(1)}, bf16[4,16,256]{2,1,0:T(8,128)(2,1)S(1)}, u32[]{:S(2)}, u32[]{:S(2)}) collective-permute-start(bf16[4,16,256]{2,1,0:T(8,128)(2,1)S(1)} %fusion.18), channel_id=1, source_target_pairs={{0,16},{4,20},{8,24},{12,28},{16,0},{20,4},{24,8},{28,12},{1,17},{... | collective-permute-start | bytes 98312 | tf_op jit(solution)/shard_map/ppermute | solution.py:238
  84.2 1.7 %collective-permute-start.32 = (bf16[4,16,256]{2,1,0:T(8,128)(2,1)S(1)}, bf16[4,16,256]{2,1,0:T(8,128)(2,1)S(1)}, u32[]{:S(2)}, u32[]{:S(2)}) collective-permute-start(bf16[4,16,256]{2,1,0:T(8,128)(2,1)S(1)} %get-tuple-element.132), channel_id=1, source_target_pairs={{0,4},{4,0},{8,12},{12,8},{16,20},{20,16},{24,28},{28,24},{1,5},{5... | collective-permute-start | bytes 98312 | tf_op jit(solution)/shard_map/ppermute | solution.py:238
  85.9 1.2 collective-permute-start.35
  87.5 1.1 collective-permute-done.32.refs_5_
  88.6 3.0 %early.5.sum_ref = f32[8,16,768]{2,1,0:T(8,128)S(1)} custom-call(s32[8,768]{1,0:T(8,128)S(1)} %get-tuple-element.42.code_ref, f32[4,1024]{1,0:T(4,128)S(1)} %copy-done, f32[4,16,256]{2,1,0:T(8,128)S(1)} %get-tuple-element.119.refs_0_, bf16[4,16,256]{2,1,0:T(8,128)(2,1)S(1)} %collective-permute-done.26.refs_1_, f32[4,16,256]{2,1,0:T(8,128)S(1)} %get-tuple-element.120.refs_2_, ...), custom_call_target="tpu_custom_call" | custom-call | flops 150994944 | bytes 9437184 | tf_op jit(solution)/shard_map/early/pallas_call | solution.py:289
  91.5 2.0 %ready.5 = (bf16[8,64,768]{2,1,0:T(8,128)(2,1)S(1)}, bf16[16,16,256]{2,1,0:T(8,128)(2,1)S(1)}, bf16[16,16,256]{2,1,0:T(8,128)(2,1)S(1)}) custom-call(s32[8,768]{1,0:T(8,128)S(1)} %get-tuple-element.42.code_ref, f32[4,1024]{1,0:T(4,128)S(1)} %copy-done, f32[8,16,768]{2,1,0:T(8,128)S(1)} %early.5.sum_ref, f32[4,16,256]{2,1,0:T(8,128)S(1)} %get-tuple-element.118.base_ref, ...), custom_call_target="tpu_custom_call" | custom-call | flops 100663296 | bytes 6291456 | tf_op jit(solution)/shard_map/ready/pallas_call | solution.py:298
  93.6 1.9 %rest.5 = (bf16[16,16,256]{2,1,0:T(8,128)(2,1)S(1)}, bf16[16,16,256]{2,1,0:T(8,128)(2,1)S(1)}, f32[16,16,256]{2,1,0:T(8,128)S(1)}, f32[16,16,256]{2,1,0:T(8,128)...) custom-call(bf16[8,64,768]{2,1,0:T(8,128)(2,1)S(1)} %get-tuple-element.71.lhs_ref, ...), custom_call_target="tpu_custom_call" | custom-call | flops 150994944 | bytes 9437184 | tf_op jit(solution)/shard_map/rest/pallas_call | solution.py:308
  95.5 1.7 %collective-permute-start.39 = (bf16[16,16,256]{2,1,0:T(8,128)(2,1)S(1)}, bf16[16,16,256]{2,1,0:T(8,128)(2,1)S(1)}, u32[]{:S(2)}, u32[]{:S(2)}) collective-permute-start(bf16[16,16,256]{2,1,0:T(8,128)(2,1)S(1)} %get-tuple-element.75), channel_id=1, source_target_pairs={{0,4},{4,0},{8,12},{12,8},{16,20},{20,16},{24,28},{28,24},{1,5},{5... | collective-permute-start | bytes 393224 | tf_op jit(solution)/shard_map/ppermute | solution.py:238
  97.6 1.6 %collective-permute-start.36 = (bf16[16,16,256]{2,1,0:T(8,128)(2,1)S(1)}, bf16[16,16,256]{2,1,0:T(8,128)(2,1)S(1)}, u32[]{:S(2)}, u32[]{:S(2)}) collective-permute-start(bf16[16,16,256]{2,1,0:T(8,128)(2,1)S(1)} %get-tuple-element.73), channel_id=1, source_target_pairs={{0,4},{4,0},{8,12},{12,8},{16,20},{20,16},{24,28},{28,24},{1,5},{5... | collective-permute-start | bytes 393224 | tf_op jit(solution)/shard_map/ppermute | solution.py:238
  99.4 1.1 collective-permute-done.39
  100.5 1.2 collective-permute-start.40
  102.3 1.2 collective-permute-start.43
  103.7 1.2 collective-permute-start.37
  104.9 2.1 %collective-permute-start.46 = (bf16[8,16,256]{2,1,0:T(8,128)(2,1)S(1)}, bf16[8,16,256]{2,1,0:T(8,128)(2,1)S(1)}, u32[]{:S(2)}, u32[]{:S(2)}) collective-permute-start(bf16[8,16,256]{2,1,0:T(8,128)(2,1)S(1)} %get-tuple-element.82), channel_id=1, source_target_pairs={{0,16},{4,20},{8,24},{12,28},{16,0},{20,4},{24,8},{28,12},{1,17},{... | collective-permute-start | bytes 196616 | tf_op jit(solution)/shard_map/ppermute | solution.py:238
  107.0 1.0 collective-permute-start.41
  108.0 2.0 %collective-permute-start.38 = (bf16[4,16,256]{2,1,0:T(8,128)(2,1)S(1)}, bf16[4,16,256]{2,1,0:T(8,128)(2,1)S(1)}, u32[]{:S(2)}, u32[]{:S(2)}) collective-permute-start(bf16[4,16,256]{2,1,0:T(8,128)(2,1)S(1)} %fusion.9), channel_id=1, source_target_pairs={{0,16},{4,20},{8,24},{12,28},{16,0},{20,4},{24,8},{28,12},{1,17},{... | collective-permute-start | bytes 98312 | tf_op jit(solution)/shard_map/ppermute | solution.py:238
  110.1 0.8 collective-permute-done.46
  110.9 1.4 %collective-permute-start.44 = (bf16[4,16,256]{2,1,0:T(8,128)(2,1)S(1)}, bf16[4,16,256]{2,1,0:T(8,128)(2,1)S(1)}, u32[]{:S(2)}, u32[]{:S(2)}) collective-permute-start(bf16[4,16,256]{2,1,0:T(8,128)(2,1)S(1)} %get-tuple-element.133), channel_id=1, source_target_pairs={{0,16},{4,20},{8,24},{12,28},{16,0},{20,4},{24,8},{28,12},{1,17},{... | collective-permute-start | bytes 98312 | tf_op jit(solution)/shard_map/ppermute | solution.py:238
  112.3 0.8 collective-permute-start.47
  113.1 2.9 %collective-permute-done.44.refs_5_ = bf16[4,16,256]{2,1,0:T(8,128)(2,1)S(1)} collective-permute-done((bf16[4,16,256]{2,1,0:T(8,128)(2,1)S(1)}, bf16[4,16,256]{2,1,0:T(8,128)(2,1)S(1)}, u32[]{:S(2)}, u32[]{:S(2)}) %collective-permute-start.44) | collective-permute-done | bytes 32800 | tf_op jit(solution)/shard_map/ppermute | solution.py:238
  116.3 0.8 finish.1
  117.1 1.5 %collective-permute-start.49 = (f32[4,1024]{1,0:T(4,128)S(1)}, f32[4,1024]{1,0:T(4,128)S(1)}, u32[]{:S(2)}, u32[]{:S(2)}) collective-permute-start(f32[4,1024]{1,0:T(4,128)S(1)} %get-tuple-element.81), channel_id=1, source_target_pairs={{0,2},{1,3},{2,0},{3,1},{4,6},{5,7},{6,4},{7,5},{8,10},{9,11},{10,... | collective-permute-start | bytes 49160 | tf_op jit(solution)/shard_map/ppermute | solution.py:415
  118.9 1.4 %collective-permute-done.50 = f32[4,1024]{1,0:T(4,128)S(1)} collective-permute-done((f32[4,1024]{1,0:T(4,128)S(1)}, f32[4,1024]{1,0:T(4,128)S(1)}, u32[]{:S(2)}, u32[]{:S(2)}) %collective-permute-start.50) | collective-permute-done | bytes 16416 | tf_op jit(solution)/shard_map/ppermute | solution.py:415
  120.9 0.6 add_multiply_fusion
  (89 shorter events, 7.3 us)
Async XLA Ops:
  0.6 20.6 %copy-start = (f32[4,1024]{1,0:T(4,128)S(1)}, f32[4,1024]{1,0:T(4,128)}, u32[]{:S(2)}) copy-start(f32[4,1024]{1,0:T(4,128)} %contrast_ref.13) | copy-start | bytes 49156
  0.6 33.7 %copy-start.2 = (f32[4,16,1024]{2,1,0:T(8,128)S(1)}, f32[4,16,1024]{2,1,0:T(8,128)}, u32[]{:S(2)}) copy-start(f32[4,16,1024]{2,1,0:T(8,128)} %refs_3_.1) | copy-start | bytes 786436
  14.6 7.4 %collective-permute-start = (bf16[16,16,256]{2,1,0:T(8,128)(2,1)S(1)}, bf16[16,16,256]{2,1,0:T(8,128)(2,1)S(1)}, u32[]{:S(2)}, u32[]{:S(2)}) collective-permute-start(bf16[16,16,256]{2,1,0:T(8,128)(2,1)S(1)} %get-tuple-element.44), channel_id=1, source_target_pairs={{0,4},{4,0},{8,12},{12,8},{16,20},{20,16},{24,28},{28,24},{1,5},{5... | collective-permute-start | bytes 393224 | tf_op jit(solution)/shard_map/ppermute | solution.py:238
  17.6 7.1 %collective-permute-start.3 = (bf16[16,16,256]{2,1,0:T(8,128)(2,1)S(1)}, bf16[16,16,256]{2,1,0:T(8,128)(2,1)S(1)}, u32[]{:S(2)}, u32[]{:S(2)}) collective-permute-start(bf16[16,16,256]{2,1,0:T(8,128)(2,1)S(1)} %get-tuple-element.46), channel_id=1, source_target_pairs={{0,4},{4,0},{8,12},{12,8},{16,20},{20,16},{24,28},{28,24},{1,5},{5... | collective-permute-start | bytes 393224 | tf_op jit(solution)/shard_map/ppermute | solution.py:238
  17.7 9.3 %collective-permute-start.6 = (bf16[16,16,256]{2,1,0:T(8,128)(2,1)S(1)}, bf16[16,16,256]{2,1,0:T(8,128)(2,1)S(1)}, u32[]{:S(2)}, u32[]{:S(2)}) collective-permute-start(bf16[16,16,256]{2,1,0:T(8,128)(2,1)S(1)} %get-tuple-element.48), channel_id=1, source_target_pairs={{0,8},{4,12},{8,0},{12,4},{16,24},{20,28},{24,16},{28,20},{1,9},{5... | collective-permute-start | bytes 393224 | tf_op jit(solution)/shard_map/ppermute | solution.py:238
  19.7 10.0 %collective-permute-start.9 = (bf16[16,16,256]{2,1,0:T(8,128)(2,1)S(1)}, bf16[16,16,256]{2,1,0:T(8,128)(2,1)S(1)}, u32[]{:S(2)}, u32[]{:S(2)}) collective-permute-start(bf16[16,16,256]{2,1,0:T(8,128)(2,1)S(1)} %get-tuple-element.51), channel_id=1, source_target_pairs={{0,4},{4,0},{8,12},{12,8},{16,20},{20,16},{24,28},{28,24},{1,5},{5... | collective-permute-start | bytes 393224 | tf_op jit(solution)/shard_map/ppermute | solution.py:238
  21.9 8.2 %collective-permute-start.1 = (bf16[8,16,256]{2,1,0:T(8,128)(2,1)S(1)}, bf16[8,16,256]{2,1,0:T(8,128)(2,1)S(1)}, u32[]{:S(2)}, u32[]{:S(2)}) collective-permute-start(bf16[8,16,256]{2,1,0:T(8,128)(2,1)S(1)} %get-tuple-element.112), channel_id=1, source_target_pairs={{0,8},{4,12},{8,0},{12,4},{16,24},{20,28},{24,16},{28,20},{1,9},{5... | collective-permute-start | bytes 196616 | tf_op jit(solution)/shard_map/ppermute | solution.py:238
  24.8 6.5 %collective-permute-start.4 = (bf16[8,16,256]{2,1,0:T(8,128)(2,1)S(1)}, bf16[8,16,256]{2,1,0:T(8,128)(2,1)S(1)}, u32[]{:S(2)}, u32[]{:S(2)}) collective-permute-start(bf16[8,16,256]{2,1,0:T(8,128)(2,1)S(1)} %get-tuple-element.110), channel_id=1, source_target_pairs={{0,8},{4,12},{8,0},{12,4},{16,24},{20,28},{24,16},{28,20},{1,9},{5... | collective-permute-start | bytes 196616 | tf_op jit(solution)/shard_map/ppermute | solution.py:238
  27.0 6.3 %collective-permute-start.7 = (bf16[8,16,256]{2,1,0:T(8,128)(2,1)S(1)}, bf16[8,16,256]{2,1,0:T(8,128)(2,1)S(1)}, u32[]{:S(2)}, u32[]{:S(2)}) collective-permute-start(bf16[8,16,256]{2,1,0:T(8,128)(2,1)S(1)} %get-tuple-element.108), channel_id=1, source_target_pairs={{0,16},{4,20},{8,24},{12,28},{16,0},{20,4},{24,8},{28,12},{1,17},{... | collective-permute-start | bytes 196616 | tf_op jit(solution)/shard_map/ppermute | solution.py:238
  29.7 4.7 %collective-permute-start.10 = (bf16[8,16,256]{2,1,0:T(8,128)(2,1)S(1)}, bf16[8,16,256]{2,1,0:T(8,128)(2,1)S(1)}, u32[]{:S(2)}, u32[]{:S(2)}) collective-permute-start(bf16[8,16,256]{2,1,0:T(8,128)(2,1)S(1)} %get-tuple-element.106), channel_id=1, source_target_pairs={{0,8},{4,12},{8,0},{12,4},{16,24},{20,28},{24,16},{28,20},{1,9},{5... | collective-permute-start | bytes 196616 | tf_op jit(solution)/shard_map/ppermute | solution.py:238
  30.2 6.5 %collective-permute-start.2 = (bf16[4,16,256]{2,1,0:T(8,128)(2,1)S(1)}, bf16[4,16,256]{2,1,0:T(8,128)(2,1)S(1)}, u32[]{:S(2)}, u32[]{:S(2)}) collective-permute-start(bf16[4,16,256]{2,1,0:T(8,128)(2,1)S(1)} %fusion.45), channel_id=1, source_target_pairs={{0,16},{4,20},{8,24},{12,28},{16,0},{20,4},{24,8},{28,12},{1,17},{... | collective-permute-start | bytes 98312 | tf_op jit(solution)/shard_map/ppermute | solution.py:238
  31.3 5.9 %collective-permute-start.5 = (bf16[4,16,256]{2,1,0:T(8,128)(2,1)S(1)}, bf16[4,16,256]{2,1,0:T(8,128)(2,1)S(1)}, u32[]{:S(2)}, u32[]{:S(2)}) collective-permute-start(bf16[4,16,256]{2,1,0:T(8,128)(2,1)S(1)} %fusion.42), channel_id=1, source_target_pairs={{0,16},{4,20},{8,24},{12,28},{16,0},{20,4},{24,8},{28,12},{1,17},{... | collective-permute-start | bytes 98312 | tf_op jit(solution)/shard_map/ppermute | solution.py:238
  34.4 4.0 %collective-permute-start.8 = (bf16[4,16,256]{2,1,0:T(8,128)(2,1)S(1)}, bf16[4,16,256]{2,1,0:T(8,128)(2,1)S(1)}, u32[]{:S(2)}, u32[]{:S(2)}) collective-permute-start(bf16[4,16,256]{2,1,0:T(8,128)(2,1)S(1)} %get-tuple-element.130), channel_id=1, source_target_pairs={{0,4},{4,0},{8,12},{12,8},{16,20},{20,16},{24,28},{28,24},{1,5},{5... | collective-permute-start | bytes 98312 | tf_op jit(solution)/shard_map/ppermute | solution.py:238
  36.4 5.0 %collective-permute-start.11 = (bf16[4,16,256]{2,1,0:T(8,128)(2,1)S(1)}, bf16[4,16,256]{2,1,0:T(8,128)(2,1)S(1)}, u32[]{:S(2)}, u32[]{:S(2)}) collective-permute-start(bf16[4,16,256]{2,1,0:T(8,128)(2,1)S(1)} %fusion.36), channel_id=1, source_target_pairs={{0,16},{4,20},{8,24},{12,28},{16,0},{20,4},{24,8},{28,12},{1,17},{... | collective-permute-start | bytes 98312 | tf_op jit(solution)/shard_map/ppermute | solution.py:238
  43.4 6.1 %collective-permute-start.18 = (bf16[16,16,256]{2,1,0:T(8,128)(2,1)S(1)}, bf16[16,16,256]{2,1,0:T(8,128)(2,1)S(1)}, u32[]{:S(2)}, u32[]{:S(2)}) collective-permute-start(bf16[16,16,256]{2,1,0:T(8,128)(2,1)S(1)} %get-tuple-element.59), channel_id=1, source_target_pairs={{0,8},{4,12},{8,0},{12,4},{16,24},{20,28},{24,16},{28,20},{1,9},{5... | collective-permute-start | bytes 393224 | tf_op jit(solution)/shard_map/ppermute | solution.py:238
  43.9 7.7 %collective-permute-start.12 = (bf16[16,16,256]{2,1,0:T(8,128)(2,1)S(1)}, bf16[16,16,256]{2,1,0:T(8,128)(2,1)S(1)}, u32[]{:S(2)}, u32[]{:S(2)}) collective-permute-start(bf16[16,16,256]{2,1,0:T(8,128)(2,1)S(1)} %get-tuple-element.55), channel_id=1, source_target_pairs={{0,4},{4,0},{8,12},{12,8},{16,20},{20,16},{24,28},{28,24},{1,5},{5... | collective-permute-start | bytes 393224 | tf_op jit(solution)/shard_map/ppermute | solution.py:238
  47.4 5.0 %collective-permute-start.15 = (bf16[16,16,256]{2,1,0:T(8,128)(2,1)S(1)}, bf16[16,16,256]{2,1,0:T(8,128)(2,1)S(1)}, u32[]{:S(2)}, u32[]{:S(2)}) collective-permute-start(bf16[16,16,256]{2,1,0:T(8,128)(2,1)S(1)} %get-tuple-element.57), channel_id=1, source_target_pairs={{0,4},{4,0},{8,12},{12,8},{16,20},{20,16},{24,28},{28,24},{1,5},{5... | collective-permute-start | bytes 393224 | tf_op jit(solution)/shard_map/ppermute | solution.py:238
  48.0 6.4 %collective-permute-start.21 = (bf16[16,16,256]{2,1,0:T(8,128)(2,1)S(1)}, bf16[16,16,256]{2,1,0:T(8,128)(2,1)S(1)}, u32[]{:S(2)}, u32[]{:S(2)}) collective-permute-start(bf16[16,16,256]{2,1,0:T(8,128)(2,1)S(1)} %get-tuple-element.61), channel_id=1, source_target_pairs={{0,4},{4,0},{8,12},{12,8},{16,20},{20,16},{24,28},{28,24},{1,5},{5... | collective-permute-start | bytes 393224 | tf_op jit(solution)/shard_map/ppermute | solution.py:238
  49.5 9.7 %collective-permute-start.19 = (bf16[8,16,256]{2,1,0:T(8,128)(2,1)S(1)}, bf16[8,16,256]{2,1,0:T(8,128)(2,1)S(1)}, u32[]{:S(2)}, u32[]{:S(2)}) collective-permute-start(bf16[8,16,256]{2,1,0:T(8,128)(2,1)S(1)} %get-tuple-element.100), channel_id=1, source_target_pairs={{0,16},{4,20},{8,24},{12,28},{16,0},{20,4},{24,8},{28,12},{1,17},{... | collective-permute-start | bytes 196616 | tf_op jit(solution)/shard_map/ppermute | solution.py:238
  51.7 4.4 %collective-permute-start.13 = (bf16[8,16,256]{2,1,0:T(8,128)(2,1)S(1)}, bf16[8,16,256]{2,1,0:T(8,128)(2,1)S(1)}, u32[]{:S(2)}, u32[]{:S(2)}) collective-permute-start(bf16[8,16,256]{2,1,0:T(8,128)(2,1)S(1)} %get-tuple-element.104), channel_id=1, source_target_pairs={{0,8},{4,12},{8,0},{12,4},{16,24},{20,28},{24,16},{28,20},{1,9},{5... | collective-permute-start | bytes 196616 | tf_op jit(solution)/shard_map/ppermute | solution.py:238
  52.4 5.3 %collective-permute-start.16 = (bf16[8,16,256]{2,1,0:T(8,128)(2,1)S(1)}, bf16[8,16,256]{2,1,0:T(8,128)(2,1)S(1)}, u32[]{:S(2)}, u32[]{:S(2)}) collective-permute-start(bf16[8,16,256]{2,1,0:T(8,128)(2,1)S(1)} %get-tuple-element.102), channel_id=1, source_target_pairs={{0,8},{4,12},{8,0},{12,4},{16,24},{20,28},{24,16},{28,20},{1,9},{5... | collective-permute-start | bytes 196616 | tf_op jit(solution)/shard_map/ppermute | solution.py:238
  54.4 4.8 %collective-permute-start.22 = (bf16[8,16,256]{2,1,0:T(8,128)(2,1)S(1)}, bf16[8,16,256]{2,1,0:T(8,128)(2,1)S(1)}, u32[]{:S(2)}, u32[]{:S(2)}) collective-permute-start(bf16[8,16,256]{2,1,0:T(8,128)(2,1)S(1)} %get-tuple-element.98), channel_id=1, source_target_pairs={{0,8},{4,12},{8,0},{12,4},{16,24},{20,28},{24,16},{28,20},{1,9},{5... | collective-permute-start | bytes 196616 | tf_op jit(solution)/shard_map/ppermute | solution.py:238
  56.2 6.6 %collective-permute-start.14 = (bf16[4,16,256]{2,1,0:T(8,128)(2,1)S(1)}, bf16[4,16,256]{2,1,0:T(8,128)(2,1)S(1)}, u32[]{:S(2)}, u32[]{:S(2)}) collective-permute-start(bf16[4,16,256]{2,1,0:T(8,128)(2,1)S(1)} %fusion.33), channel_id=1, source_target_pairs={{0,16},{4,20},{8,24},{12,28},{16,0},{20,4},{24,8},{28,12},{1,17},{... | collective-permute-start | bytes 98312 | tf_op jit(solution)/shard_map/ppermute | solution.py:238
  57.8 5.0 %collective-permute-start.17 = (bf16[4,16,256]{2,1,0:T(8,128)(2,1)S(1)}, bf16[4,16,256]{2,1,0:T(8,128)(2,1)S(1)}, u32[]{:S(2)}, u32[]{:S(2)}) collective-permute-start(bf16[4,16,256]{2,1,0:T(8,128)(2,1)S(1)} %fusion.30), channel_id=1, source_target_pairs={{0,16},{4,20},{8,24},{12,28},{16,0},{20,4},{24,8},{28,12},{1,17},{... | collective-permute-start | bytes 98312 | tf_op jit(solution)/shard_map/ppermute | solution.py:238
  59.3 4.0 %collective-permute-start.20 = (bf16[4,16,256]{2,1,0:T(8,128)(2,1)S(1)}, bf16[4,16,256]{2,1,0:T(8,128)(2,1)S(1)}, u32[]{:S(2)}, u32[]{:S(2)}) collective-permute-start(bf16[4,16,256]{2,1,0:T(8,128)(2,1)S(1)} %get-tuple-element.131), channel_id=1, source_target_pairs={{0,4},{4,0},{8,12},{12,8},{16,20},{20,16},{24,28},{28,24},{1,5},{5... | collective-permute-start | bytes 98312 | tf_op jit(solution)/shard_map/ppermute | solution.py:238
  61.3 5.0 %collective-permute-start.23 = (bf16[4,16,256]{2,1,0:T(8,128)(2,1)S(1)}, bf16[4,16,256]{2,1,0:T(8,128)(2,1)S(1)}, u32[]{:S(2)}, u32[]{:S(2)}) collective-permute-start(bf16[4,16,256]{2,1,0:T(8,128)(2,1)S(1)} %fusion.24), channel_id=1, source_target_pairs={{0,16},{4,20},{8,24},{12,28},{16,0},{20,4},{24,8},{28,12},{1,17},{... | collective-permute-start | bytes 98312 | tf_op jit(solution)/shard_map/ppermute | solution.py:238
  68.3 6.9 %collective-permute-start.30 = (bf16[16,16,256]{2,1,0:T(8,128)(2,1)S(1)}, bf16[16,16,256]{2,1,0:T(8,128)(2,1)S(1)}, u32[]{:S(2)}, u32[]{:S(2)}) collective-permute-start(bf16[16,16,256]{2,1,0:T(8,128)(2,1)S(1)} %get-tuple-element.68), channel_id=1, source_target_pairs={{0,8},{4,12},{8,0},{12,4},{16,24},{20,28},{24,16},{28,20},{1,9},{5... | collective-permute-start | bytes 393224 | tf_op jit(solution)/shard_map/ppermute | solution.py:238
  69.8 6.2 %collective-permute-start.24 = (bf16[16,16,256]{2,1,0:T(8,128)(2,1)S(1)}, bf16[16,16,256]{2,1,0:T(8,128)(2,1)S(1)}, u32[]{:S(2)}, u32[]{:S(2)}) collective-permute-start(bf16[16,16,256]{2,1,0:T(8,128)(2,1)S(1)} %get-tuple-element.64), channel_id=1, source_target_pairs={{0,4},{4,0},{8,12},{12,8},{16,20},{20,16},{24,28},{28,24},{1,5},{5... | collective-permute-start | bytes 393224 | tf_op jit(solution)/shard_map/ppermute | solution.py:238
  73.0 5.2 %collective-permute-start.27 = (bf16[16,16,256]{2,1,0:T(8,128)(2,1)S(1)}, bf16[16,16,256]{2,1,0:T(8,128)(2,1)S(1)}, u32[]{:S(2)}, u32[]{:S(2)}) collective-permute-start(bf16[16,16,256]{2,1,0:T(8,128)(2,1)S(1)} %get-tuple-element.66), channel_id=1, source_target_pairs={{0,4},{4,0},{8,12},{12,8},{16,20},{20,16},{24,28},{28,24},{1,5},{5... | collective-permute-start | bytes 393224 | tf_op jit(solution)/shard_map/ppermute | solution.py:238
  73.8 5.8 %collective-permute-start.33 = (bf16[16,16,256]{2,1,0:T(8,128)(2,1)S(1)}, bf16[16,16,256]{2,1,0:T(8,128)(2,1)S(1)}, u32[]{:S(2)}, u32[]{:S(2)}) collective-permute-start(bf16[16,16,256]{2,1,0:T(8,128)(2,1)S(1)} %get-tuple-element.70), channel_id=1, source_target_pairs={{0,4},{4,0},{8,12},{12,8},{16,20},{20,16},{24,28},{28,24},{1,5},{5... | collective-permute-start | bytes 393224 | tf_op jit(solution)/shard_map/ppermute | solution.py:238
  75.2 9.0 %collective-permute-start.31 = (bf16[8,16,256]{2,1,0:T(8,128)(2,1)S(1)}, bf16[8,16,256]{2,1,0:T(8,128)(2,1)S(1)}, u32[]{:S(2)}, u32[]{:S(2)}) collective-permute-start(bf16[8,16,256]{2,1,0:T(8,128)(2,1)S(1)} %get-tuple-element.92), channel_id=1, source_target_pairs={{0,16},{4,20},{8,24},{12,28},{16,0},{20,4},{24,8},{28,12},{1,17},{... | collective-permute-start | bytes 196616 | tf_op jit(solution)/shard_map/ppermute | solution.py:238
  76.1 5.0 %collective-permute-start.25 = (bf16[8,16,256]{2,1,0:T(8,128)(2,1)S(1)}, bf16[8,16,256]{2,1,0:T(8,128)(2,1)S(1)}, u32[]{:S(2)}, u32[]{:S(2)}) collective-permute-start(bf16[8,16,256]{2,1,0:T(8,128)(2,1)S(1)} %get-tuple-element.96), channel_id=1, source_target_pairs={{0,8},{4,12},{8,0},{12,4},{16,24},{20,28},{24,16},{28,20},{1,9},{5... | collective-permute-start | bytes 196616 | tf_op jit(solution)/shard_map/ppermute | solution.py:238
  78.2 4.4 %collective-permute-start.28 = (bf16[8,16,256]{2,1,0:T(8,128)(2,1)S(1)}, bf16[8,16,256]{2,1,0:T(8,128)(2,1)S(1)}, u32[]{:S(2)}, u32[]{:S(2)}) collective-permute-start(bf16[8,16,256]{2,1,0:T(8,128)(2,1)S(1)} %get-tuple-element.94), channel_id=1, source_target_pairs={{0,8},{4,12},{8,0},{12,4},{16,24},{20,28},{24,16},{28,20},{1,9},{5... | collective-permute-start | bytes 196616 | tf_op jit(solution)/shard_map/ppermute | solution.py:238
  79.7 4.5 %collective-permute-start.34 = (bf16[8,16,256]{2,1,0:T(8,128)(2,1)S(1)}, bf16[8,16,256]{2,1,0:T(8,128)(2,1)S(1)}, u32[]{:S(2)}, u32[]{:S(2)}) collective-permute-start(bf16[8,16,256]{2,1,0:T(8,128)(2,1)S(1)} %get-tuple-element.90), channel_id=1, source_target_pairs={{0,8},{4,12},{8,0},{12,4},{16,24},{20,28},{24,16},{28,20},{1,9},{5... | collective-permute-start | bytes 196616 | tf_op jit(solution)/shard_map/ppermute | solution.py:238
  81.1 6.1 %collective-permute-start.26 = (bf16[4,16,256]{2,1,0:T(8,128)(2,1)S(1)}, bf16[4,16,256]{2,1,0:T(8,128)(2,1)S(1)}, u32[]{:S(2)}, u32[]{:S(2)}) collective-permute-start(bf16[4,16,256]{2,1,0:T(8,128)(2,1)S(1)} %fusion.21), channel_id=1, source_target_pairs={{0,16},{4,20},{8,24},{12,28},{16,0},{20,4},{24,8},{28,12},{1,17},{... | collective-permute-start | bytes 98312 | tf_op jit(solution)/shard_map/ppermute | solution.py:238
  82.6 4.9 %collective-permute-start.29 = (bf16[4,16,256]{2,1,0:T(8,128)(2,1)S(1)}, bf16[4,16,256]{2,1,0:T(8,128)(2,1)S(1)}, u32[]{:S(2)}, u32[]{:S(2)}) collective-permute-start(bf16[4,16,256]{2,1,0:T(8,128)(2,1)S(1)} %fusion.18), channel_id=1, source_target_pairs={{0,16},{4,20},{8,24},{12,28},{16,0},{20,4},{24,8},{28,12},{1,17},{... | collective-permute-start | bytes 98312 | tf_op jit(solution)/shard_map/ppermute | solution.py:238
  84.2 4.4 %collective-permute-start.32 = (bf16[4,16,256]{2,1,0:T(8,128)(2,1)S(1)}, bf16[4,16,256]{2,1,0:T(8,128)(2,1)S(1)}, u32[]{:S(2)}, u32[]{:S(2)}) collective-permute-start(bf16[4,16,256]{2,1,0:T(8,128)(2,1)S(1)} %get-tuple-element.132), channel_id=1, source_target_pairs={{0,4},{4,0},{8,12},{12,8},{16,20},{20,16},{24,28},{28,24},{1,5},{5... | collective-permute-start | bytes 98312 | tf_op jit(solution)/shard_map/ppermute | solution.py:238
  85.9 5.6 %collective-permute-start.35 = (bf16[4,16,256]{2,1,0:T(8,128)(2,1)S(1)}, bf16[4,16,256]{2,1,0:T(8,128)(2,1)S(1)}, u32[]{:S(2)}, u32[]{:S(2)}) collective-permute-start(bf16[4,16,256]{2,1,0:T(8,128)(2,1)S(1)} %fusion.12), channel_id=1, source_target_pairs={{0,16},{4,20},{8,24},{12,28},{16,0},{20,4},{24,8},{28,12},{1,17},{... | collective-permute-start | bytes 98312 | tf_op jit(solution)/shard_map/ppermute | solution.py:238
  93.5 22.8 %copy-start.1 = (bf16[4,16,1024]{2,1,0:T(8,128)(2,1)S(1)}, bf16[4,16,1024]{2,1,0:T(8,128)(2,1)}, u32[]{:S(2)}) copy-start(bf16[4,16,1024]{2,1,0:T(8,128)(2,1)} %forward_ref.1) | copy-start | bytes 393220
  95.5 5.0 %collective-permute-start.39 = (bf16[16,16,256]{2,1,0:T(8,128)(2,1)S(1)}, bf16[16,16,256]{2,1,0:T(8,128)(2,1)S(1)}, u32[]{:S(2)}, u32[]{:S(2)}) collective-permute-start(bf16[16,16,256]{2,1,0:T(8,128)(2,1)S(1)} %get-tuple-element.75), channel_id=1, source_target_pairs={{0,4},{4,0},{8,12},{12,8},{16,20},{20,16},{24,28},{28,24},{1,5},{5... | collective-permute-start | bytes 393224 | tf_op jit(solution)/shard_map/ppermute | solution.py:238
  97.1 5.1 %collective-permute-start.42 = (bf16[16,16,256]{2,1,0:T(8,128)(2,1)S(1)}, bf16[16,16,256]{2,1,0:T(8,128)(2,1)S(1)}, u32[]{:S(2)}, u32[]{:S(2)}) collective-permute-start(bf16[16,16,256]{2,1,0:T(8,128)(2,1)S(1)} %get-tuple-element.77), channel_id=1, source_target_pairs={{0,4},{4,0},{8,12},{12,8},{16,20},{20,16},{24,28},{28,24},{1,5},{5... | collective-permute-start | bytes 393224 | tf_op jit(solution)/shard_map/ppermute | solution.py:238
  97.6 6.1 %collective-permute-start.36 = (bf16[16,16,256]{2,1,0:T(8,128)(2,1)S(1)}, bf16[16,16,256]{2,1,0:T(8,128)(2,1)S(1)}, u32[]{:S(2)}, u32[]{:S(2)}) collective-permute-start(bf16[16,16,256]{2,1,0:T(8,128)(2,1)S(1)} %get-tuple-element.73), channel_id=1, source_target_pairs={{0,4},{4,0},{8,12},{12,8},{16,20},{20,16},{24,28},{28,24},{1,5},{5... | collective-permute-start | bytes 393224 | tf_op jit(solution)/shard_map/ppermute | solution.py:238
  99.2 5.7 %collective-permute-start.45 = (bf16[16,16,256]{2,1,0:T(8,128)(2,1)S(1)}, bf16[16,16,256]{2,1,0:T(8,128)(2,1)S(1)}, u32[]{:S(2)}, u32[]{:S(2)}) collective-permute-start(bf16[16,16,256]{2,1,0:T(8,128)(2,1)S(1)} %get-tuple-element.79), channel_id=1, source_target_pairs={{0,8},{4,12},{8,0},{12,4},{16,24},{20,28},{24,16},{28,20},{1,9},{5... | collective-permute-start | bytes 393224 | tf_op jit(solution)/shard_map/ppermute | solution.py:238
  100.5 6.4 %collective-permute-start.40 = (bf16[8,16,256]{2,1,0:T(8,128)(2,1)S(1)}, bf16[8,16,256]{2,1,0:T(8,128)(2,1)S(1)}, u32[]{:S(2)}, u32[]{:S(2)}) collective-permute-start(bf16[8,16,256]{2,1,0:T(8,128)(2,1)S(1)} %get-tuple-element.86), channel_id=1, source_target_pairs={{0,8},{4,12},{8,0},{12,4},{16,24},{20,28},{24,16},{28,20},{1,9},{5... | collective-permute-start | bytes 196616 | tf_op jit(solution)/shard_map/ppermute | solution.py:238
  102.3 7.8 %collective-permute-start.43 = (bf16[8,16,256]{2,1,0:T(8,128)(2,1)S(1)}, bf16[8,16,256]{2,1,0:T(8,128)(2,1)S(1)}, u32[]{:S(2)}, u32[]{:S(2)}) collective-permute-start(bf16[8,16,256]{2,1,0:T(8,128)(2,1)S(1)} %get-tuple-element.84), channel_id=1, source_target_pairs={{0,8},{4,12},{8,0},{12,4},{16,24},{20,28},{24,16},{28,20},{1,9},{5... | collective-permute-start | bytes 196616 | tf_op jit(solution)/shard_map/ppermute | solution.py:238
  103.7 4.3 %collective-permute-start.37 = (bf16[8,16,256]{2,1,0:T(8,128)(2,1)S(1)}, bf16[8,16,256]{2,1,0:T(8,128)(2,1)S(1)}, u32[]{:S(2)}, u32[]{:S(2)}) collective-permute-start(bf16[8,16,256]{2,1,0:T(8,128)(2,1)S(1)} %get-tuple-element.88), channel_id=1, source_target_pairs={{0,8},{4,12},{8,0},{12,4},{16,24},{20,28},{24,16},{28,20},{1,9},{5... | collective-permute-start | bytes 196616 | tf_op jit(solution)/shard_map/ppermute | solution.py:238
  104.9 5.9 %collective-permute-start.46 = (bf16[8,16,256]{2,1,0:T(8,128)(2,1)S(1)}, bf16[8,16,256]{2,1,0:T(8,128)(2,1)S(1)}, u32[]{:S(2)}, u32[]{:S(2)}) collective-permute-start(bf16[8,16,256]{2,1,0:T(8,128)(2,1)S(1)} %get-tuple-element.82), channel_id=1, source_target_pairs={{0,16},{4,20},{8,24},{12,28},{16,0},{20,4},{24,8},{28,12},{1,17},{... | collective-permute-start | bytes 196616 | tf_op jit(solution)/shard_map/ppermute | solution.py:238
  107.0 6.1 %collective-permute-start.41 = (bf16[4,16,256]{2,1,0:T(8,128)(2,1)S(1)}, bf16[4,16,256]{2,1,0:T(8,128)(2,1)S(1)}, u32[]{:S(2)}, u32[]{:S(2)}) collective-permute-start(bf16[4,16,256]{2,1,0:T(8,128)(2,1)S(1)} %fusion.6), channel_id=1, source_target_pairs={{0,16},{4,20},{8,24},{12,28},{16,0},{20,4},{24,8},{28,12},{1,17},{... | collective-permute-start | bytes 98312 | tf_op jit(solution)/shard_map/ppermute | solution.py:238
  108.0 5.1 %collective-permute-start.38 = (bf16[4,16,256]{2,1,0:T(8,128)(2,1)S(1)}, bf16[4,16,256]{2,1,0:T(8,128)(2,1)S(1)}, u32[]{:S(2)}, u32[]{:S(2)}) collective-permute-start(bf16[4,16,256]{2,1,0:T(8,128)(2,1)S(1)} %fusion.9), channel_id=1, source_target_pairs={{0,16},{4,20},{8,24},{12,28},{16,0},{20,4},{24,8},{28,12},{1,17},{... | collective-permute-start | bytes 98312 | tf_op jit(solution)/shard_map/ppermute | solution.py:238
  110.9 5.1 %collective-permute-start.44 = (bf16[4,16,256]{2,1,0:T(8,128)(2,1)S(1)}, bf16[4,16,256]{2,1,0:T(8,128)(2,1)S(1)}, u32[]{:S(2)}, u32[]{:S(2)}) collective-permute-start(bf16[4,16,256]{2,1,0:T(8,128)(2,1)S(1)} %get-tuple-element.133), channel_id=1, source_target_pairs={{0,16},{4,20},{8,24},{12,28},{16,0},{20,4},{24,8},{28,12},{1,17},{... | collective-permute-start | bytes 98312 | tf_op jit(solution)/shard_map/ppermute | solution.py:238
  112.3 4.0 %collective-permute-start.47 = (bf16[4,16,256]{2,1,0:T(8,128)(2,1)S(1)}, bf16[4,16,256]{2,1,0:T(8,128)(2,1)S(1)}, u32[]{:S(2)}, u32[]{:S(2)}) collective-permute-start(bf16[4,16,256]{2,1,0:T(8,128)(2,1)S(1)} %fusion), channel_id=1, source_target_pairs={{0,4},{4,0},{8,12},{12,8},{16,20},{20,16},{24,28},{28,24},{1,5},{5... | collective-permute-start | bytes 98312 | tf_op jit(solution)/shard_map/ppermute | solution.py:238
  117.1 3.3 %collective-permute-start.50 = (f32[4,1024]{1,0:T(4,128)S(1)}, f32[4,1024]{1,0:T(4,128)S(1)}, u32[]{:S(2)}, u32[]{:S(2)}) collective-permute-start(f32[4,1024]{1,0:T(4,128)S(1)} %get-tuple-element.81), channel_id=1, source_target_pairs={{0,3},{1,2},{2,1},{3,0},{4,7},{5,6},{6,5},{7,4},{8,11},{9,10},{10,... | collective-permute-start | bytes 49160 | tf_op jit(solution)/shard_map/ppermute | solution.py:415
  117.1 3.8 %collective-permute-start.49 = (f32[4,1024]{1,0:T(4,128)S(1)}, f32[4,1024]{1,0:T(4,128)S(1)}, u32[]{:S(2)}, u32[]{:S(2)}) collective-permute-start(f32[4,1024]{1,0:T(4,128)S(1)} %get-tuple-element.81), channel_id=1, source_target_pairs={{0,2},{1,3},{2,0},{3,1},{4,6},{5,7},{6,4},{7,5},{8,10},{9,11},{10,... | collective-permute-start | bytes 49160 | tf_op jit(solution)/shard_map/ppermute | solution.py:415
  118.6 2.3 %collective-permute-start.48 = (f32[4,1024]{1,0:T(4,128)S(1)}, f32[4,1024]{1,0:T(4,128)S(1)}, u32[]{:S(2)}, u32[]{:S(2)}) collective-permute-start(f32[4,1024]{1,0:T(4,128)S(1)} %get-tuple-element.81), channel_id=1, source_target_pairs={{0,1},{1,0},{2,3},{3,2},{4,5},{5,4},{6,7},{7,6},{8,9},{9,8},{10,11... | collective-permute-start | bytes 49160 | tf_op jit(solution)/shard_map/ppermute | solution.py:415

commit v4 on v3

--- a/solution.py
+++ b/solution.py
@@ -11,9 +11,9 @@
 
 def parts_of(unknowns, peers):
     bits = list(range(peers.bit_length() - 1))
-    near, far = bits, bits[1:] + bits[:1]
-    width = unknowns // 4
-    return [(i * width, width, far if i == 3 else near) for i in range(4)]
+    turned = bits[1:2] + bits[:1] + bits[2:]
+    width = unknowns // 2
+    return [(0, width, bits), (width, width, turned)]
 
 
 def spot(order, rel):
@@ -91,7 +91,7 @@
     cols_hbm, owner_hbm, ranks_hbm, misfit_hbm, u_hbm, v_hbm = refs[:6]
     u_ref, v_ref, code_ref = refs[6:9]
     outs = refs[9 : 9 + 2 * len(parts)]
-    cols, owner, ranks, misfit, tile_at, code_at, rank_at, count, small, u_sem, v_sem = refs[
+    cols, owner, ranks, misfit, tile_at, code_at, rank_at, count, lhs_ref, small, u_sem, v_sem = refs[
         9 + 2 * len(parts) :
     ]
     here = lax.axis_index("rows")
@@ -112,38 +112,35 @@
     for copy in copies[:3]:
         copy.wait()
 
+    def load(whence, to, sem, tile, at):
+        pltpu.make_async_copy(
+            whence.at[pl.ds(pl.multiple_of(tile * rank_max, rank_max), rank_max)],
+            to.at[pl.ds(pl.multiple_of(at * rank_max, rank_max), rank_max)],
+            sem.at[lax.div(at, group_tiles)],
+        ).start()
+
     def sort_tile(tile, carry):
         row, k = lax.div(tile, tiles_row), lax.rem(tile, tiles_row)
         slot = owner[cols[k, here * rows_dev + row]]
         rel = jnp.bitwise_xor(lax.div(slot, rows_dev), here)
         at = rel * group_tiles + count[rel]
         count[rel] = count[rel] + 1
+        load(u_hbm, u_ref, u_sem, tile, at)
         tile_at[at] = tile
         code_at[at] = row * rows_dev + lax.rem(slot, rows_dev)
         rank_at[at] = ranks[row, k]
         return carry
 
-    lax.fori_loop(0, tiles, sort_tile, 0)
-
-    def load(whence, to, sem, group):
-        def one(i, carry):
-            at = group * group_tiles + i
-            pltpu.make_async_copy(
-                whence.at[pl.ds(pl.multiple_of(tile_at[at] * rank_max, rank_max), rank_max)],
-                to.at[pl.ds(pl.multiple_of(at * rank_max, rank_max), rank_max)],
-                sem.at[group],
-            ).start()
-            return carry
-
-        lax.fori_loop(0, group_tiles, one, 0)
+    def load_v(at, carry):
+        load(v_hbm, v_ref, v_sem, tile_at[at], at)
+        return carry
 
     def loaded(ref, sem, group):
         piece = ref.at[pl.ds(group * deep, deep)]
         pltpu.make_async_copy(piece, piece, sem.at[group]).wait()
 
-    for group in range(peers):
-        load(u_hbm, u_ref, u_sem, group)
-        load(v_hbm, v_ref, v_sem, group)
+    lax.fori_loop(0, tiles, sort_tile, 0)
+    lax.fori_loop(0, tiles, load_v, 0)
     lane = lax.broadcasted_iota(jnp.int32, (1, deep), 1)
     for group in range(peers):
         code = jnp.full((1, deep), -1, jnp.int32)
@@ -158,8 +155,10 @@
         loaded(u_ref, u_sem, group)
         code = code_ref[pl.ds(group, 1), :]
         every = times_u(low, u_ref[pl.ds(group * deep, deep), :])
-        lhs = by_slot(pick_rows(every, code, sources, rows_dev), code, rows_dev)
+        lhs_ref[group] = by_slot(pick_rows(every, code, sources, rows_dev), code, rows_dev)
+    for group in range(peers):
         loaded(v_ref, v_sem, group)
+        lhs = lhs_ref[group]
         for i, part in enumerate(parts):
             put_terms(lhs, v_ref, group, part, outs[2 * i : 2 * i + 2], rows_dev, peers)
 
@@ -247,7 +246,7 @@
     tiles = rows_dev * tiles_row
     deep = tiles // peers * rank_max
     parts = parts_of(unknowns, peers)
-    first_sent, then_sent, late = [0, 3], [1, 2], 2
+    first_sent, then_sent, late = [0, 1], [], 1
     early = [i for i in range(len(parts)) if i != late]
     half = (peers // 2 * rows_dev, sources)
     sent = [jax.ShapeDtypeStruct((*half, part[1]), jnp.bfloat16) for part in parts]
@@ -271,6 +270,7 @@
             smem(tiles),
             smem(tiles),
             smem(peers),
+            pltpu.VMEM((peers, rows_dev * sources, deep), jnp.bfloat16),
             pltpu.SemaphoreType.DMA((4,)),
             pltpu.SemaphoreType.DMA((peers,)),
             pltpu.SemaphoreType.DMA((peers,)),
@@ -292,7 +292,7 @@
                 in_specs=vmem(3 + 2 * len(early)),
                 out_specs=vmem(1)[0],
                 compiler_params=params(),
-                cost_estimate=cost(u.shape[0], unknowns * 3 // 4, sources),
+                cost_estimate=cost(u.shape[0], unknowns // 2, sources),
                 name="early",
             )(code, contrast, *(x for i in early for x in (base[i], came[i])), in_vmem(u))
             lhs, *some = pl.pallas_call(
@@ -311,7 +311,7 @@
                 in_specs=vmem(2),
                 out_specs=vmem(len(then_sent) + len(parts)),
                 compiler_params=params(),
-                cost_estimate=cost(u.shape[0], unknowns * 3 // 4, sources),
+                cost_estimate=cost(u.shape[0], unknowns // 2, sources),
                 name="rest",
             )(lhs, in_vmem(v))
             goes = [None] * len(parts)

time: 122 us -> 116 us (0.951)
  starting transfers between devices: 68.9 us -> 48.7 us
  waiting for transfers between devices: 14.9 us -> 28.4 us
  Pallas kernels: 35.2 us -> 36.5 us
    ppermute x48 -> x24, starting transfers between devices: 67.1 us -> 46.9 us  [swap(): return lax.ppermute(x, 'rows', [(i, i ^ 1 << bit) for i in range(peers)])]
    ppermute x48 -> x24, waiting for transfers between devices: 13 us -> 26.5 us  [swap(): return lax.ppermute(x, 'rows', [(i, i ^ 1 << bit) for i in range(peers)])]
    pallas_call x3, Pallas kernels: 5.97 us -> 11.1 us  [slot_sums(): pl.pallas_call(functools.partial(ready_kernel, dims, parts[late], [parts[...]
    pallas_call x3, Pallas kernels: 8.89 us -> 6.24 us  [slot_sums(): pl.pallas_call(functools.partial(early_kernel, dims, [parts[i] for i in e...]
    pallas_call x3, Pallas kernels: 5.72 us -> 3.69 us  [slot_sums(): pl.pallas_call(functools.partial(rest_kernel, dims, then_sent, parts), ou...]
  transfers between devices with their start and end apart: 51 -> 27, of which waited for: 20 -> 20; matrix products, arithmetic and copies ran while one was open for 1% -> 1% of each run, Pallas kernels for 10% -> 9%
where the time goes in v4:
time: 116 us
  starting transfers between devices  48.7 us (42%)
  Pallas kernels  36.5 us (31%)
  waiting for transfers between devices  28.4 us (24%)
  other arithmetic  1.58 us (1%)
    ppermute x24, starting transfers between devices, swap(): return lax.ppermute(x, 'rows', [(i, i ^ 1 << bit) for i in range(peers)])  46.9 us
    ppermute x24, waiting for transfers between devices, swap(): return lax.ppermute(x, 'rows', [(i, i ^ 1 << bit) for i in range(peers)])  26.5 us
    pallas_call x1, Pallas kernels, slot_sums(): pl.pallas_call(functools.partial(start_kernel, (rows_dev, tiles_row, rank...  14.7 us
    pallas_call x3, Pallas kernels, slot_sums(): pl.pallas_call(functools.partial(ready_kernel, dims, parts[late], [parts[...  11.1 us
    pallas_call x3, Pallas kernels, slot_sums(): pl.pallas_call(functools.partial(early_kernel, dims, [parts[i] for i in e...  6.24 us
    pallas_call x3, Pallas kernels, slot_sums(): pl.pallas_call(functools.partial(rest_kernel, dims, then_sent, parts), ou...  3.69 us
  transfers between devices with their start and end apart: 27, of which 20 were waited for; matrix products, arithmetic and copies ran while one was open for 1% of the time, Pallas kernels for 9%

profile of v4, /device:TPU:0, one launch (start us, length us, event | category | flops | bytes accessed | tf_op | source)
XLA Modules:
  0.0 116.1 jit_solution(15335536580092469772)
XLA Ops:
  0.7 14.7 %start.1 = (bf16[6144,1024]{1,0:T(8,128)(2,1)S(1)}, bf16[6144,1024]{1,0:T(8,128)(2,1)S(1)}, s32[8,768]{1,0:T(8,128)S(1)}, f32[16,16,512]{2,1,0:T(8,128)S(1)}, bf...) custom-call(s32[16,32]{1,0:T(8,128)} %bitcast.11, s32[32]{0:T(128)} %refs_1_.1, ...), custom_call_target="tpu_custom_call" | custom-call | flops 402653184 | bytes 25165824 | tf_op jit(solution)/shard_map/start/pallas_call | solution.py:257
  15.4 2.8 %collective-permute-start = (bf16[16,16,512]{2,1,0:T(8,128)(2,1)S(1)}, bf16[16,16,512]{2,1,0:T(8,128)(2,1)S(1)}, u32[]{:S(2)}, u32[]{:S(2)}) collective-permute-start(bf16[16,16,512]{2,1,0:T(8,128)(2,1)S(1)} %get-tuple-element.28), channel_id=1, source_target_pairs={{0,4},{4,0},{8,12},{12,8},{16,20},{20,16},{24,28},{28,24},{1,5},{5... | collective-permute-start | bytes 786440 | tf_op jit(solution)/shard_map/ppermute | solution.py:237
  18.2 1.6 %collective-permute-start.3 = (bf16[16,16,512]{2,1,0:T(8,128)(2,1)S(1)}, bf16[16,16,512]{2,1,0:T(8,128)(2,1)S(1)}, u32[]{:S(2)}, u32[]{:S(2)}) collective-permute-start(bf16[16,16,512]{2,1,0:T(8,128)(2,1)S(1)} %get-tuple-element.31), channel_id=1, source_target_pairs={{0,8},{4,12},{8,0},{12,4},{16,24},{20,28},{24,16},{28,20},{1,9},{5... | collective-permute-start | bytes 786440 | tf_op jit(solution)/shard_map/ppermute | solution.py:237
  19.8 4.7 %collective-permute-done = bf16[16,16,512]{2,1,0:T(8,128)(2,1)S(1)} collective-permute-done((bf16[16,16,512]{2,1,0:T(8,128)(2,1)S(1)}, bf16[16,16,512]{2,1,0:T(8,128)(2,1)S(1)}, u32[]{:S(2)}, u32[]{:S(2)}) %collective-permute-start) | collective-permute-done | bytes 262176 | tf_op jit(solution)/shard_map/ppermute | solution.py:237
  24.6 2.1 %collective-permute-start.1 = (bf16[8,16,512]{2,1,0:T(8,128)(2,1)S(1)}, bf16[8,16,512]{2,1,0:T(8,128)(2,1)S(1)}, u32[]{:S(2)}, u32[]{:S(2)}) collective-permute-start(bf16[8,16,512]{2,1,0:T(8,128)(2,1)S(1)} %get-tuple-element.64), channel_id=1, source_target_pairs={{0,8},{4,12},{8,0},{12,4},{16,24},{20,28},{24,16},{28,20},{1,9},{5... | collective-permute-start | bytes 393224 | tf_op jit(solution)/shard_map/ppermute | solution.py:237
  26.7 0.1 add_convert_fusion.6
  26.8 1.4 %collective-permute-start.4 = (bf16[8,16,512]{2,1,0:T(8,128)(2,1)S(1)}, bf16[8,16,512]{2,1,0:T(8,128)(2,1)S(1)}, u32[]{:S(2)}, u32[]{:S(2)}) collective-permute-start(bf16[8,16,512]{2,1,0:T(8,128)(2,1)S(1)} %get-tuple-element.62), channel_id=1, source_target_pairs={{0,4},{4,0},{8,12},{12,8},{16,20},{20,16},{24,28},{28,24},{1,5},{5... | collective-permute-start | bytes 393224 | tf_op jit(solution)/shard_map/ppermute | solution.py:237
  28.2 1.5 %collective-permute-done.1 = bf16[8,16,512]{2,1,0:T(8,128)(2,1)S(1)} collective-permute-done((bf16[8,16,512]{2,1,0:T(8,128)(2,1)S(1)}, bf16[8,16,512]{2,1,0:T(8,128)(2,1)S(1)}, u32[]{:S(2)}, u32[]{:S(2)}) %collective-permute-start.1) | collective-permute-done | bytes 131104 | tf_op jit(solution)/shard_map/ppermute | solution.py:237
  29.7 3.0 %collective-permute-start.2 = (bf16[4,16,512]{2,1,0:T(8,128)(2,1)S(1)}, bf16[4,16,512]{2,1,0:T(8,128)(2,1)S(1)}, u32[]{:S(2)}, u32[]{:S(2)}) collective-permute-start(bf16[4,16,512]{2,1,0:T(8,128)(2,1)S(1)} %get-tuple-element.80), channel_id=1, source_target_pairs={{0,16},{4,20},{8,24},{12,28},{16,0},{20,4},{24,8},{28,12},{1,17},{... | collective-permute-start | bytes 196616 | tf_op jit(solution)/shard_map/ppermute | solution.py:237
  32.8 1.8 %collective-permute-start.5 = (bf16[4,16,512]{2,1,0:T(8,128)(2,1)S(1)}, bf16[4,16,512]{2,1,0:T(8,128)(2,1)S(1)}, u32[]{:S(2)}, u32[]{:S(2)}) collective-permute-start(bf16[4,16,512]{2,1,0:T(8,128)(2,1)S(1)} %get-tuple-element.78), channel_id=1, source_target_pairs={{0,16},{4,20},{8,24},{12,28},{16,0},{20,4},{24,8},{28,12},{1,17},{... | collective-permute-start | bytes 196616 | tf_op jit(solution)/shard_map/ppermute | solution.py:237
  34.6 2.1 %collective-permute-done.2.refs_1_ = bf16[4,16,512]{2,1,0:T(8,128)(2,1)S(1)} collective-permute-done((bf16[4,16,512]{2,1,0:T(8,128)(2,1)S(1)}, bf16[4,16,512]{2,1,0:T(8,128)(2,1)S(1)}, u32[]{:S(2)}, u32[]{:S(2)}) %collective-permute-start.2) | collective-permute-done | bytes 65568 | tf_op jit(solution)/shard_map/ppermute | solution.py:237
  36.7 2.0 %early.3.sum_ref = f32[8,16,768]{2,1,0:T(8,128)S(1)} custom-call(s32[8,768]{1,0:T(8,128)S(1)} %get-tuple-element.26.code_ref, f32[4,1024]{1,0:T(4,128)S(1)} %copy-done, f32[4,16,512]{2,1,0:T(8,128)S(1)} %get-tuple-element.81.refs_0_, bf16[4,16,512]{2,1,0:T(8,128)(2,1)S(1)} %collective-permute-done.2.refs_1_, ...), custom_call_target="tpu_custom_call" | custom-call | flops 100663296 | bytes 6291456 | tf_op jit(solution)/shard_map/early/pallas_call | solution.py:289
  38.7 3.7 %ready.3 = (bf16[8,64,768]{2,1,0:T(8,128)(2,1)S(1)}, bf16[16,16,512]{2,1,0:T(8,128)(2,1)S(1)}, bf16[16,16,512]{2,1,0:T(8,128)(2,1)S(1)}) custom-call(s32[8,768]{1,0:T(8,128)S(1)} %get-tuple-element.26.code_ref, f32[4,1024]{1,0:T(4,128)S(1)} %copy-done, f32[8,16,768]{2,1,0:T(8,128)S(1)} %early.3.sum_ref, f32[4,16,512]{2,1,0:T(8,128)S(1)} %get-tuple-element.79.base_ref, ...), custom_call_target="tpu_custom_call" | custom-call | flops 100663296 | bytes 6291456 | tf_op jit(solution)/shard_map/ready/pallas_call | solution.py:298
  42.4 1.7 %collective-permute-start.6 = (bf16[16,16,512]{2,1,0:T(8,128)(2,1)S(1)}, bf16[16,16,512]{2,1,0:T(8,128)(2,1)S(1)}, u32[]{:S(2)}, u32[]{:S(2)}) collective-permute-start(bf16[16,16,512]{2,1,0:T(8,128)(2,1)S(1)} %get-tuple-element.35), channel_id=1, source_target_pairs={{0,4},{4,0},{8,12},{12,8},{16,20},{20,16},{24,28},{28,24},{1,5},{5... | collective-permute-start | bytes 786440 | tf_op jit(solution)/shard_map/ppermute | solution.py:237
  44.1 0.6 collective-permute-start.9
  44.7 1.2 %rest.3 = (f32[16,16,512]{2,1,0:T(8,128)S(1)}, f32[16,16,512]{2,1,0:T(8,128)S(1)}) custom-call(bf16[8,64,768]{2,1,0:T(8,128)(2,1)S(1)} %get-tuple-element.33.lhs_ref, bf16[6144,1024]{1,0:T(8,128)(2,1)S(1)} %get-tuple-element.32.refs_1_.v_ref), custom_call_target="tpu_custom_call" | custom-call | flops 100663296 | bytes 6291456 | tf_op jit(solution)/shard_map/rest/pallas_call | solution.py:308
  46.0 2.9 %collective-permute-done.6 = bf16[16,16,512]{2,1,0:T(8,128)(2,1)S(1)} collective-permute-done((bf16[16,16,512]{2,1,0:T(8,128)(2,1)S(1)}, bf16[16,16,512]{2,1,0:T(8,128)(2,1)S(1)}, u32[]{:S(2)}, u32[]{:S(2)}) %collective-permute-start.6) | collective-permute-done | bytes 262176 | tf_op jit(solution)/shard_map/ppermute | solution.py:237
  48.9 0.1 add_convert_fusion.5
  49.0 1.1 collective-permute-start.7
  50.1 1.9 %collective-permute-done.9 = bf16[16,16,512]{2,1,0:T(8,128)(2,1)S(1)} collective-permute-done((bf16[16,16,512]{2,1,0:T(8,128)(2,1)S(1)}, bf16[16,16,512]{2,1,0:T(8,128)(2,1)S(1)}, u32[]{:S(2)}, u32[]{:S(2)}) %collective-permute-start.9) | collective-permute-done | bytes 262176 | tf_op jit(solution)/shard_map/ppermute | solution.py:237
  51.9 0.1 add_convert_fusion.4
  52.1 1.9 %collective-permute-done.7 = bf16[8,16,512]{2,1,0:T(8,128)(2,1)S(1)} collective-permute-done((bf16[8,16,512]{2,1,0:T(8,128)(2,1)S(1)}, bf16[8,16,512]{2,1,0:T(8,128)(2,1)S(1)}, u32[]{:S(2)}, u32[]{:S(2)}) %collective-permute-start.7) | collective-permute-done | bytes 131104 | tf_op jit(solution)/shard_map/ppermute | solution.py:237
  54.1 2.9 %collective-permute-start.8 = (bf16[4,16,512]{2,1,0:T(8,128)(2,1)S(1)}, bf16[4,16,512]{2,1,0:T(8,128)(2,1)S(1)}, u32[]{:S(2)}, u32[]{:S(2)}) collective-permute-start(bf16[4,16,512]{2,1,0:T(8,128)(2,1)S(1)} %get-tuple-element.76), channel_id=1, source_target_pairs={{0,16},{4,20},{8,24},{12,28},{16,0},{20,4},{24,8},{28,12},{1,17},{... | collective-permute-start | bytes 196616 | tf_op jit(solution)/shard_map/ppermute | solution.py:237
  57.0 0.1 collective-permute-done.10
  57.1 1.4 %collective-permute-start.11 = (bf16[4,16,512]{2,1,0:T(8,128)(2,1)S(1)}, bf16[4,16,512]{2,1,0:T(8,128)(2,1)S(1)}, u32[]{:S(2)}, u32[]{:S(2)}) collective-permute-start(bf16[4,16,512]{2,1,0:T(8,128)(2,1)S(1)} %get-tuple-element.74), channel_id=1, source_target_pairs={{0,16},{4,20},{8,24},{12,28},{16,0},{20,4},{24,8},{28,12},{1,17},{... | collective-permute-start | bytes 196616 | tf_op jit(solution)/shard_map/ppermute | solution.py:237
  58.5 0.8 collective-permute-done.8.refs_1_
  59.3 2.2 %early.4.sum_ref = f32[8,16,768]{2,1,0:T(8,128)S(1)} custom-call(s32[8,768]{1,0:T(8,128)S(1)} %get-tuple-element.26.code_ref, f32[4,1024]{1,0:T(4,128)S(1)} %copy-done, f32[4,16,512]{2,1,0:T(8,128)S(1)} %get-tuple-element.77.refs_0_, bf16[4,16,512]{2,1,0:T(8,128)(2,1)S(1)} %collective-permute-done.8.refs_1_, ...), custom_call_target="tpu_custom_call" | custom-call | flops 100663296 | bytes 6291456 | tf_op jit(solution)/shard_map/early/pallas_call | solution.py:289
  61.5 0.8 collective-permute-done.11.came_ref
  62.3 3.7 %ready.4 = (bf16[8,64,768]{2,1,0:T(8,128)(2,1)S(1)}, bf16[16,16,512]{2,1,0:T(8,128)(2,1)S(1)}, bf16[16,16,512]{2,1,0:T(8,128)(2,1)S(1)}) custom-call(s32[8,768]{1,0:T(8,128)S(1)} %get-tuple-element.26.code_ref, f32[4,1024]{1,0:T(4,128)S(1)} %copy-done, f32[8,16,768]{2,1,0:T(8,128)S(1)} %early.4.sum_ref, f32[4,16,512]{2,1,0:T(8,128)S(1)} %get-tuple-element.75.base_ref, ...), custom_call_target="tpu_custom_call" | custom-call | flops 100663296 | bytes 6291456 | tf_op jit(solution)/shard_map/ready/pallas_call | solution.py:298
  66.0 2.4 %collective-permute-start.12 = (bf16[16,16,512]{2,1,0:T(8,128)(2,1)S(1)}, bf16[16,16,512]{2,1,0:T(8,128)(2,1)S(1)}, u32[]{:S(2)}, u32[]{:S(2)}) collective-permute-start(bf16[16,16,512]{2,1,0:T(8,128)(2,1)S(1)} %get-tuple-element.40), channel_id=1, source_target_pairs={{0,4},{4,0},{8,12},{12,8},{16,20},{20,16},{24,28},{28,24},{1,5},{5... | collective-permute-start | bytes 786440 | tf_op jit(solution)/shard_map/ppermute | solution.py:237
  68.4 2.5 %collective-permute-start.15 = (bf16[16,16,512]{2,1,0:T(8,128)(2,1)S(1)}, bf16[16,16,512]{2,1,0:T(8,128)(2,1)S(1)}, u32[]{:S(2)}, u32[]{:S(2)}) collective-permute-start(bf16[16,16,512]{2,1,0:T(8,128)(2,1)S(1)} %get-tuple-element.42), channel_id=1, source_target_pairs={{0,8},{4,12},{8,0},{12,4},{16,24},{20,28},{24,16},{28,20},{1,9},{5... | collective-permute-start | bytes 786440 | tf_op jit(solution)/shard_map/ppermute | solution.py:237
  71.0 1.2 %rest.4 = (f32[16,16,512]{2,1,0:T(8,128)S(1)}, f32[16,16,512]{2,1,0:T(8,128)S(1)}) custom-call(bf16[8,64,768]{2,1,0:T(8,128)(2,1)S(1)} %get-tuple-element.38.lhs_ref, bf16[6144,1024]{1,0:T(8,128)(2,1)S(1)} %get-tuple-element.32.refs_1_.v_ref), custom_call_target="tpu_custom_call" | custom-call | flops 100663296 | bytes 6291456 | tf_op jit(solution)/shard_map/rest/pallas_call | solution.py:308
  72.2 2.0 %collective-permute-done.12 = bf16[16,16,512]{2,1,0:T(8,128)(2,1)S(1)} collective-permute-done((bf16[16,16,512]{2,1,0:T(8,128)(2,1)S(1)}, bf16[16,16,512]{2,1,0:T(8,128)(2,1)S(1)}, u32[]{:S(2)}, u32[]{:S(2)}) %collective-permute-start.12) | collective-permute-done | bytes 262176 | tf_op jit(solution)/shard_map/ppermute | solution.py:237
  74.2 0.1 add_convert_fusion.3
  74.3 1.6 %collective-permute-start.13 = (bf16[8,16,512]{2,1,0:T(8,128)(2,1)S(1)}, bf16[8,16,512]{2,1,0:T(8,128)(2,1)S(1)}, u32[]{:S(2)}, u32[]{:S(2)}) collective-permute-start(bf16[8,16,512]{2,1,0:T(8,128)(2,1)S(1)} %get-tuple-element.56), channel_id=1, source_target_pairs={{0,8},{4,12},{8,0},{12,4},{16,24},{20,28},{24,16},{28,20},{1,9},{5... | collective-permute-start | bytes 393224 | tf_op jit(solution)/shard_map/ppermute | solution.py:237
  75.9 0.2 collective-permute-done.15
  76.0 0.1 add_convert_fusion.2
  76.1 1.5 %collective-permute-start.16 = (bf16[8,16,512]{2,1,0:T(8,128)(2,1)S(1)}, bf16[8,16,512]{2,1,0:T(8,128)(2,1)S(1)}, u32[]{:S(2)}, u32[]{:S(2)}) collective-permute-start(bf16[8,16,512]{2,1,0:T(8,128)(2,1)S(1)} %get-tuple-element.54), channel_id=1, source_target_pairs={{0,4},{4,0},{8,12},{12,8},{16,20},{20,16},{24,28},{28,24},{1,5},{5... | collective-permute-start | bytes 393224 | tf_op jit(solution)/shard_map/ppermute | solution.py:237
  77.6 1.8 %collective-permute-done.13 = bf16[8,16,512]{2,1,0:T(8,128)(2,1)S(1)} collective-permute-done((bf16[8,16,512]{2,1,0:T(8,128)(2,1)S(1)}, bf16[8,16,512]{2,1,0:T(8,128)(2,1)S(1)}, u32[]{:S(2)}, u32[]{:S(2)}) %collective-permute-start.13) | collective-permute-done | bytes 131104 | tf_op jit(solution)/shard_map/ppermute | solution.py:237
  79.5 1.7 %collective-permute-start.14 = (bf16[4,16,512]{2,1,0:T(8,128)(2,1)S(1)}, bf16[4,16,512]{2,1,0:T(8,128)(2,1)S(1)}, u32[]{:S(2)}, u32[]{:S(2)}) collective-permute-start(bf16[4,16,512]{2,1,0:T(8,128)(2,1)S(1)} %get-tuple-element.72), channel_id=1, source_target_pairs={{0,16},{4,20},{8,24},{12,28},{16,0},{20,4},{24,8},{28,12},{1,17},{... | collective-permute-start | bytes 196616 | tf_op jit(solution)/shard_map/ppermute | solution.py:237
  81.2 3.1 %collective-permute-start.17 = (bf16[4,16,512]{2,1,0:T(8,128)(2,1)S(1)}, bf16[4,16,512]{2,1,0:T(8,128)(2,1)S(1)}, u32[]{:S(2)}, u32[]{:S(2)}) collective-permute-start(bf16[4,16,512]{2,1,0:T(8,128)(2,1)S(1)} %get-tuple-element.70), channel_id=1, source_target_pairs={{0,16},{4,20},{8,24},{12,28},{16,0},{20,4},{24,8},{28,12},{1,17},{... | collective-permute-start | bytes 196616 | tf_op jit(solution)/shard_map/ppermute | solution.py:237
  84.3 0.4 collective-permute-done.14.refs_1_
  84.8 2.0 %early.5.sum_ref = f32[8,16,768]{2,1,0:T(8,128)S(1)} custom-call(s32[8,768]{1,0:T(8,128)S(1)} %get-tuple-element.26.code_ref, f32[4,1024]{1,0:T(4,128)S(1)} %copy-done, f32[4,16,512]{2,1,0:T(8,128)S(1)} %get-tuple-element.73.refs_0_, bf16[4,16,512]{2,1,0:T(8,128)(2,1)S(1)} %collective-permute-done.14.refs_1_, ...), custom_call_target="tpu_custom_call" | custom-call | flops 100663296 | bytes 6291456 | tf_op jit(solution)/shard_map/early/pallas_call | solution.py:289
  86.8 0.1 collective-permute-done.17.came_ref
  86.9 3.7 %ready.5 = (bf16[8,64,768]{2,1,0:T(8,128)(2,1)S(1)}, bf16[16,16,512]{2,1,0:T(8,128)(2,1)S(1)}, bf16[16,16,512]{2,1,0:T(8,128)(2,1)S(1)}) custom-call(s32[8,768]{1,0:T(8,128)S(1)} %get-tuple-element.26.code_ref, f32[4,1024]{1,0:T(4,128)S(1)} %copy-done, f32[8,16,768]{2,1,0:T(8,128)S(1)} %early.5.sum_ref, f32[4,16,512]{2,1,0:T(8,128)S(1)} %get-tuple-element.71.base_ref, ...), custom_call_target="tpu_custom_call" | custom-call | flops 100663296 | bytes 6291456 | tf_op jit(solution)/shard_map/ready/pallas_call | solution.py:298
  90.6 1.7 %collective-permute-start.18 = (bf16[16,16,512]{2,1,0:T(8,128)(2,1)S(1)}, bf16[16,16,512]{2,1,0:T(8,128)(2,1)S(1)}, u32[]{:S(2)}, u32[]{:S(2)}) collective-permute-start(bf16[16,16,512]{2,1,0:T(8,128)(2,1)S(1)} %get-tuple-element.45), channel_id=1, source_target_pairs={{0,4},{4,0},{8,12},{12,8},{16,20},{20,16},{24,28},{28,24},{1,5},{5... | collective-permute-start | bytes 786440 | tf_op jit(solution)/shard_map/ppermute | solution.py:237
  92.3 2.6 %collective-permute-start.21 = (bf16[16,16,512]{2,1,0:T(8,128)(2,1)S(1)}, bf16[16,16,512]{2,1,0:T(8,128)(2,1)S(1)}, u32[]{:S(2)}, u32[]{:S(2)}) collective-permute-start(bf16[16,16,512]{2,1,0:T(8,128)(2,1)S(1)} %get-tuple-element.47), channel_id=1, source_target_pairs={{0,8},{4,12},{8,0},{12,4},{16,24},{20,28},{24,16},{28,20},{1,9},{5... | collective-permute-start | bytes 786440 | tf_op jit(solution)/shard_map/ppermute | solution.py:237
  94.8 1.2 %rest.5 = (f32[16,16,512]{2,1,0:T(8,128)S(1)}, f32[16,16,512]{2,1,0:T(8,128)S(1)}) custom-call(bf16[8,64,768]{2,1,0:T(8,128)(2,1)S(1)} %get-tuple-element.43.lhs_ref, bf16[6144,1024]{1,0:T(8,128)(2,1)S(1)} %get-tuple-element.32.refs_1_.v_ref), custom_call_target="tpu_custom_call" | custom-call | flops 100663296 | bytes 6291456 | tf_op jit(solution)/shard_map/rest/pallas_call | solution.py:308
  96.1 0.9 collective-permute-done.18
  97.0 0.1 add_convert_fusion.1
  97.1 2.6 %collective-permute-start.19 = (bf16[8,16,512]{2,1,0:T(8,128)(2,1)S(1)}, bf16[8,16,512]{2,1,0:T(8,128)(2,1)S(1)}, u32[]{:S(2)}, u32[]{:S(2)}) collective-permute-start(bf16[8,16,512]{2,1,0:T(8,128)(2,1)S(1)} %get-tuple-element.52), channel_id=1, source_target_pairs={{0,8},{4,12},{8,0},{12,4},{16,24},{20,28},{24,16},{28,20},{1,9},{5... | collective-permute-start | bytes 393224 | tf_op jit(solution)/shard_map/ppermute | solution.py:237
  99.7 0.1 add_convert_fusion
  99.7 1.8 %collective-permute-start.22 = (bf16[8,16,512]{2,1,0:T(8,128)(2,1)S(1)}, bf16[8,16,512]{2,1,0:T(8,128)(2,1)S(1)}, u32[]{:S(2)}, u32[]{:S(2)}) collective-permute-start(bf16[8,16,512]{2,1,0:T(8,128)(2,1)S(1)} %get-tuple-element.50), channel_id=1, source_target_pairs={{0,4},{4,0},{8,12},{12,8},{16,20},{20,16},{24,28},{28,24},{1,5},{5... | collective-permute-start | bytes 393224 | tf_op jit(solution)/shard_map/ppermute | solution.py:237
  101.5 1.1 collective-permute-done.19
  102.7 3.0 %collective-permute-start.20 = (bf16[4,16,512]{2,1,0:T(8,128)(2,1)S(1)}, bf16[4,16,512]{2,1,0:T(8,128)(2,1)S(1)}, u32[]{:S(2)}, u32[]{:S(2)}) collective-permute-start(bf16[4,16,512]{2,1,0:T(8,128)(2,1)S(1)} %get-tuple-element.68), channel_id=1, source_target_pairs={{0,16},{4,20},{8,24},{12,28},{16,0},{20,4},{24,8},{28,12},{1,17},{... | collective-permute-start | bytes 196616 | tf_op jit(solution)/shard_map/ppermute | solution.py:237
  105.7 1.9 %collective-permute-start.23 = (bf16[4,16,512]{2,1,0:T(8,128)(2,1)S(1)}, bf16[4,16,512]{2,1,0:T(8,128)(2,1)S(1)}, u32[]{:S(2)}, u32[]{:S(2)}) collective-permute-start(bf16[4,16,512]{2,1,0:T(8,128)(2,1)S(1)} %get-tuple-element.66), channel_id=1, source_target_pairs={{0,16},{4,20},{8,24},{12,28},{16,0},{20,4},{24,8},{28,12},{1,17},{... | collective-permute-start | bytes 196616 | tf_op jit(solution)/shard_map/ppermute | solution.py:237
  107.6 0.3 collective-permute-done.20.refs_1_
  107.9 3.0 %collective-permute-done.23.refs_3_ = bf16[4,16,512]{2,1,0:T(8,128)(2,1)S(1)} collective-permute-done((bf16[4,16,512]{2,1,0:T(8,128)(2,1)S(1)}, bf16[4,16,512]{2,1,0:T(8,128)(2,1)S(1)}, u32[]{:S(2)}, u32[]{:S(2)}) %collective-permute-start.23) | collective-permute-done | bytes 65568 | tf_op jit(solution)/shard_map/ppermute | solution.py:237
  110.9 0.8 finish.1
  111.7 1.5 %collective-permute-start.25 = (f32[4,1024]{1,0:T(4,128)S(1)}, f32[4,1024]{1,0:T(4,128)S(1)}, u32[]{:S(2)}, u32[]{:S(2)}) collective-permute-start(f32[4,1024]{1,0:T(4,128)S(1)} %get-tuple-element.49), channel_id=1, source_target_pairs={{0,2},{1,3},{2,0},{3,1},{4,6},{5,7},{6,4},{7,5},{8,10},{9,11},{10,... | collective-permute-start | bytes 49160 | tf_op jit(solution)/shard_map/ppermute | solution.py:415
  113.2 0.3 collective-permute-start.24
  113.5 1.4 %collective-permute-done.26 = f32[4,1024]{1,0:T(4,128)S(1)} collective-permute-done((f32[4,1024]{1,0:T(4,128)S(1)}, f32[4,1024]{1,0:T(4,128)S(1)}, u32[]{:S(2)}, u32[]{:S(2)}) %collective-permute-start.26) | collective-permute-done | bytes 16416 | tf_op jit(solution)/shard_map/ppermute | solution.py:415
  115.0 0.5 collective-permute-done.25
  115.5 0.6 add_multiply_fusion
  (25 shorter events, 0.6 us)
Async XLA Ops:
  0.6 19.2 %copy-start = (f32[4,1024]{1,0:T(4,128)S(1)}, f32[4,1024]{1,0:T(4,128)}, u32[]{:S(2)}) copy-start(f32[4,1024]{1,0:T(4,128)} %contrast_ref.13) | copy-start | bytes 49156
  0.6 29.0 %copy-start.2 = (f32[4,16,1024]{2,1,0:T(8,128)S(1)}, f32[4,16,1024]{2,1,0:T(8,128)}, u32[]{:S(2)}) copy-start(f32[4,16,1024]{2,1,0:T(8,128)} %refs_3_.1) | copy-start | bytes 786436
  15.4 9.1 %collective-permute-start = (bf16[16,16,512]{2,1,0:T(8,128)(2,1)S(1)}, bf16[16,16,512]{2,1,0:T(8,128)(2,1)S(1)}, u32[]{:S(2)}, u32[]{:S(2)}) collective-permute-start(bf16[16,16,512]{2,1,0:T(8,128)(2,1)S(1)} %get-tuple-element.28), channel_id=1, source_target_pairs={{0,4},{4,0},{8,12},{12,8},{16,20},{20,16},{24,28},{28,24},{1,5},{5... | collective-permute-start | bytes 786440 | tf_op jit(solution)/shard_map/ppermute | solution.py:237
  18.2 8.5 %collective-permute-start.3 = (bf16[16,16,512]{2,1,0:T(8,128)(2,1)S(1)}, bf16[16,16,512]{2,1,0:T(8,128)(2,1)S(1)}, u32[]{:S(2)}, u32[]{:S(2)}) collective-permute-start(bf16[16,16,512]{2,1,0:T(8,128)(2,1)S(1)} %get-tuple-element.31), channel_id=1, source_target_pairs={{0,8},{4,12},{8,0},{12,4},{16,24},{20,28},{24,16},{28,20},{1,9},{5... | collective-permute-start | bytes 786440 | tf_op jit(solution)/shard_map/ppermute | solution.py:237
  24.6 5.1 %collective-permute-start.1 = (bf16[8,16,512]{2,1,0:T(8,128)(2,1)S(1)}, bf16[8,16,512]{2,1,0:T(8,128)(2,1)S(1)}, u32[]{:S(2)}, u32[]{:S(2)}) collective-permute-start(bf16[8,16,512]{2,1,0:T(8,128)(2,1)S(1)} %get-tuple-element.64), channel_id=1, source_target_pairs={{0,8},{4,12},{8,0},{12,4},{16,24},{20,28},{24,16},{28,20},{1,9},{5... | collective-permute-start | bytes 393224 | tf_op jit(solution)/shard_map/ppermute | solution.py:237
  26.8 6.0 %collective-permute-start.4 = (bf16[8,16,512]{2,1,0:T(8,128)(2,1)S(1)}, bf16[8,16,512]{2,1,0:T(8,128)(2,1)S(1)}, u32[]{:S(2)}, u32[]{:S(2)}) collective-permute-start(bf16[8,16,512]{2,1,0:T(8,128)(2,1)S(1)} %get-tuple-element.62), channel_id=1, source_target_pairs={{0,4},{4,0},{8,12},{12,8},{16,20},{20,16},{24,28},{28,24},{1,5},{5... | collective-permute-start | bytes 393224 | tf_op jit(solution)/shard_map/ppermute | solution.py:237
  29.7 7.0 %collective-permute-start.2 = (bf16[4,16,512]{2,1,0:T(8,128)(2,1)S(1)}, bf16[4,16,512]{2,1,0:T(8,128)(2,1)S(1)}, u32[]{:S(2)}, u32[]{:S(2)}) collective-permute-start(bf16[4,16,512]{2,1,0:T(8,128)(2,1)S(1)} %get-tuple-element.80), channel_id=1, source_target_pairs={{0,16},{4,20},{8,24},{12,28},{16,0},{20,4},{24,8},{28,12},{1,17},{... | collective-permute-start | bytes 196616 | tf_op jit(solution)/shard_map/ppermute | solution.py:237
  32.8 5.9 %collective-permute-start.5 = (bf16[4,16,512]{2,1,0:T(8,128)(2,1)S(1)}, bf16[4,16,512]{2,1,0:T(8,128)(2,1)S(1)}, u32[]{:S(2)}, u32[]{:S(2)}) collective-permute-start(bf16[4,16,512]{2,1,0:T(8,128)(2,1)S(1)} %get-tuple-element.78), channel_id=1, source_target_pairs={{0,16},{4,20},{8,24},{12,28},{16,0},{20,4},{24,8},{28,12},{1,17},{... | collective-permute-start | bytes 196616 | tf_op jit(solution)/shard_map/ppermute | solution.py:237
  42.4 6.4 %collective-permute-start.6 = (bf16[16,16,512]{2,1,0:T(8,128)(2,1)S(1)}, bf16[16,16,512]{2,1,0:T(8,128)(2,1)S(1)}, u32[]{:S(2)}, u32[]{:S(2)}) collective-permute-start(bf16[16,16,512]{2,1,0:T(8,128)(2,1)S(1)} %get-tuple-element.35), channel_id=1, source_target_pairs={{0,4},{4,0},{8,12},{12,8},{16,20},{20,16},{24,28},{28,24},{1,5},{5... | collective-permute-start | bytes 786440 | tf_op jit(solution)/shard_map/ppermute | solution.py:237
  44.1 7.8 %collective-permute-start.9 = (bf16[16,16,512]{2,1,0:T(8,128)(2,1)S(1)}, bf16[16,16,512]{2,1,0:T(8,128)(2,1)S(1)}, u32[]{:S(2)}, u32[]{:S(2)}) collective-permute-start(bf16[16,16,512]{2,1,0:T(8,128)(2,1)S(1)} %get-tuple-element.37), channel_id=1, source_target_pairs={{0,8},{4,12},{8,0},{12,4},{16,24},{20,28},{24,16},{28,20},{1,9},{5... | collective-permute-start | bytes 786440 | tf_op jit(solution)/shard_map/ppermute | solution.py:237
  49.0 5.0 %collective-permute-start.7 = (bf16[8,16,512]{2,1,0:T(8,128)(2,1)S(1)}, bf16[8,16,512]{2,1,0:T(8,128)(2,1)S(1)}, u32[]{:S(2)}, u32[]{:S(2)}) collective-permute-start(bf16[8,16,512]{2,1,0:T(8,128)(2,1)S(1)} %get-tuple-element.60), channel_id=1, source_target_pairs={{0,8},{4,12},{8,0},{12,4},{16,24},{20,28},{24,16},{28,20},{1,9},{5... | collective-permute-start | bytes 393224 | tf_op jit(solution)/shard_map/ppermute | solution.py:237
  52.0 5.0 %collective-permute-start.10 = (bf16[8,16,512]{2,1,0:T(8,128)(2,1)S(1)}, bf16[8,16,512]{2,1,0:T(8,128)(2,1)S(1)}, u32[]{:S(2)}, u32[]{:S(2)}) collective-permute-start(bf16[8,16,512]{2,1,0:T(8,128)(2,1)S(1)} %get-tuple-element.58), channel_id=1, source_target_pairs={{0,4},{4,0},{8,12},{12,8},{16,20},{20,16},{24,28},{28,24},{1,5},{5... | collective-permute-start | bytes 393224 | tf_op jit(solution)/shard_map/ppermute | solution.py:237
  54.1 5.2 %collective-permute-start.8 = (bf16[4,16,512]{2,1,0:T(8,128)(2,1)S(1)}, bf16[4,16,512]{2,1,0:T(8,128)(2,1)S(1)}, u32[]{:S(2)}, u32[]{:S(2)}) collective-permute-start(bf16[4,16,512]{2,1,0:T(8,128)(2,1)S(1)} %get-tuple-element.76), channel_id=1, source_target_pairs={{0,16},{4,20},{8,24},{12,28},{16,0},{20,4},{24,8},{28,12},{1,17},{... | collective-permute-start | bytes 196616 | tf_op jit(solution)/shard_map/ppermute | solution.py:237
  57.1 5.2 %collective-permute-start.11 = (bf16[4,16,512]{2,1,0:T(8,128)(2,1)S(1)}, bf16[4,16,512]{2,1,0:T(8,128)(2,1)S(1)}, u32[]{:S(2)}, u32[]{:S(2)}) collective-permute-start(bf16[4,16,512]{2,1,0:T(8,128)(2,1)S(1)} %get-tuple-element.74), channel_id=1, source_target_pairs={{0,16},{4,20},{8,24},{12,28},{16,0},{20,4},{24,8},{28,12},{1,17},{... | collective-permute-start | bytes 196616 | tf_op jit(solution)/shard_map/ppermute | solution.py:237
  66.0 8.2 %collective-permute-start.12 = (bf16[16,16,512]{2,1,0:T(8,128)(2,1)S(1)}, bf16[16,16,512]{2,1,0:T(8,128)(2,1)S(1)}, u32[]{:S(2)}, u32[]{:S(2)}) collective-permute-start(bf16[16,16,512]{2,1,0:T(8,128)(2,1)S(1)} %get-tuple-element.40), channel_id=1, source_target_pairs={{0,4},{4,0},{8,12},{12,8},{16,20},{20,16},{24,28},{28,24},{1,5},{5... | collective-permute-start | bytes 786440 | tf_op jit(solution)/shard_map/ppermute | solution.py:237
  68.4 7.6 %collective-permute-start.15 = (bf16[16,16,512]{2,1,0:T(8,128)(2,1)S(1)}, bf16[16,16,512]{2,1,0:T(8,128)(2,1)S(1)}, u32[]{:S(2)}, u32[]{:S(2)}) collective-permute-start(bf16[16,16,512]{2,1,0:T(8,128)(2,1)S(1)} %get-tuple-element.42), channel_id=1, source_target_pairs={{0,8},{4,12},{8,0},{12,4},{16,24},{20,28},{24,16},{28,20},{1,9},{5... | collective-permute-start | bytes 786440 | tf_op jit(solution)/shard_map/ppermute | solution.py:237
  74.3 5.2 %collective-permute-start.13 = (bf16[8,16,512]{2,1,0:T(8,128)(2,1)S(1)}, bf16[8,16,512]{2,1,0:T(8,128)(2,1)S(1)}, u32[]{:S(2)}, u32[]{:S(2)}) collective-permute-start(bf16[8,16,512]{2,1,0:T(8,128)(2,1)S(1)} %get-tuple-element.56), channel_id=1, source_target_pairs={{0,8},{4,12},{8,0},{12,4},{16,24},{20,28},{24,16},{28,20},{1,9},{5... | collective-permute-start | bytes 393224 | tf_op jit(solution)/shard_map/ppermute | solution.py:237
  76.1 5.1 %collective-permute-start.16 = (bf16[8,16,512]{2,1,0:T(8,128)(2,1)S(1)}, bf16[8,16,512]{2,1,0:T(8,128)(2,1)S(1)}, u32[]{:S(2)}, u32[]{:S(2)}) collective-permute-start(bf16[8,16,512]{2,1,0:T(8,128)(2,1)S(1)} %get-tuple-element.54), channel_id=1, source_target_pairs={{0,4},{4,0},{8,12},{12,8},{16,20},{20,16},{24,28},{28,24},{1,5},{5... | collective-permute-start | bytes 393224 | tf_op jit(solution)/shard_map/ppermute | solution.py:237
  79.5 5.2 %collective-permute-start.14 = (bf16[4,16,512]{2,1,0:T(8,128)(2,1)S(1)}, bf16[4,16,512]{2,1,0:T(8,128)(2,1)S(1)}, u32[]{:S(2)}, u32[]{:S(2)}) collective-permute-start(bf16[4,16,512]{2,1,0:T(8,128)(2,1)S(1)} %get-tuple-element.72), channel_id=1, source_target_pairs={{0,16},{4,20},{8,24},{12,28},{16,0},{20,4},{24,8},{28,12},{1,17},{... | collective-permute-start | bytes 196616 | tf_op jit(solution)/shard_map/ppermute | solution.py:237
  81.2 5.6 %collective-permute-start.17 = (bf16[4,16,512]{2,1,0:T(8,128)(2,1)S(1)}, bf16[4,16,512]{2,1,0:T(8,128)(2,1)S(1)}, u32[]{:S(2)}, u32[]{:S(2)}) collective-permute-start(bf16[4,16,512]{2,1,0:T(8,128)(2,1)S(1)} %get-tuple-element.70), channel_id=1, source_target_pairs={{0,16},{4,20},{8,24},{12,28},{16,0},{20,4},{24,8},{28,12},{1,17},{... | collective-permute-start | bytes 196616 | tf_op jit(solution)/shard_map/ppermute | solution.py:237
  90.6 20.3 %copy-start.1 = (bf16[4,16,1024]{2,1,0:T(8,128)(2,1)S(1)}, bf16[4,16,1024]{2,1,0:T(8,128)(2,1)}, u32[]{:S(2)}) copy-start(bf16[4,16,1024]{2,1,0:T(8,128)(2,1)} %forward_ref.1) | copy-start | bytes 393220
  90.6 6.4 %collective-permute-start.18 = (bf16[16,16,512]{2,1,0:T(8,128)(2,1)S(1)}, bf16[16,16,512]{2,1,0:T(8,128)(2,1)S(1)}, u32[]{:S(2)}, u32[]{:S(2)}) collective-permute-start(bf16[16,16,512]{2,1,0:T(8,128)(2,1)S(1)} %get-tuple-element.45), channel_id=1, source_target_pairs={{0,4},{4,0},{8,12},{12,8},{16,20},{20,16},{24,28},{28,24},{1,5},{5... | collective-permute-start | bytes 786440 | tf_op jit(solution)/shard_map/ppermute | solution.py:237
  92.3 7.4 %collective-permute-start.21 = (bf16[16,16,512]{2,1,0:T(8,128)(2,1)S(1)}, bf16[16,16,512]{2,1,0:T(8,128)(2,1)S(1)}, u32[]{:S(2)}, u32[]{:S(2)}) collective-permute-start(bf16[16,16,512]{2,1,0:T(8,128)(2,1)S(1)} %get-tuple-element.47), channel_id=1, source_target_pairs={{0,8},{4,12},{8,0},{12,4},{16,24},{20,28},{24,16},{28,20},{1,9},{5... | collective-permute-start | bytes 786440 | tf_op jit(solution)/shard_map/ppermute | solution.py:237
  97.1 5.5 %collective-permute-start.19 = (bf16[8,16,512]{2,1,0:T(8,128)(2,1)S(1)}, bf16[8,16,512]{2,1,0:T(8,128)(2,1)S(1)}, u32[]{:S(2)}, u32[]{:S(2)}) collective-permute-start(bf16[8,16,512]{2,1,0:T(8,128)(2,1)S(1)} %get-tuple-element.52), channel_id=1, source_target_pairs={{0,8},{4,12},{8,0},{12,4},{16,24},{20,28},{24,16},{28,20},{1,9},{5... | collective-permute-start | bytes 393224 | tf_op jit(solution)/shard_map/ppermute | solution.py:237
  99.7 5.9 %collective-permute-start.22 = (bf16[8,16,512]{2,1,0:T(8,128)(2,1)S(1)}, bf16[8,16,512]{2,1,0:T(8,128)(2,1)S(1)}, u32[]{:S(2)}, u32[]{:S(2)}) collective-permute-start(bf16[8,16,512]{2,1,0:T(8,128)(2,1)S(1)} %get-tuple-element.50), channel_id=1, source_target_pairs={{0,4},{4,0},{8,12},{12,8},{16,20},{20,16},{24,28},{28,24},{1,5},{5... | collective-permute-start | bytes 393224 | tf_op jit(solution)/shard_map/ppermute | solution.py:237
  102.7 5.2 %collective-permute-start.20 = (bf16[4,16,512]{2,1,0:T(8,128)(2,1)S(1)}, bf16[4,16,512]{2,1,0:T(8,128)(2,1)S(1)}, u32[]{:S(2)}, u32[]{:S(2)}) collective-permute-start(bf16[4,16,512]{2,1,0:T(8,128)(2,1)S(1)} %get-tuple-element.68), channel_id=1, source_target_pairs={{0,16},{4,20},{8,24},{12,28},{16,0},{20,4},{24,8},{28,12},{1,17},{... | collective-permute-start | bytes 196616 | tf_op jit(solution)/shard_map/ppermute | solution.py:237
  105.7 5.2 %collective-permute-start.23 = (bf16[4,16,512]{2,1,0:T(8,128)(2,1)S(1)}, bf16[4,16,512]{2,1,0:T(8,128)(2,1)S(1)}, u32[]{:S(2)}, u32[]{:S(2)}) collective-permute-start(bf16[4,16,512]{2,1,0:T(8,128)(2,1)S(1)} %get-tuple-element.66), channel_id=1, source_target_pairs={{0,16},{4,20},{8,24},{12,28},{16,0},{20,4},{24,8},{28,12},{1,17},{... | collective-permute-start | bytes 196616 | tf_op jit(solution)/shard_map/ppermute | solution.py:237
  111.7 3.3 %collective-permute-start.26 = (f32[4,1024]{1,0:T(4,128)S(1)}, f32[4,1024]{1,0:T(4,128)S(1)}, u32[]{:S(2)}, u32[]{:S(2)}) collective-permute-start(f32[4,1024]{1,0:T(4,128)S(1)} %get-tuple-element.49), channel_id=1, source_target_pairs={{0,3},{1,2},{2,1},{3,0},{4,7},{5,6},{6,5},{7,4},{8,11},{9,10},{10,... | collective-permute-start | bytes 49160 | tf_op jit(solution)/shard_map/ppermute | solution.py:415
  111.7 3.8 %collective-permute-start.25 = (f32[4,1024]{1,0:T(4,128)S(1)}, f32[4,1024]{1,0:T(4,128)S(1)}, u32[]{:S(2)}, u32[]{:S(2)}) collective-permute-start(f32[4,1024]{1,0:T(4,128)S(1)} %get-tuple-element.49), channel_id=1, source_target_pairs={{0,2},{1,3},{2,0},{3,1},{4,6},{5,7},{6,4},{7,5},{8,10},{9,11},{10,... | collective-permute-start | bytes 49160 | tf_op jit(solution)/shard_map/ppermute | solution.py:415
  113.2 2.3 %collective-permute-start.24 = (f32[4,1024]{1,0:T(4,128)S(1)}, f32[4,1024]{1,0:T(4,128)S(1)}, u32[]{:S(2)}, u32[]{:S(2)}) collective-permute-start(f32[4,1024]{1,0:T(4,128)S(1)} %get-tuple-element.49), channel_id=1, source_target_pairs={{0,1},{1,0},{2,3},{3,2},{4,5},{5,4},{6,7},{7,6},{8,9},{9,8},{10,11... | collective-permute-start | bytes 49160 | tf_op jit(solution)/shard_map/ppermute | solution.py:415

commit v5 on v4

--- a/solution.py
+++ b/solution.py
@@ -112,35 +112,30 @@
     for copy in copies[:3]:
         copy.wait()
 
-    def load(whence, to, sem, tile, at):
+    def load(whence, to, sem, tile, at, group):
         pltpu.make_async_copy(
             whence.at[pl.ds(pl.multiple_of(tile * rank_max, rank_max), rank_max)],
             to.at[pl.ds(pl.multiple_of(at * rank_max, rank_max), rank_max)],
-            sem.at[lax.div(at, group_tiles)],
+            sem.at[group],
         ).start()
 
-    def sort_tile(tile, carry):
-        row, k = lax.div(tile, tiles_row), lax.rem(tile, tiles_row)
+    for tile in range(tiles):
+        row, k = divmod(tile, tiles_row)
         slot = owner[cols[k, here * rows_dev + row]]
         rel = jnp.bitwise_xor(lax.div(slot, rows_dev), here)
         at = rel * group_tiles + count[rel]
+        load(u_hbm, u_ref, u_sem, tile, at, rel)
         count[rel] = count[rel] + 1
-        load(u_hbm, u_ref, u_sem, tile, at)
         tile_at[at] = tile
         code_at[at] = row * rows_dev + lax.rem(slot, rows_dev)
         rank_at[at] = ranks[row, k]
-        return carry
-
-    def load_v(at, carry):
-        load(v_hbm, v_ref, v_sem, tile_at[at], at)
-        return carry
 
     def loaded(ref, sem, group):
         piece = ref.at[pl.ds(group * deep, deep)]
         pltpu.make_async_copy(piece, piece, sem.at[group]).wait()
 
-    lax.fori_loop(0, tiles, sort_tile, 0)
-    lax.fori_loop(0, tiles, load_v, 0)
+    for at in range(tiles):
+        load(v_hbm, v_ref, v_sem, tile_at[at], at, at // group_tiles)
     lane = lax.broadcasted_iota(jnp.int32, (1, deep), 1)
     for group in range(peers):
         code = jnp.full((1, deep), -1, jnp.int32)
@@ -209,16 +204,12 @@
                 put_terms(lhs, v_ref, group, part, (None, out), rows_dev, peers)
 
 
-def rest_kernel(dims, sent, parts, lhs_ref, v_ref, *refs):
+def more_kernel(dims, parts, lhs_ref, v_ref, *outs):
     rows_dev, peers = dims
-    sends = refs[: len(sent)]
-    keeps = refs[len(sent) :]
-    for out, i in zip(sends, sent):
-        for group in in_order(parts[i][2], peers)[peers // 2 :]:
-            put_terms(lhs_ref[group], v_ref, group, parts[i], (None, out), rows_dev, peers)
-    for keep, part in zip(keeps, parts):
-        for group in in_order(part[2], peers)[: peers // 2]:
-            put_terms(lhs_ref[group], v_ref, group, part, (keep, None), rows_dev, peers)
+    for out, (part, kept) in zip(outs, parts):
+        for group in range(peers):
+            if (spot(part[2], group) < peers // 2) == kept:
+                put_terms(lhs_ref[group], v_ref, group, part, (out, out), rows_dev, peers)
 
 
 def finish_kernel(parts, contrast_ref, forward_ref, *refs):
@@ -246,7 +237,7 @@
     tiles = rows_dev * tiles_row
     deep = tiles // peers * rank_max
     parts = parts_of(unknowns, peers)
-    first_sent, then_sent, late = [0, 1], [], 1
+    first_sent, late = [0], 1
     early = [i for i in range(len(parts)) if i != late]
     half = (peers // 2 * rows_dev, sources)
     sent = [jax.ShapeDtypeStruct((*half, part[1]), jnp.bfloat16) for part in parts]
@@ -305,19 +296,20 @@
                 cost_estimate=cost(u.shape[0], unknowns // 2, sources),
                 name="ready",
             )(code, contrast, coeff, base[late], came[late], in_vmem(u), in_vmem(v))
-            rest = pl.pallas_call(
-                functools.partial(rest_kernel, dims, then_sent, parts),
-                out_shape=[sent[i] for i in then_sent] + kept,
-                in_specs=vmem(2),
-                out_specs=vmem(len(then_sent) + len(parts)),
-                compiler_params=params(),
-                cost_estimate=cost(u.shape[0], unknowns // 2, sources),
-                name="rest",
-            )(lhs, in_vmem(v))
-            goes = [None] * len(parts)
-            for i, x in zip(first_sent + then_sent, [*some, *rest[: len(then_sent)]]):
-                goes[i] = x
-            keeps = list(rest[len(then_sent) :])
+            goes, keeps = [*some], []
+            for names, shapes, to in (
+                [[(parts[1], False)], sent[1:], goes],
+                [[(part, True) for part in parts], kept, keeps],
+            ):
+                to += pl.pallas_call(
+                    functools.partial(more_kernel, dims, names),
+                    out_shape=shapes,
+                    in_specs=vmem(2),
+                    out_specs=vmem(len(shapes)),
+                    compiler_params=params(),
+                    cost_estimate=cost(u.shape[0], unknowns // 4 * len(shapes), sources),
+                    name="more",
+                )(lhs, in_vmem(v))
         base, came = [None] * len(parts), [None] * len(parts)
         levels = len(parts[0][2])
         for level in range(levels):

time: 116 us -> 119 us (1.026)
  starting transfers between devices: 48.7 us -> 41 us
  waiting for transfers between devices: 28.4 us -> 35.3 us
  Pallas kernels: 36.5 us -> 39.7 us
    ppermute x24, starting transfers between devices: 46.9 us -> 39.1 us  [swap(): return lax.ppermute(x, 'rows', [(i, i ^ 1 << bit) for i in range(peers)])]
    ppermute x24, waiting for transfers between devices: 26.5 us -> 33.4 us  [swap(): return lax.ppermute(x, 'rows', [(i, i ^ 1 << bit) for i in range(peers)])]
    pallas_call x1, Pallas kernels: 14.7 us -> 18.3 us  [slot_sums(): pl.pallas_call(functools.partial(start_kernel, (rows_dev, tiles_row, rank...]
    pallas_call x3, Pallas kernels: 11.1 us -> 8.86 us  [slot_sums(): pl.pallas_call(functools.partial(ready_kernel, dims, parts[late], [parts[...]
    pallas_call x3 -> x6, Pallas kernels: 3.69 us -> 5.55 us  [slot_sums(): pl.pallas_call(functools.partial(more_kernel, dims, names), out_shape=sha...]
  transfers between devices with their start and end apart: 27 -> 27, of which waited for: 20 -> 19; matrix products, arithmetic and copies ran while one was open for 1% -> 1% of each run, Pallas kernels for 9% -> 9%
where the time goes in v5:
time: 119 us; the launch traced here: 118 us
  starting transfers between devices  41 us (34%)
  Pallas kernels  39.7 us (33%)
  waiting for transfers between devices  35.3 us (30%)
  other arithmetic  1.52 us (1%)
    ppermute x24, starting transfers between devices, swap(): return lax.ppermute(x, 'rows', [(i, i ^ 1 << bit) for i in range(peers)])  39.1 us
    ppermute x24, waiting for transfers between devices, swap(): return lax.ppermute(x, 'rows', [(i, i ^ 1 << bit) for i in range(peers)])  33.4 us
    pallas_call x1, Pallas kernels, slot_sums(): pl.pallas_call(functools.partial(start_kernel, (rows_dev, tiles_row, rank...  18.3 us
    pallas_call x3, Pallas kernels, slot_sums(): pl.pallas_call(functools.partial(ready_kernel, dims, parts[late], [parts[...  8.86 us
    pallas_call x3, Pallas kernels, slot_sums(): pl.pallas_call(functools.partial(early_kernel, dims, [parts[i] for i in e...  6.24 us
    pallas_call x6, Pallas kernels, slot_sums(): pl.pallas_call(functools.partial(more_kernel, dims, names), out_shape=sha...  5.55 us
  transfers between devices with their start and end apart: 27, of which 19 were waited for; matrix products, arithmetic and copies ran while one was open for 1% of the time, Pallas kernels for 9%

profile of v5, /device:TPU:0, one launch (start us, length us, event | category | flops | bytes accessed | tf_op | source)
XLA Modules:
  0.0 118.4 jit_solution(16539610725852571904)
XLA Ops:
  0.7 18.3 %start.1 = (bf16[6144,1024]{1,0:T(8,128)(2,1)S(1)}, bf16[6144,1024]{1,0:T(8,128)(2,1)S(1)}, s32[8,768]{1,0:T(8,128)S(1)}, f32[16,16,512]{2,1,0:T(8,128)S(1)}, bf...) custom-call(s32[16,32]{1,0:T(8,128)} %bitcast.11, s32[32]{0:T(128)} %refs_1_.1, ...), custom_call_target="tpu_custom_call" | custom-call | flops 402653184 | bytes 25165824 | tf_op jit(solution)/shard_map/start/pallas_call | solution.py:248
  19.0 2.9 %collective-permute-start = (bf16[16,16,512]{2,1,0:T(8,128)(2,1)S(1)}, bf16[16,16,512]{2,1,0:T(8,128)(2,1)S(1)}, u32[]{:S(2)}, u32[]{:S(2)}) collective-permute-start(bf16[16,16,512]{2,1,0:T(8,128)(2,1)S(1)} %get-tuple-element.25), channel_id=1, source_target_pairs={{0,4},{4,0},{8,12},{12,8},{16,20},{20,16},{24,28},{28,24},{1,5},{5... | collective-permute-start | bytes 786440 | tf_op jit(solution)/shard_map/ppermute | solution.py:228
  21.9 1.5 %collective-permute-start.3 = (bf16[16,16,512]{2,1,0:T(8,128)(2,1)S(1)}, bf16[16,16,512]{2,1,0:T(8,128)(2,1)S(1)}, u32[]{:S(2)}, u32[]{:S(2)}) collective-permute-start(bf16[16,16,512]{2,1,0:T(8,128)(2,1)S(1)} %get-tuple-element.28), channel_id=1, source_target_pairs={{0,8},{4,12},{8,0},{12,4},{16,24},{20,28},{24,16},{28,20},{1,9},{5... | collective-permute-start | bytes 786440 | tf_op jit(solution)/shard_map/ppermute | solution.py:228
  23.4 4.8 %collective-permute-done = bf16[16,16,512]{2,1,0:T(8,128)(2,1)S(1)} collective-permute-done((bf16[16,16,512]{2,1,0:T(8,128)(2,1)S(1)}, bf16[16,16,512]{2,1,0:T(8,128)(2,1)S(1)}, u32[]{:S(2)}, u32[]{:S(2)}) %collective-permute-start) | collective-permute-done | bytes 262176 | tf_op jit(solution)/shard_map/ppermute | solution.py:228
  28.2 0.1 add_convert_fusion.7
  28.3 2.1 %collective-permute-start.1 = (bf16[8,16,512]{2,1,0:T(8,128)(2,1)S(1)}, bf16[8,16,512]{2,1,0:T(8,128)(2,1)S(1)}, u32[]{:S(2)}, u32[]{:S(2)}) collective-permute-start(bf16[8,16,512]{2,1,0:T(8,128)(2,1)S(1)} %get-tuple-element.58), channel_id=1, source_target_pairs={{0,8},{4,12},{8,0},{12,4},{16,24},{20,28},{24,16},{28,20},{1,9},{5... | collective-permute-start | bytes 393224 | tf_op jit(solution)/shard_map/ppermute | solution.py:228
  30.3 0.1 add_convert_fusion.6
  30.4 1.2 %collective-permute-start.4 = (bf16[8,16,512]{2,1,0:T(8,128)(2,1)S(1)}, bf16[8,16,512]{2,1,0:T(8,128)(2,1)S(1)}, u32[]{:S(2)}, u32[]{:S(2)}) collective-permute-start(bf16[8,16,512]{2,1,0:T(8,128)(2,1)S(1)} %get-tuple-element.56), channel_id=1, source_target_pairs={{0,4},{4,0},{8,12},{12,8},{16,20},{20,16},{24,28},{28,24},{1,5},{5... | collective-permute-start | bytes 393224 | tf_op jit(solution)/shard_map/ppermute | solution.py:228
  31.7 1.6 %collective-permute-done.1 = bf16[8,16,512]{2,1,0:T(8,128)(2,1)S(1)} collective-permute-done((bf16[8,16,512]{2,1,0:T(8,128)(2,1)S(1)}, bf16[8,16,512]{2,1,0:T(8,128)(2,1)S(1)}, u32[]{:S(2)}, u32[]{:S(2)}) %collective-permute-start.1) | collective-permute-done | bytes 131104 | tf_op jit(solution)/shard_map/ppermute | solution.py:228
  33.3 3.1 %collective-permute-start.2 = (bf16[4,16,512]{2,1,0:T(8,128)(2,1)S(1)}, bf16[4,16,512]{2,1,0:T(8,128)(2,1)S(1)}, u32[]{:S(2)}, u32[]{:S(2)}) collective-permute-start(bf16[4,16,512]{2,1,0:T(8,128)(2,1)S(1)} %get-tuple-element.74), channel_id=1, source_target_pairs={{0,16},{4,20},{8,24},{12,28},{16,0},{20,4},{24,8},{28,12},{1,17},{... | collective-permute-start | bytes 196616 | tf_op jit(solution)/shard_map/ppermute | solution.py:228
  36.5 1.7 %collective-permute-start.5 = (bf16[4,16,512]{2,1,0:T(8,128)(2,1)S(1)}, bf16[4,16,512]{2,1,0:T(8,128)(2,1)S(1)}, u32[]{:S(2)}, u32[]{:S(2)}) collective-permute-start(bf16[4,16,512]{2,1,0:T(8,128)(2,1)S(1)} %get-tuple-element.72), channel_id=1, source_target_pairs={{0,16},{4,20},{8,24},{12,28},{16,0},{20,4},{24,8},{28,12},{1,17},{... | collective-permute-start | bytes 196616 | tf_op jit(solution)/shard_map/ppermute | solution.py:228
  38.2 2.2 %collective-permute-done.2.refs_1_ = bf16[4,16,512]{2,1,0:T(8,128)(2,1)S(1)} collective-permute-done((bf16[4,16,512]{2,1,0:T(8,128)(2,1)S(1)}, bf16[4,16,512]{2,1,0:T(8,128)(2,1)S(1)}, u32[]{:S(2)}, u32[]{:S(2)}) %collective-permute-start.2) | collective-permute-done | bytes 65568 | tf_op jit(solution)/shard_map/ppermute | solution.py:228
  40.4 2.0 %early.3.sum_ref = f32[8,16,768]{2,1,0:T(8,128)S(1)} custom-call(s32[8,768]{1,0:T(8,128)S(1)} %get-tuple-element.23.code_ref, f32[4,1024]{1,0:T(4,128)S(1)} %copy-done, f32[4,16,512]{2,1,0:T(8,128)S(1)} %get-tuple-element.75.refs_0_, bf16[4,16,512]{2,1,0:T(8,128)(2,1)S(1)} %collective-permute-done.2.refs_1_, ...), custom_call_target="tpu_custom_call" | custom-call | flops 100663296 | bytes 6291456 | tf_op jit(solution)/shard_map/early/pallas_call | solution.py:280
  42.4 3.0 %ready.3 = (bf16[8,64,768]{2,1,0:T(8,128)(2,1)S(1)}, bf16[16,16,512]{2,1,0:T(8,128)(2,1)S(1)}) custom-call(s32[8,768]{1,0:T(8,128)S(1)} %get-tuple-element.23.code_ref, f32[4,1024]{1,0:T(4,128)S(1)} %copy-done, f32[8,16,768]{2,1,0:T(8,128)S(1)} %early.3.sum_ref, f32[4,16,512]{2,1,0:T(8,128)S(1)} %get-tuple-element.73.base_ref, ...), custom_call_target="tpu_custom_call" | custom-call | flops 100663296 | bytes 6291456 | tf_op jit(solution)/shard_map/ready/pallas_call | solution.py:289
  45.4 1.6 %collective-permute-start.6 = (bf16[16,16,512]{2,1,0:T(8,128)(2,1)S(1)}, bf16[16,16,512]{2,1,0:T(8,128)(2,1)S(1)}, u32[]{:S(2)}, u32[]{:S(2)}) collective-permute-start(bf16[16,16,512]{2,1,0:T(8,128)(2,1)S(1)} %get-tuple-element.32), channel_id=1, source_target_pairs={{0,4},{4,0},{8,12},{12,8},{16,20},{20,16},{24,28},{28,24},{1,5},{5... | collective-permute-start | bytes 786440 | tf_op jit(solution)/shard_map/ppermute | solution.py:228
  47.0 0.7 more.7
  47.7 1.1 collective-permute-start.9
  48.8 1.2 %more.6 = (f32[16,16,512]{2,1,0:T(8,128)S(1)}, f32[16,16,512]{2,1,0:T(8,128)S(1)}) custom-call(bf16[8,64,768]{2,1,0:T(8,128)(2,1)S(1)} %get-tuple-element.30.lhs_ref, bf16[6144,1024]{1,0:T(8,128)(2,1)S(1)} %get-tuple-element.29.refs_1_.v_ref), custom_call_target="tpu_custom_call" | custom-call | flops 100663296 | bytes 6291456 | tf_op jit(solution)/shard_map/more/pallas_call | solution.py:304
  50.0 1.8 %collective-permute-done.6 = bf16[16,16,512]{2,1,0:T(8,128)(2,1)S(1)} collective-permute-done((bf16[16,16,512]{2,1,0:T(8,128)(2,1)S(1)}, bf16[16,16,512]{2,1,0:T(8,128)(2,1)S(1)}, u32[]{:S(2)}, u32[]{:S(2)}) %collective-permute-start.6) | collective-permute-done | bytes 262176 | tf_op jit(solution)/shard_map/ppermute | solution.py:228
  51.9 0.9 collective-permute-start.7
  52.8 1.3 %collective-permute-done.9 = bf16[16,16,512]{2,1,0:T(8,128)(2,1)S(1)} collective-permute-done((bf16[16,16,512]{2,1,0:T(8,128)(2,1)S(1)}, bf16[16,16,512]{2,1,0:T(8,128)(2,1)S(1)}, u32[]{:S(2)}, u32[]{:S(2)}) %collective-permute-start.9) | collective-permute-done | bytes 262176 | tf_op jit(solution)/shard_map/ppermute | solution.py:228
  54.2 1.5 %collective-permute-start.10 = (bf16[8,16,512]{2,1,0:T(8,128)(2,1)S(1)}, bf16[8,16,512]{2,1,0:T(8,128)(2,1)S(1)}, u32[]{:S(2)}, u32[]{:S(2)}) collective-permute-start(bf16[8,16,512]{2,1,0:T(8,128)(2,1)S(1)} %get-tuple-element.52), channel_id=1, source_target_pairs={{0,4},{4,0},{8,12},{12,8},{16,20},{20,16},{24,28},{28,24},{1,5},{5... | collective-permute-start | bytes 393224 | tf_op jit(solution)/shard_map/ppermute | solution.py:228
  55.7 1.3 %collective-permute-done.7 = bf16[8,16,512]{2,1,0:T(8,128)(2,1)S(1)} collective-permute-done((bf16[8,16,512]{2,1,0:T(8,128)(2,1)S(1)}, bf16[8,16,512]{2,1,0:T(8,128)(2,1)S(1)}, u32[]{:S(2)}, u32[]{:S(2)}) %collective-permute-start.7) | collective-permute-done | bytes 131104 | tf_op jit(solution)/shard_map/ppermute | solution.py:228
  57.0 2.1 %collective-permute-start.8 = (bf16[4,16,512]{2,1,0:T(8,128)(2,1)S(1)}, bf16[4,16,512]{2,1,0:T(8,128)(2,1)S(1)}, u32[]{:S(2)}, u32[]{:S(2)}) collective-permute-start(bf16[4,16,512]{2,1,0:T(8,128)(2,1)S(1)} %get-tuple-element.70), channel_id=1, source_target_pairs={{0,16},{4,20},{8,24},{12,28},{16,0},{20,4},{24,8},{28,12},{1,17},{... | collective-permute-start | bytes 196616 | tf_op jit(solution)/shard_map/ppermute | solution.py:228
  59.1 0.1 collective-permute-done.10
  59.3 1.9 %collective-permute-start.11 = (bf16[4,16,512]{2,1,0:T(8,128)(2,1)S(1)}, bf16[4,16,512]{2,1,0:T(8,128)(2,1)S(1)}, u32[]{:S(2)}, u32[]{:S(2)}) collective-permute-start(bf16[4,16,512]{2,1,0:T(8,128)(2,1)S(1)} %get-tuple-element.68), channel_id=1, source_target_pairs={{0,16},{4,20},{8,24},{12,28},{16,0},{20,4},{24,8},{28,12},{1,17},{... | collective-permute-start | bytes 196616 | tf_op jit(solution)/shard_map/ppermute | solution.py:228
  61.1 1.1 collective-permute-done.8.refs_1_
  62.3 2.2 %early.4.sum_ref = f32[8,16,768]{2,1,0:T(8,128)S(1)} custom-call(s32[8,768]{1,0:T(8,128)S(1)} %get-tuple-element.23.code_ref, f32[4,1024]{1,0:T(4,128)S(1)} %copy-done, f32[4,16,512]{2,1,0:T(8,128)S(1)} %get-tuple-element.71.refs_0_, bf16[4,16,512]{2,1,0:T(8,128)(2,1)S(1)} %collective-permute-done.8.refs_1_, ...), custom_call_target="tpu_custom_call" | custom-call | flops 100663296 | bytes 6291456 | tf_op jit(solution)/shard_map/early/pallas_call | solution.py:280
  64.5 2.9 %ready.4 = (bf16[8,64,768]{2,1,0:T(8,128)(2,1)S(1)}, bf16[16,16,512]{2,1,0:T(8,128)(2,1)S(1)}) custom-call(s32[8,768]{1,0:T(8,128)S(1)} %get-tuple-element.23.code_ref, f32[4,1024]{1,0:T(4,128)S(1)} %copy-done, f32[8,16,768]{2,1,0:T(8,128)S(1)} %early.4.sum_ref, f32[4,16,512]{2,1,0:T(8,128)S(1)} %get-tuple-element.69.base_ref, ...), custom_call_target="tpu_custom_call" | custom-call | flops 100663296 | bytes 6291456 | tf_op jit(solution)/shard_map/ready/pallas_call | solution.py:289
  67.4 2.6 %collective-permute-start.12 = (bf16[16,16,512]{2,1,0:T(8,128)(2,1)S(1)}, bf16[16,16,512]{2,1,0:T(8,128)(2,1)S(1)}, u32[]{:S(2)}, u32[]{:S(2)}) collective-permute-start(bf16[16,16,512]{2,1,0:T(8,128)(2,1)S(1)} %get-tuple-element.36), channel_id=1, source_target_pairs={{0,4},{4,0},{8,12},{12,8},{16,20},{20,16},{24,28},{28,24},{1,5},{5... | collective-permute-start | bytes 786440 | tf_op jit(solution)/shard_map/ppermute | solution.py:228
  70.1 0.7 more.9
  70.7 1.4 %collective-permute-start.15 = (bf16[16,16,512]{2,1,0:T(8,128)(2,1)S(1)}, bf16[16,16,512]{2,1,0:T(8,128)(2,1)S(1)}, u32[]{:S(2)}, u32[]{:S(2)}) collective-permute-start(bf16[16,16,512]{2,1,0:T(8,128)(2,1)S(1)} %more.9), channel_id=1, source_target_pairs={{0,8},{4,12},{8,0},{12,4},{16,24},{20,28},{24,16},{28,20},{1,9},{5... | collective-permute-start | bytes 786440 | tf_op jit(solution)/shard_map/ppermute | solution.py:228
  72.2 1.2 %more.8 = (f32[16,16,512]{2,1,0:T(8,128)S(1)}, f32[16,16,512]{2,1,0:T(8,128)S(1)}) custom-call(bf16[8,64,768]{2,1,0:T(8,128)(2,1)S(1)} %get-tuple-element.34.lhs_ref, bf16[6144,1024]{1,0:T(8,128)(2,1)S(1)} %get-tuple-element.29.refs_1_.v_ref), custom_call_target="tpu_custom_call" | custom-call | flops 100663296 | bytes 6291456 | tf_op jit(solution)/shard_map/more/pallas_call | solution.py:304
  73.4 2.5 %collective-permute-done.12 = bf16[16,16,512]{2,1,0:T(8,128)(2,1)S(1)} collective-permute-done((bf16[16,16,512]{2,1,0:T(8,128)(2,1)S(1)}, bf16[16,16,512]{2,1,0:T(8,128)(2,1)S(1)}, u32[]{:S(2)}, u32[]{:S(2)}) %collective-permute-start.12) | collective-permute-done | bytes 262176 | tf_op jit(solution)/shard_map/ppermute | solution.py:228
  75.9 1.5 %collective-permute-start.13 = (bf16[8,16,512]{2,1,0:T(8,128)(2,1)S(1)}, bf16[8,16,512]{2,1,0:T(8,128)(2,1)S(1)}, u32[]{:S(2)}, u32[]{:S(2)}) collective-permute-start(bf16[8,16,512]{2,1,0:T(8,128)(2,1)S(1)} %get-tuple-element.50), channel_id=1, source_target_pairs={{0,8},{4,12},{8,0},{12,4},{16,24},{20,28},{24,16},{28,20},{1,9},{5... | collective-permute-start | bytes 393224 | tf_op jit(solution)/shard_map/ppermute | solution.py:228
  77.4 0.5 collective-permute-done.15
  77.9 1.3 %collective-permute-start.16 = (bf16[8,16,512]{2,1,0:T(8,128)(2,1)S(1)}, bf16[8,16,512]{2,1,0:T(8,128)(2,1)S(1)}, u32[]{:S(2)}, u32[]{:S(2)}) collective-permute-start(bf16[8,16,512]{2,1,0:T(8,128)(2,1)S(1)} %get-tuple-element.48), channel_id=1, source_target_pairs={{0,4},{4,0},{8,12},{12,8},{16,20},{20,16},{24,28},{28,24},{1,5},{5... | collective-permute-start | bytes 393224 | tf_op jit(solution)/shard_map/ppermute | solution.py:228
  79.2 2.1 %collective-permute-done.13 = bf16[8,16,512]{2,1,0:T(8,128)(2,1)S(1)} collective-permute-done((bf16[8,16,512]{2,1,0:T(8,128)(2,1)S(1)}, bf16[8,16,512]{2,1,0:T(8,128)(2,1)S(1)}, u32[]{:S(2)}, u32[]{:S(2)}) %collective-permute-start.13) | collective-permute-done | bytes 131104 | tf_op jit(solution)/shard_map/ppermute | solution.py:228
  81.4 1.8 %collective-permute-start.14 = (bf16[4,16,512]{2,1,0:T(8,128)(2,1)S(1)}, bf16[4,16,512]{2,1,0:T(8,128)(2,1)S(1)}, u32[]{:S(2)}, u32[]{:S(2)}) collective-permute-start(bf16[4,16,512]{2,1,0:T(8,128)(2,1)S(1)} %get-tuple-element.66), channel_id=1, source_target_pairs={{0,16},{4,20},{8,24},{12,28},{16,0},{20,4},{24,8},{28,12},{1,17},{... | collective-permute-start | bytes 196616 | tf_op jit(solution)/shard_map/ppermute | solution.py:228
  83.3 1.5 %collective-permute-start.17 = (bf16[4,16,512]{2,1,0:T(8,128)(2,1)S(1)}, bf16[4,16,512]{2,1,0:T(8,128)(2,1)S(1)}, u32[]{:S(2)}, u32[]{:S(2)}) collective-permute-start(bf16[4,16,512]{2,1,0:T(8,128)(2,1)S(1)} %get-tuple-element.64), channel_id=1, source_target_pairs={{0,16},{4,20},{8,24},{12,28},{16,0},{20,4},{24,8},{28,12},{1,17},{... | collective-permute-start | bytes 196616 | tf_op jit(solution)/shard_map/ppermute | solution.py:228
  84.8 2.7 %collective-permute-done.14.refs_1_ = bf16[4,16,512]{2,1,0:T(8,128)(2,1)S(1)} collective-permute-done((bf16[4,16,512]{2,1,0:T(8,128)(2,1)S(1)}, bf16[4,16,512]{2,1,0:T(8,128)(2,1)S(1)}, u32[]{:S(2)}, u32[]{:S(2)}) %collective-permute-start.14) | collective-permute-done | bytes 65568 | tf_op jit(solution)/shard_map/ppermute | solution.py:228
  87.4 2.0 %early.5.sum_ref = f32[8,16,768]{2,1,0:T(8,128)S(1)} custom-call(s32[8,768]{1,0:T(8,128)S(1)} %get-tuple-element.23.code_ref, f32[4,1024]{1,0:T(4,128)S(1)} %copy-done, f32[4,16,512]{2,1,0:T(8,128)S(1)} %get-tuple-element.67.refs_0_, bf16[4,16,512]{2,1,0:T(8,128)(2,1)S(1)} %collective-permute-done.14.refs_1_, ...), custom_call_target="tpu_custom_call" | custom-call | flops 100663296 | bytes 6291456 | tf_op jit(solution)/shard_map/early/pallas_call | solution.py:280
  89.5 3.0 %ready.5 = (bf16[8,64,768]{2,1,0:T(8,128)(2,1)S(1)}, bf16[16,16,512]{2,1,0:T(8,128)(2,1)S(1)}) custom-call(s32[8,768]{1,0:T(8,128)S(1)} %get-tuple-element.23.code_ref, f32[4,1024]{1,0:T(4,128)S(1)} %copy-done, f32[8,16,768]{2,1,0:T(8,128)S(1)} %early.5.sum_ref, f32[4,16,512]{2,1,0:T(8,128)S(1)} %get-tuple-element.65.base_ref, ...), custom_call_target="tpu_custom_call" | custom-call | flops 100663296 | bytes 6291456 | tf_op jit(solution)/shard_map/ready/pallas_call | solution.py:289
  92.4 0.7 more.11
  93.1 2.0 %collective-permute-start.21 = (bf16[16,16,512]{2,1,0:T(8,128)(2,1)S(1)}, bf16[16,16,512]{2,1,0:T(8,128)(2,1)S(1)}, u32[]{:S(2)}, u32[]{:S(2)}) collective-permute-start(bf16[16,16,512]{2,1,0:T(8,128)(2,1)S(1)} %more.11), channel_id=1, source_target_pairs={{0,8},{4,12},{8,0},{12,4},{16,24},{20,28},{24,16},{28,20},{1,9},{5... | collective-permute-start | bytes 786440 | tf_op jit(solution)/shard_map/ppermute | solution.py:228
  95.0 0.7 collective-permute-start.18
  95.7 1.2 %more.10 = (f32[16,16,512]{2,1,0:T(8,128)S(1)}, f32[16,16,512]{2,1,0:T(8,128)S(1)}) custom-call(bf16[8,64,768]{2,1,0:T(8,128)(2,1)S(1)} %get-tuple-element.38.lhs_ref, bf16[6144,1024]{1,0:T(8,128)(2,1)S(1)} %get-tuple-element.29.refs_1_.v_ref), custom_call_target="tpu_custom_call" | custom-call | flops 100663296 | bytes 6291456 | tf_op jit(solution)/shard_map/more/pallas_call | solution.py:304
  96.9 4.0 %collective-permute-done.21 = bf16[16,16,512]{2,1,0:T(8,128)(2,1)S(1)} collective-permute-done((bf16[16,16,512]{2,1,0:T(8,128)(2,1)S(1)}, bf16[16,16,512]{2,1,0:T(8,128)(2,1)S(1)}, u32[]{:S(2)}, u32[]{:S(2)}) %collective-permute-start.21) | collective-permute-done | bytes 262176 | tf_op jit(solution)/shard_map/ppermute | solution.py:228
  100.9 0.1 add_convert_fusion
  101.0 1.8 %collective-permute-start.22 = (bf16[8,16,512]{2,1,0:T(8,128)(2,1)S(1)}, bf16[8,16,512]{2,1,0:T(8,128)(2,1)S(1)}, u32[]{:S(2)}, u32[]{:S(2)}) collective-permute-start(bf16[8,16,512]{2,1,0:T(8,128)(2,1)S(1)} %get-tuple-element.44), channel_id=1, source_target_pairs={{0,4},{4,0},{8,12},{12,8},{16,20},{20,16},{24,28},{28,24},{1,5},{5... | collective-permute-start | bytes 393224 | tf_op jit(solution)/shard_map/ppermute | solution.py:228
  102.8 0.1 add_convert_fusion.1
  102.9 0.9 collective-permute-start.19
  103.8 2.3 %collective-permute-done.22 = bf16[8,16,512]{2,1,0:T(8,128)(2,1)S(1)} collective-permute-done((bf16[8,16,512]{2,1,0:T(8,128)(2,1)S(1)}, bf16[8,16,512]{2,1,0:T(8,128)(2,1)S(1)}, u32[]{:S(2)}, u32[]{:S(2)}) %collective-permute-start.22) | collective-permute-done | bytes 131104 | tf_op jit(solution)/shard_map/ppermute | solution.py:228
  106.1 0.8 collective-permute-start.23
  106.9 1.0 collective-permute-done.19
  108.0 1.2 %collective-permute-start.20 = (bf16[4,16,512]{2,1,0:T(8,128)(2,1)S(1)}, bf16[4,16,512]{2,1,0:T(8,128)(2,1)S(1)}, u32[]{:S(2)}, u32[]{:S(2)}) collective-permute-start(bf16[4,16,512]{2,1,0:T(8,128)(2,1)S(1)} %get-tuple-element.62), channel_id=1, source_target_pairs={{0,16},{4,20},{8,24},{12,28},{16,0},{20,4},{24,8},{28,12},{1,17},{... | collective-permute-start | bytes 196616 | tf_op jit(solution)/shard_map/ppermute | solution.py:228
  109.2 2.1 %collective-permute-done.23.refs_3_ = bf16[4,16,512]{2,1,0:T(8,128)(2,1)S(1)} collective-permute-done((bf16[4,16,512]{2,1,0:T(8,128)(2,1)S(1)}, bf16[4,16,512]{2,1,0:T(8,128)(2,1)S(1)}, u32[]{:S(2)}, u32[]{:S(2)}) %collective-permute-start.23) | collective-permute-done | bytes 65568 | tf_op jit(solution)/shard_map/ppermute | solution.py:228
  111.3 1.9 %collective-permute-done.20.refs_1_ = bf16[4,16,512]{2,1,0:T(8,128)(2,1)S(1)} collective-permute-done((bf16[4,16,512]{2,1,0:T(8,128)(2,1)S(1)}, bf16[4,16,512]{2,1,0:T(8,128)(2,1)S(1)}, u32[]{:S(2)}, u32[]{:S(2)}) %collective-permute-start.20) | collective-permute-done | bytes 65568 | tf_op jit(solution)/shard_map/ppermute | solution.py:228
  113.2 0.8 finish.1
  114.0 1.5 %collective-permute-start.25 = (f32[4,1024]{1,0:T(4,128)S(1)}, f32[4,1024]{1,0:T(4,128)S(1)}, u32[]{:S(2)}, u32[]{:S(2)}) collective-permute-start(f32[4,1024]{1,0:T(4,128)S(1)} %get-tuple-element.43), channel_id=1, source_target_pairs={{0,2},{1,3},{2,0},{3,1},{4,6},{5,7},{6,4},{7,5},{8,10},{9,11},{10,... | collective-permute-start | bytes 49160 | tf_op jit(solution)/shard_map/ppermute | solution.py:407
  115.4 0.4 collective-permute-start.24
  115.8 1.5 %collective-permute-done.26 = f32[4,1024]{1,0:T(4,128)S(1)} collective-permute-done((f32[4,1024]{1,0:T(4,128)S(1)}, f32[4,1024]{1,0:T(4,128)S(1)}, u32[]{:S(2)}, u32[]{:S(2)}) %collective-permute-start.26) | collective-permute-done | bytes 16416 | tf_op jit(solution)/shard_map/ppermute | solution.py:407
  117.3 0.5 collective-permute-done.25
  117.8 0.6 add_multiply_fusion
  (28 shorter events, 0.7 us)
Async XLA Ops:
  0.6 22.7 %copy-start = (f32[4,1024]{1,0:T(4,128)S(1)}, f32[4,1024]{1,0:T(4,128)}, u32[]{:S(2)}) copy-start(f32[4,1024]{1,0:T(4,128)} %contrast_ref.13) | copy-start | bytes 49156
  0.6 32.6 %copy-start.2 = (f32[4,16,1024]{2,1,0:T(8,128)S(1)}, f32[4,16,1024]{2,1,0:T(8,128)}, u32[]{:S(2)}) copy-start(f32[4,16,1024]{2,1,0:T(8,128)} %refs_3_.1) | copy-start | bytes 786436
  19.0 9.2 %collective-permute-start = (bf16[16,16,512]{2,1,0:T(8,128)(2,1)S(1)}, bf16[16,16,512]{2,1,0:T(8,128)(2,1)S(1)}, u32[]{:S(2)}, u32[]{:S(2)}) collective-permute-start(bf16[16,16,512]{2,1,0:T(8,128)(2,1)S(1)} %get-tuple-element.25), channel_id=1, source_target_pairs={{0,4},{4,0},{8,12},{12,8},{16,20},{20,16},{24,28},{28,24},{1,5},{5... | collective-permute-start | bytes 786440 | tf_op jit(solution)/shard_map/ppermute | solution.py:228
  21.9 8.5 %collective-permute-start.3 = (bf16[16,16,512]{2,1,0:T(8,128)(2,1)S(1)}, bf16[16,16,512]{2,1,0:T(8,128)(2,1)S(1)}, u32[]{:S(2)}, u32[]{:S(2)}) collective-permute-start(bf16[16,16,512]{2,1,0:T(8,128)(2,1)S(1)} %get-tuple-element.28), channel_id=1, source_target_pairs={{0,8},{4,12},{8,0},{12,4},{16,24},{20,28},{24,16},{28,20},{1,9},{5... | collective-permute-start | bytes 786440 | tf_op jit(solution)/shard_map/ppermute | solution.py:228
  28.3 5.0 %collective-permute-start.1 = (bf16[8,16,512]{2,1,0:T(8,128)(2,1)S(1)}, bf16[8,16,512]{2,1,0:T(8,128)(2,1)S(1)}, u32[]{:S(2)}, u32[]{:S(2)}) collective-permute-start(bf16[8,16,512]{2,1,0:T(8,128)(2,1)S(1)} %get-tuple-element.58), channel_id=1, source_target_pairs={{0,8},{4,12},{8,0},{12,4},{16,24},{20,28},{24,16},{28,20},{1,9},{5... | collective-permute-start | bytes 393224 | tf_op jit(solution)/shard_map/ppermute | solution.py:228
  30.4 6.0 %collective-permute-start.4 = (bf16[8,16,512]{2,1,0:T(8,128)(2,1)S(1)}, bf16[8,16,512]{2,1,0:T(8,128)(2,1)S(1)}, u32[]{:S(2)}, u32[]{:S(2)}) collective-permute-start(bf16[8,16,512]{2,1,0:T(8,128)(2,1)S(1)} %get-tuple-element.56), channel_id=1, source_target_pairs={{0,4},{4,0},{8,12},{12,8},{16,20},{20,16},{24,28},{28,24},{1,5},{5... | collective-permute-start | bytes 393224 | tf_op jit(solution)/shard_map/ppermute | solution.py:228
  33.3 7.1 %collective-permute-start.2 = (bf16[4,16,512]{2,1,0:T(8,128)(2,1)S(1)}, bf16[4,16,512]{2,1,0:T(8,128)(2,1)S(1)}, u32[]{:S(2)}, u32[]{:S(2)}) collective-permute-start(bf16[4,16,512]{2,1,0:T(8,128)(2,1)S(1)} %get-tuple-element.74), channel_id=1, source_target_pairs={{0,16},{4,20},{8,24},{12,28},{16,0},{20,4},{24,8},{28,12},{1,17},{... | collective-permute-start | bytes 196616 | tf_op jit(solution)/shard_map/ppermute | solution.py:228
  36.5 5.9 %collective-permute-start.5 = (bf16[4,16,512]{2,1,0:T(8,128)(2,1)S(1)}, bf16[4,16,512]{2,1,0:T(8,128)(2,1)S(1)}, u32[]{:S(2)}, u32[]{:S(2)}) collective-permute-start(bf16[4,16,512]{2,1,0:T(8,128)(2,1)S(1)} %get-tuple-element.72), channel_id=1, source_target_pairs={{0,16},{4,20},{8,24},{12,28},{16,0},{20,4},{24,8},{28,12},{1,17},{... | collective-permute-start | bytes 196616 | tf_op jit(solution)/shard_map/ppermute | solution.py:228
  45.4 6.4 %collective-permute-start.6 = (bf16[16,16,512]{2,1,0:T(8,128)(2,1)S(1)}, bf16[16,16,512]{2,1,0:T(8,128)(2,1)S(1)}, u32[]{:S(2)}, u32[]{:S(2)}) collective-permute-start(bf16[16,16,512]{2,1,0:T(8,128)(2,1)S(1)} %get-tuple-element.32), channel_id=1, source_target_pairs={{0,4},{4,0},{8,12},{12,8},{16,20},{20,16},{24,28},{28,24},{1,5},{5... | collective-permute-start | bytes 786440 | tf_op jit(solution)/shard_map/ppermute | solution.py:228
  47.7 6.4 %collective-permute-start.9 = (bf16[16,16,512]{2,1,0:T(8,128)(2,1)S(1)}, bf16[16,16,512]{2,1,0:T(8,128)(2,1)S(1)}, u32[]{:S(2)}, u32[]{:S(2)}) collective-permute-start(bf16[16,16,512]{2,1,0:T(8,128)(2,1)S(1)} %more.7), channel_id=1, source_target_pairs={{0,8},{4,12},{8,0},{12,4},{16,24},{20,28},{24,16},{28,20},{1,9},{5... | collective-permute-start | bytes 786440 | tf_op jit(solution)/shard_map/ppermute | solution.py:228
  51.9 5.1 %collective-permute-start.7 = (bf16[8,16,512]{2,1,0:T(8,128)(2,1)S(1)}, bf16[8,16,512]{2,1,0:T(8,128)(2,1)S(1)}, u32[]{:S(2)}, u32[]{:S(2)}) collective-permute-start(bf16[8,16,512]{2,1,0:T(8,128)(2,1)S(1)} %get-tuple-element.54), channel_id=1, source_target_pairs={{0,8},{4,12},{8,0},{12,4},{16,24},{20,28},{24,16},{28,20},{1,9},{5... | collective-permute-start | bytes 393224 | tf_op jit(solution)/shard_map/ppermute | solution.py:228
  54.2 5.0 %collective-permute-start.10 = (bf16[8,16,512]{2,1,0:T(8,128)(2,1)S(1)}, bf16[8,16,512]{2,1,0:T(8,128)(2,1)S(1)}, u32[]{:S(2)}, u32[]{:S(2)}) collective-permute-start(bf16[8,16,512]{2,1,0:T(8,128)(2,1)S(1)} %get-tuple-element.52), channel_id=1, source_target_pairs={{0,4},{4,0},{8,12},{12,8},{16,20},{20,16},{24,28},{28,24},{1,5},{5... | collective-permute-start | bytes 393224 | tf_op jit(solution)/shard_map/ppermute | solution.py:228
  57.0 5.2 %collective-permute-start.8 = (bf16[4,16,512]{2,1,0:T(8,128)(2,1)S(1)}, bf16[4,16,512]{2,1,0:T(8,128)(2,1)S(1)}, u32[]{:S(2)}, u32[]{:S(2)}) collective-permute-start(bf16[4,16,512]{2,1,0:T(8,128)(2,1)S(1)} %get-tuple-element.70), channel_id=1, source_target_pairs={{0,16},{4,20},{8,24},{12,28},{16,0},{20,4},{24,8},{28,12},{1,17},{... | collective-permute-start | bytes 196616 | tf_op jit(solution)/shard_map/ppermute | solution.py:228
  59.3 5.2 %collective-permute-start.11 = (bf16[4,16,512]{2,1,0:T(8,128)(2,1)S(1)}, bf16[4,16,512]{2,1,0:T(8,128)(2,1)S(1)}, u32[]{:S(2)}, u32[]{:S(2)}) collective-permute-start(bf16[4,16,512]{2,1,0:T(8,128)(2,1)S(1)} %get-tuple-element.68), channel_id=1, source_target_pairs={{0,16},{4,20},{8,24},{12,28},{16,0},{20,4},{24,8},{28,12},{1,17},{... | collective-permute-start | bytes 196616 | tf_op jit(solution)/shard_map/ppermute | solution.py:228
  67.4 8.4 %collective-permute-start.12 = (bf16[16,16,512]{2,1,0:T(8,128)(2,1)S(1)}, bf16[16,16,512]{2,1,0:T(8,128)(2,1)S(1)}, u32[]{:S(2)}, u32[]{:S(2)}) collective-permute-start(bf16[16,16,512]{2,1,0:T(8,128)(2,1)S(1)} %get-tuple-element.36), channel_id=1, source_target_pairs={{0,4},{4,0},{8,12},{12,8},{16,20},{20,16},{24,28},{28,24},{1,5},{5... | collective-permute-start | bytes 786440 | tf_op jit(solution)/shard_map/ppermute | solution.py:228
  70.7 7.1 %collective-permute-start.15 = (bf16[16,16,512]{2,1,0:T(8,128)(2,1)S(1)}, bf16[16,16,512]{2,1,0:T(8,128)(2,1)S(1)}, u32[]{:S(2)}, u32[]{:S(2)}) collective-permute-start(bf16[16,16,512]{2,1,0:T(8,128)(2,1)S(1)} %more.9), channel_id=1, source_target_pairs={{0,8},{4,12},{8,0},{12,4},{16,24},{20,28},{24,16},{28,20},{1,9},{5... | collective-permute-start | bytes 786440 | tf_op jit(solution)/shard_map/ppermute | solution.py:228
  75.9 5.4 %collective-permute-start.13 = (bf16[8,16,512]{2,1,0:T(8,128)(2,1)S(1)}, bf16[8,16,512]{2,1,0:T(8,128)(2,1)S(1)}, u32[]{:S(2)}, u32[]{:S(2)}) collective-permute-start(bf16[8,16,512]{2,1,0:T(8,128)(2,1)S(1)} %get-tuple-element.50), channel_id=1, source_target_pairs={{0,8},{4,12},{8,0},{12,4},{16,24},{20,28},{24,16},{28,20},{1,9},{5... | collective-permute-start | bytes 393224 | tf_op jit(solution)/shard_map/ppermute | solution.py:228
  77.9 5.3 %collective-permute-start.16 = (bf16[8,16,512]{2,1,0:T(8,128)(2,1)S(1)}, bf16[8,16,512]{2,1,0:T(8,128)(2,1)S(1)}, u32[]{:S(2)}, u32[]{:S(2)}) collective-permute-start(bf16[8,16,512]{2,1,0:T(8,128)(2,1)S(1)} %get-tuple-element.48), channel_id=1, source_target_pairs={{0,4},{4,0},{8,12},{12,8},{16,20},{20,16},{24,28},{28,24},{1,5},{5... | collective-permute-start | bytes 393224 | tf_op jit(solution)/shard_map/ppermute | solution.py:228
  81.4 6.0 %collective-permute-start.14 = (bf16[4,16,512]{2,1,0:T(8,128)(2,1)S(1)}, bf16[4,16,512]{2,1,0:T(8,128)(2,1)S(1)}, u32[]{:S(2)}, u32[]{:S(2)}) collective-permute-start(bf16[4,16,512]{2,1,0:T(8,128)(2,1)S(1)} %get-tuple-element.66), channel_id=1, source_target_pairs={{0,16},{4,20},{8,24},{12,28},{16,0},{20,4},{24,8},{28,12},{1,17},{... | collective-permute-start | bytes 196616 | tf_op jit(solution)/shard_map/ppermute | solution.py:228
  83.3 6.2 %collective-permute-start.17 = (bf16[4,16,512]{2,1,0:T(8,128)(2,1)S(1)}, bf16[4,16,512]{2,1,0:T(8,128)(2,1)S(1)}, u32[]{:S(2)}, u32[]{:S(2)}) collective-permute-start(bf16[4,16,512]{2,1,0:T(8,128)(2,1)S(1)} %get-tuple-element.64), channel_id=1, source_target_pairs={{0,16},{4,20},{8,24},{12,28},{16,0},{20,4},{24,8},{28,12},{1,17},{... | collective-permute-start | bytes 196616 | tf_op jit(solution)/shard_map/ppermute | solution.py:228
  92.4 20.8 %copy-start.1 = (bf16[4,16,1024]{2,1,0:T(8,128)(2,1)S(1)}, bf16[4,16,1024]{2,1,0:T(8,128)(2,1)}, u32[]{:S(2)}) copy-start(bf16[4,16,1024]{2,1,0:T(8,128)(2,1)} %forward_ref.1) | copy-start | bytes 393220
  93.1 7.8 %collective-permute-start.21 = (bf16[16,16,512]{2,1,0:T(8,128)(2,1)S(1)}, bf16[16,16,512]{2,1,0:T(8,128)(2,1)S(1)}, u32[]{:S(2)}, u32[]{:S(2)}) collective-permute-start(bf16[16,16,512]{2,1,0:T(8,128)(2,1)S(1)} %more.11), channel_id=1, source_target_pairs={{0,8},{4,12},{8,0},{12,4},{16,24},{20,28},{24,16},{28,20},{1,9},{5... | collective-permute-start | bytes 786440 | tf_op jit(solution)/shard_map/ppermute | solution.py:228
  95.0 7.8 %collective-permute-start.18 = (bf16[16,16,512]{2,1,0:T(8,128)(2,1)S(1)}, bf16[16,16,512]{2,1,0:T(8,128)(2,1)S(1)}, u32[]{:S(2)}, u32[]{:S(2)}) collective-permute-start(bf16[16,16,512]{2,1,0:T(8,128)(2,1)S(1)} %get-tuple-element.40), channel_id=1, source_target_pairs={{0,4},{4,0},{8,12},{12,8},{16,20},{20,16},{24,28},{28,24},{1,5},{5... | collective-permute-start | bytes 786440 | tf_op jit(solution)/shard_map/ppermute | solution.py:228
  101.0 5.0 %collective-permute-start.22 = (bf16[8,16,512]{2,1,0:T(8,128)(2,1)S(1)}, bf16[8,16,512]{2,1,0:T(8,128)(2,1)S(1)}, u32[]{:S(2)}, u32[]{:S(2)}) collective-permute-start(bf16[8,16,512]{2,1,0:T(8,128)(2,1)S(1)} %get-tuple-element.44), channel_id=1, source_target_pairs={{0,4},{4,0},{8,12},{12,8},{16,20},{20,16},{24,28},{28,24},{1,5},{5... | collective-permute-start | bytes 393224 | tf_op jit(solution)/shard_map/ppermute | solution.py:228
  102.9 5.0 %collective-permute-start.19 = (bf16[8,16,512]{2,1,0:T(8,128)(2,1)S(1)}, bf16[8,16,512]{2,1,0:T(8,128)(2,1)S(1)}, u32[]{:S(2)}, u32[]{:S(2)}) collective-permute-start(bf16[8,16,512]{2,1,0:T(8,128)(2,1)S(1)} %get-tuple-element.46), channel_id=1, source_target_pairs={{0,8},{4,12},{8,0},{12,4},{16,24},{20,28},{24,16},{28,20},{1,9},{5... | collective-permute-start | bytes 393224 | tf_op jit(solution)/shard_map/ppermute | solution.py:228
  106.1 5.2 %collective-permute-start.23 = (bf16[4,16,512]{2,1,0:T(8,128)(2,1)S(1)}, bf16[4,16,512]{2,1,0:T(8,128)(2,1)S(1)}, u32[]{:S(2)}, u32[]{:S(2)}) collective-permute-start(bf16[4,16,512]{2,1,0:T(8,128)(2,1)S(1)} %get-tuple-element.60), channel_id=1, source_target_pairs={{0,16},{4,20},{8,24},{12,28},{16,0},{20,4},{24,8},{28,12},{1,17},{... | collective-permute-start | bytes 196616 | tf_op jit(solution)/shard_map/ppermute | solution.py:228
  108.0 5.2 %collective-permute-start.20 = (bf16[4,16,512]{2,1,0:T(8,128)(2,1)S(1)}, bf16[4,16,512]{2,1,0:T(8,128)(2,1)S(1)}, u32[]{:S(2)}, u32[]{:S(2)}) collective-permute-start(bf16[4,16,512]{2,1,0:T(8,128)(2,1)S(1)} %get-tuple-element.62), channel_id=1, source_target_pairs={{0,16},{4,20},{8,24},{12,28},{16,0},{20,4},{24,8},{28,12},{1,17},{... | collective-permute-start | bytes 196616 | tf_op jit(solution)/shard_map/ppermute | solution.py:228
  114.0 3.3 %collective-permute-start.26 = (f32[4,1024]{1,0:T(4,128)S(1)}, f32[4,1024]{1,0:T(4,128)S(1)}, u32[]{:S(2)}, u32[]{:S(2)}) collective-permute-start(f32[4,1024]{1,0:T(4,128)S(1)} %get-tuple-element.43), channel_id=1, source_target_pairs={{0,3},{1,2},{2,1},{3,0},{4,7},{5,6},{6,5},{7,4},{8,11},{9,10},{10,... | collective-permute-start | bytes 49160 | tf_op jit(solution)/shard_map/ppermute | solution.py:407
  114.0 3.8 %collective-permute-start.25 = (f32[4,1024]{1,0:T(4,128)S(1)}, f32[4,1024]{1,0:T(4,128)S(1)}, u32[]{:S(2)}, u32[]{:S(2)}) collective-permute-start(f32[4,1024]{1,0:T(4,128)S(1)} %get-tuple-element.43), channel_id=1, source_target_pairs={{0,2},{1,3},{2,0},{3,1},{4,6},{5,7},{6,4},{7,5},{8,10},{9,11},{10,... | collective-permute-start | bytes 49160 | tf_op jit(solution)/shard_map/ppermute | solution.py:407
  115.4 2.3 %collective-permute-start.24 = (f32[4,1024]{1,0:T(4,128)S(1)}, f32[4,1024]{1,0:T(4,128)S(1)}, u32[]{:S(2)}, u32[]{:S(2)}) collective-permute-start(f32[4,1024]{1,0:T(4,128)S(1)} %get-tuple-element.43), channel_id=1, source_target_pairs={{0,1},{1,0},{2,3},{3,2},{4,5},{5,4},{6,7},{7,6},{8,9},{9,8},{10,11... | collective-permute-start | bytes 49160 | tf_op jit(solution)/shard_map/ppermute | solution.py:407

commit v6 on v5

--- a/solution.py
+++ b/solution.py
@@ -119,23 +119,28 @@
             sem.at[group],
         ).start()
 
-    for tile in range(tiles):
-        row, k = divmod(tile, tiles_row)
+    def sort_tile(tile, carry):
+        row, k = lax.div(tile, tiles_row), lax.rem(tile, tiles_row)
         slot = owner[cols[k, here * rows_dev + row]]
-        rel = jnp.bitwise_xor(lax.div(slot, rows_dev), here)
+        rel = turned(jnp.bitwise_xor(lax.div(slot, rows_dev), here), peers, lax.axis_index("src"))
         at = rel * group_tiles + count[rel]
         load(u_hbm, u_ref, u_sem, tile, at, rel)
         count[rel] = count[rel] + 1
         tile_at[at] = tile
         code_at[at] = row * rows_dev + lax.rem(slot, rows_dev)
         rank_at[at] = ranks[row, k]
+        return carry
+
+    def load_v(at, carry):
+        load(v_hbm, v_ref, v_sem, tile_at[at], at, lax.div(at, group_tiles))
+        return carry
 
     def loaded(ref, sem, group):
         piece = ref.at[pl.ds(group * deep, deep)]
         pltpu.make_async_copy(piece, piece, sem.at[group]).wait()
 
-    for at in range(tiles):
-        load(v_hbm, v_ref, v_sem, tile_at[at], at, at // group_tiles)
+    lax.fori_loop(0, tiles, sort_tile, 0)
+    lax.fori_loop(0, tiles, load_v, 0)
     lane = lax.broadcasted_iota(jnp.int32, (1, deep), 1)
     for group in range(peers):
         code = jnp.full((1, deep), -1, jnp.int32)
@@ -224,8 +229,22 @@
             total_ref[pl.ds(row, 1), here] = jnp.sum(product, axis=0, keepdims=True)
 
 
+def turned(rel, peers, src):
+    if peers < 4:
+        return rel
+    swapped = (rel >> 2 << 2) | ((rel & 1) << 1) | ((rel >> 1) & 1)
+    odd = src % 2
+    return swapped * odd + rel * (1 - odd)
+
+
 def swap(x, bit, peers):
-    return lax.ppermute(x, "rows", [(i, i ^ (1 << bit)) for i in range(peers)])
+    count = lax.axis_size("src")
+    pairs = [
+        (row * count + src, (row ^ turned(1 << bit, peers, src)) * count + src)
+        for row in range(peers)
+        for src in range(count)
+    ]
+    return lax.ppermute(x, ("rows", "src"), pairs)
 
 
 def slot_sums(

time: 119 us -> 116 us (0.975)
  waiting for transfers between devices: 35.3 us -> 46.5 us
  starting transfers between devices: 41 us -> 30.9 us
  Pallas kernels: 39.7 us -> 36.2 us
    ppermute x24, waiting for transfers between devices: 33.4 us -> 44.6 us  [swap(): return lax.ppermute(x, ('rows', 'src'), pairs)]
    ppermute x24, starting transfers between devices: 39.1 us -> 29 us  [swap(): return lax.ppermute(x, ('rows', 'src'), pairs)]
    pallas_call x1, Pallas kernels: 18.3 us -> 14.8 us  [slot_sums(): pl.pallas_call(functools.partial(start_kernel, (rows_dev, tiles_row, rank...]
  transfers between devices with their start and end apart: 27 -> 27, of which waited for: 19 -> 21; matrix products, arithmetic and copies ran while one was open for 1% -> 1% of each run, Pallas kernels for 9% -> 10%
where the time goes in v6:
time: 116 us
  waiting for transfers between devices  46.5 us (40%)
  Pallas kernels  36.2 us (31%)
  starting transfers between devices  30.9 us (27%)
  other arithmetic  1.52 us (1%)
    ppermute x24, waiting for transfers between devices, swap(): return lax.ppermute(x, ('rows', 'src'), pairs)  44.6 us
    ppermute x24, starting transfers between devices, swap(): return lax.ppermute(x, ('rows', 'src'), pairs)  29 us
    pallas_call x1, Pallas kernels, slot_sums(): pl.pallas_call(functools.partial(start_kernel, (rows_dev, tiles_row, rank...  14.8 us
    pallas_call x3, Pallas kernels, slot_sums(): pl.pallas_call(functools.partial(ready_kernel, dims, parts[late], [parts[...  8.85 us
    pallas_call x3, Pallas kernels, slot_sums(): pl.pallas_call(functools.partial(early_kernel, dims, [parts[i] for i in e...  6.24 us
    pallas_call x6, Pallas kernels, slot_sums(): pl.pallas_call(functools.partial(more_kernel, dims, names), out_shape=sha...  5.55 us
  transfers between devices with their start and end apart: 27, of which 21 were waited for; matrix products, arithmetic and copies ran while one was open for 1% of the time, Pallas kernels for 10%

profile of v6, /device:TPU:0, one launch (start us, length us, event | category | flops | bytes accessed | tf_op | source)
XLA Modules:
  0.0 116.0 jit_solution(6441670241186862396)
XLA Ops:
  0.7 14.8 %start.1 = (bf16[6144,1024]{1,0:T(8,128)(2,1)S(1)}, bf16[6144,1024]{1,0:T(8,128)(2,1)S(1)}, s32[8,768]{1,0:T(8,128)S(1)}, f32[16,16,512]{2,1,0:T(8,128)S(1)}, bf...) custom-call(s32[16,32]{1,0:T(8,128)} %bitcast.11, s32[32]{0:T(128)} %refs_1_.1, ...), custom_call_target="tpu_custom_call" | custom-call | flops 402653184 | bytes 25165824 | tf_op jit(solution)/shard_map/start/pallas_call | solution.py:267
  15.5 3.0 %collective-permute-start = (bf16[16,16,512]{2,1,0:T(8,128)(2,1)S(1)}, bf16[16,16,512]{2,1,0:T(8,128)(2,1)S(1)}, u32[]{:S(2)}, u32[]{:S(2)}) collective-permute-start(bf16[16,16,512]{2,1,0:T(8,128)(2,1)S(1)} %get-tuple-element.25), channel_id=1, source_target_pairs={{0,4},{1,9},{2,6},{3,11},{4,0},{5,13},{6,2},{7,15},{8,12},{9,1},{1... | collective-permute-start | bytes 786440 | tf_op jit(solution)/shard_map/ppermute | solution.py:247
  18.4 1.4 %collective-permute-start.3 = (bf16[16,16,512]{2,1,0:T(8,128)(2,1)S(1)}, bf16[16,16,512]{2,1,0:T(8,128)(2,1)S(1)}, u32[]{:S(2)}, u32[]{:S(2)}) collective-permute-start(bf16[16,16,512]{2,1,0:T(8,128)(2,1)S(1)} %get-tuple-element.28), channel_id=1, source_target_pairs={{0,8},{1,5},{2,10},{3,7},{4,12},{5,1},{6,14},{7,3},{8,0},{9,13},{1... | collective-permute-start | bytes 786440 | tf_op jit(solution)/shard_map/ppermute | solution.py:247
  19.8 5.3 %collective-permute-done = bf16[16,16,512]{2,1,0:T(8,128)(2,1)S(1)} collective-permute-done((bf16[16,16,512]{2,1,0:T(8,128)(2,1)S(1)}, bf16[16,16,512]{2,1,0:T(8,128)(2,1)S(1)}, u32[]{:S(2)}, u32[]{:S(2)}) %collective-permute-start) | collective-permute-done | bytes 262176 | tf_op jit(solution)/shard_map/ppermute | solution.py:247
  25.1 1.8 %collective-permute-start.1 = (bf16[8,16,512]{2,1,0:T(8,128)(2,1)S(1)}, bf16[8,16,512]{2,1,0:T(8,128)(2,1)S(1)}, u32[]{:S(2)}, u32[]{:S(2)}) collective-permute-start(bf16[8,16,512]{2,1,0:T(8,128)(2,1)S(1)} %get-tuple-element.58), channel_id=1, source_target_pairs={{0,8},{1,5},{2,10},{3,7},{4,12},{5,1},{6,14},{7,3},{8,0},{9,13},{1... | collective-permute-start | bytes 393224 | tf_op jit(solution)/shard_map/ppermute | solution.py:247
  26.9 0.1 add_convert_fusion.6
  27.0 1.5 %collective-permute-start.4 = (bf16[8,16,512]{2,1,0:T(8,128)(2,1)S(1)}, bf16[8,16,512]{2,1,0:T(8,128)(2,1)S(1)}, u32[]{:S(2)}, u32[]{:S(2)}) collective-permute-start(bf16[8,16,512]{2,1,0:T(8,128)(2,1)S(1)} %get-tuple-element.56), channel_id=1, source_target_pairs={{0,4},{1,9},{2,6},{3,11},{4,0},{5,13},{6,2},{7,15},{8,12},{9,1},{1... | collective-permute-start | bytes 393224 | tf_op jit(solution)/shard_map/ppermute | solution.py:247
  28.5 2.5 %collective-permute-done.1 = bf16[8,16,512]{2,1,0:T(8,128)(2,1)S(1)} collective-permute-done((bf16[8,16,512]{2,1,0:T(8,128)(2,1)S(1)}, bf16[8,16,512]{2,1,0:T(8,128)(2,1)S(1)}, u32[]{:S(2)}, u32[]{:S(2)}) %collective-permute-start.1) | collective-permute-done | bytes 131104 | tf_op jit(solution)/shard_map/ppermute | solution.py:247
  31.0 3.5 %collective-permute-start.2 = (bf16[4,16,512]{2,1,0:T(8,128)(2,1)S(1)}, bf16[4,16,512]{2,1,0:T(8,128)(2,1)S(1)}, u32[]{:S(2)}, u32[]{:S(2)}) collective-permute-start(bf16[4,16,512]{2,1,0:T(8,128)(2,1)S(1)} %get-tuple-element.74), channel_id=1, source_target_pairs={{0,16},{1,17},{2,18},{3,19},{4,20},{5,21},{6,22},{7,23},{8,24},{9,... | collective-permute-start | bytes 196616 | tf_op jit(solution)/shard_map/ppermute | solution.py:247
  34.6 0.2 collective-permute-start.5
  34.7 2.6 %collective-permute-done.2.refs_1_ = bf16[4,16,512]{2,1,0:T(8,128)(2,1)S(1)} collective-permute-done((bf16[4,16,512]{2,1,0:T(8,128)(2,1)S(1)}, bf16[4,16,512]{2,1,0:T(8,128)(2,1)S(1)}, u32[]{:S(2)}, u32[]{:S(2)}) %collective-permute-start.2) | collective-permute-done | bytes 65568 | tf_op jit(solution)/shard_map/ppermute | solution.py:247
  37.3 2.0 %early.3.sum_ref = f32[8,16,768]{2,1,0:T(8,128)S(1)} custom-call(s32[8,768]{1,0:T(8,128)S(1)} %get-tuple-element.23.code_ref, f32[4,1024]{1,0:T(4,128)S(1)} %copy-done, f32[4,16,512]{2,1,0:T(8,128)S(1)} %get-tuple-element.75.refs_0_, bf16[4,16,512]{2,1,0:T(8,128)(2,1)S(1)} %collective-permute-done.2.refs_1_, ...), custom_call_target="tpu_custom_call" | custom-call | flops 100663296 | bytes 6291456 | tf_op jit(solution)/shard_map/early/pallas_call | solution.py:299
  39.3 0.7 collective-permute-done.5.came_ref
  40.0 2.9 %ready.3 = (bf16[8,64,768]{2,1,0:T(8,128)(2,1)S(1)}, bf16[16,16,512]{2,1,0:T(8,128)(2,1)S(1)}) custom-call(s32[8,768]{1,0:T(8,128)S(1)} %get-tuple-element.23.code_ref, f32[4,1024]{1,0:T(4,128)S(1)} %copy-done, f32[8,16,768]{2,1,0:T(8,128)S(1)} %early.3.sum_ref, f32[4,16,512]{2,1,0:T(8,128)S(1)} %get-tuple-element.73.base_ref, ...), custom_call_target="tpu_custom_call" | custom-call | flops 100663296 | bytes 6291456 | tf_op jit(solution)/shard_map/ready/pallas_call | solution.py:308
  43.0 2.2 %collective-permute-start.6 = (bf16[16,16,512]{2,1,0:T(8,128)(2,1)S(1)}, bf16[16,16,512]{2,1,0:T(8,128)(2,1)S(1)}, u32[]{:S(2)}, u32[]{:S(2)}) collective-permute-start(bf16[16,16,512]{2,1,0:T(8,128)(2,1)S(1)} %get-tuple-element.32), channel_id=1, source_target_pairs={{0,4},{1,9},{2,6},{3,11},{4,0},{5,13},{6,2},{7,15},{8,12},{9,1},{1... | collective-permute-start | bytes 786440 | tf_op jit(solution)/shard_map/ppermute | solution.py:247
  45.2 0.7 more.7
  45.9 1.2 %more.6 = (f32[16,16,512]{2,1,0:T(8,128)S(1)}, f32[16,16,512]{2,1,0:T(8,128)S(1)}) custom-call(bf16[8,64,768]{2,1,0:T(8,128)(2,1)S(1)} %get-tuple-element.30.lhs_ref, bf16[6144,1024]{1,0:T(8,128)(2,1)S(1)} %get-tuple-element.29.refs_1_.v_ref), custom_call_target="tpu_custom_call" | custom-call | flops 100663296 | bytes 6291456 | tf_op jit(solution)/shard_map/more/pallas_call | solution.py:323
  47.1 3.4 %collective-permute-done.6 = bf16[16,16,512]{2,1,0:T(8,128)(2,1)S(1)} collective-permute-done((bf16[16,16,512]{2,1,0:T(8,128)(2,1)S(1)}, bf16[16,16,512]{2,1,0:T(8,128)(2,1)S(1)}, u32[]{:S(2)}, u32[]{:S(2)}) %collective-permute-start.6) | collective-permute-done | bytes 262176 | tf_op jit(solution)/shard_map/ppermute | solution.py:247
  50.5 0.3 collective-permute-start.7
  50.8 1.4 %collective-permute-done.9 = bf16[16,16,512]{2,1,0:T(8,128)(2,1)S(1)} collective-permute-done((bf16[16,16,512]{2,1,0:T(8,128)(2,1)S(1)}, bf16[16,16,512]{2,1,0:T(8,128)(2,1)S(1)}, u32[]{:S(2)}, u32[]{:S(2)}) %collective-permute-start.9) | collective-permute-done | bytes 262176 | tf_op jit(solution)/shard_map/ppermute | solution.py:247
  52.3 1.5 %collective-permute-start.10 = (bf16[8,16,512]{2,1,0:T(8,128)(2,1)S(1)}, bf16[8,16,512]{2,1,0:T(8,128)(2,1)S(1)}, u32[]{:S(2)}, u32[]{:S(2)}) collective-permute-start(bf16[8,16,512]{2,1,0:T(8,128)(2,1)S(1)} %get-tuple-element.52), channel_id=1, source_target_pairs={{0,4},{1,9},{2,6},{3,11},{4,0},{5,13},{6,2},{7,15},{8,12},{9,1},{1... | collective-permute-start | bytes 393224 | tf_op jit(solution)/shard_map/ppermute | solution.py:247
  53.8 2.5 %collective-permute-done.7 = bf16[8,16,512]{2,1,0:T(8,128)(2,1)S(1)} collective-permute-done((bf16[8,16,512]{2,1,0:T(8,128)(2,1)S(1)}, bf16[8,16,512]{2,1,0:T(8,128)(2,1)S(1)}, u32[]{:S(2)}, u32[]{:S(2)}) %collective-permute-start.7) | collective-permute-done | bytes 131104 | tf_op jit(solution)/shard_map/ppermute | solution.py:247
  56.3 1.6 %collective-permute-start.8 = (bf16[4,16,512]{2,1,0:T(8,128)(2,1)S(1)}, bf16[4,16,512]{2,1,0:T(8,128)(2,1)S(1)}, u32[]{:S(2)}, u32[]{:S(2)}) collective-permute-start(bf16[4,16,512]{2,1,0:T(8,128)(2,1)S(1)} %get-tuple-element.70), channel_id=1, source_target_pairs={{0,16},{1,17},{2,18},{3,19},{4,20},{5,21},{6,22},{7,23},{8,24},{9,... | collective-permute-start | bytes 196616 | tf_op jit(solution)/shard_map/ppermute | solution.py:247
  57.9 1.8 %collective-permute-start.11 = (bf16[4,16,512]{2,1,0:T(8,128)(2,1)S(1)}, bf16[4,16,512]{2,1,0:T(8,128)(2,1)S(1)}, u32[]{:S(2)}, u32[]{:S(2)}) collective-permute-start(bf16[4,16,512]{2,1,0:T(8,128)(2,1)S(1)} %get-tuple-element.68), channel_id=1, source_target_pairs={{0,16},{1,17},{2,18},{3,19},{4,20},{5,21},{6,22},{7,23},{8,24},{9,... | collective-permute-start | bytes 196616 | tf_op jit(solution)/shard_map/ppermute | solution.py:247
  59.7 2.5 %collective-permute-done.8.refs_1_ = bf16[4,16,512]{2,1,0:T(8,128)(2,1)S(1)} collective-permute-done((bf16[4,16,512]{2,1,0:T(8,128)(2,1)S(1)}, bf16[4,16,512]{2,1,0:T(8,128)(2,1)S(1)}, u32[]{:S(2)}, u32[]{:S(2)}) %collective-permute-start.8) | collective-permute-done | bytes 65568 | tf_op jit(solution)/shard_map/ppermute | solution.py:247
  62.2 2.2 %early.4.sum_ref = f32[8,16,768]{2,1,0:T(8,128)S(1)} custom-call(s32[8,768]{1,0:T(8,128)S(1)} %get-tuple-element.23.code_ref, f32[4,1024]{1,0:T(4,128)S(1)} %copy-done, f32[4,16,512]{2,1,0:T(8,128)S(1)} %get-tuple-element.71.refs_0_, bf16[4,16,512]{2,1,0:T(8,128)(2,1)S(1)} %collective-permute-done.8.refs_1_, ...), custom_call_target="tpu_custom_call" | custom-call | flops 100663296 | bytes 6291456 | tf_op jit(solution)/shard_map/early/pallas_call | solution.py:299
  64.4 3.0 %ready.4 = (bf16[8,64,768]{2,1,0:T(8,128)(2,1)S(1)}, bf16[16,16,512]{2,1,0:T(8,128)(2,1)S(1)}) custom-call(s32[8,768]{1,0:T(8,128)S(1)} %get-tuple-element.23.code_ref, f32[4,1024]{1,0:T(4,128)S(1)} %copy-done, f32[8,16,768]{2,1,0:T(8,128)S(1)} %early.4.sum_ref, f32[4,16,512]{2,1,0:T(8,128)S(1)} %get-tuple-element.69.base_ref, ...), custom_call_target="tpu_custom_call" | custom-call | flops 100663296 | bytes 6291456 | tf_op jit(solution)/shard_map/ready/pallas_call | solution.py:308
  67.4 1.2 %collective-permute-start.12 = (bf16[16,16,512]{2,1,0:T(8,128)(2,1)S(1)}, bf16[16,16,512]{2,1,0:T(8,128)(2,1)S(1)}, u32[]{:S(2)}, u32[]{:S(2)}) collective-permute-start(bf16[16,16,512]{2,1,0:T(8,128)(2,1)S(1)} %get-tuple-element.36), channel_id=1, source_target_pairs={{0,4},{1,9},{2,6},{3,11},{4,0},{5,13},{6,2},{7,15},{8,12},{9,1},{1... | collective-permute-start | bytes 786440 | tf_op jit(solution)/shard_map/ppermute | solution.py:247
  68.6 0.7 more.9
  69.3 0.7 collective-permute-start.15
  70.0 1.2 %more.8 = (f32[16,16,512]{2,1,0:T(8,128)S(1)}, f32[16,16,512]{2,1,0:T(8,128)S(1)}) custom-call(bf16[8,64,768]{2,1,0:T(8,128)(2,1)S(1)} %get-tuple-element.34.lhs_ref, bf16[6144,1024]{1,0:T(8,128)(2,1)S(1)} %get-tuple-element.29.refs_1_.v_ref), custom_call_target="tpu_custom_call" | custom-call | flops 100663296 | bytes 6291456 | tf_op jit(solution)/shard_map/more/pallas_call | solution.py:323
  71.2 2.7 %collective-permute-done.12 = bf16[16,16,512]{2,1,0:T(8,128)(2,1)S(1)} collective-permute-done((bf16[16,16,512]{2,1,0:T(8,128)(2,1)S(1)}, bf16[16,16,512]{2,1,0:T(8,128)(2,1)S(1)}, u32[]{:S(2)}, u32[]{:S(2)}) %collective-permute-start.12) | collective-permute-done | bytes 262176 | tf_op jit(solution)/shard_map/ppermute | solution.py:247
  73.9 0.5 collective-permute-start.13
  74.4 2.7 %collective-permute-done.15 = bf16[16,16,512]{2,1,0:T(8,128)(2,1)S(1)} collective-permute-done((bf16[16,16,512]{2,1,0:T(8,128)(2,1)S(1)}, bf16[16,16,512]{2,1,0:T(8,128)(2,1)S(1)}, u32[]{:S(2)}, u32[]{:S(2)}) %collective-permute-start.15) | collective-permute-done | bytes 262176 | tf_op jit(solution)/shard_map/ppermute | solution.py:247
  77.2 0.9 collective-permute-start.16
  78.1 0.8 collective-permute-done.13
  79.0 1.1 collective-permute-start.14
  80.1 2.1 %collective-permute-done.16 = bf16[8,16,512]{2,1,0:T(8,128)(2,1)S(1)} collective-permute-done((bf16[8,16,512]{2,1,0:T(8,128)(2,1)S(1)}, bf16[8,16,512]{2,1,0:T(8,128)(2,1)S(1)}, u32[]{:S(2)}, u32[]{:S(2)}) %collective-permute-start.16) | collective-permute-done | bytes 131104 | tf_op jit(solution)/shard_map/ppermute | solution.py:247
  82.3 0.8 collective-permute-start.17
  83.1 1.8 %collective-permute-done.14.refs_1_ = bf16[4,16,512]{2,1,0:T(8,128)(2,1)S(1)} collective-permute-done((bf16[4,16,512]{2,1,0:T(8,128)(2,1)S(1)}, bf16[4,16,512]{2,1,0:T(8,128)(2,1)S(1)}, u32[]{:S(2)}, u32[]{:S(2)}) %collective-permute-start.14) | collective-permute-done | bytes 65568 | tf_op jit(solution)/shard_map/ppermute | solution.py:247
  84.9 2.0 %early.5.sum_ref = f32[8,16,768]{2,1,0:T(8,128)S(1)} custom-call(s32[8,768]{1,0:T(8,128)S(1)} %get-tuple-element.23.code_ref, f32[4,1024]{1,0:T(4,128)S(1)} %copy-done, f32[4,16,512]{2,1,0:T(8,128)S(1)} %get-tuple-element.67.refs_0_, bf16[4,16,512]{2,1,0:T(8,128)(2,1)S(1)} %collective-permute-done.14.refs_1_, ...), custom_call_target="tpu_custom_call" | custom-call | flops 100663296 | bytes 6291456 | tf_op jit(solution)/shard_map/early/pallas_call | solution.py:299
  86.9 1.4 %collective-permute-done.17.came_ref = bf16[4,16,512]{2,1,0:T(8,128)(2,1)S(1)} collective-permute-done((bf16[4,16,512]{2,1,0:T(8,128)(2,1)S(1)}, bf16[4,16,512]{2,1,0:T(8,128)(2,1)S(1)}, u32[]{:S(2)}, u32[]{:S(2)}) %collective-permute-start.17) | collective-permute-done | bytes 65568 | tf_op jit(solution)/shard_map/ppermute | solution.py:247
  88.2 2.9 %ready.5 = (bf16[8,64,768]{2,1,0:T(8,128)(2,1)S(1)}, bf16[16,16,512]{2,1,0:T(8,128)(2,1)S(1)}) custom-call(s32[8,768]{1,0:T(8,128)S(1)} %get-tuple-element.23.code_ref, f32[4,1024]{1,0:T(4,128)S(1)} %copy-done, f32[8,16,768]{2,1,0:T(8,128)S(1)} %early.5.sum_ref, f32[4,16,512]{2,1,0:T(8,128)S(1)} %get-tuple-element.65.base_ref, ...), custom_call_target="tpu_custom_call" | custom-call | flops 100663296 | bytes 6291456 | tf_op jit(solution)/shard_map/ready/pallas_call | solution.py:308
  91.2 0.7 more.11
  91.9 0.1 collective-permute-start.21
  92.0 1.3 %collective-permute-start.18 = (bf16[16,16,512]{2,1,0:T(8,128)(2,1)S(1)}, bf16[16,16,512]{2,1,0:T(8,128)(2,1)S(1)}, u32[]{:S(2)}, u32[]{:S(2)}) collective-permute-start(bf16[16,16,512]{2,1,0:T(8,128)(2,1)S(1)} %get-tuple-element.40), channel_id=1, source_target_pairs={{0,4},{1,9},{2,6},{3,11},{4,0},{5,13},{6,2},{7,15},{8,12},{9,1},{1... | collective-permute-start | bytes 786440 | tf_op jit(solution)/shard_map/ppermute | solution.py:247
  93.3 1.2 %more.10 = (f32[16,16,512]{2,1,0:T(8,128)S(1)}, f32[16,16,512]{2,1,0:T(8,128)S(1)}) custom-call(bf16[8,64,768]{2,1,0:T(8,128)(2,1)S(1)} %get-tuple-element.38.lhs_ref, bf16[6144,1024]{1,0:T(8,128)(2,1)S(1)} %get-tuple-element.29.refs_1_.v_ref), custom_call_target="tpu_custom_call" | custom-call | flops 100663296 | bytes 6291456 | tf_op jit(solution)/shard_map/more/pallas_call | solution.py:323
  94.5 4.5 %collective-permute-done.21 = bf16[16,16,512]{2,1,0:T(8,128)(2,1)S(1)} collective-permute-done((bf16[16,16,512]{2,1,0:T(8,128)(2,1)S(1)}, bf16[16,16,512]{2,1,0:T(8,128)(2,1)S(1)}, u32[]{:S(2)}, u32[]{:S(2)}) %collective-permute-start.21) | collective-permute-done | bytes 262176 | tf_op jit(solution)/shard_map/ppermute | solution.py:247
  99.0 0.1 add_convert_fusion
  99.1 0.7 collective-permute-start.22
  99.7 0.1 add_convert_fusion.1
  99.8 0.7 collective-permute-start.19
  100.5 3.6 %collective-permute-done.22 = bf16[8,16,512]{2,1,0:T(8,128)(2,1)S(1)} collective-permute-done((bf16[8,16,512]{2,1,0:T(8,128)(2,1)S(1)}, bf16[8,16,512]{2,1,0:T(8,128)(2,1)S(1)}, u32[]{:S(2)}, u32[]{:S(2)}) %collective-permute-start.22) | collective-permute-done | bytes 131104 | tf_op jit(solution)/shard_map/ppermute | solution.py:247
  104.1 0.1 collective-permute-start.23
  104.2 0.6 collective-permute-done.19
  104.9 2.3 %collective-permute-start.20 = (bf16[4,16,512]{2,1,0:T(8,128)(2,1)S(1)}, bf16[4,16,512]{2,1,0:T(8,128)(2,1)S(1)}, u32[]{:S(2)}, u32[]{:S(2)}) collective-permute-start(bf16[4,16,512]{2,1,0:T(8,128)(2,1)S(1)} %get-tuple-element.62), channel_id=1, source_target_pairs={{0,16},{1,17},{2,18},{3,19},{4,20},{5,21},{6,22},{7,23},{8,24},{9,... | collective-permute-start | bytes 196616 | tf_op jit(solution)/shard_map/ppermute | solution.py:247
  107.2 2.1 %collective-permute-done.23.refs_3_ = bf16[4,16,512]{2,1,0:T(8,128)(2,1)S(1)} collective-permute-done((bf16[4,16,512]{2,1,0:T(8,128)(2,1)S(1)}, bf16[4,16,512]{2,1,0:T(8,128)(2,1)S(1)}, u32[]{:S(2)}, u32[]{:S(2)}) %collective-permute-start.23) | collective-permute-done | bytes 65568 | tf_op jit(solution)/shard_map/ppermute | solution.py:247
  109.4 1.5 %collective-permute-done.20.refs_1_ = bf16[4,16,512]{2,1,0:T(8,128)(2,1)S(1)} collective-permute-done((bf16[4,16,512]{2,1,0:T(8,128)(2,1)S(1)}, bf16[4,16,512]{2,1,0:T(8,128)(2,1)S(1)}, u32[]{:S(2)}, u32[]{:S(2)}) %collective-permute-start.20) | collective-permute-done | bytes 65568 | tf_op jit(solution)/shard_map/ppermute | solution.py:247
  110.8 0.8 finish.1
  111.6 1.5 %collective-permute-start.25 = (f32[4,1024]{1,0:T(4,128)S(1)}, f32[4,1024]{1,0:T(4,128)S(1)}, u32[]{:S(2)}, u32[]{:S(2)}) collective-permute-start(f32[4,1024]{1,0:T(4,128)S(1)} %get-tuple-element.43), channel_id=1, source_target_pairs={{0,2},{1,3},{2,0},{3,1},{4,6},{5,7},{6,4},{7,5},{8,10},{9,11},{10,... | collective-permute-start | bytes 49160 | tf_op jit(solution)/shard_map/ppermute | solution.py:426
  113.1 0.3 collective-permute-start.24
  113.5 1.4 %collective-permute-done.26 = f32[4,1024]{1,0:T(4,128)S(1)} collective-permute-done((f32[4,1024]{1,0:T(4,128)S(1)}, f32[4,1024]{1,0:T(4,128)S(1)}, u32[]{:S(2)}, u32[]{:S(2)}) %collective-permute-start.26) | collective-permute-done | bytes 16416 | tf_op jit(solution)/shard_map/ppermute | solution.py:426
  114.9 0.5 collective-permute-done.25
  115.4 0.6 add_multiply_fusion
  (28 shorter events, 0.8 us)
Async XLA Ops:
  0.6 19.1 %copy-start = (f32[4,1024]{1,0:T(4,128)S(1)}, f32[4,1024]{1,0:T(4,128)}, u32[]{:S(2)}) copy-start(f32[4,1024]{1,0:T(4,128)} %contrast_ref.13) | copy-start | bytes 49156
  0.6 30.3 %copy-start.2 = (f32[4,16,1024]{2,1,0:T(8,128)S(1)}, f32[4,16,1024]{2,1,0:T(8,128)}, u32[]{:S(2)}) copy-start(f32[4,16,1024]{2,1,0:T(8,128)} %refs_3_.1) | copy-start | bytes 786436
  15.5 9.6 %collective-permute-start = (bf16[16,16,512]{2,1,0:T(8,128)(2,1)S(1)}, bf16[16,16,512]{2,1,0:T(8,128)(2,1)S(1)}, u32[]{:S(2)}, u32[]{:S(2)}) collective-permute-start(bf16[16,16,512]{2,1,0:T(8,128)(2,1)S(1)} %get-tuple-element.25), channel_id=1, source_target_pairs={{0,4},{1,9},{2,6},{3,11},{4,0},{5,13},{6,2},{7,15},{8,12},{9,1},{1... | collective-permute-start | bytes 786440 | tf_op jit(solution)/shard_map/ppermute | solution.py:247
  18.4 8.5 %collective-permute-start.3 = (bf16[16,16,512]{2,1,0:T(8,128)(2,1)S(1)}, bf16[16,16,512]{2,1,0:T(8,128)(2,1)S(1)}, u32[]{:S(2)}, u32[]{:S(2)}) collective-permute-start(bf16[16,16,512]{2,1,0:T(8,128)(2,1)S(1)} %get-tuple-element.28), channel_id=1, source_target_pairs={{0,8},{1,5},{2,10},{3,7},{4,12},{5,1},{6,14},{7,3},{8,0},{9,13},{1... | collective-permute-start | bytes 786440 | tf_op jit(solution)/shard_map/ppermute | solution.py:247
  25.1 5.8 %collective-permute-start.1 = (bf16[8,16,512]{2,1,0:T(8,128)(2,1)S(1)}, bf16[8,16,512]{2,1,0:T(8,128)(2,1)S(1)}, u32[]{:S(2)}, u32[]{:S(2)}) collective-permute-start(bf16[8,16,512]{2,1,0:T(8,128)(2,1)S(1)} %get-tuple-element.58), channel_id=1, source_target_pairs={{0,8},{1,5},{2,10},{3,7},{4,12},{5,1},{6,14},{7,3},{8,0},{9,13},{1... | collective-permute-start | bytes 393224 | tf_op jit(solution)/shard_map/ppermute | solution.py:247
  27.0 7.5 %collective-permute-start.4 = (bf16[8,16,512]{2,1,0:T(8,128)(2,1)S(1)}, bf16[8,16,512]{2,1,0:T(8,128)(2,1)S(1)}, u32[]{:S(2)}, u32[]{:S(2)}) collective-permute-start(bf16[8,16,512]{2,1,0:T(8,128)(2,1)S(1)} %get-tuple-element.56), channel_id=1, source_target_pairs={{0,4},{1,9},{2,6},{3,11},{4,0},{5,13},{6,2},{7,15},{8,12},{9,1},{1... | collective-permute-start | bytes 393224 | tf_op jit(solution)/shard_map/ppermute | solution.py:247
  31.0 6.3 %collective-permute-start.2 = (bf16[4,16,512]{2,1,0:T(8,128)(2,1)S(1)}, bf16[4,16,512]{2,1,0:T(8,128)(2,1)S(1)}, u32[]{:S(2)}, u32[]{:S(2)}) collective-permute-start(bf16[4,16,512]{2,1,0:T(8,128)(2,1)S(1)} %get-tuple-element.74), channel_id=1, source_target_pairs={{0,16},{1,17},{2,18},{3,19},{4,20},{5,21},{6,22},{7,23},{8,24},{9,... | collective-permute-start | bytes 196616 | tf_op jit(solution)/shard_map/ppermute | solution.py:247
  34.6 5.4 %collective-permute-start.5 = (bf16[4,16,512]{2,1,0:T(8,128)(2,1)S(1)}, bf16[4,16,512]{2,1,0:T(8,128)(2,1)S(1)}, u32[]{:S(2)}, u32[]{:S(2)}) collective-permute-start(bf16[4,16,512]{2,1,0:T(8,128)(2,1)S(1)} %get-tuple-element.72), channel_id=1, source_target_pairs={{0,16},{1,17},{2,18},{3,19},{4,20},{5,21},{6,22},{7,23},{8,24},{9,... | collective-permute-start | bytes 196616 | tf_op jit(solution)/shard_map/ppermute | solution.py:247
  43.0 7.5 %collective-permute-start.6 = (bf16[16,16,512]{2,1,0:T(8,128)(2,1)S(1)}, bf16[16,16,512]{2,1,0:T(8,128)(2,1)S(1)}, u32[]{:S(2)}, u32[]{:S(2)}) collective-permute-start(bf16[16,16,512]{2,1,0:T(8,128)(2,1)S(1)} %get-tuple-element.32), channel_id=1, source_target_pairs={{0,4},{1,9},{2,6},{3,11},{4,0},{5,13},{6,2},{7,15},{8,12},{9,1},{1... | collective-permute-start | bytes 786440 | tf_op jit(solution)/shard_map/ppermute | solution.py:247
  45.8 6.4 %collective-permute-start.9 = (bf16[16,16,512]{2,1,0:T(8,128)(2,1)S(1)}, bf16[16,16,512]{2,1,0:T(8,128)(2,1)S(1)}, u32[]{:S(2)}, u32[]{:S(2)}) collective-permute-start(bf16[16,16,512]{2,1,0:T(8,128)(2,1)S(1)} %more.7), channel_id=1, source_target_pairs={{0,8},{1,5},{2,10},{3,7},{4,12},{5,1},{6,14},{7,3},{8,0},{9,13},{1... | collective-permute-start | bytes 786440 | tf_op jit(solution)/shard_map/ppermute | solution.py:247
  50.5 5.7 %collective-permute-start.7 = (bf16[8,16,512]{2,1,0:T(8,128)(2,1)S(1)}, bf16[8,16,512]{2,1,0:T(8,128)(2,1)S(1)}, u32[]{:S(2)}, u32[]{:S(2)}) collective-permute-start(bf16[8,16,512]{2,1,0:T(8,128)(2,1)S(1)} %get-tuple-element.54), channel_id=1, source_target_pairs={{0,8},{1,5},{2,10},{3,7},{4,12},{5,1},{6,14},{7,3},{8,0},{9,13},{1... | collective-permute-start | bytes 393224 | tf_op jit(solution)/shard_map/ppermute | solution.py:247
  52.3 5.6 %collective-permute-start.10 = (bf16[8,16,512]{2,1,0:T(8,128)(2,1)S(1)}, bf16[8,16,512]{2,1,0:T(8,128)(2,1)S(1)}, u32[]{:S(2)}, u32[]{:S(2)}) collective-permute-start(bf16[8,16,512]{2,1,0:T(8,128)(2,1)S(1)} %get-tuple-element.52), channel_id=1, source_target_pairs={{0,4},{1,9},{2,6},{3,11},{4,0},{5,13},{6,2},{7,15},{8,12},{9,1},{1... | collective-permute-start | bytes 393224 | tf_op jit(solution)/shard_map/ppermute | solution.py:247
  56.3 5.9 %collective-permute-start.8 = (bf16[4,16,512]{2,1,0:T(8,128)(2,1)S(1)}, bf16[4,16,512]{2,1,0:T(8,128)(2,1)S(1)}, u32[]{:S(2)}, u32[]{:S(2)}) collective-permute-start(bf16[4,16,512]{2,1,0:T(8,128)(2,1)S(1)} %get-tuple-element.70), channel_id=1, source_target_pairs={{0,16},{1,17},{2,18},{3,19},{4,20},{5,21},{6,22},{7,23},{8,24},{9,... | collective-permute-start | bytes 196616 | tf_op jit(solution)/shard_map/ppermute | solution.py:247
  57.9 6.5 %collective-permute-start.11 = (bf16[4,16,512]{2,1,0:T(8,128)(2,1)S(1)}, bf16[4,16,512]{2,1,0:T(8,128)(2,1)S(1)}, u32[]{:S(2)}, u32[]{:S(2)}) collective-permute-start(bf16[4,16,512]{2,1,0:T(8,128)(2,1)S(1)} %get-tuple-element.68), channel_id=1, source_target_pairs={{0,16},{1,17},{2,18},{3,19},{4,20},{5,21},{6,22},{7,23},{8,24},{9,... | collective-permute-start | bytes 196616 | tf_op jit(solution)/shard_map/ppermute | solution.py:247
  67.4 6.4 %collective-permute-start.12 = (bf16[16,16,512]{2,1,0:T(8,128)(2,1)S(1)}, bf16[16,16,512]{2,1,0:T(8,128)(2,1)S(1)}, u32[]{:S(2)}, u32[]{:S(2)}) collective-permute-start(bf16[16,16,512]{2,1,0:T(8,128)(2,1)S(1)} %get-tuple-element.36), channel_id=1, source_target_pairs={{0,4},{1,9},{2,6},{3,11},{4,0},{5,13},{6,2},{7,15},{8,12},{9,1},{1... | collective-permute-start | bytes 786440 | tf_op jit(solution)/shard_map/ppermute | solution.py:247
  69.3 7.8 %collective-permute-start.15 = (bf16[16,16,512]{2,1,0:T(8,128)(2,1)S(1)}, bf16[16,16,512]{2,1,0:T(8,128)(2,1)S(1)}, u32[]{:S(2)}, u32[]{:S(2)}) collective-permute-start(bf16[16,16,512]{2,1,0:T(8,128)(2,1)S(1)} %more.9), channel_id=1, source_target_pairs={{0,8},{1,5},{2,10},{3,7},{4,12},{5,1},{6,14},{7,3},{8,0},{9,13},{1... | collective-permute-start | bytes 786440 | tf_op jit(solution)/shard_map/ppermute | solution.py:247
  73.9 5.0 %collective-permute-start.13 = (bf16[8,16,512]{2,1,0:T(8,128)(2,1)S(1)}, bf16[8,16,512]{2,1,0:T(8,128)(2,1)S(1)}, u32[]{:S(2)}, u32[]{:S(2)}) collective-permute-start(bf16[8,16,512]{2,1,0:T(8,128)(2,1)S(1)} %get-tuple-element.50), channel_id=1, source_target_pairs={{0,8},{1,5},{2,10},{3,7},{4,12},{5,1},{6,14},{7,3},{8,0},{9,13},{1... | collective-permute-start | bytes 393224 | tf_op jit(solution)/shard_map/ppermute | solution.py:247
  77.2 5.0 %collective-permute-start.16 = (bf16[8,16,512]{2,1,0:T(8,128)(2,1)S(1)}, bf16[8,16,512]{2,1,0:T(8,128)(2,1)S(1)}, u32[]{:S(2)}, u32[]{:S(2)}) collective-permute-start(bf16[8,16,512]{2,1,0:T(8,128)(2,1)S(1)} %get-tuple-element.48), channel_id=1, source_target_pairs={{0,4},{1,9},{2,6},{3,11},{4,0},{5,13},{6,2},{7,15},{8,12},{9,1},{1... | collective-permute-start | bytes 393224 | tf_op jit(solution)/shard_map/ppermute | solution.py:247
  79.0 5.9 %collective-permute-start.14 = (bf16[4,16,512]{2,1,0:T(8,128)(2,1)S(1)}, bf16[4,16,512]{2,1,0:T(8,128)(2,1)S(1)}, u32[]{:S(2)}, u32[]{:S(2)}) collective-permute-start(bf16[4,16,512]{2,1,0:T(8,128)(2,1)S(1)} %get-tuple-element.66), channel_id=1, source_target_pairs={{0,16},{1,17},{2,18},{3,19},{4,20},{5,21},{6,22},{7,23},{8,24},{9,... | collective-permute-start | bytes 196616 | tf_op jit(solution)/shard_map/ppermute | solution.py:247
  82.3 6.0 %collective-permute-start.17 = (bf16[4,16,512]{2,1,0:T(8,128)(2,1)S(1)}, bf16[4,16,512]{2,1,0:T(8,128)(2,1)S(1)}, u32[]{:S(2)}, u32[]{:S(2)}) collective-permute-start(bf16[4,16,512]{2,1,0:T(8,128)(2,1)S(1)} %get-tuple-element.64), channel_id=1, source_target_pairs={{0,16},{1,17},{2,18},{3,19},{4,20},{5,21},{6,22},{7,23},{8,24},{9,... | collective-permute-start | bytes 196616 | tf_op jit(solution)/shard_map/ppermute | solution.py:247
  91.2 19.6 %copy-start.1 = (bf16[4,16,1024]{2,1,0:T(8,128)(2,1)S(1)}, bf16[4,16,1024]{2,1,0:T(8,128)(2,1)}, u32[]{:S(2)}) copy-start(bf16[4,16,1024]{2,1,0:T(8,128)(2,1)} %forward_ref.1) | copy-start | bytes 393220
  91.9 7.1 %collective-permute-start.21 = (bf16[16,16,512]{2,1,0:T(8,128)(2,1)S(1)}, bf16[16,16,512]{2,1,0:T(8,128)(2,1)S(1)}, u32[]{:S(2)}, u32[]{:S(2)}) collective-permute-start(bf16[16,16,512]{2,1,0:T(8,128)(2,1)S(1)} %more.11), channel_id=1, source_target_pairs={{0,8},{1,5},{2,10},{3,7},{4,12},{5,1},{6,14},{7,3},{8,0},{9,13},{1... | collective-permute-start | bytes 786440 | tf_op jit(solution)/shard_map/ppermute | solution.py:247
  92.0 7.7 %collective-permute-start.18 = (bf16[16,16,512]{2,1,0:T(8,128)(2,1)S(1)}, bf16[16,16,512]{2,1,0:T(8,128)(2,1)S(1)}, u32[]{:S(2)}, u32[]{:S(2)}) collective-permute-start(bf16[16,16,512]{2,1,0:T(8,128)(2,1)S(1)} %get-tuple-element.40), channel_id=1, source_target_pairs={{0,4},{1,9},{2,6},{3,11},{4,0},{5,13},{6,2},{7,15},{8,12},{9,1},{1... | collective-permute-start | bytes 786440 | tf_op jit(solution)/shard_map/ppermute | solution.py:247
  99.1 5.0 %collective-permute-start.22 = (bf16[8,16,512]{2,1,0:T(8,128)(2,1)S(1)}, bf16[8,16,512]{2,1,0:T(8,128)(2,1)S(1)}, u32[]{:S(2)}, u32[]{:S(2)}) collective-permute-start(bf16[8,16,512]{2,1,0:T(8,128)(2,1)S(1)} %get-tuple-element.44), channel_id=1, source_target_pairs={{0,4},{1,9},{2,6},{3,11},{4,0},{5,13},{6,2},{7,15},{8,12},{9,1},{1... | collective-permute-start | bytes 393224 | tf_op jit(solution)/shard_map/ppermute | solution.py:247
  99.8 5.0 %collective-permute-start.19 = (bf16[8,16,512]{2,1,0:T(8,128)(2,1)S(1)}, bf16[8,16,512]{2,1,0:T(8,128)(2,1)S(1)}, u32[]{:S(2)}, u32[]{:S(2)}) collective-permute-start(bf16[8,16,512]{2,1,0:T(8,128)(2,1)S(1)} %get-tuple-element.46), channel_id=1, source_target_pairs={{0,8},{1,5},{2,10},{3,7},{4,12},{5,1},{6,14},{7,3},{8,0},{9,13},{1... | collective-permute-start | bytes 393224 | tf_op jit(solution)/shard_map/ppermute | solution.py:247
  104.1 5.2 %collective-permute-start.23 = (bf16[4,16,512]{2,1,0:T(8,128)(2,1)S(1)}, bf16[4,16,512]{2,1,0:T(8,128)(2,1)S(1)}, u32[]{:S(2)}, u32[]{:S(2)}) collective-permute-start(bf16[4,16,512]{2,1,0:T(8,128)(2,1)S(1)} %get-tuple-element.60), channel_id=1, source_target_pairs={{0,16},{1,17},{2,18},{3,19},{4,20},{5,21},{6,22},{7,23},{8,24},{9,... | collective-permute-start | bytes 196616 | tf_op jit(solution)/shard_map/ppermute | solution.py:247
  104.9 5.9 %collective-permute-start.20 = (bf16[4,16,512]{2,1,0:T(8,128)(2,1)S(1)}, bf16[4,16,512]{2,1,0:T(8,128)(2,1)S(1)}, u32[]{:S(2)}, u32[]{:S(2)}) collective-permute-start(bf16[4,16,512]{2,1,0:T(8,128)(2,1)S(1)} %get-tuple-element.62), channel_id=1, source_target_pairs={{0,16},{1,17},{2,18},{3,19},{4,20},{5,21},{6,22},{7,23},{8,24},{9,... | collective-permute-start | bytes 196616 | tf_op jit(solution)/shard_map/ppermute | solution.py:247
  111.6 3.3 %collective-permute-start.26 = (f32[4,1024]{1,0:T(4,128)S(1)}, f32[4,1024]{1,0:T(4,128)S(1)}, u32[]{:S(2)}, u32[]{:S(2)}) collective-permute-start(f32[4,1024]{1,0:T(4,128)S(1)} %get-tuple-element.43), channel_id=1, source_target_pairs={{0,3},{1,2},{2,1},{3,0},{4,7},{5,6},{6,5},{7,4},{8,11},{9,10},{10,... | collective-permute-start | bytes 49160 | tf_op jit(solution)/shard_map/ppermute | solution.py:426
  111.6 3.8 %collective-permute-start.25 = (f32[4,1024]{1,0:T(4,128)S(1)}, f32[4,1024]{1,0:T(4,128)S(1)}, u32[]{:S(2)}, u32[]{:S(2)}) collective-permute-start(f32[4,1024]{1,0:T(4,128)S(1)} %get-tuple-element.43), channel_id=1, source_target_pairs={{0,2},{1,3},{2,0},{3,1},{4,6},{5,7},{6,4},{7,5},{8,10},{9,11},{10,... | collective-permute-start | bytes 49160 | tf_op jit(solution)/shard_map/ppermute | solution.py:426
  113.1 2.3 %collective-permute-start.24 = (f32[4,1024]{1,0:T(4,128)S(1)}, f32[4,1024]{1,0:T(4,128)S(1)}, u32[]{:S(2)}, u32[]{:S(2)}) collective-permute-start(f32[4,1024]{1,0:T(4,128)S(1)} %get-tuple-element.43), channel_id=1, source_target_pairs={{0,1},{1,0},{2,3},{3,2},{4,5},{5,4},{6,7},{7,6},{8,9},{9,8},{10,11... | collective-permute-start | bytes 49160 | tf_op jit(solution)/shard_map/ppermute | solution.py:426

commit v7 on v6

--- a/solution.py
+++ b/solution.py
@@ -91,10 +91,9 @@
     cols_hbm, owner_hbm, ranks_hbm, misfit_hbm, u_hbm, v_hbm = refs[:6]
     u_ref, v_ref, code_ref = refs[6:9]
     outs = refs[9 : 9 + 2 * len(parts)]
-    cols, owner, ranks, misfit, tile_at, code_at, rank_at, count, lhs_ref, small, u_sem, v_sem = refs[
-        9 + 2 * len(parts) :
-    ]
-    here = lax.axis_index("rows")
+    cols, owner, ranks, misfit, word_at, lhs_ref, small, u_sem, v_sem = refs[9 + 2 * len(parts) :]
+    here, src = lax.axis_index("rows"), lax.axis_index("src")
+    codes = rows_dev * rows_dev
     tiles = rows_dev * tiles_row
     group_tiles = tiles // peers
     deep = group_tiles * rank_max
@@ -107,8 +106,6 @@
     ]
     for copy in copies:
         copy.start()
-    for rel in range(peers):
-        count[rel] = 0
     for copy in copies[:3]:
         copy.wait()
 
@@ -119,35 +116,41 @@
             sem.at[group],
         ).start()
 
-    def sort_tile(tile, carry):
-        row, k = lax.div(tile, tiles_row), lax.rem(tile, tiles_row)
-        slot = owner[cols[k, here * rows_dev + row]]
-        rel = turned(jnp.bitwise_xor(lax.div(slot, rows_dev), here), peers, lax.axis_index("src"))
-        at = rel * group_tiles + count[rel]
-        load(u_hbm, u_ref, u_sem, tile, at, rel)
-        count[rel] = count[rel] + 1
-        tile_at[at] = tile
-        code_at[at] = row * rows_dev + lax.rem(slot, rows_dev)
-        rank_at[at] = ranks[row, k]
-        return carry
-
-    def load_v(at, carry):
-        load(v_hbm, v_ref, v_sem, tile_at[at], at, lax.div(at, group_tiles))
-        return carry
+    def sort_tiles(k, filled):
+        slots = [owner[cols[k, here * rows_dev + row]] for row in range(rows_dev)]
+        for row, slot in enumerate(slots):
+            rel = turned(jnp.bitwise_xor(lax.div(slot, rows_dev), here), peers, src)
+            shift = rel * 4
+            at = rel * group_tiles + (lax.shift_right_logical(filled, shift) & 15)
+            filled = filled + lax.shift_left(jnp.int32(1), shift)
+            tile = row * tiles_row + k
+            word_at[at] = tile * codes + row * rows_dev + lax.rem(slot, rows_dev)
+        return filled
+
+    def load_all(whence, to, sem):
+        def one(at, carry):
+            load(whence, to, sem, lax.div(word_at[at], codes), at, lax.div(at, group_tiles))
+            return carry
+
+        lax.fori_loop(0, tiles, one, 0)
 
     def loaded(ref, sem, group):
         piece = ref.at[pl.ds(group * deep, deep)]
         pltpu.make_async_copy(piece, piece, sem.at[group]).wait()
 
-    lax.fori_loop(0, tiles, sort_tile, 0)
-    lax.fori_loop(0, tiles, load_v, 0)
+    lax.fori_loop(0, tiles_row, sort_tiles, jnp.int32(0))
+    load_all(u_hbm, u_ref, u_sem)
+    load_all(v_hbm, v_ref, v_sem)
     lane = lax.broadcasted_iota(jnp.int32, (1, deep), 1)
     for group in range(peers):
         code = jnp.full((1, deep), -1, jnp.int32)
         for i in range(group_tiles):
             at = group * group_tiles + i
-            inside = (lane >= i * rank_max) & (lane < i * rank_max + rank_at[at])
-            code = jnp.where(inside, code_at[at], code)
+            word = word_at[at]
+            tile = lax.div(word, codes)
+            rank = ranks[lax.div(tile, tiles_row), lax.rem(tile, tiles_row)]
+            inside = (lane >= i * rank_max) & (lane < i * rank_max + rank)
+            code = jnp.where(inside, lax.rem(word, codes), code)
         code_ref[pl.ds(group, 1), :] = code
     copies[3].wait()
     low = misfit[...].astype(jnp.bfloat16).reshape(rows_dev * sources, -1)
@@ -277,9 +280,6 @@
             smem(*ranks.shape),
             pltpu.VMEM(misfit.shape, misfit.dtype),
             smem(tiles),
-            smem(tiles),
-            smem(tiles),
-            smem(peers),
             pltpu.VMEM((peers, rows_dev * sources, deep), jnp.bfloat16),
             pltpu.SemaphoreType.DMA((4,)),
             pltpu.SemaphoreType.DMA((peers,)),
@@ -437,7 +437,8 @@
     tiles = rows_dev * tiles_row
     cap = (tiles + peers - 1) // peers
     dense = (
-        peers > 1
+        1 < peers <= 8
+        and cap < 16
         and peers & (peers - 1) == 0
         and tiles == cap * peers
         and cap >= rows_dev

time: 116 us -> 114 us (0.983)
  Pallas kernels: 36.2 us -> 34.2 us
    pallas_call x1, Pallas kernels: 14.8 us -> 12.8 us  [slot_sums(): pl.pallas_call(functools.partial(start_kernel, (rows_dev, tiles_row, rank...]
  transfers between devices with their start and end apart: 27 -> 27, of which waited for: 21 -> 20; matrix products, arithmetic and copies ran while one was open for 1% -> 1% of each run, Pallas kernels for 10% -> 10%
where the time goes in v7:
time: 114 us; the launch traced here: 113 us
  waiting for transfers between devices  46 us (40%)
  Pallas kernels  34.2 us (30%)
  starting transfers between devices  30.9 us (27%)
  other arithmetic  1.52 us (1%)
    ppermute x24, waiting for transfers between devices, swap(): return lax.ppermute(x, ('rows', 'src'), pairs)  44.1 us
    ppermute x24, starting transfers between devices, swap(): return lax.ppermute(x, ('rows', 'src'), pairs)  29 us
    pallas_call x1, Pallas kernels, slot_sums(): pl.pallas_call(functools.partial(start_kernel, (rows_dev, tiles_row, rank...  12.8 us
    pallas_call x3, Pallas kernels, slot_sums(): pl.pallas_call(functools.partial(ready_kernel, dims, parts[late], [parts[...  8.85 us
    pallas_call x3, Pallas kernels, slot_sums(): pl.pallas_call(functools.partial(early_kernel, dims, [parts[i] for i in e...  6.24 us
    pallas_call x6, Pallas kernels, slot_sums(): pl.pallas_call(functools.partial(more_kernel, dims, names), out_shape=sha...  5.55 us
  transfers between devices with their start and end apart: 27, of which 20 were waited for; matrix products, arithmetic and copies ran while one was open for 1% of the time, Pallas kernels for 10%

profile of v7, /device:TPU:0, one launch (start us, length us, event | category | flops | bytes accessed | tf_op | source)
XLA Modules:
  0.0 113.4 jit_solution(7639138379700362936)
XLA Ops:
  0.7 12.8 %start.1 = (bf16[6144,1024]{1,0:T(8,128)(2,1)S(1)}, bf16[6144,1024]{1,0:T(8,128)(2,1)S(1)}, s32[8,768]{1,0:T(8,128)S(1)}, f32[16,16,512]{2,1,0:T(8,128)S(1)}, bf...) custom-call(s32[16,32]{1,0:T(8,128)} %bitcast.11, s32[32]{0:T(128)} %refs_1_.1, ...), custom_call_target="tpu_custom_call" | custom-call | flops 402653184 | bytes 25165824 | tf_op jit(solution)/shard_map/start/pallas_call | solution.py:270
  13.4 3.0 %collective-permute-start = (bf16[16,16,512]{2,1,0:T(8,128)(2,1)S(1)}, bf16[16,16,512]{2,1,0:T(8,128)(2,1)S(1)}, u32[]{:S(2)}, u32[]{:S(2)}) collective-permute-start(bf16[16,16,512]{2,1,0:T(8,128)(2,1)S(1)} %get-tuple-element.25), channel_id=1, source_target_pairs={{0,4},{1,9},{2,6},{3,11},{4,0},{5,13},{6,2},{7,15},{8,12},{9,1},{1... | collective-permute-start | bytes 786440 | tf_op jit(solution)/shard_map/ppermute | solution.py:250
  16.4 1.6 %collective-permute-start.3 = (bf16[16,16,512]{2,1,0:T(8,128)(2,1)S(1)}, bf16[16,16,512]{2,1,0:T(8,128)(2,1)S(1)}, u32[]{:S(2)}, u32[]{:S(2)}) collective-permute-start(bf16[16,16,512]{2,1,0:T(8,128)(2,1)S(1)} %get-tuple-element.28), channel_id=1, source_target_pairs={{0,8},{1,5},{2,10},{3,7},{4,12},{5,1},{6,14},{7,3},{8,0},{9,13},{1... | collective-permute-start | bytes 786440 | tf_op jit(solution)/shard_map/ppermute | solution.py:250
  18.0 5.0 %collective-permute-done = bf16[16,16,512]{2,1,0:T(8,128)(2,1)S(1)} collective-permute-done((bf16[16,16,512]{2,1,0:T(8,128)(2,1)S(1)}, bf16[16,16,512]{2,1,0:T(8,128)(2,1)S(1)}, u32[]{:S(2)}, u32[]{:S(2)}) %collective-permute-start) | collective-permute-done | bytes 262176 | tf_op jit(solution)/shard_map/ppermute | solution.py:250
  23.1 1.7 %collective-permute-start.1 = (bf16[8,16,512]{2,1,0:T(8,128)(2,1)S(1)}, bf16[8,16,512]{2,1,0:T(8,128)(2,1)S(1)}, u32[]{:S(2)}, u32[]{:S(2)}) collective-permute-start(bf16[8,16,512]{2,1,0:T(8,128)(2,1)S(1)} %get-tuple-element.58), channel_id=1, source_target_pairs={{0,8},{1,5},{2,10},{3,7},{4,12},{5,1},{6,14},{7,3},{8,0},{9,13},{1... | collective-permute-start | bytes 393224 | tf_op jit(solution)/shard_map/ppermute | solution.py:250
  24.8 0.1 add_convert_fusion.6
  24.8 1.7 %collective-permute-start.4 = (bf16[8,16,512]{2,1,0:T(8,128)(2,1)S(1)}, bf16[8,16,512]{2,1,0:T(8,128)(2,1)S(1)}, u32[]{:S(2)}, u32[]{:S(2)}) collective-permute-start(bf16[8,16,512]{2,1,0:T(8,128)(2,1)S(1)} %get-tuple-element.56), channel_id=1, source_target_pairs={{0,4},{1,9},{2,6},{3,11},{4,0},{5,13},{6,2},{7,15},{8,12},{9,1},{1... | collective-permute-start | bytes 393224 | tf_op jit(solution)/shard_map/ppermute | solution.py:250
  26.5 2.5 %collective-permute-done.1 = bf16[8,16,512]{2,1,0:T(8,128)(2,1)S(1)} collective-permute-done((bf16[8,16,512]{2,1,0:T(8,128)(2,1)S(1)}, bf16[8,16,512]{2,1,0:T(8,128)(2,1)S(1)}, u32[]{:S(2)}, u32[]{:S(2)}) %collective-permute-start.1) | collective-permute-done | bytes 131104 | tf_op jit(solution)/shard_map/ppermute | solution.py:250
  29.0 4.1 %collective-permute-start.2 = (bf16[4,16,512]{2,1,0:T(8,128)(2,1)S(1)}, bf16[4,16,512]{2,1,0:T(8,128)(2,1)S(1)}, u32[]{:S(2)}, u32[]{:S(2)}) collective-permute-start(bf16[4,16,512]{2,1,0:T(8,128)(2,1)S(1)} %get-tuple-element.74), channel_id=1, source_target_pairs={{0,16},{1,17},{2,18},{3,19},{4,20},{5,21},{6,22},{7,23},{8,24},{9,... | collective-permute-start | bytes 196616 | tf_op jit(solution)/shard_map/ppermute | solution.py:250
  33.2 0.1 collective-permute-start.5
  33.3 2.1 %collective-permute-done.2.refs_1_ = bf16[4,16,512]{2,1,0:T(8,128)(2,1)S(1)} collective-permute-done((bf16[4,16,512]{2,1,0:T(8,128)(2,1)S(1)}, bf16[4,16,512]{2,1,0:T(8,128)(2,1)S(1)}, u32[]{:S(2)}, u32[]{:S(2)}) %collective-permute-start.2) | collective-permute-done | bytes 65568 | tf_op jit(solution)/shard_map/ppermute | solution.py:250
  35.4 2.0 %early.3.sum_ref = f32[8,16,768]{2,1,0:T(8,128)S(1)} custom-call(s32[8,768]{1,0:T(8,128)S(1)} %get-tuple-element.23.code_ref, f32[4,1024]{1,0:T(4,128)S(1)} %copy-done, f32[4,16,512]{2,1,0:T(8,128)S(1)} %get-tuple-element.75.refs_0_, bf16[4,16,512]{2,1,0:T(8,128)(2,1)S(1)} %collective-permute-done.2.refs_1_, ...), custom_call_target="tpu_custom_call" | custom-call | flops 100663296 | bytes 6291456 | tf_op jit(solution)/shard_map/early/pallas_call | solution.py:299
  37.4 1.0 collective-permute-done.5.came_ref
  38.4 2.9 %ready.3 = (bf16[8,64,768]{2,1,0:T(8,128)(2,1)S(1)}, bf16[16,16,512]{2,1,0:T(8,128)(2,1)S(1)}) custom-call(s32[8,768]{1,0:T(8,128)S(1)} %get-tuple-element.23.code_ref, f32[4,1024]{1,0:T(4,128)S(1)} %copy-done, f32[8,16,768]{2,1,0:T(8,128)S(1)} %early.3.sum_ref, f32[4,16,512]{2,1,0:T(8,128)S(1)} %get-tuple-element.73.base_ref, ...), custom_call_target="tpu_custom_call" | custom-call | flops 100663296 | bytes 6291456 | tf_op jit(solution)/shard_map/ready/pallas_call | solution.py:308
  41.4 1.5 %collective-permute-start.6 = (bf16[16,16,512]{2,1,0:T(8,128)(2,1)S(1)}, bf16[16,16,512]{2,1,0:T(8,128)(2,1)S(1)}, u32[]{:S(2)}, u32[]{:S(2)}) collective-permute-start(bf16[16,16,512]{2,1,0:T(8,128)(2,1)S(1)} %get-tuple-element.32), channel_id=1, source_target_pairs={{0,4},{1,9},{2,6},{3,11},{4,0},{5,13},{6,2},{7,15},{8,12},{9,1},{1... | collective-permute-start | bytes 786440 | tf_op jit(solution)/shard_map/ppermute | solution.py:250
  42.8 0.7 more.7
  43.5 0.1 collective-permute-start.9
  43.6 1.2 %more.6 = (f32[16,16,512]{2,1,0:T(8,128)S(1)}, f32[16,16,512]{2,1,0:T(8,128)S(1)}) custom-call(bf16[8,64,768]{2,1,0:T(8,128)(2,1)S(1)} %get-tuple-element.30.lhs_ref, bf16[6144,1024]{1,0:T(8,128)(2,1)S(1)} %get-tuple-element.29.refs_1_.v_ref), custom_call_target="tpu_custom_call" | custom-call | flops 100663296 | bytes 6291456 | tf_op jit(solution)/shard_map/more/pallas_call | solution.py:323
  44.8 4.0 %collective-permute-done.6 = bf16[16,16,512]{2,1,0:T(8,128)(2,1)S(1)} collective-permute-done((bf16[16,16,512]{2,1,0:T(8,128)(2,1)S(1)}, bf16[16,16,512]{2,1,0:T(8,128)(2,1)S(1)}, u32[]{:S(2)}, u32[]{:S(2)}) %collective-permute-start.6) | collective-permute-done | bytes 262176 | tf_op jit(solution)/shard_map/ppermute | solution.py:250
  48.8 0.1 collective-permute-start.7
  48.9 1.4 %collective-permute-done.9 = bf16[16,16,512]{2,1,0:T(8,128)(2,1)S(1)} collective-permute-done((bf16[16,16,512]{2,1,0:T(8,128)(2,1)S(1)}, bf16[16,16,512]{2,1,0:T(8,128)(2,1)S(1)}, u32[]{:S(2)}, u32[]{:S(2)}) %collective-permute-start.9) | collective-permute-done | bytes 262176 | tf_op jit(solution)/shard_map/ppermute | solution.py:250
  50.3 1.6 %collective-permute-start.10 = (bf16[8,16,512]{2,1,0:T(8,128)(2,1)S(1)}, bf16[8,16,512]{2,1,0:T(8,128)(2,1)S(1)}, u32[]{:S(2)}, u32[]{:S(2)}) collective-permute-start(bf16[8,16,512]{2,1,0:T(8,128)(2,1)S(1)} %get-tuple-element.52), channel_id=1, source_target_pairs={{0,4},{1,9},{2,6},{3,11},{4,0},{5,13},{6,2},{7,15},{8,12},{9,1},{1... | collective-permute-start | bytes 393224 | tf_op jit(solution)/shard_map/ppermute | solution.py:250
  51.9 2.6 %collective-permute-done.7 = bf16[8,16,512]{2,1,0:T(8,128)(2,1)S(1)} collective-permute-done((bf16[8,16,512]{2,1,0:T(8,128)(2,1)S(1)}, bf16[8,16,512]{2,1,0:T(8,128)(2,1)S(1)}, u32[]{:S(2)}, u32[]{:S(2)}) %collective-permute-start.7) | collective-permute-done | bytes 131104 | tf_op jit(solution)/shard_map/ppermute | solution.py:250
  54.6 1.4 %collective-permute-start.8 = (bf16[4,16,512]{2,1,0:T(8,128)(2,1)S(1)}, bf16[4,16,512]{2,1,0:T(8,128)(2,1)S(1)}, u32[]{:S(2)}, u32[]{:S(2)}) collective-permute-start(bf16[4,16,512]{2,1,0:T(8,128)(2,1)S(1)} %get-tuple-element.70), channel_id=1, source_target_pairs={{0,16},{1,17},{2,18},{3,19},{4,20},{5,21},{6,22},{7,23},{8,24},{9,... | collective-permute-start | bytes 196616 | tf_op jit(solution)/shard_map/ppermute | solution.py:250
  56.1 1.6 %collective-permute-start.11 = (bf16[4,16,512]{2,1,0:T(8,128)(2,1)S(1)}, bf16[4,16,512]{2,1,0:T(8,128)(2,1)S(1)}, u32[]{:S(2)}, u32[]{:S(2)}) collective-permute-start(bf16[4,16,512]{2,1,0:T(8,128)(2,1)S(1)} %get-tuple-element.68), channel_id=1, source_target_pairs={{0,16},{1,17},{2,18},{3,19},{4,20},{5,21},{6,22},{7,23},{8,24},{9,... | collective-permute-start | bytes 196616 | tf_op jit(solution)/shard_map/ppermute | solution.py:250
  57.7 2.5 %collective-permute-done.8.refs_1_ = bf16[4,16,512]{2,1,0:T(8,128)(2,1)S(1)} collective-permute-done((bf16[4,16,512]{2,1,0:T(8,128)(2,1)S(1)}, bf16[4,16,512]{2,1,0:T(8,128)(2,1)S(1)}, u32[]{:S(2)}, u32[]{:S(2)}) %collective-permute-start.8) | collective-permute-done | bytes 65568 | tf_op jit(solution)/shard_map/ppermute | solution.py:250
  60.3 2.2 %early.4.sum_ref = f32[8,16,768]{2,1,0:T(8,128)S(1)} custom-call(s32[8,768]{1,0:T(8,128)S(1)} %get-tuple-element.23.code_ref, f32[4,1024]{1,0:T(4,128)S(1)} %copy-done, f32[4,16,512]{2,1,0:T(8,128)S(1)} %get-tuple-element.71.refs_0_, bf16[4,16,512]{2,1,0:T(8,128)(2,1)S(1)} %collective-permute-done.8.refs_1_, ...), custom_call_target="tpu_custom_call" | custom-call | flops 100663296 | bytes 6291456 | tf_op jit(solution)/shard_map/early/pallas_call | solution.py:299
  62.5 3.0 %ready.4 = (bf16[8,64,768]{2,1,0:T(8,128)(2,1)S(1)}, bf16[16,16,512]{2,1,0:T(8,128)(2,1)S(1)}) custom-call(s32[8,768]{1,0:T(8,128)S(1)} %get-tuple-element.23.code_ref, f32[4,1024]{1,0:T(4,128)S(1)} %copy-done, f32[8,16,768]{2,1,0:T(8,128)S(1)} %early.4.sum_ref, f32[4,16,512]{2,1,0:T(8,128)S(1)} %get-tuple-element.69.base_ref, ...), custom_call_target="tpu_custom_call" | custom-call | flops 100663296 | bytes 6291456 | tf_op jit(solution)/shard_map/ready/pallas_call | solution.py:308
  65.4 1.6 %collective-permute-start.12 = (bf16[16,16,512]{2,1,0:T(8,128)(2,1)S(1)}, bf16[16,16,512]{2,1,0:T(8,128)(2,1)S(1)}, u32[]{:S(2)}, u32[]{:S(2)}) collective-permute-start(bf16[16,16,512]{2,1,0:T(8,128)(2,1)S(1)} %get-tuple-element.36), channel_id=1, source_target_pairs={{0,4},{1,9},{2,6},{3,11},{4,0},{5,13},{6,2},{7,15},{8,12},{9,1},{1... | collective-permute-start | bytes 786440 | tf_op jit(solution)/shard_map/ppermute | solution.py:250
  67.0 0.7 more.9
  67.6 0.8 collective-permute-start.15
  68.4 1.2 %more.8 = (f32[16,16,512]{2,1,0:T(8,128)S(1)}, f32[16,16,512]{2,1,0:T(8,128)S(1)}) custom-call(bf16[8,64,768]{2,1,0:T(8,128)(2,1)S(1)} %get-tuple-element.34.lhs_ref, bf16[6144,1024]{1,0:T(8,128)(2,1)S(1)} %get-tuple-element.29.refs_1_.v_ref), custom_call_target="tpu_custom_call" | custom-call | flops 100663296 | bytes 6291456 | tf_op jit(solution)/shard_map/more/pallas_call | solution.py:323
  69.6 2.2 %collective-permute-done.12 = bf16[16,16,512]{2,1,0:T(8,128)(2,1)S(1)} collective-permute-done((bf16[16,16,512]{2,1,0:T(8,128)(2,1)S(1)}, bf16[16,16,512]{2,1,0:T(8,128)(2,1)S(1)}, u32[]{:S(2)}, u32[]{:S(2)}) %collective-permute-start.12) | collective-permute-done | bytes 262176 | tf_op jit(solution)/shard_map/ppermute | solution.py:250
  71.9 0.3 collective-permute-start.13
  72.2 3.3 %collective-permute-done.15 = bf16[16,16,512]{2,1,0:T(8,128)(2,1)S(1)} collective-permute-done((bf16[16,16,512]{2,1,0:T(8,128)(2,1)S(1)}, bf16[16,16,512]{2,1,0:T(8,128)(2,1)S(1)}, u32[]{:S(2)}, u32[]{:S(2)}) %collective-permute-start.15) | collective-permute-done | bytes 262176 | tf_op jit(solution)/shard_map/ppermute | solution.py:250
  75.5 0.6 collective-permute-start.16
  76.1 0.8 collective-permute-done.13
  77.0 1.1 %collective-permute-start.14 = (bf16[4,16,512]{2,1,0:T(8,128)(2,1)S(1)}, bf16[4,16,512]{2,1,0:T(8,128)(2,1)S(1)}, u32[]{:S(2)}, u32[]{:S(2)}) collective-permute-start(bf16[4,16,512]{2,1,0:T(8,128)(2,1)S(1)} %get-tuple-element.66), channel_id=1, source_target_pairs={{0,16},{1,17},{2,18},{3,19},{4,20},{5,21},{6,22},{7,23},{8,24},{9,... | collective-permute-start | bytes 196616 | tf_op jit(solution)/shard_map/ppermute | solution.py:250
  78.1 2.4 %collective-permute-done.16 = bf16[8,16,512]{2,1,0:T(8,128)(2,1)S(1)} collective-permute-done((bf16[8,16,512]{2,1,0:T(8,128)(2,1)S(1)}, bf16[8,16,512]{2,1,0:T(8,128)(2,1)S(1)}, u32[]{:S(2)}, u32[]{:S(2)}) %collective-permute-start.16) | collective-permute-done | bytes 131104 | tf_op jit(solution)/shard_map/ppermute | solution.py:250
  80.6 0.5 collective-permute-start.17
  81.2 1.5 %collective-permute-done.14.refs_1_ = bf16[4,16,512]{2,1,0:T(8,128)(2,1)S(1)} collective-permute-done((bf16[4,16,512]{2,1,0:T(8,128)(2,1)S(1)}, bf16[4,16,512]{2,1,0:T(8,128)(2,1)S(1)}, u32[]{:S(2)}, u32[]{:S(2)}) %collective-permute-start.14) | collective-permute-done | bytes 65568 | tf_op jit(solution)/shard_map/ppermute | solution.py:250
  82.7 2.0 %early.5.sum_ref = f32[8,16,768]{2,1,0:T(8,128)S(1)} custom-call(s32[8,768]{1,0:T(8,128)S(1)} %get-tuple-element.23.code_ref, f32[4,1024]{1,0:T(4,128)S(1)} %copy-done, f32[4,16,512]{2,1,0:T(8,128)S(1)} %get-tuple-element.67.refs_0_, bf16[4,16,512]{2,1,0:T(8,128)(2,1)S(1)} %collective-permute-done.14.refs_1_, ...), custom_call_target="tpu_custom_call" | custom-call | flops 100663296 | bytes 6291456 | tf_op jit(solution)/shard_map/early/pallas_call | solution.py:299
  84.7 1.8 %collective-permute-done.17.came_ref = bf16[4,16,512]{2,1,0:T(8,128)(2,1)S(1)} collective-permute-done((bf16[4,16,512]{2,1,0:T(8,128)(2,1)S(1)}, bf16[4,16,512]{2,1,0:T(8,128)(2,1)S(1)}, u32[]{:S(2)}, u32[]{:S(2)}) %collective-permute-start.17) | collective-permute-done | bytes 65568 | tf_op jit(solution)/shard_map/ppermute | solution.py:250
  86.5 2.9 %ready.5 = (bf16[8,64,768]{2,1,0:T(8,128)(2,1)S(1)}, bf16[16,16,512]{2,1,0:T(8,128)(2,1)S(1)}) custom-call(s32[8,768]{1,0:T(8,128)S(1)} %get-tuple-element.23.code_ref, f32[4,1024]{1,0:T(4,128)S(1)} %copy-done, f32[8,16,768]{2,1,0:T(8,128)S(1)} %early.5.sum_ref, f32[4,16,512]{2,1,0:T(8,128)S(1)} %get-tuple-element.65.base_ref, ...), custom_call_target="tpu_custom_call" | custom-call | flops 100663296 | bytes 6291456 | tf_op jit(solution)/shard_map/ready/pallas_call | solution.py:308
  89.5 0.7 more.11
  90.2 0.2 collective-permute-start.21
  90.4 0.9 collective-permute-start.18
  91.3 1.2 %more.10 = (f32[16,16,512]{2,1,0:T(8,128)S(1)}, f32[16,16,512]{2,1,0:T(8,128)S(1)}) custom-call(bf16[8,64,768]{2,1,0:T(8,128)(2,1)S(1)} %get-tuple-element.38.lhs_ref, bf16[6144,1024]{1,0:T(8,128)(2,1)S(1)} %get-tuple-element.29.refs_1_.v_ref), custom_call_target="tpu_custom_call" | custom-call | flops 100663296 | bytes 6291456 | tf_op jit(solution)/shard_map/more/pallas_call | solution.py:323
  92.5 4.6 %collective-permute-done.21 = bf16[16,16,512]{2,1,0:T(8,128)(2,1)S(1)} collective-permute-done((bf16[16,16,512]{2,1,0:T(8,128)(2,1)S(1)}, bf16[16,16,512]{2,1,0:T(8,128)(2,1)S(1)}, u32[]{:S(2)}, u32[]{:S(2)}) %collective-permute-start.21) | collective-permute-done | bytes 262176 | tf_op jit(solution)/shard_map/ppermute | solution.py:250
  97.1 0.1 add_convert_fusion
  97.2 0.2 collective-permute-start.22
  97.4 0.1 add_convert_fusion.1
  97.5 1.3 %collective-permute-start.19 = (bf16[8,16,512]{2,1,0:T(8,128)(2,1)S(1)}, bf16[8,16,512]{2,1,0:T(8,128)(2,1)S(1)}, u32[]{:S(2)}, u32[]{:S(2)}) collective-permute-start(bf16[8,16,512]{2,1,0:T(8,128)(2,1)S(1)} %get-tuple-element.46), channel_id=1, source_target_pairs={{0,8},{1,5},{2,10},{3,7},{4,12},{5,1},{6,14},{7,3},{8,0},{9,13},{1... | collective-permute-start | bytes 393224 | tf_op jit(solution)/shard_map/ppermute | solution.py:250
  98.8 3.5 %collective-permute-done.22 = bf16[8,16,512]{2,1,0:T(8,128)(2,1)S(1)} collective-permute-done((bf16[8,16,512]{2,1,0:T(8,128)(2,1)S(1)}, bf16[8,16,512]{2,1,0:T(8,128)(2,1)S(1)}, u32[]{:S(2)}, u32[]{:S(2)}) %collective-permute-start.22) | collective-permute-done | bytes 131104 | tf_op jit(solution)/shard_map/ppermute | solution.py:250
  102.3 0.2 collective-permute-start.23
  102.6 2.8 %collective-permute-start.20 = (bf16[4,16,512]{2,1,0:T(8,128)(2,1)S(1)}, bf16[4,16,512]{2,1,0:T(8,128)(2,1)S(1)}, u32[]{:S(2)}, u32[]{:S(2)}) collective-permute-start(bf16[4,16,512]{2,1,0:T(8,128)(2,1)S(1)} %get-tuple-element.62), channel_id=1, source_target_pairs={{0,16},{1,17},{2,18},{3,19},{4,20},{5,21},{6,22},{7,23},{8,24},{9,... | collective-permute-start | bytes 196616 | tf_op jit(solution)/shard_map/ppermute | solution.py:250
  105.4 2.1 %collective-permute-done.23.refs_3_ = bf16[4,16,512]{2,1,0:T(8,128)(2,1)S(1)} collective-permute-done((bf16[4,16,512]{2,1,0:T(8,128)(2,1)S(1)}, bf16[4,16,512]{2,1,0:T(8,128)(2,1)S(1)}, u32[]{:S(2)}, u32[]{:S(2)}) %collective-permute-start.23) | collective-permute-done | bytes 65568 | tf_op jit(solution)/shard_map/ppermute | solution.py:250
  107.5 0.7 collective-permute-done.20.refs_1_
  108.2 0.8 finish.1
  109.0 1.5 %collective-permute-start.25 = (f32[4,1024]{1,0:T(4,128)S(1)}, f32[4,1024]{1,0:T(4,128)S(1)}, u32[]{:S(2)}, u32[]{:S(2)}) collective-permute-start(f32[4,1024]{1,0:T(4,128)S(1)} %get-tuple-element.43), channel_id=1, source_target_pairs={{0,2},{1,3},{2,0},{3,1},{4,6},{5,7},{6,4},{7,5},{8,10},{9,11},{10,... | collective-permute-start | bytes 49160 | tf_op jit(solution)/shard_map/ppermute | solution.py:426
  110.5 0.3 collective-permute-start.24
  110.9 1.4 %collective-permute-done.26 = f32[4,1024]{1,0:T(4,128)S(1)} collective-permute-done((f32[4,1024]{1,0:T(4,128)S(1)}, f32[4,1024]{1,0:T(4,128)S(1)}, u32[]{:S(2)}, u32[]{:S(2)}) %collective-permute-start.26) | collective-permute-done | bytes 16416 | tf_op jit(solution)/shard_map/ppermute | solution.py:426
  112.3 0.5 collective-permute-done.25
  112.8 0.6 add_multiply_fusion
  (28 shorter events, 0.7 us)
Async XLA Ops:
  0.6 17.4 %copy-start = (f32[4,1024]{1,0:T(4,128)S(1)}, f32[4,1024]{1,0:T(4,128)}, u32[]{:S(2)}) copy-start(f32[4,1024]{1,0:T(4,128)} %contrast_ref.13) | copy-start | bytes 49156
  0.6 28.3 %copy-start.2 = (f32[4,16,1024]{2,1,0:T(8,128)S(1)}, f32[4,16,1024]{2,1,0:T(8,128)}, u32[]{:S(2)}) copy-start(f32[4,16,1024]{2,1,0:T(8,128)} %refs_3_.1) | copy-start | bytes 786436
  13.4 9.6 %collective-permute-start = (bf16[16,16,512]{2,1,0:T(8,128)(2,1)S(1)}, bf16[16,16,512]{2,1,0:T(8,128)(2,1)S(1)}, u32[]{:S(2)}, u32[]{:S(2)}) collective-permute-start(bf16[16,16,512]{2,1,0:T(8,128)(2,1)S(1)} %get-tuple-element.25), channel_id=1, source_target_pairs={{0,4},{1,9},{2,6},{3,11},{4,0},{5,13},{6,2},{7,15},{8,12},{9,1},{1... | collective-permute-start | bytes 786440 | tf_op jit(solution)/shard_map/ppermute | solution.py:250
  16.4 8.3 %collective-permute-start.3 = (bf16[16,16,512]{2,1,0:T(8,128)(2,1)S(1)}, bf16[16,16,512]{2,1,0:T(8,128)(2,1)S(1)}, u32[]{:S(2)}, u32[]{:S(2)}) collective-permute-start(bf16[16,16,512]{2,1,0:T(8,128)(2,1)S(1)} %get-tuple-element.28), channel_id=1, source_target_pairs={{0,8},{1,5},{2,10},{3,7},{4,12},{5,1},{6,14},{7,3},{8,0},{9,13},{1... | collective-permute-start | bytes 786440 | tf_op jit(solution)/shard_map/ppermute | solution.py:250
  23.1 5.9 %collective-permute-start.1 = (bf16[8,16,512]{2,1,0:T(8,128)(2,1)S(1)}, bf16[8,16,512]{2,1,0:T(8,128)(2,1)S(1)}, u32[]{:S(2)}, u32[]{:S(2)}) collective-permute-start(bf16[8,16,512]{2,1,0:T(8,128)(2,1)S(1)} %get-tuple-element.58), channel_id=1, source_target_pairs={{0,8},{1,5},{2,10},{3,7},{4,12},{5,1},{6,14},{7,3},{8,0},{9,13},{1... | collective-permute-start | bytes 393224 | tf_op jit(solution)/shard_map/ppermute | solution.py:250
  24.8 8.3 %collective-permute-start.4 = (bf16[8,16,512]{2,1,0:T(8,128)(2,1)S(1)}, bf16[8,16,512]{2,1,0:T(8,128)(2,1)S(1)}, u32[]{:S(2)}, u32[]{:S(2)}) collective-permute-start(bf16[8,16,512]{2,1,0:T(8,128)(2,1)S(1)} %get-tuple-element.56), channel_id=1, source_target_pairs={{0,4},{1,9},{2,6},{3,11},{4,0},{5,13},{6,2},{7,15},{8,12},{9,1},{1... | collective-permute-start | bytes 393224 | tf_op jit(solution)/shard_map/ppermute | solution.py:250
  29.0 6.4 %collective-permute-start.2 = (bf16[4,16,512]{2,1,0:T(8,128)(2,1)S(1)}, bf16[4,16,512]{2,1,0:T(8,128)(2,1)S(1)}, u32[]{:S(2)}, u32[]{:S(2)}) collective-permute-start(bf16[4,16,512]{2,1,0:T(8,128)(2,1)S(1)} %get-tuple-element.74), channel_id=1, source_target_pairs={{0,16},{1,17},{2,18},{3,19},{4,20},{5,21},{6,22},{7,23},{8,24},{9,... | collective-permute-start | bytes 196616 | tf_op jit(solution)/shard_map/ppermute | solution.py:250
  33.2 5.2 %collective-permute-start.5 = (bf16[4,16,512]{2,1,0:T(8,128)(2,1)S(1)}, bf16[4,16,512]{2,1,0:T(8,128)(2,1)S(1)}, u32[]{:S(2)}, u32[]{:S(2)}) collective-permute-start(bf16[4,16,512]{2,1,0:T(8,128)(2,1)S(1)} %get-tuple-element.72), channel_id=1, source_target_pairs={{0,16},{1,17},{2,18},{3,19},{4,20},{5,21},{6,22},{7,23},{8,24},{9,... | collective-permute-start | bytes 196616 | tf_op jit(solution)/shard_map/ppermute | solution.py:250
  41.4 7.4 %collective-permute-start.6 = (bf16[16,16,512]{2,1,0:T(8,128)(2,1)S(1)}, bf16[16,16,512]{2,1,0:T(8,128)(2,1)S(1)}, u32[]{:S(2)}, u32[]{:S(2)}) collective-permute-start(bf16[16,16,512]{2,1,0:T(8,128)(2,1)S(1)} %get-tuple-element.32), channel_id=1, source_target_pairs={{0,4},{1,9},{2,6},{3,11},{4,0},{5,13},{6,2},{7,15},{8,12},{9,1},{1... | collective-permute-start | bytes 786440 | tf_op jit(solution)/shard_map/ppermute | solution.py:250
  43.5 6.8 %collective-permute-start.9 = (bf16[16,16,512]{2,1,0:T(8,128)(2,1)S(1)}, bf16[16,16,512]{2,1,0:T(8,128)(2,1)S(1)}, u32[]{:S(2)}, u32[]{:S(2)}) collective-permute-start(bf16[16,16,512]{2,1,0:T(8,128)(2,1)S(1)} %more.7), channel_id=1, source_target_pairs={{0,8},{1,5},{2,10},{3,7},{4,12},{5,1},{6,14},{7,3},{8,0},{9,13},{1... | collective-permute-start | bytes 786440 | tf_op jit(solution)/shard_map/ppermute | solution.py:250
  48.8 5.7 %collective-permute-start.7 = (bf16[8,16,512]{2,1,0:T(8,128)(2,1)S(1)}, bf16[8,16,512]{2,1,0:T(8,128)(2,1)S(1)}, u32[]{:S(2)}, u32[]{:S(2)}) collective-permute-start(bf16[8,16,512]{2,1,0:T(8,128)(2,1)S(1)} %get-tuple-element.54), channel_id=1, source_target_pairs={{0,8},{1,5},{2,10},{3,7},{4,12},{5,1},{6,14},{7,3},{8,0},{9,13},{1... | collective-permute-start | bytes 393224 | tf_op jit(solution)/shard_map/ppermute | solution.py:250
  50.3 5.7 %collective-permute-start.10 = (bf16[8,16,512]{2,1,0:T(8,128)(2,1)S(1)}, bf16[8,16,512]{2,1,0:T(8,128)(2,1)S(1)}, u32[]{:S(2)}, u32[]{:S(2)}) collective-permute-start(bf16[8,16,512]{2,1,0:T(8,128)(2,1)S(1)} %get-tuple-element.52), channel_id=1, source_target_pairs={{0,4},{1,9},{2,6},{3,11},{4,0},{5,13},{6,2},{7,15},{8,12},{9,1},{1... | collective-permute-start | bytes 393224 | tf_op jit(solution)/shard_map/ppermute | solution.py:250
  54.6 5.7 %collective-permute-start.8 = (bf16[4,16,512]{2,1,0:T(8,128)(2,1)S(1)}, bf16[4,16,512]{2,1,0:T(8,128)(2,1)S(1)}, u32[]{:S(2)}, u32[]{:S(2)}) collective-permute-start(bf16[4,16,512]{2,1,0:T(8,128)(2,1)S(1)} %get-tuple-element.70), channel_id=1, source_target_pairs={{0,16},{1,17},{2,18},{3,19},{4,20},{5,21},{6,22},{7,23},{8,24},{9,... | collective-permute-start | bytes 196616 | tf_op jit(solution)/shard_map/ppermute | solution.py:250
  56.1 6.4 %collective-permute-start.11 = (bf16[4,16,512]{2,1,0:T(8,128)(2,1)S(1)}, bf16[4,16,512]{2,1,0:T(8,128)(2,1)S(1)}, u32[]{:S(2)}, u32[]{:S(2)}) collective-permute-start(bf16[4,16,512]{2,1,0:T(8,128)(2,1)S(1)} %get-tuple-element.68), channel_id=1, source_target_pairs={{0,16},{1,17},{2,18},{3,19},{4,20},{5,21},{6,22},{7,23},{8,24},{9,... | collective-permute-start | bytes 196616 | tf_op jit(solution)/shard_map/ppermute | solution.py:250
  65.4 6.4 %collective-permute-start.12 = (bf16[16,16,512]{2,1,0:T(8,128)(2,1)S(1)}, bf16[16,16,512]{2,1,0:T(8,128)(2,1)S(1)}, u32[]{:S(2)}, u32[]{:S(2)}) collective-permute-start(bf16[16,16,512]{2,1,0:T(8,128)(2,1)S(1)} %get-tuple-element.36), channel_id=1, source_target_pairs={{0,4},{1,9},{2,6},{3,11},{4,0},{5,13},{6,2},{7,15},{8,12},{9,1},{1... | collective-permute-start | bytes 786440 | tf_op jit(solution)/shard_map/ppermute | solution.py:250
  67.6 7.8 %collective-permute-start.15 = (bf16[16,16,512]{2,1,0:T(8,128)(2,1)S(1)}, bf16[16,16,512]{2,1,0:T(8,128)(2,1)S(1)}, u32[]{:S(2)}, u32[]{:S(2)}) collective-permute-start(bf16[16,16,512]{2,1,0:T(8,128)(2,1)S(1)} %more.9), channel_id=1, source_target_pairs={{0,8},{1,5},{2,10},{3,7},{4,12},{5,1},{6,14},{7,3},{8,0},{9,13},{1... | collective-permute-start | bytes 786440 | tf_op jit(solution)/shard_map/ppermute | solution.py:250
  71.9 5.0 %collective-permute-start.13 = (bf16[8,16,512]{2,1,0:T(8,128)(2,1)S(1)}, bf16[8,16,512]{2,1,0:T(8,128)(2,1)S(1)}, u32[]{:S(2)}, u32[]{:S(2)}) collective-permute-start(bf16[8,16,512]{2,1,0:T(8,128)(2,1)S(1)} %get-tuple-element.50), channel_id=1, source_target_pairs={{0,8},{1,5},{2,10},{3,7},{4,12},{5,1},{6,14},{7,3},{8,0},{9,13},{1... | collective-permute-start | bytes 393224 | tf_op jit(solution)/shard_map/ppermute | solution.py:250
  75.5 5.0 %collective-permute-start.16 = (bf16[8,16,512]{2,1,0:T(8,128)(2,1)S(1)}, bf16[8,16,512]{2,1,0:T(8,128)(2,1)S(1)}, u32[]{:S(2)}, u32[]{:S(2)}) collective-permute-start(bf16[8,16,512]{2,1,0:T(8,128)(2,1)S(1)} %get-tuple-element.48), channel_id=1, source_target_pairs={{0,4},{1,9},{2,6},{3,11},{4,0},{5,13},{6,2},{7,15},{8,12},{9,1},{1... | collective-permute-start | bytes 393224 | tf_op jit(solution)/shard_map/ppermute | solution.py:250
  77.0 5.7 %collective-permute-start.14 = (bf16[4,16,512]{2,1,0:T(8,128)(2,1)S(1)}, bf16[4,16,512]{2,1,0:T(8,128)(2,1)S(1)}, u32[]{:S(2)}, u32[]{:S(2)}) collective-permute-start(bf16[4,16,512]{2,1,0:T(8,128)(2,1)S(1)} %get-tuple-element.66), channel_id=1, source_target_pairs={{0,16},{1,17},{2,18},{3,19},{4,20},{5,21},{6,22},{7,23},{8,24},{9,... | collective-permute-start | bytes 196616 | tf_op jit(solution)/shard_map/ppermute | solution.py:250
  80.6 5.9 %collective-permute-start.17 = (bf16[4,16,512]{2,1,0:T(8,128)(2,1)S(1)}, bf16[4,16,512]{2,1,0:T(8,128)(2,1)S(1)}, u32[]{:S(2)}, u32[]{:S(2)}) collective-permute-start(bf16[4,16,512]{2,1,0:T(8,128)(2,1)S(1)} %get-tuple-element.64), channel_id=1, source_target_pairs={{0,16},{1,17},{2,18},{3,19},{4,20},{5,21},{6,22},{7,23},{8,24},{9,... | collective-permute-start | bytes 196616 | tf_op jit(solution)/shard_map/ppermute | solution.py:250
  89.5 18.8 %copy-start.1 = (bf16[4,16,1024]{2,1,0:T(8,128)(2,1)S(1)}, bf16[4,16,1024]{2,1,0:T(8,128)(2,1)}, u32[]{:S(2)}) copy-start(bf16[4,16,1024]{2,1,0:T(8,128)(2,1)} %forward_ref.1) | copy-start | bytes 393220
  90.2 7.0 %collective-permute-start.21 = (bf16[16,16,512]{2,1,0:T(8,128)(2,1)S(1)}, bf16[16,16,512]{2,1,0:T(8,128)(2,1)S(1)}, u32[]{:S(2)}, u32[]{:S(2)}) collective-permute-start(bf16[16,16,512]{2,1,0:T(8,128)(2,1)S(1)} %more.11), channel_id=1, source_target_pairs={{0,8},{1,5},{2,10},{3,7},{4,12},{5,1},{6,14},{7,3},{8,0},{9,13},{1... | collective-permute-start | bytes 786440 | tf_op jit(solution)/shard_map/ppermute | solution.py:250
  90.4 7.0 %collective-permute-start.18 = (bf16[16,16,512]{2,1,0:T(8,128)(2,1)S(1)}, bf16[16,16,512]{2,1,0:T(8,128)(2,1)S(1)}, u32[]{:S(2)}, u32[]{:S(2)}) collective-permute-start(bf16[16,16,512]{2,1,0:T(8,128)(2,1)S(1)} %get-tuple-element.40), channel_id=1, source_target_pairs={{0,4},{1,9},{2,6},{3,11},{4,0},{5,13},{6,2},{7,15},{8,12},{9,1},{1... | collective-permute-start | bytes 786440 | tf_op jit(solution)/shard_map/ppermute | solution.py:250
  97.2 5.0 %collective-permute-start.22 = (bf16[8,16,512]{2,1,0:T(8,128)(2,1)S(1)}, bf16[8,16,512]{2,1,0:T(8,128)(2,1)S(1)}, u32[]{:S(2)}, u32[]{:S(2)}) collective-permute-start(bf16[8,16,512]{2,1,0:T(8,128)(2,1)S(1)} %get-tuple-element.44), channel_id=1, source_target_pairs={{0,4},{1,9},{2,6},{3,11},{4,0},{5,13},{6,2},{7,15},{8,12},{9,1},{1... | collective-permute-start | bytes 393224 | tf_op jit(solution)/shard_map/ppermute | solution.py:250
  97.5 5.1 %collective-permute-start.19 = (bf16[8,16,512]{2,1,0:T(8,128)(2,1)S(1)}, bf16[8,16,512]{2,1,0:T(8,128)(2,1)S(1)}, u32[]{:S(2)}, u32[]{:S(2)}) collective-permute-start(bf16[8,16,512]{2,1,0:T(8,128)(2,1)S(1)} %get-tuple-element.46), channel_id=1, source_target_pairs={{0,8},{1,5},{2,10},{3,7},{4,12},{5,1},{6,14},{7,3},{8,0},{9,13},{1... | collective-permute-start | bytes 393224 | tf_op jit(solution)/shard_map/ppermute | solution.py:250
  102.3 5.2 %collective-permute-start.23 = (bf16[4,16,512]{2,1,0:T(8,128)(2,1)S(1)}, bf16[4,16,512]{2,1,0:T(8,128)(2,1)S(1)}, u32[]{:S(2)}, u32[]{:S(2)}) collective-permute-start(bf16[4,16,512]{2,1,0:T(8,128)(2,1)S(1)} %get-tuple-element.60), channel_id=1, source_target_pairs={{0,16},{1,17},{2,18},{3,19},{4,20},{5,21},{6,22},{7,23},{8,24},{9,... | collective-permute-start | bytes 196616 | tf_op jit(solution)/shard_map/ppermute | solution.py:250
  102.6 5.6 %collective-permute-start.20 = (bf16[4,16,512]{2,1,0:T(8,128)(2,1)S(1)}, bf16[4,16,512]{2,1,0:T(8,128)(2,1)S(1)}, u32[]{:S(2)}, u32[]{:S(2)}) collective-permute-start(bf16[4,16,512]{2,1,0:T(8,128)(2,1)S(1)} %get-tuple-element.62), channel_id=1, source_target_pairs={{0,16},{1,17},{2,18},{3,19},{4,20},{5,21},{6,22},{7,23},{8,24},{9,... | collective-permute-start | bytes 196616 | tf_op jit(solution)/shard_map/ppermute | solution.py:250
  109.0 3.3 %collective-permute-start.26 = (f32[4,1024]{1,0:T(4,128)S(1)}, f32[4,1024]{1,0:T(4,128)S(1)}, u32[]{:S(2)}, u32[]{:S(2)}) collective-permute-start(f32[4,1024]{1,0:T(4,128)S(1)} %get-tuple-element.43), channel_id=1, source_target_pairs={{0,3},{1,2},{2,1},{3,0},{4,7},{5,6},{6,5},{7,4},{8,11},{9,10},{10,... | collective-permute-start | bytes 49160 | tf_op jit(solution)/shard_map/ppermute | solution.py:426
  109.0 3.8 %collective-permute-start.25 = (f32[4,1024]{1,0:T(4,128)S(1)}, f32[4,1024]{1,0:T(4,128)S(1)}, u32[]{:S(2)}, u32[]{:S(2)}) collective-permute-start(f32[4,1024]{1,0:T(4,128)S(1)} %get-tuple-element.43), channel_id=1, source_target_pairs={{0,2},{1,3},{2,0},{3,1},{4,6},{5,7},{6,4},{7,5},{8,10},{9,11},{10,... | collective-permute-start | bytes 49160 | tf_op jit(solution)/shard_map/ppermute | solution.py:426
  110.5 2.3 %collective-permute-start.24 = (f32[4,1024]{1,0:T(4,128)S(1)}, f32[4,1024]{1,0:T(4,128)S(1)}, u32[]{:S(2)}, u32[]{:S(2)}) collective-permute-start(f32[4,1024]{1,0:T(4,128)S(1)} %get-tuple-element.43), channel_id=1, source_target_pairs={{0,1},{1,0},{2,3},{3,2},{4,5},{5,4},{6,7},{7,6},{8,9},{9,8},{10,11... | collective-permute-start | bytes 49160 | tf_op jit(solution)/shard_map/ppermute | solution.py:426

commit v8 on v7

--- a/solution.py
+++ b/solution.py
@@ -11,9 +11,8 @@
 
 def parts_of(unknowns, peers):
     bits = list(range(peers.bit_length() - 1))
-    turned = bits[1:2] + bits[:1] + bits[2:]
     width = unknowns // 2
-    return [(0, width, bits), (width, width, turned)]
+    return [(0, width, bits), (width, width, bits)]
 
 
 def spot(order, rel):
@@ -193,31 +192,40 @@
         out_ref[group] = pick_rows(every, code, sources, rows_dev)
 
 
-def ready_kernel(dims, late, parts, code_ref, contrast_ref, sum_ref, base_ref, came_ref, *refs):
+def complete(dims, late, group, low, code_ref, sum_ref, u_ref):
+    rows_dev, _ = dims
+    deep = code_ref.shape[1]
+    first, width, _ = late
+    every = times_u(low, u_ref[pl.ds(group * deep, deep), pl.ds(first, width)])
+    code = code_ref[pl.ds(group, 1), :]
+    coeff = sum_ref[group] + pick_rows(every, code, sum_ref.shape[1], rows_dev)
+    return by_slot(coeff, code, rows_dev)
+
+
+def ready_kernel(dims, late, part, groups, code_ref, contrast_ref, sum_ref, *refs):
+    base_ref, came_ref, u_ref, v_ref, lhs_ref, out = refs
     rows_dev, peers = dims
-    u_ref, v_ref, lhs_ref = refs[:3]
-    outs = refs[3:]
-    deep = code_ref.shape[1]
-    sources = sum_ref.shape[1]
     low = low_field(base_ref, came_ref, contrast_ref, late)
-    first, width, _ = late
-    for group in reversed(range(peers)):
-        every = times_u(low, u_ref[pl.ds(group * deep, deep), pl.ds(first, width)])
-        code = code_ref[pl.ds(group, 1), :]
-        coeff = sum_ref[group] + pick_rows(every, code, sources, rows_dev)
-        lhs = by_slot(coeff, code, rows_dev)
-        lhs_ref[group] = lhs
+    for i, group in enumerate(groups):
+        lhs = complete(dims, late, group, low, code_ref, sum_ref, u_ref)
+        lhs_ref[i] = lhs
+        put_terms(lhs, v_ref, group, part, (None, out), rows_dev, peers)
+
+
+def more_kernel(dims, part, groups, lhs_ref, v_ref, out):
+    rows_dev, peers = dims
+    for i, group in enumerate(groups):
+        put_terms(lhs_ref[i], v_ref, group, part, (None, out), rows_dev, peers)
+
+
+def rest_kernel(dims, late, parts, groups, code_ref, contrast_ref, sum_ref, *refs):
+    base_ref, came_ref, u_ref, v_ref, *outs = refs
+    rows_dev, peers = dims
+    low = low_field(base_ref, came_ref, contrast_ref, late)
+    for group in groups:
+        lhs = complete(dims, late, group, low, code_ref, sum_ref, u_ref)
         for out, part in zip(outs, parts):
-            if spot(part[2], group) >= peers // 2:
-                put_terms(lhs, v_ref, group, part, (None, out), rows_dev, peers)
-
-
-def more_kernel(dims, parts, lhs_ref, v_ref, *outs):
-    rows_dev, peers = dims
-    for out, (part, kept) in zip(outs, parts):
-        for group in range(peers):
-            if (spot(part[2], group) < peers // 2) == kept:
-                put_terms(lhs_ref[group], v_ref, group, part, (out, out), rows_dev, peers)
+            put_terms(lhs, v_ref, group, part, (out, None), rows_dev, peers)
 
 
 def finish_kernel(parts, contrast_ref, forward_ref, *refs):
@@ -259,7 +267,11 @@
     tiles = rows_dev * tiles_row
     deep = tiles // peers * rank_max
     parts = parts_of(unknowns, peers)
-    first_sent, late = [0], 1
+    late = 1
+    staying, leaving = (
+        [group for group in range(peers) if (spot(parts[0][2], group) >= peers // 2) == goes]
+        for goes in (False, True)
+    )
     early = [i for i in range(len(parts)) if i != late]
     half = (peers // 2 * rows_dev, sources)
     sent = [jax.ShapeDtypeStruct((*half, part[1]), jnp.bfloat16) for part in parts]
@@ -305,30 +317,39 @@
                 cost_estimate=cost(u.shape[0], unknowns // 2, sources),
                 name="early",
             )(code, contrast, *(x for i in early for x in (base[i], came[i])), in_vmem(u))
-            lhs, *some = pl.pallas_call(
-                functools.partial(ready_kernel, dims, parts[late], [parts[i] for i in first_sent]),
-                out_shape=[jax.ShapeDtypeStruct((peers, rows_dev * sources, deep), jnp.bfloat16)]
-                + [sent[i] for i in first_sent],
+            state = (code, contrast, coeff, base[late], came[late], in_vmem(u), in_vmem(v))
+            lhs, ahead = pl.pallas_call(
+                functools.partial(ready_kernel, dims, parts[late], parts[0], leaving),
+                out_shape=[
+                    jax.ShapeDtypeStruct((peers // 2, rows_dev * sources, deep), jnp.bfloat16),
+                    sent[0],
+                ],
                 in_specs=vmem(7),
-                out_specs=vmem(1 + len(first_sent)),
+                out_specs=vmem(2),
                 compiler_params=params(),
                 cost_estimate=cost(u.shape[0], unknowns // 2, sources),
                 name="ready",
-            )(code, contrast, coeff, base[late], came[late], in_vmem(u), in_vmem(v))
-            goes, keeps = [*some], []
-            for names, shapes, to in (
-                [[(parts[1], False)], sent[1:], goes],
-                [[(part, True) for part in parts], kept, keeps],
-            ):
-                to += pl.pallas_call(
-                    functools.partial(more_kernel, dims, names),
-                    out_shape=shapes,
-                    in_specs=vmem(2),
-                    out_specs=vmem(len(shapes)),
-                    compiler_params=params(),
-                    cost_estimate=cost(u.shape[0], unknowns // 4 * len(shapes), sources),
-                    name="more",
-                )(lhs, in_vmem(v))
+            )(*state)
+            behind = pl.pallas_call(
+                functools.partial(more_kernel, dims, parts[1], leaving),
+                out_shape=sent[1],
+                in_specs=vmem(2),
+                out_specs=vmem(1)[0],
+                compiler_params=params(),
+                cost_estimate=cost(u.shape[0], unknowns // 4, sources),
+                name="more",
+            )(lhs, in_vmem(v))
+            goes = [ahead, behind]
+            keeps = pl.pallas_call(
+                functools.partial(rest_kernel, dims, parts[late], parts, staying),
+                out_shape=kept,
+                in_specs=vmem(7),
+                out_specs=vmem(2),
+                compiler_params=params(),
+                cost_estimate=cost(u.shape[0], unknowns * 3 // 4, sources),
+                name="rest",
+            )(*state)
+            keeps = list(keeps)
         base, came = [None] * len(parts), [None] * len(parts)
         levels = len(parts[0][2])
         for level in range(levels):

time: 114 us -> 115 us (level)
  starting transfers between devices: 30.9 us -> 40.6 us
  waiting for transfers between devices: 46 us -> 37.2 us
    ppermute x24, starting transfers between devices: 29 us -> 38.7 us  [swap(): return lax.ppermute(x, ('rows', 'src'), pairs)]
    ppermute x24, waiting for transfers between devices: 44.1 us -> 34.4 us  [swap(): return lax.ppermute(x, ('rows', 'src'), pairs)]
  transfers between devices with their start and end apart: 27 -> 27, of which waited for: 20 -> 21; matrix products, arithmetic and copies ran while one was open for 1% -> 1% of each run, Pallas kernels for 10% -> 13%
where the time goes in v8:
time: 115 us
  starting transfers between devices  40.6 us (35%)
  waiting for transfers between devices  37.2 us (32%)
  Pallas kernels  35.2 us (31%)
  other arithmetic  1.52 us (1%)
    ppermute x24, starting transfers between devices, swap(): return lax.ppermute(x, ('rows', 'src'), pairs)  38.7 us
    ppermute x24, waiting for transfers between devices, swap(): return lax.ppermute(x, ('rows', 'src'), pairs)  34.4 us
    pallas_call x1, Pallas kernels, slot_sums(): pl.pallas_call(functools.partial(start_kernel, (rows_dev, tiles_row, rank...  12.7 us
    pallas_call x3, Pallas kernels, slot_sums(): pl.pallas_call(functools.partial(rest_kernel, dims, parts[late], parts, s...  7.55 us
    pallas_call x3, Pallas kernels, slot_sums(): pl.pallas_call(functools.partial(early_kernel, dims, [parts[i] for i in e...  6.24 us
    pallas_call x3, Pallas kernels, slot_sums(): pl.pallas_call(functools.partial(ready_kernel, dims, parts[late], parts[0...  5.89 us
    ppermute x3, waiting for transfers between devices, src_sum(): terms.append(lax.ppermute(x, 'src', [(i, i ^ step) for i in range(count)]))  2.79 us
  transfers between devices with their start and end apart: 27, of which 21 were waited for; matrix products, arithmetic and copies ran while one was open for 1% of the time, Pallas kernels for 13%

profile of v8, /device:TPU:0, one launch (start us, length us, event | category | flops | bytes accessed | tf_op | source)
XLA Modules:
  0.0 115.3 jit_solution(100643431751302599)
XLA Ops:
  0.7 12.7 %start.1 = (bf16[6144,1024]{1,0:T(8,128)(2,1)S(1)}, bf16[6144,1024]{1,0:T(8,128)(2,1)S(1)}, s32[8,768]{1,0:T(8,128)S(1)}, f32[16,16,512]{2,1,0:T(8,128)S(1)}, bf...) custom-call(s32[16,32]{1,0:T(8,128)} %bitcast.11, s32[32]{0:T(128)} %refs_1_.1, ...), custom_call_target="tpu_custom_call" | custom-call | flops 402653184 | bytes 25165824 | tf_op jit(solution)/shard_map/start/pallas_call | solution.py:282
  13.4 3.0 %collective-permute-start = (bf16[16,16,512]{2,1,0:T(8,128)(2,1)S(1)}, bf16[16,16,512]{2,1,0:T(8,128)(2,1)S(1)}, u32[]{:S(2)}, u32[]{:S(2)}) collective-permute-start(bf16[16,16,512]{2,1,0:T(8,128)(2,1)S(1)} %get-tuple-element.25), channel_id=1, source_target_pairs={{0,4},{1,9},{2,6},{3,11},{4,0},{5,13},{6,2},{7,15},{8,12},{9,1},{1... | collective-permute-start | bytes 786440 | tf_op jit(solution)/shard_map/ppermute | solution.py:258
  16.4 0.1 collective-permute-start.3
  16.5 4.3 %collective-permute-done = bf16[16,16,512]{2,1,0:T(8,128)(2,1)S(1)} collective-permute-done((bf16[16,16,512]{2,1,0:T(8,128)(2,1)S(1)}, bf16[16,16,512]{2,1,0:T(8,128)(2,1)S(1)}, u32[]{:S(2)}, u32[]{:S(2)}) %collective-permute-start) | collective-permute-done | bytes 262176 | tf_op jit(solution)/shard_map/ppermute | solution.py:258
  20.8 0.1 add_convert_fusion.7
  20.9 2.1 %collective-permute-start.1 = (bf16[8,16,512]{2,1,0:T(8,128)(2,1)S(1)}, bf16[8,16,512]{2,1,0:T(8,128)(2,1)S(1)}, u32[]{:S(2)}, u32[]{:S(2)}) collective-permute-start(bf16[8,16,512]{2,1,0:T(8,128)(2,1)S(1)} %get-tuple-element.58), channel_id=1, source_target_pairs={{0,8},{1,5},{2,10},{3,7},{4,12},{5,1},{6,14},{7,3},{8,0},{9,13},{1... | collective-permute-start | bytes 393224 | tf_op jit(solution)/shard_map/ppermute | solution.py:258
  23.0 1.3 %collective-permute-done.3 = bf16[16,16,512]{2,1,0:T(8,128)(2,1)S(1)} collective-permute-done((bf16[16,16,512]{2,1,0:T(8,128)(2,1)S(1)}, bf16[16,16,512]{2,1,0:T(8,128)(2,1)S(1)}, u32[]{:S(2)}, u32[]{:S(2)}) %collective-permute-start.3) | collective-permute-done | bytes 262176 | tf_op jit(solution)/shard_map/ppermute | solution.py:258
  24.3 0.1 add_convert_fusion.6
  24.3 2.5 %collective-permute-start.4 = (bf16[8,16,512]{2,1,0:T(8,128)(2,1)S(1)}, bf16[8,16,512]{2,1,0:T(8,128)(2,1)S(1)}, u32[]{:S(2)}, u32[]{:S(2)}) collective-permute-start(bf16[8,16,512]{2,1,0:T(8,128)(2,1)S(1)} %get-tuple-element.56), channel_id=1, source_target_pairs={{0,8},{1,5},{2,10},{3,7},{4,12},{5,1},{6,14},{7,3},{8,0},{9,13},{1... | collective-permute-start | bytes 393224 | tf_op jit(solution)/shard_map/ppermute | solution.py:258
  26.9 2.7 %collective-permute-start.2 = (bf16[4,16,512]{2,1,0:T(8,128)(2,1)S(1)}, bf16[4,16,512]{2,1,0:T(8,128)(2,1)S(1)}, u32[]{:S(2)}, u32[]{:S(2)}) collective-permute-start(bf16[4,16,512]{2,1,0:T(8,128)(2,1)S(1)} %get-tuple-element.74), channel_id=1, source_target_pairs={{0,16},{1,17},{2,18},{3,19},{4,20},{5,21},{6,22},{7,23},{8,24},{9,... | collective-permute-start | bytes 196616 | tf_op jit(solution)/shard_map/ppermute | solution.py:258
  29.5 0.9 collective-permute-done.4
  30.5 2.5 %collective-permute-start.5 = (bf16[4,16,512]{2,1,0:T(8,128)(2,1)S(1)}, bf16[4,16,512]{2,1,0:T(8,128)(2,1)S(1)}, u32[]{:S(2)}, u32[]{:S(2)}) collective-permute-start(bf16[4,16,512]{2,1,0:T(8,128)(2,1)S(1)} %get-tuple-element.72), channel_id=1, source_target_pairs={{0,16},{1,17},{2,18},{3,19},{4,20},{5,21},{6,22},{7,23},{8,24},{9,... | collective-permute-start | bytes 196616 | tf_op jit(solution)/shard_map/ppermute | solution.py:258
  33.0 1.0 collective-permute-done.2.refs_1_
  34.0 2.0 %early.3.sum_ref = f32[8,16,768]{2,1,0:T(8,128)S(1)} custom-call(s32[8,768]{1,0:T(8,128)S(1)} %get-tuple-element.23.code_ref, f32[4,1024]{1,0:T(4,128)S(1)} %copy-done, f32[4,16,512]{2,1,0:T(8,128)S(1)} %get-tuple-element.75.refs_0_, bf16[4,16,512]{2,1,0:T(8,128)(2,1)S(1)} %collective-permute-done.2.refs_1_, bf16[6144,1024]{1,0:T(8,128)(2,1)S(1)} %get-tuple-element.26.refs_2_), custom_call_target="tpu_custom_call" | custom-call | flops 100663296 | bytes 6291456 | tf_op jit(solution)/shard_map/early/pallas_call | solution.py:311
  36.0 2.0 %ready.3 = (bf16[4,64,768]{2,1,0:T(8,128)(2,1)S(1)}, bf16[16,16,512]{2,1,0:T(8,128)(2,1)S(1)}) custom-call(s32[8,768]{1,0:T(8,128)S(1)} %get-tuple-element.23.code_ref, f32[4,1024]{1,0:T(4,128)S(1)} %copy-done, f32[8,16,768]{2,1,0:T(8,128)S(1)} %early.3.sum_ref, f32[4,16,512]{2,1,0:T(8,128)S(1)} %get-tuple-element.73.refs_0_, ...), custom_call_target="tpu_custom_call" | custom-call | flops 100663296 | bytes 6291456 | tf_op jit(solution)/shard_map/ready/pallas_call | solution.py:321
  38.0 1.8 %collective-permute-start.6 = (bf16[16,16,512]{2,1,0:T(8,128)(2,1)S(1)}, bf16[16,16,512]{2,1,0:T(8,128)(2,1)S(1)}, u32[]{:S(2)}, u32[]{:S(2)}) collective-permute-start(bf16[16,16,512]{2,1,0:T(8,128)(2,1)S(1)} %get-tuple-element.31), channel_id=1, source_target_pairs={{0,4},{1,9},{2,6},{3,11},{4,0},{5,13},{6,2},{7,15},{8,12},{9,1},{1... | collective-permute-start | bytes 786440 | tf_op jit(solution)/shard_map/ppermute | solution.py:258
  39.8 0.7 more.3
  40.4 0.4 collective-permute-start.9
  40.8 2.5 %rest.3 = (f32[16,16,512]{2,1,0:T(8,128)S(1)}, f32[16,16,512]{2,1,0:T(8,128)S(1)}) custom-call(s32[8,768]{1,0:T(8,128)S(1)} %get-tuple-element.23.code_ref, f32[4,1024]{1,0:T(4,128)S(1)} %copy-done, f32[8,16,768]{2,1,0:T(8,128)S(1)} %early.3.sum_ref, f32[4,16,512]{2,1,0:T(8,128)S(1)} %get-tuple-element.73.refs_0_, ...), custom_call_target="tpu_custom_call" | custom-call | flops 150994944 | bytes 9437184 | tf_op jit(solution)/shard_map/rest/pallas_call | solution.py:343
  43.3 1.4 %collective-permute-done.6 = bf16[16,16,512]{2,1,0:T(8,128)(2,1)S(1)} collective-permute-done((bf16[16,16,512]{2,1,0:T(8,128)(2,1)S(1)}, bf16[16,16,512]{2,1,0:T(8,128)(2,1)S(1)}, u32[]{:S(2)}, u32[]{:S(2)}) %collective-permute-start.6) | collective-permute-done | bytes 262176 | tf_op jit(solution)/shard_map/ppermute | solution.py:258
  44.8 3.2 %collective-permute-start.7 = (bf16[8,16,512]{2,1,0:T(8,128)(2,1)S(1)}, bf16[8,16,512]{2,1,0:T(8,128)(2,1)S(1)}, u32[]{:S(2)}, u32[]{:S(2)}) collective-permute-start(bf16[8,16,512]{2,1,0:T(8,128)(2,1)S(1)} %get-tuple-element.54), channel_id=1, source_target_pairs={{0,8},{1,5},{2,10},{3,7},{4,12},{5,1},{6,14},{7,3},{8,0},{9,13},{1... | collective-permute-start | bytes 393224 | tf_op jit(solution)/shard_map/ppermute | solution.py:258
  48.0 2.1 %collective-permute-done.9 = bf16[16,16,512]{2,1,0:T(8,128)(2,1)S(1)} collective-permute-done((bf16[16,16,512]{2,1,0:T(8,128)(2,1)S(1)}, bf16[16,16,512]{2,1,0:T(8,128)(2,1)S(1)}, u32[]{:S(2)}, u32[]{:S(2)}) %collective-permute-start.9) | collective-permute-done | bytes 262176 | tf_op jit(solution)/shard_map/ppermute | solution.py:258
  50.1 1.9 %collective-permute-start.10 = (bf16[8,16,512]{2,1,0:T(8,128)(2,1)S(1)}, bf16[8,16,512]{2,1,0:T(8,128)(2,1)S(1)}, u32[]{:S(2)}, u32[]{:S(2)}) collective-permute-start(bf16[8,16,512]{2,1,0:T(8,128)(2,1)S(1)} %get-tuple-element.52), channel_id=1, source_target_pairs={{0,8},{1,5},{2,10},{3,7},{4,12},{5,1},{6,14},{7,3},{8,0},{9,13},{1... | collective-permute-start | bytes 393224 | tf_op jit(solution)/shard_map/ppermute | solution.py:258
  52.1 2.7 %collective-permute-start.8 = (bf16[4,16,512]{2,1,0:T(8,128)(2,1)S(1)}, bf16[4,16,512]{2,1,0:T(8,128)(2,1)S(1)}, u32[]{:S(2)}, u32[]{:S(2)}) collective-permute-start(bf16[4,16,512]{2,1,0:T(8,128)(2,1)S(1)} %get-tuple-element.70), channel_id=1, source_target_pairs={{0,16},{1,17},{2,18},{3,19},{4,20},{5,21},{6,22},{7,23},{8,24},{9,... | collective-permute-start | bytes 196616 | tf_op jit(solution)/shard_map/ppermute | solution.py:258
  54.8 1.0 collective-permute-done.10
  55.9 1.9 %collective-permute-start.11 = (bf16[4,16,512]{2,1,0:T(8,128)(2,1)S(1)}, bf16[4,16,512]{2,1,0:T(8,128)(2,1)S(1)}, u32[]{:S(2)}, u32[]{:S(2)}) collective-permute-start(bf16[4,16,512]{2,1,0:T(8,128)(2,1)S(1)} %get-tuple-element.68), channel_id=1, source_target_pairs={{0,16},{1,17},{2,18},{3,19},{4,20},{5,21},{6,22},{7,23},{8,24},{9,... | collective-permute-start | bytes 196616 | tf_op jit(solution)/shard_map/ppermute | solution.py:258
  57.8 2.2 %early.4.sum_ref = f32[8,16,768]{2,1,0:T(8,128)S(1)} custom-call(s32[8,768]{1,0:T(8,128)S(1)} %get-tuple-element.23.code_ref, f32[4,1024]{1,0:T(4,128)S(1)} %copy-done, f32[4,16,512]{2,1,0:T(8,128)S(1)} %get-tuple-element.71.refs_0_, bf16[4,16,512]{2,1,0:T(8,128)(2,1)S(1)} %collective-permute-done.8.refs_1_, bf16[6144,1024]{1,0:T(8,128)(2,1)S(1)} %get-tuple-element.26.refs_2_), custom_call_target="tpu_custom_call" | custom-call | flops 100663296 | bytes 6291456 | tf_op jit(solution)/shard_map/early/pallas_call | solution.py:311
  60.0 1.2 %collective-permute-done.11.refs_1_ = bf16[4,16,512]{2,1,0:T(8,128)(2,1)S(1)} collective-permute-done((bf16[4,16,512]{2,1,0:T(8,128)(2,1)S(1)}, bf16[4,16,512]{2,1,0:T(8,128)(2,1)S(1)}, u32[]{:S(2)}, u32[]{:S(2)}) %collective-permute-start.11) | collective-permute-done | bytes 65568 | tf_op jit(solution)/shard_map/ppermute | solution.py:258
  61.2 2.0 %ready.4 = (bf16[4,64,768]{2,1,0:T(8,128)(2,1)S(1)}, bf16[16,16,512]{2,1,0:T(8,128)(2,1)S(1)}) custom-call(s32[8,768]{1,0:T(8,128)S(1)} %get-tuple-element.23.code_ref, f32[4,1024]{1,0:T(4,128)S(1)} %copy-done, f32[8,16,768]{2,1,0:T(8,128)S(1)} %early.4.sum_ref, f32[4,16,512]{2,1,0:T(8,128)S(1)} %get-tuple-element.69.refs_0_, ...), custom_call_target="tpu_custom_call" | custom-call | flops 100663296 | bytes 6291456 | tf_op jit(solution)/shard_map/ready/pallas_call | solution.py:321
  63.2 1.8 %collective-permute-start.12 = (bf16[16,16,512]{2,1,0:T(8,128)(2,1)S(1)}, bf16[16,16,512]{2,1,0:T(8,128)(2,1)S(1)}, u32[]{:S(2)}, u32[]{:S(2)}) collective-permute-start(bf16[16,16,512]{2,1,0:T(8,128)(2,1)S(1)} %get-tuple-element.35), channel_id=1, source_target_pairs={{0,4},{1,9},{2,6},{3,11},{4,0},{5,13},{6,2},{7,15},{8,12},{9,1},{1... | collective-permute-start | bytes 786440 | tf_op jit(solution)/shard_map/ppermute | solution.py:258
  65.0 0.7 more.4
  65.6 0.4 collective-permute-start.15
  66.0 2.5 %rest.4 = (f32[16,16,512]{2,1,0:T(8,128)S(1)}, f32[16,16,512]{2,1,0:T(8,128)S(1)}) custom-call(s32[8,768]{1,0:T(8,128)S(1)} %get-tuple-element.23.code_ref, f32[4,1024]{1,0:T(4,128)S(1)} %copy-done, f32[8,16,768]{2,1,0:T(8,128)S(1)} %early.4.sum_ref, f32[4,16,512]{2,1,0:T(8,128)S(1)} %get-tuple-element.69.refs_0_, ...), custom_call_target="tpu_custom_call" | custom-call | flops 150994944 | bytes 9437184 | tf_op jit(solution)/shard_map/rest/pallas_call | solution.py:343
  68.5 2.8 %collective-permute-done.12 = bf16[16,16,512]{2,1,0:T(8,128)(2,1)S(1)} collective-permute-done((bf16[16,16,512]{2,1,0:T(8,128)(2,1)S(1)}, bf16[16,16,512]{2,1,0:T(8,128)(2,1)S(1)}, u32[]{:S(2)}, u32[]{:S(2)}) %collective-permute-start.12) | collective-permute-done | bytes 262176 | tf_op jit(solution)/shard_map/ppermute | solution.py:258
  71.4 1.4 %collective-permute-start.13 = (bf16[8,16,512]{2,1,0:T(8,128)(2,1)S(1)}, bf16[8,16,512]{2,1,0:T(8,128)(2,1)S(1)}, u32[]{:S(2)}, u32[]{:S(2)}) collective-permute-start(bf16[8,16,512]{2,1,0:T(8,128)(2,1)S(1)} %get-tuple-element.50), channel_id=1, source_target_pairs={{0,8},{1,5},{2,10},{3,7},{4,12},{5,1},{6,14},{7,3},{8,0},{9,13},{1... | collective-permute-start | bytes 393224 | tf_op jit(solution)/shard_map/ppermute | solution.py:258
  72.9 1.4 %collective-permute-done.15 = bf16[16,16,512]{2,1,0:T(8,128)(2,1)S(1)} collective-permute-done((bf16[16,16,512]{2,1,0:T(8,128)(2,1)S(1)}, bf16[16,16,512]{2,1,0:T(8,128)(2,1)S(1)}, u32[]{:S(2)}, u32[]{:S(2)}) %collective-permute-start.15) | collective-permute-done | bytes 262176 | tf_op jit(solution)/shard_map/ppermute | solution.py:258
  74.3 1.4 %collective-permute-start.16 = (bf16[8,16,512]{2,1,0:T(8,128)(2,1)S(1)}, bf16[8,16,512]{2,1,0:T(8,128)(2,1)S(1)}, u32[]{:S(2)}, u32[]{:S(2)}) collective-permute-start(bf16[8,16,512]{2,1,0:T(8,128)(2,1)S(1)} %get-tuple-element.48), channel_id=1, source_target_pairs={{0,8},{1,5},{2,10},{3,7},{4,12},{5,1},{6,14},{7,3},{8,0},{9,13},{1... | collective-permute-start | bytes 393224 | tf_op jit(solution)/shard_map/ppermute | solution.py:258
  75.7 1.5 %collective-permute-done.13 = bf16[8,16,512]{2,1,0:T(8,128)(2,1)S(1)} collective-permute-done((bf16[8,16,512]{2,1,0:T(8,128)(2,1)S(1)}, bf16[8,16,512]{2,1,0:T(8,128)(2,1)S(1)}, u32[]{:S(2)}, u32[]{:S(2)}) %collective-permute-start.13) | collective-permute-done | bytes 131104 | tf_op jit(solution)/shard_map/ppermute | solution.py:258
  77.2 1.5 %collective-permute-start.14 = (bf16[4,16,512]{2,1,0:T(8,128)(2,1)S(1)}, bf16[4,16,512]{2,1,0:T(8,128)(2,1)S(1)}, u32[]{:S(2)}, u32[]{:S(2)}) collective-permute-start(bf16[4,16,512]{2,1,0:T(8,128)(2,1)S(1)} %get-tuple-element.66), channel_id=1, source_target_pairs={{0,16},{1,17},{2,18},{3,19},{4,20},{5,21},{6,22},{7,23},{8,24},{9,... | collective-permute-start | bytes 196616 | tf_op jit(solution)/shard_map/ppermute | solution.py:258
  78.7 0.6 collective-permute-done.16
  79.4 2.1 %collective-permute-start.17 = (bf16[4,16,512]{2,1,0:T(8,128)(2,1)S(1)}, bf16[4,16,512]{2,1,0:T(8,128)(2,1)S(1)}, u32[]{:S(2)}, u32[]{:S(2)}) collective-permute-start(bf16[4,16,512]{2,1,0:T(8,128)(2,1)S(1)} %get-tuple-element.64), channel_id=1, source_target_pairs={{0,16},{1,17},{2,18},{3,19},{4,20},{5,21},{6,22},{7,23},{8,24},{9,... | collective-permute-start | bytes 196616 | tf_op jit(solution)/shard_map/ppermute | solution.py:258
  81.5 1.7 %collective-permute-done.14.refs_1_ = bf16[4,16,512]{2,1,0:T(8,128)(2,1)S(1)} collective-permute-done((bf16[4,16,512]{2,1,0:T(8,128)(2,1)S(1)}, bf16[4,16,512]{2,1,0:T(8,128)(2,1)S(1)}, u32[]{:S(2)}, u32[]{:S(2)}) %collective-permute-start.14) | collective-permute-done | bytes 65568 | tf_op jit(solution)/shard_map/ppermute | solution.py:258
  83.1 2.0 %early.5.sum_ref = f32[8,16,768]{2,1,0:T(8,128)S(1)} custom-call(s32[8,768]{1,0:T(8,128)S(1)} %get-tuple-element.23.code_ref, f32[4,1024]{1,0:T(4,128)S(1)} %copy-done, f32[4,16,512]{2,1,0:T(8,128)S(1)} %get-tuple-element.67.refs_0_, bf16[4,16,512]{2,1,0:T(8,128)(2,1)S(1)} %collective-permute-done.14.refs_1_, bf16[6144,1024]{1,0:T(8,128)(2,1)S(1)} %get-tuple-element.26.refs_2_), custom_call_target="tpu_custom_call" | custom-call | flops 100663296 | bytes 6291456 | tf_op jit(solution)/shard_map/early/pallas_call | solution.py:311
  85.2 2.0 %ready.5 = (bf16[4,64,768]{2,1,0:T(8,128)(2,1)S(1)}, bf16[16,16,512]{2,1,0:T(8,128)(2,1)S(1)}) custom-call(s32[8,768]{1,0:T(8,128)S(1)} %get-tuple-element.23.code_ref, f32[4,1024]{1,0:T(4,128)S(1)} %copy-done, f32[8,16,768]{2,1,0:T(8,128)S(1)} %early.5.sum_ref, f32[4,16,512]{2,1,0:T(8,128)S(1)} %get-tuple-element.65.refs_0_, ...), custom_call_target="tpu_custom_call" | custom-call | flops 100663296 | bytes 6291456 | tf_op jit(solution)/shard_map/ready/pallas_call | solution.py:321
  87.1 0.7 more.5
  87.8 1.6 %collective-permute-start.21 = (bf16[16,16,512]{2,1,0:T(8,128)(2,1)S(1)}, bf16[16,16,512]{2,1,0:T(8,128)(2,1)S(1)}, u32[]{:S(2)}, u32[]{:S(2)}) collective-permute-start(bf16[16,16,512]{2,1,0:T(8,128)(2,1)S(1)} %more.5), channel_id=1, source_target_pairs={{0,4},{1,9},{2,6},{3,11},{4,0},{5,13},{6,2},{7,15},{8,12},{9,1},{1... | collective-permute-start | bytes 786440 | tf_op jit(solution)/shard_map/ppermute | solution.py:258
  89.4 0.5 collective-permute-start.18
  89.9 2.5 %rest.5 = (f32[16,16,512]{2,1,0:T(8,128)S(1)}, f32[16,16,512]{2,1,0:T(8,128)S(1)}) custom-call(s32[8,768]{1,0:T(8,128)S(1)} %get-tuple-element.23.code_ref, f32[4,1024]{1,0:T(4,128)S(1)} %copy-done, f32[8,16,768]{2,1,0:T(8,128)S(1)} %early.5.sum_ref, f32[4,16,512]{2,1,0:T(8,128)S(1)} %get-tuple-element.65.refs_0_, ...), custom_call_target="tpu_custom_call" | custom-call | flops 150994944 | bytes 9437184 | tf_op jit(solution)/shard_map/rest/pallas_call | solution.py:343
  92.4 3.0 %collective-permute-done.21 = bf16[16,16,512]{2,1,0:T(8,128)(2,1)S(1)} collective-permute-done((bf16[16,16,512]{2,1,0:T(8,128)(2,1)S(1)}, bf16[16,16,512]{2,1,0:T(8,128)(2,1)S(1)}, u32[]{:S(2)}, u32[]{:S(2)}) %collective-permute-start.21) | collective-permute-done | bytes 262176 | tf_op jit(solution)/shard_map/ppermute | solution.py:258
  95.5 0.5 collective-permute-start.22
  96.0 2.2 %collective-permute-done.18 = bf16[16,16,512]{2,1,0:T(8,128)(2,1)S(1)} collective-permute-done((bf16[16,16,512]{2,1,0:T(8,128)(2,1)S(1)}, bf16[16,16,512]{2,1,0:T(8,128)(2,1)S(1)}, u32[]{:S(2)}, u32[]{:S(2)}) %collective-permute-start.18) | collective-permute-done | bytes 262176 | tf_op jit(solution)/shard_map/ppermute | solution.py:258
  98.3 0.5 collective-permute-start.19
  98.9 1.7 %collective-permute-done.22 = bf16[8,16,512]{2,1,0:T(8,128)(2,1)S(1)} collective-permute-done((bf16[8,16,512]{2,1,0:T(8,128)(2,1)S(1)}, bf16[8,16,512]{2,1,0:T(8,128)(2,1)S(1)}, u32[]{:S(2)}, u32[]{:S(2)}) %collective-permute-start.22) | collective-permute-done | bytes 131104 | tf_op jit(solution)/shard_map/ppermute | solution.py:258
  100.6 1.1 collective-permute-start.23
  101.7 1.7 %collective-permute-done.19 = bf16[8,16,512]{2,1,0:T(8,128)(2,1)S(1)} collective-permute-done((bf16[8,16,512]{2,1,0:T(8,128)(2,1)S(1)}, bf16[8,16,512]{2,1,0:T(8,128)(2,1)S(1)}, u32[]{:S(2)}, u32[]{:S(2)}) %collective-permute-start.19) | collective-permute-done | bytes 131104 | tf_op jit(solution)/shard_map/ppermute | solution.py:258
  103.4 1.1 collective-permute-start.20
  104.5 1.9 %collective-permute-done.23.refs_3_ = bf16[4,16,512]{2,1,0:T(8,128)(2,1)S(1)} collective-permute-done((bf16[4,16,512]{2,1,0:T(8,128)(2,1)S(1)}, bf16[4,16,512]{2,1,0:T(8,128)(2,1)S(1)}, u32[]{:S(2)}, u32[]{:S(2)}) %collective-permute-start.23) | collective-permute-done | bytes 65568 | tf_op jit(solution)/shard_map/ppermute | solution.py:258
  106.4 2.8 %collective-permute-done.20.refs_1_ = bf16[4,16,512]{2,1,0:T(8,128)(2,1)S(1)} collective-permute-done((bf16[4,16,512]{2,1,0:T(8,128)(2,1)S(1)}, bf16[4,16,512]{2,1,0:T(8,128)(2,1)S(1)}, u32[]{:S(2)}, u32[]{:S(2)}) %collective-permute-start.20) | collective-permute-done | bytes 65568 | tf_op jit(solution)/shard_map/ppermute | solution.py:258
  109.2 0.8 finish.1
  110.0 1.5 %collective-permute-start.25 = (f32[4,1024]{1,0:T(4,128)S(1)}, f32[4,1024]{1,0:T(4,128)S(1)}, u32[]{:S(2)}, u32[]{:S(2)}) collective-permute-start(f32[4,1024]{1,0:T(4,128)S(1)} %get-tuple-element.43), channel_id=1, source_target_pairs={{0,2},{1,3},{2,0},{3,1},{4,6},{5,7},{6,4},{7,5},{8,10},{9,11},{10,... | collective-permute-start | bytes 49160 | tf_op jit(solution)/shard_map/ppermute | solution.py:447
  111.5 0.4 collective-permute-start.26
  111.9 1.9 %collective-permute-done.25 = f32[4,1024]{1,0:T(4,128)S(1)} collective-permute-done((f32[4,1024]{1,0:T(4,128)S(1)}, f32[4,1024]{1,0:T(4,128)S(1)}, u32[]{:S(2)}, u32[]{:S(2)}) %collective-permute-start.25) | collective-permute-done | bytes 16416 | tf_op jit(solution)/shard_map/ppermute | solution.py:447
  113.8 0.9 collective-permute-done.26
  114.7 0.6 add_multiply_fusion
  (28 shorter events, 0.8 us)
Async XLA Ops:
  0.6 15.9 %copy-start = (f32[4,1024]{1,0:T(4,128)S(1)}, f32[4,1024]{1,0:T(4,128)}, u32[]{:S(2)}) copy-start(f32[4,1024]{1,0:T(4,128)} %contrast_ref.19) | copy-start | bytes 49156
  0.6 26.2 %copy-start.2 = (f32[4,16,1024]{2,1,0:T(8,128)S(1)}, f32[4,16,1024]{2,1,0:T(8,128)}, u32[]{:S(2)}) copy-start(f32[4,16,1024]{2,1,0:T(8,128)} %refs_3_.1) | copy-start | bytes 786436
  13.4 7.4 %collective-permute-start = (bf16[16,16,512]{2,1,0:T(8,128)(2,1)S(1)}, bf16[16,16,512]{2,1,0:T(8,128)(2,1)S(1)}, u32[]{:S(2)}, u32[]{:S(2)}) collective-permute-start(bf16[16,16,512]{2,1,0:T(8,128)(2,1)S(1)} %get-tuple-element.25), channel_id=1, source_target_pairs={{0,4},{1,9},{2,6},{3,11},{4,0},{5,13},{6,2},{7,15},{8,12},{9,1},{1... | collective-permute-start | bytes 786440 | tf_op jit(solution)/shard_map/ppermute | solution.py:258
  16.4 7.8 %collective-permute-start.3 = (bf16[16,16,512]{2,1,0:T(8,128)(2,1)S(1)}, bf16[16,16,512]{2,1,0:T(8,128)(2,1)S(1)}, u32[]{:S(2)}, u32[]{:S(2)}) collective-permute-start(bf16[16,16,512]{2,1,0:T(8,128)(2,1)S(1)} %get-tuple-element.28), channel_id=1, source_target_pairs={{0,4},{1,9},{2,6},{3,11},{4,0},{5,13},{6,2},{7,15},{8,12},{9,1},{1... | collective-permute-start | bytes 786440 | tf_op jit(solution)/shard_map/ppermute | solution.py:258
  20.9 6.0 %collective-permute-start.1 = (bf16[8,16,512]{2,1,0:T(8,128)(2,1)S(1)}, bf16[8,16,512]{2,1,0:T(8,128)(2,1)S(1)}, u32[]{:S(2)}, u32[]{:S(2)}) collective-permute-start(bf16[8,16,512]{2,1,0:T(8,128)(2,1)S(1)} %get-tuple-element.58), channel_id=1, source_target_pairs={{0,8},{1,5},{2,10},{3,7},{4,12},{5,1},{6,14},{7,3},{8,0},{9,13},{1... | collective-permute-start | bytes 393224 | tf_op jit(solution)/shard_map/ppermute | solution.py:258
  24.3 6.1 %collective-permute-start.4 = (bf16[8,16,512]{2,1,0:T(8,128)(2,1)S(1)}, bf16[8,16,512]{2,1,0:T(8,128)(2,1)S(1)}, u32[]{:S(2)}, u32[]{:S(2)}) collective-permute-start(bf16[8,16,512]{2,1,0:T(8,128)(2,1)S(1)} %get-tuple-element.56), channel_id=1, source_target_pairs={{0,8},{1,5},{2,10},{3,7},{4,12},{5,1},{6,14},{7,3},{8,0},{9,13},{1... | collective-permute-start | bytes 393224 | tf_op jit(solution)/shard_map/ppermute | solution.py:258
  26.9 7.1 %collective-permute-start.2 = (bf16[4,16,512]{2,1,0:T(8,128)(2,1)S(1)}, bf16[4,16,512]{2,1,0:T(8,128)(2,1)S(1)}, u32[]{:S(2)}, u32[]{:S(2)}) collective-permute-start(bf16[4,16,512]{2,1,0:T(8,128)(2,1)S(1)} %get-tuple-element.74), channel_id=1, source_target_pairs={{0,16},{1,17},{2,18},{3,19},{4,20},{5,21},{6,22},{7,23},{8,24},{9,... | collective-permute-start | bytes 196616 | tf_op jit(solution)/shard_map/ppermute | solution.py:258
  30.5 5.5 %collective-permute-start.5 = (bf16[4,16,512]{2,1,0:T(8,128)(2,1)S(1)}, bf16[4,16,512]{2,1,0:T(8,128)(2,1)S(1)}, u32[]{:S(2)}, u32[]{:S(2)}) collective-permute-start(bf16[4,16,512]{2,1,0:T(8,128)(2,1)S(1)} %get-tuple-element.72), channel_id=1, source_target_pairs={{0,16},{1,17},{2,18},{3,19},{4,20},{5,21},{6,22},{7,23},{8,24},{9,... | collective-permute-start | bytes 196616 | tf_op jit(solution)/shard_map/ppermute | solution.py:258
  38.0 6.7 %collective-permute-start.6 = (bf16[16,16,512]{2,1,0:T(8,128)(2,1)S(1)}, bf16[16,16,512]{2,1,0:T(8,128)(2,1)S(1)}, u32[]{:S(2)}, u32[]{:S(2)}) collective-permute-start(bf16[16,16,512]{2,1,0:T(8,128)(2,1)S(1)} %get-tuple-element.31), channel_id=1, source_target_pairs={{0,4},{1,9},{2,6},{3,11},{4,0},{5,13},{6,2},{7,15},{8,12},{9,1},{1... | collective-permute-start | bytes 786440 | tf_op jit(solution)/shard_map/ppermute | solution.py:258
  40.4 9.6 %collective-permute-start.9 = (bf16[16,16,512]{2,1,0:T(8,128)(2,1)S(1)}, bf16[16,16,512]{2,1,0:T(8,128)(2,1)S(1)}, u32[]{:S(2)}, u32[]{:S(2)}) collective-permute-start(bf16[16,16,512]{2,1,0:T(8,128)(2,1)S(1)} %more.3), channel_id=1, source_target_pairs={{0,4},{1,9},{2,6},{3,11},{4,0},{5,13},{6,2},{7,15},{8,12},{9,1},{1... | collective-permute-start | bytes 786440 | tf_op jit(solution)/shard_map/ppermute | solution.py:258
  44.8 7.3 %collective-permute-start.7 = (bf16[8,16,512]{2,1,0:T(8,128)(2,1)S(1)}, bf16[8,16,512]{2,1,0:T(8,128)(2,1)S(1)}, u32[]{:S(2)}, u32[]{:S(2)}) collective-permute-start(bf16[8,16,512]{2,1,0:T(8,128)(2,1)S(1)} %get-tuple-element.54), channel_id=1, source_target_pairs={{0,8},{1,5},{2,10},{3,7},{4,12},{5,1},{6,14},{7,3},{8,0},{9,13},{1... | collective-permute-start | bytes 393224 | tf_op jit(solution)/shard_map/ppermute | solution.py:258
  50.1 5.7 %collective-permute-start.10 = (bf16[8,16,512]{2,1,0:T(8,128)(2,1)S(1)}, bf16[8,16,512]{2,1,0:T(8,128)(2,1)S(1)}, u32[]{:S(2)}, u32[]{:S(2)}) collective-permute-start(bf16[8,16,512]{2,1,0:T(8,128)(2,1)S(1)} %get-tuple-element.52), channel_id=1, source_target_pairs={{0,8},{1,5},{2,10},{3,7},{4,12},{5,1},{6,14},{7,3},{8,0},{9,13},{1... | collective-permute-start | bytes 393224 | tf_op jit(solution)/shard_map/ppermute | solution.py:258
  52.1 5.7 %collective-permute-start.8 = (bf16[4,16,512]{2,1,0:T(8,128)(2,1)S(1)}, bf16[4,16,512]{2,1,0:T(8,128)(2,1)S(1)}, u32[]{:S(2)}, u32[]{:S(2)}) collective-permute-start(bf16[4,16,512]{2,1,0:T(8,128)(2,1)S(1)} %get-tuple-element.70), channel_id=1, source_target_pairs={{0,16},{1,17},{2,18},{3,19},{4,20},{5,21},{6,22},{7,23},{8,24},{9,... | collective-permute-start | bytes 196616 | tf_op jit(solution)/shard_map/ppermute | solution.py:258
  55.9 5.3 %collective-permute-start.11 = (bf16[4,16,512]{2,1,0:T(8,128)(2,1)S(1)}, bf16[4,16,512]{2,1,0:T(8,128)(2,1)S(1)}, u32[]{:S(2)}, u32[]{:S(2)}) collective-permute-start(bf16[4,16,512]{2,1,0:T(8,128)(2,1)S(1)} %get-tuple-element.68), channel_id=1, source_target_pairs={{0,16},{1,17},{2,18},{3,19},{4,20},{5,21},{6,22},{7,23},{8,24},{9,... | collective-permute-start | bytes 196616 | tf_op jit(solution)/shard_map/ppermute | solution.py:258
  63.2 8.2 %collective-permute-start.12 = (bf16[16,16,512]{2,1,0:T(8,128)(2,1)S(1)}, bf16[16,16,512]{2,1,0:T(8,128)(2,1)S(1)}, u32[]{:S(2)}, u32[]{:S(2)}) collective-permute-start(bf16[16,16,512]{2,1,0:T(8,128)(2,1)S(1)} %get-tuple-element.35), channel_id=1, source_target_pairs={{0,4},{1,9},{2,6},{3,11},{4,0},{5,13},{6,2},{7,15},{8,12},{9,1},{1... | collective-permute-start | bytes 786440 | tf_op jit(solution)/shard_map/ppermute | solution.py:258
  65.6 8.6 %collective-permute-start.15 = (bf16[16,16,512]{2,1,0:T(8,128)(2,1)S(1)}, bf16[16,16,512]{2,1,0:T(8,128)(2,1)S(1)}, u32[]{:S(2)}, u32[]{:S(2)}) collective-permute-start(bf16[16,16,512]{2,1,0:T(8,128)(2,1)S(1)} %more.4), channel_id=1, source_target_pairs={{0,4},{1,9},{2,6},{3,11},{4,0},{5,13},{6,2},{7,15},{8,12},{9,1},{1... | collective-permute-start | bytes 786440 | tf_op jit(solution)/shard_map/ppermute | solution.py:258
  71.4 5.7 %collective-permute-start.13 = (bf16[8,16,512]{2,1,0:T(8,128)(2,1)S(1)}, bf16[8,16,512]{2,1,0:T(8,128)(2,1)S(1)}, u32[]{:S(2)}, u32[]{:S(2)}) collective-permute-start(bf16[8,16,512]{2,1,0:T(8,128)(2,1)S(1)} %get-tuple-element.50), channel_id=1, source_target_pairs={{0,8},{1,5},{2,10},{3,7},{4,12},{5,1},{6,14},{7,3},{8,0},{9,13},{1... | collective-permute-start | bytes 393224 | tf_op jit(solution)/shard_map/ppermute | solution.py:258
  74.3 5.0 %collective-permute-start.16 = (bf16[8,16,512]{2,1,0:T(8,128)(2,1)S(1)}, bf16[8,16,512]{2,1,0:T(8,128)(2,1)S(1)}, u32[]{:S(2)}, u32[]{:S(2)}) collective-permute-start(bf16[8,16,512]{2,1,0:T(8,128)(2,1)S(1)} %get-tuple-element.48), channel_id=1, source_target_pairs={{0,8},{1,5},{2,10},{3,7},{4,12},{5,1},{6,14},{7,3},{8,0},{9,13},{1... | collective-permute-start | bytes 393224 | tf_op jit(solution)/shard_map/ppermute | solution.py:258
  77.2 5.9 %collective-permute-start.14 = (bf16[4,16,512]{2,1,0:T(8,128)(2,1)S(1)}, bf16[4,16,512]{2,1,0:T(8,128)(2,1)S(1)}, u32[]{:S(2)}, u32[]{:S(2)}) collective-permute-start(bf16[4,16,512]{2,1,0:T(8,128)(2,1)S(1)} %get-tuple-element.66), channel_id=1, source_target_pairs={{0,16},{1,17},{2,18},{3,19},{4,20},{5,21},{6,22},{7,23},{8,24},{9,... | collective-permute-start | bytes 196616 | tf_op jit(solution)/shard_map/ppermute | solution.py:258
  79.4 5.8 %collective-permute-start.17 = (bf16[4,16,512]{2,1,0:T(8,128)(2,1)S(1)}, bf16[4,16,512]{2,1,0:T(8,128)(2,1)S(1)}, u32[]{:S(2)}, u32[]{:S(2)}) collective-permute-start(bf16[4,16,512]{2,1,0:T(8,128)(2,1)S(1)} %get-tuple-element.64), channel_id=1, source_target_pairs={{0,16},{1,17},{2,18},{3,19},{4,20},{5,21},{6,22},{7,23},{8,24},{9,... | collective-permute-start | bytes 196616 | tf_op jit(solution)/shard_map/ppermute | solution.py:258
  87.8 7.7 %collective-permute-start.21 = (bf16[16,16,512]{2,1,0:T(8,128)(2,1)S(1)}, bf16[16,16,512]{2,1,0:T(8,128)(2,1)S(1)}, u32[]{:S(2)}, u32[]{:S(2)}) collective-permute-start(bf16[16,16,512]{2,1,0:T(8,128)(2,1)S(1)} %more.5), channel_id=1, source_target_pairs={{0,4},{1,9},{2,6},{3,11},{4,0},{5,13},{6,2},{7,15},{8,12},{9,1},{1... | collective-permute-start | bytes 786440 | tf_op jit(solution)/shard_map/ppermute | solution.py:258
  89.4 19.8 %copy-start.1 = (bf16[4,16,1024]{2,1,0:T(8,128)(2,1)S(1)}, bf16[4,16,1024]{2,1,0:T(8,128)(2,1)}, u32[]{:S(2)}) copy-start(bf16[4,16,1024]{2,1,0:T(8,128)(2,1)} %forward_ref.1) | copy-start | bytes 393220
  89.4 8.9 %collective-permute-start.18 = (bf16[16,16,512]{2,1,0:T(8,128)(2,1)S(1)}, bf16[16,16,512]{2,1,0:T(8,128)(2,1)S(1)}, u32[]{:S(2)}, u32[]{:S(2)}) collective-permute-start(bf16[16,16,512]{2,1,0:T(8,128)(2,1)S(1)} %get-tuple-element.39), channel_id=1, source_target_pairs={{0,4},{1,9},{2,6},{3,11},{4,0},{5,13},{6,2},{7,15},{8,12},{9,1},{1... | collective-permute-start | bytes 786440 | tf_op jit(solution)/shard_map/ppermute | solution.py:258
  95.5 5.0 %collective-permute-start.22 = (bf16[8,16,512]{2,1,0:T(8,128)(2,1)S(1)}, bf16[8,16,512]{2,1,0:T(8,128)(2,1)S(1)}, u32[]{:S(2)}, u32[]{:S(2)}) collective-permute-start(bf16[8,16,512]{2,1,0:T(8,128)(2,1)S(1)} %get-tuple-element.44), channel_id=1, source_target_pairs={{0,8},{1,5},{2,10},{3,7},{4,12},{5,1},{6,14},{7,3},{8,0},{9,13},{1... | collective-permute-start | bytes 393224 | tf_op jit(solution)/shard_map/ppermute | solution.py:258
  98.3 5.0 %collective-permute-start.19 = (bf16[8,16,512]{2,1,0:T(8,128)(2,1)S(1)}, bf16[8,16,512]{2,1,0:T(8,128)(2,1)S(1)}, u32[]{:S(2)}, u32[]{:S(2)}) collective-permute-start(bf16[8,16,512]{2,1,0:T(8,128)(2,1)S(1)} %get-tuple-element.46), channel_id=1, source_target_pairs={{0,8},{1,5},{2,10},{3,7},{4,12},{5,1},{6,14},{7,3},{8,0},{9,13},{1... | collective-permute-start | bytes 393224 | tf_op jit(solution)/shard_map/ppermute | solution.py:258
  100.6 5.8 %collective-permute-start.23 = (bf16[4,16,512]{2,1,0:T(8,128)(2,1)S(1)}, bf16[4,16,512]{2,1,0:T(8,128)(2,1)S(1)}, u32[]{:S(2)}, u32[]{:S(2)}) collective-permute-start(bf16[4,16,512]{2,1,0:T(8,128)(2,1)S(1)} %get-tuple-element.60), channel_id=1, source_target_pairs={{0,16},{1,17},{2,18},{3,19},{4,20},{5,21},{6,22},{7,23},{8,24},{9,... | collective-permute-start | bytes 196616 | tf_op jit(solution)/shard_map/ppermute | solution.py:258
  103.4 5.8 %collective-permute-start.20 = (bf16[4,16,512]{2,1,0:T(8,128)(2,1)S(1)}, bf16[4,16,512]{2,1,0:T(8,128)(2,1)S(1)}, u32[]{:S(2)}, u32[]{:S(2)}) collective-permute-start(bf16[4,16,512]{2,1,0:T(8,128)(2,1)S(1)} %get-tuple-element.62), channel_id=1, source_target_pairs={{0,16},{1,17},{2,18},{3,19},{4,20},{5,21},{6,22},{7,23},{8,24},{9,... | collective-permute-start | bytes 196616 | tf_op jit(solution)/shard_map/ppermute | solution.py:258
  110.0 1.9 %collective-permute-start.24 = (f32[4,1024]{1,0:T(4,128)S(1)}, f32[4,1024]{1,0:T(4,128)S(1)}, u32[]{:S(2)}, u32[]{:S(2)}) collective-permute-start(f32[4,1024]{1,0:T(4,128)S(1)} %get-tuple-element.43), channel_id=1, source_target_pairs={{0,1},{1,0},{2,3},{3,2},{4,5},{5,4},{6,7},{7,6},{8,9},{9,8},{10,11... | collective-permute-start | bytes 49160 | tf_op jit(solution)/shard_map/ppermute | solution.py:447
  110.0 3.7 %collective-permute-start.25 = (f32[4,1024]{1,0:T(4,128)S(1)}, f32[4,1024]{1,0:T(4,128)S(1)}, u32[]{:S(2)}, u32[]{:S(2)}) collective-permute-start(f32[4,1024]{1,0:T(4,128)S(1)} %get-tuple-element.43), channel_id=1, source_target_pairs={{0,2},{1,3},{2,0},{3,1},{4,6},{5,7},{6,4},{7,5},{8,10},{9,11},{10,... | collective-permute-start | bytes 49160 | tf_op jit(solution)/shard_map/ppermute | solution.py:447
  111.5 3.2 %collective-permute-start.26 = (f32[4,1024]{1,0:T(4,128)S(1)}, f32[4,1024]{1,0:T(4,128)S(1)}, u32[]{:S(2)}, u32[]{:S(2)}) collective-permute-start(f32[4,1024]{1,0:T(4,128)S(1)} %get-tuple-element.43), channel_id=1, source_target_pairs={{0,3},{1,2},{2,1},{3,0},{4,7},{5,6},{6,5},{7,4},{8,11},{9,10},{10,... | collective-permute-start | bytes 49160 | tf_op jit(solution)/shard_map/ppermute | solution.py:447

commit v9 on v7

--- a/solution.py
+++ b/solution.py
@@ -193,31 +193,37 @@
         out_ref[group] = pick_rows(every, code, sources, rows_dev)
 
 
-def ready_kernel(dims, late, parts, code_ref, contrast_ref, sum_ref, base_ref, came_ref, *refs):
+def complete(dims, late, group, low, code_ref, sum_ref, u_ref):
+    rows_dev, _ = dims
+    deep = code_ref.shape[1]
+    first, width, _ = late
+    every = times_u(low, u_ref[pl.ds(group * deep, deep), pl.ds(first, width)])
+    code = code_ref[pl.ds(group, 1), :]
+    coeff = sum_ref[group] + pick_rows(every, code, sum_ref.shape[1], rows_dev)
+    return by_slot(coeff, code, rows_dev)
+
+
+def step_kernel(dims, late, known, todo, parts, code_ref, contrast_ref, sum_ref, *refs):
+    base_ref, came_ref, u_ref, v_ref = refs[:4]
+    held, refs = refs[4 : 4 + len(known)], refs[4 + len(known) :]
     rows_dev, peers = dims
-    u_ref, v_ref, lhs_ref = refs[:3]
-    outs = refs[3:]
-    deep = code_ref.shape[1]
-    sources = sum_ref.shape[1]
     low = low_field(base_ref, came_ref, contrast_ref, late)
-    first, width, _ = late
-    for group in reversed(range(peers)):
-        every = times_u(low, u_ref[pl.ds(group * deep, deep), pl.ds(first, width)])
-        code = code_ref[pl.ds(group, 1), :]
-        coeff = sum_ref[group] + pick_rows(every, code, sources, rows_dev)
-        lhs = by_slot(coeff, code, rows_dev)
-        lhs_ref[group] = lhs
-        for out, part in zip(outs, parts):
-            if spot(part[2], group) >= peers // 2:
-                put_terms(lhs, v_ref, group, part, (None, out), rows_dev, peers)
-
-
-def more_kernel(dims, parts, lhs_ref, v_ref, *outs):
-    rows_dev, peers = dims
-    for out, (part, kept) in zip(outs, parts):
-        for group in range(peers):
+    ready = {group: (ref, i) for ref, some in zip(held, known) for i, group in enumerate(some)}
+    outs, lhs_ref = refs[: len(parts)], refs[len(parts) :]
+
+    def put(lhs, group):
+        for out, (part, kept) in zip(outs, parts):
             if (spot(part[2], group) < peers // 2) == kept:
-                put_terms(lhs_ref[group], v_ref, group, part, (out, out), rows_dev, peers)
+                put_terms(lhs, v_ref, group, part, (out, out), rows_dev, peers)
+
+    for i, group in enumerate(todo):
+        lhs = complete(dims, late, group, low, code_ref, sum_ref, u_ref)
+        if lhs_ref:
+            lhs_ref[0][i] = lhs
+        put(lhs, group)
+    for group, (ref, i) in ready.items():
+        if any((spot(part[2], group) < peers // 2) == kept for part, kept in parts):
+            put(ref[i], group)
 
 
 def finish_kernel(parts, contrast_ref, forward_ref, *refs):
@@ -259,8 +265,12 @@
     tiles = rows_dev * tiles_row
     deep = tiles // peers * rank_max
     parts = parts_of(unknowns, peers)
-    first_sent, late = [0], 1
+    late = 1
     early = [i for i in range(len(parts)) if i != late]
+    leaving, staying = [], list(range(peers))
+    for part in parts:
+        leaving.append([x for x in staying if spot(part[2], x) >= peers // 2])
+        staying = [x for x in staying if x not in leaving[-1]]
     half = (peers // 2 * rows_dev, sources)
     sent = [jax.ShapeDtypeStruct((*half, part[1]), jnp.bfloat16) for part in parts]
     kept = [jax.ShapeDtypeStruct((*half, part[1]), jnp.float32) for part in parts]
@@ -305,30 +315,30 @@
                 cost_estimate=cost(u.shape[0], unknowns // 2, sources),
                 name="early",
             )(code, contrast, *(x for i in early for x in (base[i], came[i])), in_vmem(u))
-            lhs, *some = pl.pallas_call(
-                functools.partial(ready_kernel, dims, parts[late], [parts[i] for i in first_sent]),
-                out_shape=[jax.ShapeDtypeStruct((peers, rows_dev * sources, deep), jnp.bfloat16)]
-                + [sent[i] for i in first_sent],
-                in_specs=vmem(7),
-                out_specs=vmem(1 + len(first_sent)),
-                compiler_params=params(),
-                cost_estimate=cost(u.shape[0], unknowns // 2, sources),
-                name="ready",
-            )(code, contrast, coeff, base[late], came[late], in_vmem(u), in_vmem(v))
-            goes, keeps = [*some], []
-            for names, shapes, to in (
-                [[(parts[1], False)], sent[1:], goes],
-                [[(part, True) for part in parts], kept, keeps],
+            state = (code, contrast, coeff, base[late], came[late], in_vmem(u), in_vmem(v))
+            known, held, made = [], [], []
+            for todo, names, shapes in (
+                (leaving[0], [(parts[0], False)], [sent[0]]),
+                (leaving[1], [(parts[1], False)], [sent[1]]),
+                (staying, [(part, True) for part in parts], kept),
             ):
-                to += pl.pallas_call(
-                    functools.partial(more_kernel, dims, names),
-                    out_shape=shapes,
-                    in_specs=vmem(2),
-                    out_specs=vmem(len(shapes)),
+                hand = []
+                if todo is not staying:
+                    shape = (len(todo), rows_dev * sources, deep)
+                    hand = [jax.ShapeDtypeStruct(shape, jnp.bfloat16)]
+                got = pl.pallas_call(
+                    functools.partial(step_kernel, dims, parts[late], [*known], todo, names),
+                    out_shape=[*shapes, *hand],
+                    in_specs=vmem(7 + len(held)),
+                    out_specs=vmem(len(shapes) + len(hand)),
                     compiler_params=params(),
-                    cost_estimate=cost(u.shape[0], unknowns // 4 * len(shapes), sources),
-                    name="more",
-                )(lhs, in_vmem(v))
+                    cost_estimate=cost(u.shape[0], unknowns // 2, sources),
+                    name="step",
+                )(*state, *held)
+                made += got[: len(shapes)]
+                known.append(todo)
+                held += got[len(shapes) :]
+            goes, keeps = made[:2], made[2:]
         base, came = [None] * len(parts), [None] * len(parts)
         levels = len(parts[0][2])
         for level in range(levels):
@@ -437,7 +447,7 @@
     tiles = rows_dev * tiles_row
     cap = (tiles + peers - 1) // peers
     dense = (
-        1 < peers <= 8
+        4 <= peers <= 8
         and cap < 16
         and peers & (peers - 1) == 0
         and tiles == cap * peers

time: 114 us -> 112 us (0.982)
  waiting for transfers between devices: 46 us -> 38.6 us
  starting transfers between devices: 30.9 us -> 35.1 us
    ppermute x24, waiting for transfers between devices: 44.1 us -> 36.7 us  [swap(): return lax.ppermute(x, ('rows', 'src'), pairs)]
    ppermute x24, starting transfers between devices: 29 us -> 33.2 us  [swap(): return lax.ppermute(x, ('rows', 'src'), pairs)]
    pallas_call x9, Pallas kernels: 14.4 us -> 15.6 us  [slot_sums(): pl.pallas_call(functools.partial(step_kernel, dims, parts[late], [*known]...]
  transfers between devices with their start and end apart: 27 -> 27, of which waited for: 20 -> 22; matrix products, arithmetic and copies ran while one was open for 1% -> 1% of each run, Pallas kernels for 10% -> 14%
where the time goes in v9:
time: 112 us; the launch traced here: 111 us
  waiting for transfers between devices  38.6 us (34%)
  Pallas kernels  35.3 us (32%)
  starting transfers between devices  35.1 us (31%)
  other arithmetic  1.58 us (1%)
    ppermute x24, waiting for transfers between devices, swap(): return lax.ppermute(x, ('rows', 'src'), pairs)  36.7 us
    ppermute x24, starting transfers between devices, swap(): return lax.ppermute(x, ('rows', 'src'), pairs)  33.2 us
    pallas_call x9, Pallas kernels, slot_sums(): pl.pallas_call(functools.partial(step_kernel, dims, parts[late], [*known]...  15.6 us
    pallas_call x1, Pallas kernels, slot_sums(): pl.pallas_call(functools.partial(start_kernel, (rows_dev, tiles_row, rank...  12.7 us
    pallas_call x3, Pallas kernels, slot_sums(): pl.pallas_call(functools.partial(early_kernel, dims, [parts[i] for i in e...  6.24 us
  transfers between devices with their start and end apart: 27, of which 22 were waited for; matrix products, arithmetic and copies ran while one was open for 1% of the time, Pallas kernels for 14%

profile of v9, /device:TPU:0, one launch (start us, length us, event | category | flops | bytes accessed | tf_op | source)
XLA Modules:
  0.0 111.4 jit_solution(3381050745297120114)
XLA Ops:
  0.7 12.7 %start.1 = (bf16[6144,1024]{1,0:T(8,128)(2,1)S(1)}, bf16[6144,1024]{1,0:T(8,128)(2,1)S(1)}, s32[8,768]{1,0:T(8,128)S(1)}, f32[16,16,512]{2,1,0:T(8,128)S(1)}, bf...) custom-call(s32[16,32]{1,0:T(8,128)} %bitcast.11, s32[32]{0:T(128)} %refs_1_.1, ...), custom_call_target="tpu_custom_call" | custom-call | flops 402653184 | bytes 25165824 | tf_op jit(solution)/shard_map/start/pallas_call | solution.py:280
  13.4 3.0 %collective-permute-start = (bf16[16,16,512]{2,1,0:T(8,128)(2,1)S(1)}, bf16[16,16,512]{2,1,0:T(8,128)(2,1)S(1)}, u32[]{:S(2)}, u32[]{:S(2)}) collective-permute-start(bf16[16,16,512]{2,1,0:T(8,128)(2,1)S(1)} %get-tuple-element.31), channel_id=1, source_target_pairs={{0,4},{1,9},{2,6},{3,11},{4,0},{5,13},{6,2},{7,15},{8,12},{9,1},{1... | collective-permute-start | bytes 786440 | tf_op jit(solution)/shard_map/ppermute | solution.py:256
  16.4 1.6 %collective-permute-start.3 = (bf16[16,16,512]{2,1,0:T(8,128)(2,1)S(1)}, bf16[16,16,512]{2,1,0:T(8,128)(2,1)S(1)}, u32[]{:S(2)}, u32[]{:S(2)}) collective-permute-start(bf16[16,16,512]{2,1,0:T(8,128)(2,1)S(1)} %get-tuple-element.34), channel_id=1, source_target_pairs={{0,8},{1,5},{2,10},{3,7},{4,12},{5,1},{6,14},{7,3},{8,0},{9,13},{1... | collective-permute-start | bytes 786440 | tf_op jit(solution)/shard_map/ppermute | solution.py:256
  18.0 5.0 %collective-permute-done = bf16[16,16,512]{2,1,0:T(8,128)(2,1)S(1)} collective-permute-done((bf16[16,16,512]{2,1,0:T(8,128)(2,1)S(1)}, bf16[16,16,512]{2,1,0:T(8,128)(2,1)S(1)}, u32[]{:S(2)}, u32[]{:S(2)}) %collective-permute-start) | collective-permute-done | bytes 262176 | tf_op jit(solution)/shard_map/ppermute | solution.py:256
  23.0 1.7 %collective-permute-start.1 = (bf16[8,16,512]{2,1,0:T(8,128)(2,1)S(1)}, bf16[8,16,512]{2,1,0:T(8,128)(2,1)S(1)}, u32[]{:S(2)}, u32[]{:S(2)}) collective-permute-start(bf16[8,16,512]{2,1,0:T(8,128)(2,1)S(1)} %get-tuple-element.70), channel_id=1, source_target_pairs={{0,8},{1,5},{2,10},{3,7},{4,12},{5,1},{6,14},{7,3},{8,0},{9,13},{1... | collective-permute-start | bytes 393224 | tf_op jit(solution)/shard_map/ppermute | solution.py:256
  24.8 1.7 %collective-permute-start.4 = (bf16[8,16,512]{2,1,0:T(8,128)(2,1)S(1)}, bf16[8,16,512]{2,1,0:T(8,128)(2,1)S(1)}, u32[]{:S(2)}, u32[]{:S(2)}) collective-permute-start(bf16[8,16,512]{2,1,0:T(8,128)(2,1)S(1)} %get-tuple-element.68), channel_id=1, source_target_pairs={{0,4},{1,9},{2,6},{3,11},{4,0},{5,13},{6,2},{7,15},{8,12},{9,1},{1... | collective-permute-start | bytes 393224 | tf_op jit(solution)/shard_map/ppermute | solution.py:256
  26.5 2.5 %collective-permute-done.1 = bf16[8,16,512]{2,1,0:T(8,128)(2,1)S(1)} collective-permute-done((bf16[8,16,512]{2,1,0:T(8,128)(2,1)S(1)}, bf16[8,16,512]{2,1,0:T(8,128)(2,1)S(1)}, u32[]{:S(2)}, u32[]{:S(2)}) %collective-permute-start.1) | collective-permute-done | bytes 131104 | tf_op jit(solution)/shard_map/ppermute | solution.py:256
  29.0 4.1 %collective-permute-start.2 = (bf16[4,16,512]{2,1,0:T(8,128)(2,1)S(1)}, bf16[4,16,512]{2,1,0:T(8,128)(2,1)S(1)}, u32[]{:S(2)}, u32[]{:S(2)}) collective-permute-start(bf16[4,16,512]{2,1,0:T(8,128)(2,1)S(1)} %get-tuple-element.86), channel_id=1, source_target_pairs={{0,16},{1,17},{2,18},{3,19},{4,20},{5,21},{6,22},{7,23},{8,24},{9,... | collective-permute-start | bytes 196616 | tf_op jit(solution)/shard_map/ppermute | solution.py:256
  33.2 0.1 collective-permute-start.5
  33.3 2.1 %collective-permute-done.2.refs_1_ = bf16[4,16,512]{2,1,0:T(8,128)(2,1)S(1)} collective-permute-done((bf16[4,16,512]{2,1,0:T(8,128)(2,1)S(1)}, bf16[4,16,512]{2,1,0:T(8,128)(2,1)S(1)}, u32[]{:S(2)}, u32[]{:S(2)}) %collective-permute-start.2) | collective-permute-done | bytes 65568 | tf_op jit(solution)/shard_map/ppermute | solution.py:256
  35.4 2.0 %early.3.sum_ref = f32[8,16,768]{2,1,0:T(8,128)S(1)} custom-call(s32[8,768]{1,0:T(8,128)S(1)} %get-tuple-element.29.code_ref, f32[4,1024]{1,0:T(4,128)S(1)} %copy-done, f32[4,16,512]{2,1,0:T(8,128)S(1)} %get-tuple-element.87.refs_0_, bf16[4,16,512]{2,1,0:T(8,128)(2,1)S(1)} %collective-permute-done.2.refs_1_, bf16[6144,1024]{1,0:T(8,128)(2,1)S(1)} %get-tuple-element.32.refs_2_), custom_call_target="tpu_custom_call" | custom-call | flops 100663296 | bytes 6291456 | tf_op jit(solution)/shard_map/early/pallas_call | solution.py:309
  37.4 1.0 collective-permute-done.5.refs_1_
  38.4 2.0 %step.9 = (bf16[16,16,512]{2,1,0:T(8,128)(2,1)S(1)}, bf16[4,64,768]{2,1,0:T(8,128)(2,1)S(1)}) custom-call(s32[8,768]{1,0:T(8,128)S(1)} %get-tuple-element.29.code_ref, f32[4,1024]{1,0:T(4,128)S(1)} %copy-done, f32[8,16,768]{2,1,0:T(8,128)S(1)} %early.3.sum_ref, f32[4,16,512]{2,1,0:T(8,128)S(1)} %get-tuple-element.85.refs_0_, ...), custom_call_target="tpu_custom_call" | custom-call | flops 100663296 | bytes 6291456 | tf_op jit(solution)/shard_map/step/pallas_call | solution.py:329
  40.4 1.4 %collective-permute-start.6 = (bf16[16,16,512]{2,1,0:T(8,128)(2,1)S(1)}, bf16[16,16,512]{2,1,0:T(8,128)(2,1)S(1)}, u32[]{:S(2)}, u32[]{:S(2)}) collective-permute-start(bf16[16,16,512]{2,1,0:T(8,128)(2,1)S(1)} %get-tuple-element.39), channel_id=1, source_target_pairs={{0,4},{1,9},{2,6},{3,11},{4,0},{5,13},{6,2},{7,15},{8,12},{9,1},{1... | collective-permute-start | bytes 786440 | tf_op jit(solution)/shard_map/ppermute | solution.py:256
  41.8 1.3 %step.10 = (bf16[16,16,512]{2,1,0:T(8,128)(2,1)S(1)}, bf16[2,64,768]{2,1,0:T(8,128)(2,1)S(1)}) custom-call(s32[8,768]{1,0:T(8,128)S(1)} %get-tuple-element.29.code_ref, f32[4,1024]{1,0:T(4,128)S(1)} %copy-done, f32[8,16,768]{2,1,0:T(8,128)S(1)} %early.3.sum_ref, f32[4,16,512]{2,1,0:T(8,128)S(1)} %get-tuple-element.85.refs_0_, ...), custom_call_target="tpu_custom_call" | custom-call | flops 100663296 | bytes 6291456 | tf_op jit(solution)/shard_map/step/pallas_call | solution.py:329
  43.2 1.9 %step.11 = (f32[16,16,512]{2,1,0:T(8,128)S(1)}, f32[16,16,512]{2,1,0:T(8,128)S(1)}) custom-call(s32[8,768]{1,0:T(8,128)S(1)} %get-tuple-element.29.code_ref, f32[4,1024]{1,0:T(4,128)S(1)} %copy-done, f32[8,16,768]{2,1,0:T(8,128)S(1)} %early.3.sum_ref, f32[4,16,512]{2,1,0:T(8,128)S(1)} %get-tuple-element.85.refs_0_, ...), custom_call_target="tpu_custom_call" | custom-call | flops 100663296 | bytes 6291456 | tf_op jit(solution)/shard_map/step/pallas_call | solution.py:329
  45.1 2.8 %collective-permute-done.6 = bf16[16,16,512]{2,1,0:T(8,128)(2,1)S(1)} collective-permute-done((bf16[16,16,512]{2,1,0:T(8,128)(2,1)S(1)}, bf16[16,16,512]{2,1,0:T(8,128)(2,1)S(1)}, u32[]{:S(2)}, u32[]{:S(2)}) %collective-permute-start.6) | collective-permute-done | bytes 262176 | tf_op jit(solution)/shard_map/ppermute | solution.py:256
  48.0 0.1 add_convert_fusion.5
  48.0 0.4 collective-permute-start.7
  48.5 1.5 %collective-permute-done.9 = bf16[16,16,512]{2,1,0:T(8,128)(2,1)S(1)} collective-permute-done((bf16[16,16,512]{2,1,0:T(8,128)(2,1)S(1)}, bf16[16,16,512]{2,1,0:T(8,128)(2,1)S(1)}, u32[]{:S(2)}, u32[]{:S(2)}) %collective-permute-start.9) | collective-permute-done | bytes 262176 | tf_op jit(solution)/shard_map/ppermute | solution.py:256
  49.9 0.1 add_convert_fusion.4
  50.0 2.5 %collective-permute-start.10 = (bf16[8,16,512]{2,1,0:T(8,128)(2,1)S(1)}, bf16[8,16,512]{2,1,0:T(8,128)(2,1)S(1)}, u32[]{:S(2)}, u32[]{:S(2)}) collective-permute-start(bf16[8,16,512]{2,1,0:T(8,128)(2,1)S(1)} %get-tuple-element.64), channel_id=1, source_target_pairs={{0,4},{1,9},{2,6},{3,11},{4,0},{5,13},{6,2},{7,15},{8,12},{9,1},{1... | collective-permute-start | bytes 393224 | tf_op jit(solution)/shard_map/ppermute | solution.py:256
  52.5 1.3 %collective-permute-done.7 = bf16[8,16,512]{2,1,0:T(8,128)(2,1)S(1)} collective-permute-done((bf16[8,16,512]{2,1,0:T(8,128)(2,1)S(1)}, bf16[8,16,512]{2,1,0:T(8,128)(2,1)S(1)}, u32[]{:S(2)}, u32[]{:S(2)}) %collective-permute-start.7) | collective-permute-done | bytes 131104 | tf_op jit(solution)/shard_map/ppermute | solution.py:256
  53.8 1.9 %collective-permute-start.8 = (bf16[4,16,512]{2,1,0:T(8,128)(2,1)S(1)}, bf16[4,16,512]{2,1,0:T(8,128)(2,1)S(1)}, u32[]{:S(2)}, u32[]{:S(2)}) collective-permute-start(bf16[4,16,512]{2,1,0:T(8,128)(2,1)S(1)} %get-tuple-element.82), channel_id=1, source_target_pairs={{0,16},{1,17},{2,18},{3,19},{4,20},{5,21},{6,22},{7,23},{8,24},{9,... | collective-permute-start | bytes 196616 | tf_op jit(solution)/shard_map/ppermute | solution.py:256
  55.8 2.2 %collective-permute-start.11 = (bf16[4,16,512]{2,1,0:T(8,128)(2,1)S(1)}, bf16[4,16,512]{2,1,0:T(8,128)(2,1)S(1)}, u32[]{:S(2)}, u32[]{:S(2)}) collective-permute-start(bf16[4,16,512]{2,1,0:T(8,128)(2,1)S(1)} %get-tuple-element.80), channel_id=1, source_target_pairs={{0,16},{1,17},{2,18},{3,19},{4,20},{5,21},{6,22},{7,23},{8,24},{9,... | collective-permute-start | bytes 196616 | tf_op jit(solution)/shard_map/ppermute | solution.py:256
  57.9 1.7 %collective-permute-done.8.refs_1_ = bf16[4,16,512]{2,1,0:T(8,128)(2,1)S(1)} collective-permute-done((bf16[4,16,512]{2,1,0:T(8,128)(2,1)S(1)}, bf16[4,16,512]{2,1,0:T(8,128)(2,1)S(1)}, u32[]{:S(2)}, u32[]{:S(2)}) %collective-permute-start.8) | collective-permute-done | bytes 65568 | tf_op jit(solution)/shard_map/ppermute | solution.py:256
  59.7 2.2 %early.4.sum_ref = f32[8,16,768]{2,1,0:T(8,128)S(1)} custom-call(s32[8,768]{1,0:T(8,128)S(1)} %get-tuple-element.29.code_ref, f32[4,1024]{1,0:T(4,128)S(1)} %copy-done, f32[4,16,512]{2,1,0:T(8,128)S(1)} %get-tuple-element.83.refs_0_, bf16[4,16,512]{2,1,0:T(8,128)(2,1)S(1)} %collective-permute-done.8.refs_1_, bf16[6144,1024]{1,0:T(8,128)(2,1)S(1)} %get-tuple-element.32.refs_2_), custom_call_target="tpu_custom_call" | custom-call | flops 100663296 | bytes 6291456 | tf_op jit(solution)/shard_map/early/pallas_call | solution.py:309
  61.9 2.0 %step.12 = (bf16[16,16,512]{2,1,0:T(8,128)(2,1)S(1)}, bf16[4,64,768]{2,1,0:T(8,128)(2,1)S(1)}) custom-call(s32[8,768]{1,0:T(8,128)S(1)} %get-tuple-element.29.code_ref, f32[4,1024]{1,0:T(4,128)S(1)} %copy-done, f32[8,16,768]{2,1,0:T(8,128)S(1)} %early.4.sum_ref, f32[4,16,512]{2,1,0:T(8,128)S(1)} %get-tuple-element.81.refs_0_, ...), custom_call_target="tpu_custom_call" | custom-call | flops 100663296 | bytes 6291456 | tf_op jit(solution)/shard_map/step/pallas_call | solution.py:329
  63.8 1.7 %collective-permute-start.12 = (bf16[16,16,512]{2,1,0:T(8,128)(2,1)S(1)}, bf16[16,16,512]{2,1,0:T(8,128)(2,1)S(1)}, u32[]{:S(2)}, u32[]{:S(2)}) collective-permute-start(bf16[16,16,512]{2,1,0:T(8,128)(2,1)S(1)} %get-tuple-element.45), channel_id=1, source_target_pairs={{0,4},{1,9},{2,6},{3,11},{4,0},{5,13},{6,2},{7,15},{8,12},{9,1},{1... | collective-permute-start | bytes 786440 | tf_op jit(solution)/shard_map/ppermute | solution.py:256
  65.5 1.3 %step.13 = (bf16[16,16,512]{2,1,0:T(8,128)(2,1)S(1)}, bf16[2,64,768]{2,1,0:T(8,128)(2,1)S(1)}) custom-call(s32[8,768]{1,0:T(8,128)S(1)} %get-tuple-element.29.code_ref, f32[4,1024]{1,0:T(4,128)S(1)} %copy-done, f32[8,16,768]{2,1,0:T(8,128)S(1)} %early.4.sum_ref, f32[4,16,512]{2,1,0:T(8,128)S(1)} %get-tuple-element.81.refs_0_, ...), custom_call_target="tpu_custom_call" | custom-call | flops 100663296 | bytes 6291456 | tf_op jit(solution)/shard_map/step/pallas_call | solution.py:329
  66.9 1.9 %step.14 = (f32[16,16,512]{2,1,0:T(8,128)S(1)}, f32[16,16,512]{2,1,0:T(8,128)S(1)}) custom-call(s32[8,768]{1,0:T(8,128)S(1)} %get-tuple-element.29.code_ref, f32[4,1024]{1,0:T(4,128)S(1)} %copy-done, f32[8,16,768]{2,1,0:T(8,128)S(1)} %early.4.sum_ref, f32[4,16,512]{2,1,0:T(8,128)S(1)} %get-tuple-element.81.refs_0_, ...), custom_call_target="tpu_custom_call" | custom-call | flops 100663296 | bytes 6291456 | tf_op jit(solution)/shard_map/step/pallas_call | solution.py:329
  68.8 1.5 %collective-permute-done.12 = bf16[16,16,512]{2,1,0:T(8,128)(2,1)S(1)} collective-permute-done((bf16[16,16,512]{2,1,0:T(8,128)(2,1)S(1)}, bf16[16,16,512]{2,1,0:T(8,128)(2,1)S(1)}, u32[]{:S(2)}, u32[]{:S(2)}) %collective-permute-start.12) | collective-permute-done | bytes 262176 | tf_op jit(solution)/shard_map/ppermute | solution.py:256
  70.3 0.1 add_convert_fusion.3
  70.3 0.6 collective-permute-start.13
  71.0 3.0 %collective-permute-done.15 = bf16[16,16,512]{2,1,0:T(8,128)(2,1)S(1)} collective-permute-done((bf16[16,16,512]{2,1,0:T(8,128)(2,1)S(1)}, bf16[16,16,512]{2,1,0:T(8,128)(2,1)S(1)}, u32[]{:S(2)}, u32[]{:S(2)}) %collective-permute-start.15) | collective-permute-done | bytes 262176 | tf_op jit(solution)/shard_map/ppermute | solution.py:256
  74.0 0.1 add_convert_fusion.2
  74.0 1.2 %collective-permute-start.16 = (bf16[8,16,512]{2,1,0:T(8,128)(2,1)S(1)}, bf16[8,16,512]{2,1,0:T(8,128)(2,1)S(1)}, u32[]{:S(2)}, u32[]{:S(2)}) collective-permute-start(bf16[8,16,512]{2,1,0:T(8,128)(2,1)S(1)} %get-tuple-element.60), channel_id=1, source_target_pairs={{0,4},{1,9},{2,6},{3,11},{4,0},{5,13},{6,2},{7,15},{8,12},{9,1},{1... | collective-permute-start | bytes 393224 | tf_op jit(solution)/shard_map/ppermute | solution.py:256
  75.2 0.1 collective-permute-done.13
  75.4 2.1 %collective-permute-start.14 = (bf16[4,16,512]{2,1,0:T(8,128)(2,1)S(1)}, bf16[4,16,512]{2,1,0:T(8,128)(2,1)S(1)}, u32[]{:S(2)}, u32[]{:S(2)}) collective-permute-start(bf16[4,16,512]{2,1,0:T(8,128)(2,1)S(1)} %get-tuple-element.78), channel_id=1, source_target_pairs={{0,16},{1,17},{2,18},{3,19},{4,20},{5,21},{6,22},{7,23},{8,24},{9,... | collective-permute-start | bytes 196616 | tf_op jit(solution)/shard_map/ppermute | solution.py:256
  77.5 1.6 %collective-permute-done.16 = bf16[8,16,512]{2,1,0:T(8,128)(2,1)S(1)} collective-permute-done((bf16[8,16,512]{2,1,0:T(8,128)(2,1)S(1)}, bf16[8,16,512]{2,1,0:T(8,128)(2,1)S(1)}, u32[]{:S(2)}, u32[]{:S(2)}) %collective-permute-start.16) | collective-permute-done | bytes 131104 | tf_op jit(solution)/shard_map/ppermute | solution.py:256
  79.1 1.8 %collective-permute-start.17 = (bf16[4,16,512]{2,1,0:T(8,128)(2,1)S(1)}, bf16[4,16,512]{2,1,0:T(8,128)(2,1)S(1)}, u32[]{:S(2)}, u32[]{:S(2)}) collective-permute-start(bf16[4,16,512]{2,1,0:T(8,128)(2,1)S(1)} %get-tuple-element.76), channel_id=1, source_target_pairs={{0,16},{1,17},{2,18},{3,19},{4,20},{5,21},{6,22},{7,23},{8,24},{9,... | collective-permute-start | bytes 196616 | tf_op jit(solution)/shard_map/ppermute | solution.py:256
  80.9 0.4 collective-permute-done.14.refs_1_
  81.3 2.0 %early.5.sum_ref = f32[8,16,768]{2,1,0:T(8,128)S(1)} custom-call(s32[8,768]{1,0:T(8,128)S(1)} %get-tuple-element.29.code_ref, f32[4,1024]{1,0:T(4,128)S(1)} %copy-done, f32[4,16,512]{2,1,0:T(8,128)S(1)} %get-tuple-element.79.refs_0_, bf16[4,16,512]{2,1,0:T(8,128)(2,1)S(1)} %collective-permute-done.14.refs_1_, bf16[6144,1024]{1,0:T(8,128)(2,1)S(1)} %get-tuple-element.32.refs_2_), custom_call_target="tpu_custom_call" | custom-call | flops 100663296 | bytes 6291456 | tf_op jit(solution)/shard_map/early/pallas_call | solution.py:309
  83.3 1.4 %collective-permute-done.17.refs_1_ = bf16[4,16,512]{2,1,0:T(8,128)(2,1)S(1)} collective-permute-done((bf16[4,16,512]{2,1,0:T(8,128)(2,1)S(1)}, bf16[4,16,512]{2,1,0:T(8,128)(2,1)S(1)}, u32[]{:S(2)}, u32[]{:S(2)}) %collective-permute-start.17) | collective-permute-done | bytes 65568 | tf_op jit(solution)/shard_map/ppermute | solution.py:256
  84.7 2.0 %step.15 = (bf16[16,16,512]{2,1,0:T(8,128)(2,1)S(1)}, bf16[4,64,768]{2,1,0:T(8,128)(2,1)S(1)}) custom-call(s32[8,768]{1,0:T(8,128)S(1)} %get-tuple-element.29.code_ref, f32[4,1024]{1,0:T(4,128)S(1)} %copy-done, f32[8,16,768]{2,1,0:T(8,128)S(1)} %early.5.sum_ref, f32[4,16,512]{2,1,0:T(8,128)S(1)} %get-tuple-element.77.refs_0_, ...), custom_call_target="tpu_custom_call" | custom-call | flops 100663296 | bytes 6291456 | tf_op jit(solution)/shard_map/step/pallas_call | solution.py:329
  86.7 1.2 %collective-permute-start.18 = (bf16[16,16,512]{2,1,0:T(8,128)(2,1)S(1)}, bf16[16,16,512]{2,1,0:T(8,128)(2,1)S(1)}, u32[]{:S(2)}, u32[]{:S(2)}) collective-permute-start(bf16[16,16,512]{2,1,0:T(8,128)(2,1)S(1)} %get-tuple-element.51), channel_id=1, source_target_pairs={{0,4},{1,9},{2,6},{3,11},{4,0},{5,13},{6,2},{7,15},{8,12},{9,1},{1... | collective-permute-start | bytes 786440 | tf_op jit(solution)/shard_map/ppermute | solution.py:256
  87.9 1.3 %step.16 = (bf16[16,16,512]{2,1,0:T(8,128)(2,1)S(1)}, bf16[2,64,768]{2,1,0:T(8,128)(2,1)S(1)}) custom-call(s32[8,768]{1,0:T(8,128)S(1)} %get-tuple-element.29.code_ref, f32[4,1024]{1,0:T(4,128)S(1)} %copy-done, f32[8,16,768]{2,1,0:T(8,128)S(1)} %early.5.sum_ref, f32[4,16,512]{2,1,0:T(8,128)S(1)} %get-tuple-element.77.refs_0_, ...), custom_call_target="tpu_custom_call" | custom-call | flops 100663296 | bytes 6291456 | tf_op jit(solution)/shard_map/step/pallas_call | solution.py:329
  89.3 1.9 %step.17 = (f32[16,16,512]{2,1,0:T(8,128)S(1)}, f32[16,16,512]{2,1,0:T(8,128)S(1)}) custom-call(s32[8,768]{1,0:T(8,128)S(1)} %get-tuple-element.29.code_ref, f32[4,1024]{1,0:T(4,128)S(1)} %copy-done, f32[8,16,768]{2,1,0:T(8,128)S(1)} %early.5.sum_ref, f32[4,16,512]{2,1,0:T(8,128)S(1)} %get-tuple-element.77.refs_0_, ...), custom_call_target="tpu_custom_call" | custom-call | flops 100663296 | bytes 6291456 | tf_op jit(solution)/shard_map/step/pallas_call | solution.py:329
  91.2 1.9 %collective-permute-done.18 = bf16[16,16,512]{2,1,0:T(8,128)(2,1)S(1)} collective-permute-done((bf16[16,16,512]{2,1,0:T(8,128)(2,1)S(1)}, bf16[16,16,512]{2,1,0:T(8,128)(2,1)S(1)}, u32[]{:S(2)}, u32[]{:S(2)}) %collective-permute-start.18) | collective-permute-done | bytes 262176 | tf_op jit(solution)/shard_map/ppermute | solution.py:256
  93.2 0.2 collective-permute-start.19
  93.4 2.3 %collective-permute-done.21 = bf16[16,16,512]{2,1,0:T(8,128)(2,1)S(1)} collective-permute-done((bf16[16,16,512]{2,1,0:T(8,128)(2,1)S(1)}, bf16[16,16,512]{2,1,0:T(8,128)(2,1)S(1)}, u32[]{:S(2)}, u32[]{:S(2)}) %collective-permute-start.21) | collective-permute-done | bytes 262176 | tf_op jit(solution)/shard_map/ppermute | solution.py:256
  95.8 0.9 collective-permute-start.22
  96.7 1.5 %collective-permute-done.19 = bf16[8,16,512]{2,1,0:T(8,128)(2,1)S(1)} collective-permute-done((bf16[8,16,512]{2,1,0:T(8,128)(2,1)S(1)}, bf16[8,16,512]{2,1,0:T(8,128)(2,1)S(1)}, u32[]{:S(2)}, u32[]{:S(2)}) %collective-permute-start.19) | collective-permute-done | bytes 131104 | tf_op jit(solution)/shard_map/ppermute | solution.py:256
  98.3 1.5 %collective-permute-start.20 = (bf16[4,16,512]{2,1,0:T(8,128)(2,1)S(1)}, bf16[4,16,512]{2,1,0:T(8,128)(2,1)S(1)}, u32[]{:S(2)}, u32[]{:S(2)}) collective-permute-start(bf16[4,16,512]{2,1,0:T(8,128)(2,1)S(1)} %get-tuple-element.74), channel_id=1, source_target_pairs={{0,16},{1,17},{2,18},{3,19},{4,20},{5,21},{6,22},{7,23},{8,24},{9,... | collective-permute-start | bytes 196616 | tf_op jit(solution)/shard_map/ppermute | solution.py:256
  99.7 1.1 collective-permute-done.22
  100.9 1.2 %collective-permute-start.23 = (bf16[4,16,512]{2,1,0:T(8,128)(2,1)S(1)}, bf16[4,16,512]{2,1,0:T(8,128)(2,1)S(1)}, u32[]{:S(2)}, u32[]{:S(2)}) collective-permute-start(bf16[4,16,512]{2,1,0:T(8,128)(2,1)S(1)} %get-tuple-element.72), channel_id=1, source_target_pairs={{0,16},{1,17},{2,18},{3,19},{4,20},{5,21},{6,22},{7,23},{8,24},{9,... | collective-permute-start | bytes 196616 | tf_op jit(solution)/shard_map/ppermute | solution.py:256
  102.1 1.7 %collective-permute-done.20.refs_1_ = bf16[4,16,512]{2,1,0:T(8,128)(2,1)S(1)} collective-permute-done((bf16[4,16,512]{2,1,0:T(8,128)(2,1)S(1)}, bf16[4,16,512]{2,1,0:T(8,128)(2,1)S(1)}, u32[]{:S(2)}, u32[]{:S(2)}) %collective-permute-start.20) | collective-permute-done | bytes 65568 | tf_op jit(solution)/shard_map/ppermute | solution.py:256
  103.8 2.4 %collective-permute-done.23.refs_3_ = bf16[4,16,512]{2,1,0:T(8,128)(2,1)S(1)} collective-permute-done((bf16[4,16,512]{2,1,0:T(8,128)(2,1)S(1)}, bf16[4,16,512]{2,1,0:T(8,128)(2,1)S(1)}, u32[]{:S(2)}, u32[]{:S(2)}) %collective-permute-start.23) | collective-permute-done | bytes 65568 | tf_op jit(solution)/shard_map/ppermute | solution.py:256
  106.2 0.8 finish.1
  107.0 1.5 %collective-permute-start.25 = (f32[4,1024]{1,0:T(4,128)S(1)}, f32[4,1024]{1,0:T(4,128)S(1)}, u32[]{:S(2)}, u32[]{:S(2)}) collective-permute-start(f32[4,1024]{1,0:T(4,128)S(1)} %get-tuple-element.55), channel_id=1, source_target_pairs={{0,2},{1,3},{2,0},{3,1},{4,6},{5,7},{6,4},{7,5},{8,10},{9,11},{10,... | collective-permute-start | bytes 49160 | tf_op jit(solution)/shard_map/ppermute | solution.py:436
  108.5 0.3 collective-permute-start.24
  108.9 1.4 %collective-permute-done.26 = f32[4,1024]{1,0:T(4,128)S(1)} collective-permute-done((f32[4,1024]{1,0:T(4,128)S(1)}, f32[4,1024]{1,0:T(4,128)S(1)}, u32[]{:S(2)}, u32[]{:S(2)}) %collective-permute-start.26) | collective-permute-done | bytes 16416 | tf_op jit(solution)/shard_map/ppermute | solution.py:436
  110.3 0.5 collective-permute-done.25
  110.8 0.6 add_multiply_fusion
  (28 shorter events, 0.9 us)
Async XLA Ops:
  0.6 17.4 %copy-start = (f32[4,1024]{1,0:T(4,128)S(1)}, f32[4,1024]{1,0:T(4,128)}, u32[]{:S(2)}) copy-start(f32[4,1024]{1,0:T(4,128)} %contrast_ref.25) | copy-start | bytes 49156
  0.6 28.3 %copy-start.2 = (f32[4,16,1024]{2,1,0:T(8,128)S(1)}, f32[4,16,1024]{2,1,0:T(8,128)}, u32[]{:S(2)}) copy-start(f32[4,16,1024]{2,1,0:T(8,128)} %refs_3_.1) | copy-start | bytes 786436
  13.4 9.6 %collective-permute-start = (bf16[16,16,512]{2,1,0:T(8,128)(2,1)S(1)}, bf16[16,16,512]{2,1,0:T(8,128)(2,1)S(1)}, u32[]{:S(2)}, u32[]{:S(2)}) collective-permute-start(bf16[16,16,512]{2,1,0:T(8,128)(2,1)S(1)} %get-tuple-element.31), channel_id=1, source_target_pairs={{0,4},{1,9},{2,6},{3,11},{4,0},{5,13},{6,2},{7,15},{8,12},{9,1},{1... | collective-permute-start | bytes 786440 | tf_op jit(solution)/shard_map/ppermute | solution.py:256
  16.4 8.3 %collective-permute-start.3 = (bf16[16,16,512]{2,1,0:T(8,128)(2,1)S(1)}, bf16[16,16,512]{2,1,0:T(8,128)(2,1)S(1)}, u32[]{:S(2)}, u32[]{:S(2)}) collective-permute-start(bf16[16,16,512]{2,1,0:T(8,128)(2,1)S(1)} %get-tuple-element.34), channel_id=1, source_target_pairs={{0,8},{1,5},{2,10},{3,7},{4,12},{5,1},{6,14},{7,3},{8,0},{9,13},{1... | collective-permute-start | bytes 786440 | tf_op jit(solution)/shard_map/ppermute | solution.py:256
  23.0 5.9 %collective-permute-start.1 = (bf16[8,16,512]{2,1,0:T(8,128)(2,1)S(1)}, bf16[8,16,512]{2,1,0:T(8,128)(2,1)S(1)}, u32[]{:S(2)}, u32[]{:S(2)}) collective-permute-start(bf16[8,16,512]{2,1,0:T(8,128)(2,1)S(1)} %get-tuple-element.70), channel_id=1, source_target_pairs={{0,8},{1,5},{2,10},{3,7},{4,12},{5,1},{6,14},{7,3},{8,0},{9,13},{1... | collective-permute-start | bytes 393224 | tf_op jit(solution)/shard_map/ppermute | solution.py:256
  24.8 8.3 %collective-permute-start.4 = (bf16[8,16,512]{2,1,0:T(8,128)(2,1)S(1)}, bf16[8,16,512]{2,1,0:T(8,128)(2,1)S(1)}, u32[]{:S(2)}, u32[]{:S(2)}) collective-permute-start(bf16[8,16,512]{2,1,0:T(8,128)(2,1)S(1)} %get-tuple-element.68), channel_id=1, source_target_pairs={{0,4},{1,9},{2,6},{3,11},{4,0},{5,13},{6,2},{7,15},{8,12},{9,1},{1... | collective-permute-start | bytes 393224 | tf_op jit(solution)/shard_map/ppermute | solution.py:256
  29.0 6.4 %collective-permute-start.2 = (bf16[4,16,512]{2,1,0:T(8,128)(2,1)S(1)}, bf16[4,16,512]{2,1,0:T(8,128)(2,1)S(1)}, u32[]{:S(2)}, u32[]{:S(2)}) collective-permute-start(bf16[4,16,512]{2,1,0:T(8,128)(2,1)S(1)} %get-tuple-element.86), channel_id=1, source_target_pairs={{0,16},{1,17},{2,18},{3,19},{4,20},{5,21},{6,22},{7,23},{8,24},{9,... | collective-permute-start | bytes 196616 | tf_op jit(solution)/shard_map/ppermute | solution.py:256
  33.2 5.3 %collective-permute-start.5 = (bf16[4,16,512]{2,1,0:T(8,128)(2,1)S(1)}, bf16[4,16,512]{2,1,0:T(8,128)(2,1)S(1)}, u32[]{:S(2)}, u32[]{:S(2)}) collective-permute-start(bf16[4,16,512]{2,1,0:T(8,128)(2,1)S(1)} %get-tuple-element.84), channel_id=1, source_target_pairs={{0,16},{1,17},{2,18},{3,19},{4,20},{5,21},{6,22},{7,23},{8,24},{9,... | collective-permute-start | bytes 196616 | tf_op jit(solution)/shard_map/ppermute | solution.py:256
  40.4 7.6 %collective-permute-start.6 = (bf16[16,16,512]{2,1,0:T(8,128)(2,1)S(1)}, bf16[16,16,512]{2,1,0:T(8,128)(2,1)S(1)}, u32[]{:S(2)}, u32[]{:S(2)}) collective-permute-start(bf16[16,16,512]{2,1,0:T(8,128)(2,1)S(1)} %get-tuple-element.39), channel_id=1, source_target_pairs={{0,4},{1,9},{2,6},{3,11},{4,0},{5,13},{6,2},{7,15},{8,12},{9,1},{1... | collective-permute-start | bytes 786440 | tf_op jit(solution)/shard_map/ppermute | solution.py:256
  43.2 6.8 %collective-permute-start.9 = (bf16[16,16,512]{2,1,0:T(8,128)(2,1)S(1)}, bf16[16,16,512]{2,1,0:T(8,128)(2,1)S(1)}, u32[]{:S(2)}, u32[]{:S(2)}) collective-permute-start(bf16[16,16,512]{2,1,0:T(8,128)(2,1)S(1)} %get-tuple-element.41), channel_id=1, source_target_pairs={{0,8},{1,5},{2,10},{3,7},{4,12},{5,1},{6,14},{7,3},{8,0},{9,13},{1... | collective-permute-start | bytes 786440 | tf_op jit(solution)/shard_map/ppermute | solution.py:256
  48.0 5.7 %collective-permute-start.7 = (bf16[8,16,512]{2,1,0:T(8,128)(2,1)S(1)}, bf16[8,16,512]{2,1,0:T(8,128)(2,1)S(1)}, u32[]{:S(2)}, u32[]{:S(2)}) collective-permute-start(bf16[8,16,512]{2,1,0:T(8,128)(2,1)S(1)} %get-tuple-element.66), channel_id=1, source_target_pairs={{0,8},{1,5},{2,10},{3,7},{4,12},{5,1},{6,14},{7,3},{8,0},{9,13},{1... | collective-permute-start | bytes 393224 | tf_op jit(solution)/shard_map/ppermute | solution.py:256
  50.0 5.7 %collective-permute-start.10 = (bf16[8,16,512]{2,1,0:T(8,128)(2,1)S(1)}, bf16[8,16,512]{2,1,0:T(8,128)(2,1)S(1)}, u32[]{:S(2)}, u32[]{:S(2)}) collective-permute-start(bf16[8,16,512]{2,1,0:T(8,128)(2,1)S(1)} %get-tuple-element.64), channel_id=1, source_target_pairs={{0,4},{1,9},{2,6},{3,11},{4,0},{5,13},{6,2},{7,15},{8,12},{9,1},{1... | collective-permute-start | bytes 393224 | tf_op jit(solution)/shard_map/ppermute | solution.py:256
  53.8 5.8 %collective-permute-start.8 = (bf16[4,16,512]{2,1,0:T(8,128)(2,1)S(1)}, bf16[4,16,512]{2,1,0:T(8,128)(2,1)S(1)}, u32[]{:S(2)}, u32[]{:S(2)}) collective-permute-start(bf16[4,16,512]{2,1,0:T(8,128)(2,1)S(1)} %get-tuple-element.82), channel_id=1, source_target_pairs={{0,16},{1,17},{2,18},{3,19},{4,20},{5,21},{6,22},{7,23},{8,24},{9,... | collective-permute-start | bytes 196616 | tf_op jit(solution)/shard_map/ppermute | solution.py:256
  55.8 6.1 %collective-permute-start.11 = (bf16[4,16,512]{2,1,0:T(8,128)(2,1)S(1)}, bf16[4,16,512]{2,1,0:T(8,128)(2,1)S(1)}, u32[]{:S(2)}, u32[]{:S(2)}) collective-permute-start(bf16[4,16,512]{2,1,0:T(8,128)(2,1)S(1)} %get-tuple-element.80), channel_id=1, source_target_pairs={{0,16},{1,17},{2,18},{3,19},{4,20},{5,21},{6,22},{7,23},{8,24},{9,... | collective-permute-start | bytes 196616 | tf_op jit(solution)/shard_map/ppermute | solution.py:256
  63.8 6.4 %collective-permute-start.12 = (bf16[16,16,512]{2,1,0:T(8,128)(2,1)S(1)}, bf16[16,16,512]{2,1,0:T(8,128)(2,1)S(1)}, u32[]{:S(2)}, u32[]{:S(2)}) collective-permute-start(bf16[16,16,512]{2,1,0:T(8,128)(2,1)S(1)} %get-tuple-element.45), channel_id=1, source_target_pairs={{0,4},{1,9},{2,6},{3,11},{4,0},{5,13},{6,2},{7,15},{8,12},{9,1},{1... | collective-permute-start | bytes 786440 | tf_op jit(solution)/shard_map/ppermute | solution.py:256
  66.8 7.1 %collective-permute-start.15 = (bf16[16,16,512]{2,1,0:T(8,128)(2,1)S(1)}, bf16[16,16,512]{2,1,0:T(8,128)(2,1)S(1)}, u32[]{:S(2)}, u32[]{:S(2)}) collective-permute-start(bf16[16,16,512]{2,1,0:T(8,128)(2,1)S(1)} %get-tuple-element.47), channel_id=1, source_target_pairs={{0,8},{1,5},{2,10},{3,7},{4,12},{5,1},{6,14},{7,3},{8,0},{9,13},{1... | collective-permute-start | bytes 786440 | tf_op jit(solution)/shard_map/ppermute | solution.py:256
  70.3 5.0 %collective-permute-start.13 = (bf16[8,16,512]{2,1,0:T(8,128)(2,1)S(1)}, bf16[8,16,512]{2,1,0:T(8,128)(2,1)S(1)}, u32[]{:S(2)}, u32[]{:S(2)}) collective-permute-start(bf16[8,16,512]{2,1,0:T(8,128)(2,1)S(1)} %get-tuple-element.62), channel_id=1, source_target_pairs={{0,8},{1,5},{2,10},{3,7},{4,12},{5,1},{6,14},{7,3},{8,0},{9,13},{1... | collective-permute-start | bytes 393224 | tf_op jit(solution)/shard_map/ppermute | solution.py:256
  74.0 5.0 %collective-permute-start.16 = (bf16[8,16,512]{2,1,0:T(8,128)(2,1)S(1)}, bf16[8,16,512]{2,1,0:T(8,128)(2,1)S(1)}, u32[]{:S(2)}, u32[]{:S(2)}) collective-permute-start(bf16[8,16,512]{2,1,0:T(8,128)(2,1)S(1)} %get-tuple-element.60), channel_id=1, source_target_pairs={{0,4},{1,9},{2,6},{3,11},{4,0},{5,13},{6,2},{7,15},{8,12},{9,1},{1... | collective-permute-start | bytes 393224 | tf_op jit(solution)/shard_map/ppermute | solution.py:256
  75.4 5.9 %collective-permute-start.14 = (bf16[4,16,512]{2,1,0:T(8,128)(2,1)S(1)}, bf16[4,16,512]{2,1,0:T(8,128)(2,1)S(1)}, u32[]{:S(2)}, u32[]{:S(2)}) collective-permute-start(bf16[4,16,512]{2,1,0:T(8,128)(2,1)S(1)} %get-tuple-element.78), channel_id=1, source_target_pairs={{0,16},{1,17},{2,18},{3,19},{4,20},{5,21},{6,22},{7,23},{8,24},{9,... | collective-permute-start | bytes 196616 | tf_op jit(solution)/shard_map/ppermute | solution.py:256
  79.1 5.6 %collective-permute-start.17 = (bf16[4,16,512]{2,1,0:T(8,128)(2,1)S(1)}, bf16[4,16,512]{2,1,0:T(8,128)(2,1)S(1)}, u32[]{:S(2)}, u32[]{:S(2)}) collective-permute-start(bf16[4,16,512]{2,1,0:T(8,128)(2,1)S(1)} %get-tuple-element.76), channel_id=1, source_target_pairs={{0,16},{1,17},{2,18},{3,19},{4,20},{5,21},{6,22},{7,23},{8,24},{9,... | collective-permute-start | bytes 196616 | tf_op jit(solution)/shard_map/ppermute | solution.py:256
  86.7 6.4 %collective-permute-start.18 = (bf16[16,16,512]{2,1,0:T(8,128)(2,1)S(1)}, bf16[16,16,512]{2,1,0:T(8,128)(2,1)S(1)}, u32[]{:S(2)}, u32[]{:S(2)}) collective-permute-start(bf16[16,16,512]{2,1,0:T(8,128)(2,1)S(1)} %get-tuple-element.51), channel_id=1, source_target_pairs={{0,4},{1,9},{2,6},{3,11},{4,0},{5,13},{6,2},{7,15},{8,12},{9,1},{1... | collective-permute-start | bytes 786440 | tf_op jit(solution)/shard_map/ppermute | solution.py:256
  89.3 6.4 %collective-permute-start.21 = (bf16[16,16,512]{2,1,0:T(8,128)(2,1)S(1)}, bf16[16,16,512]{2,1,0:T(8,128)(2,1)S(1)}, u32[]{:S(2)}, u32[]{:S(2)}) collective-permute-start(bf16[16,16,512]{2,1,0:T(8,128)(2,1)S(1)} %get-tuple-element.53), channel_id=1, source_target_pairs={{0,8},{1,5},{2,10},{3,7},{4,12},{5,1},{6,14},{7,3},{8,0},{9,13},{1... | collective-permute-start | bytes 786440 | tf_op jit(solution)/shard_map/ppermute | solution.py:256
  89.3 16.9 %copy-start.1 = (bf16[4,16,1024]{2,1,0:T(8,128)(2,1)S(1)}, bf16[4,16,1024]{2,1,0:T(8,128)(2,1)}, u32[]{:S(2)}) copy-start(bf16[4,16,1024]{2,1,0:T(8,128)(2,1)} %forward_ref.1) | copy-start | bytes 393220
  93.2 5.0 %collective-permute-start.19 = (bf16[8,16,512]{2,1,0:T(8,128)(2,1)S(1)}, bf16[8,16,512]{2,1,0:T(8,128)(2,1)S(1)}, u32[]{:S(2)}, u32[]{:S(2)}) collective-permute-start(bf16[8,16,512]{2,1,0:T(8,128)(2,1)S(1)} %get-tuple-element.58), channel_id=1, source_target_pairs={{0,8},{1,5},{2,10},{3,7},{4,12},{5,1},{6,14},{7,3},{8,0},{9,13},{1... | collective-permute-start | bytes 393224 | tf_op jit(solution)/shard_map/ppermute | solution.py:256
  95.8 5.0 %collective-permute-start.22 = (bf16[8,16,512]{2,1,0:T(8,128)(2,1)S(1)}, bf16[8,16,512]{2,1,0:T(8,128)(2,1)S(1)}, u32[]{:S(2)}, u32[]{:S(2)}) collective-permute-start(bf16[8,16,512]{2,1,0:T(8,128)(2,1)S(1)} %get-tuple-element.56), channel_id=1, source_target_pairs={{0,4},{1,9},{2,6},{3,11},{4,0},{5,13},{6,2},{7,15},{8,12},{9,1},{1... | collective-permute-start | bytes 393224 | tf_op jit(solution)/shard_map/ppermute | solution.py:256
  98.3 5.5 %collective-permute-start.20 = (bf16[4,16,512]{2,1,0:T(8,128)(2,1)S(1)}, bf16[4,16,512]{2,1,0:T(8,128)(2,1)S(1)}, u32[]{:S(2)}, u32[]{:S(2)}) collective-permute-start(bf16[4,16,512]{2,1,0:T(8,128)(2,1)S(1)} %get-tuple-element.74), channel_id=1, source_target_pairs={{0,16},{1,17},{2,18},{3,19},{4,20},{5,21},{6,22},{7,23},{8,24},{9,... | collective-permute-start | bytes 196616 | tf_op jit(solution)/shard_map/ppermute | solution.py:256
  100.9 5.4 %collective-permute-start.23 = (bf16[4,16,512]{2,1,0:T(8,128)(2,1)S(1)}, bf16[4,16,512]{2,1,0:T(8,128)(2,1)S(1)}, u32[]{:S(2)}, u32[]{:S(2)}) collective-permute-start(bf16[4,16,512]{2,1,0:T(8,128)(2,1)S(1)} %get-tuple-element.72), channel_id=1, source_target_pairs={{0,16},{1,17},{2,18},{3,19},{4,20},{5,21},{6,22},{7,23},{8,24},{9,... | collective-permute-start | bytes 196616 | tf_op jit(solution)/shard_map/ppermute | solution.py:256
  107.0 3.3 %collective-permute-start.26 = (f32[4,1024]{1,0:T(4,128)S(1)}, f32[4,1024]{1,0:T(4,128)S(1)}, u32[]{:S(2)}, u32[]{:S(2)}) collective-permute-start(f32[4,1024]{1,0:T(4,128)S(1)} %get-tuple-element.55), channel_id=1, source_target_pairs={{0,3},{1,2},{2,1},{3,0},{4,7},{5,6},{6,5},{7,4},{8,11},{9,10},{10,... | collective-permute-start | bytes 49160 | tf_op jit(solution)/shard_map/ppermute | solution.py:436
  107.0 3.8 %collective-permute-start.25 = (f32[4,1024]{1,0:T(4,128)S(1)}, f32[4,1024]{1,0:T(4,128)S(1)}, u32[]{:S(2)}, u32[]{:S(2)}) collective-permute-start(f32[4,1024]{1,0:T(4,128)S(1)} %get-tuple-element.55), channel_id=1, source_target_pairs={{0,2},{1,3},{2,0},{3,1},{4,6},{5,7},{6,4},{7,5},{8,10},{9,11},{10,... | collective-permute-start | bytes 49160 | tf_op jit(solution)/shard_map/ppermute | solution.py:436
  108.5 2.3 %collective-permute-start.24 = (f32[4,1024]{1,0:T(4,128)S(1)}, f32[4,1024]{1,0:T(4,128)S(1)}, u32[]{:S(2)}, u32[]{:S(2)}) collective-permute-start(f32[4,1024]{1,0:T(4,128)S(1)} %get-tuple-element.55), channel_id=1, source_target_pairs={{0,1},{1,0},{2,3},{3,2},{4,5},{5,4},{6,7},{7,6},{8,9},{9,8},{10,11... | collective-permute-start | bytes 49160 | tf_op jit(solution)/shard_map/ppermute | solution.py:436

commit v10 on v9

--- a/solution.py
+++ b/solution.py
@@ -132,13 +132,13 @@
             load(whence, to, sem, lax.div(word_at[at], codes), at, lax.div(at, group_tiles))
             return carry
 
-        lax.fori_loop(0, tiles, one, 0)
+        lax.fori_loop(0, tiles, one, 0, unroll=4)
 
     def loaded(ref, sem, group):
         piece = ref.at[pl.ds(group * deep, deep)]
         pltpu.make_async_copy(piece, piece, sem.at[group]).wait()
 
-    lax.fori_loop(0, tiles_row, sort_tiles, jnp.int32(0))
+    lax.fori_loop(0, tiles_row, sort_tiles, jnp.int32(0), unroll=4)
     load_all(u_hbm, u_ref, u_sem)
     load_all(v_hbm, v_ref, v_sem)
     lane = lax.broadcasted_iota(jnp.int32, (1, deep), 1)

time: 112 us -> 111 us (level)
  no operation moved by 1% of the time
where the time goes in v10:
time: 111 us
  waiting for transfers between devices  38.6 us (35%)
  starting transfers between devices  35 us (32%)
  Pallas kernels  34.9 us (31%)
  other arithmetic  1.58 us (1%)
    ppermute x24, waiting for transfers between devices, swap(): return lax.ppermute(x, ('rows', 'src'), pairs)  36.7 us
    ppermute x24, starting transfers between devices, swap(): return lax.ppermute(x, ('rows', 'src'), pairs)  33.2 us
    pallas_call x9, Pallas kernels, slot_sums(): pl.pallas_call(functools.partial(step_kernel, dims, parts[late], [*known]...  15.6 us
    pallas_call x1, Pallas kernels, slot_sums(): pl.pallas_call(functools.partial(start_kernel, (rows_dev, tiles_row, rank...  12.3 us
    pallas_call x3, Pallas kernels, slot_sums(): pl.pallas_call(functools.partial(early_kernel, dims, [parts[i] for i in e...  6.23 us
  transfers between devices with their start and end apart: 27, of which 22 were waited for; matrix products, arithmetic and copies ran while one was open for 1% of the time, Pallas kernels for 14%

profile of v10, /device:TPU:0, one launch (start us, length us, event | category | flops | bytes accessed | tf_op | source)
XLA Modules:
  0.0 110.9 jit_solution(6953518946711259179)
XLA Ops:
  0.7 12.3 %start.1 = (bf16[6144,1024]{1,0:T(8,128)(2,1)S(1)}, bf16[6144,1024]{1,0:T(8,128)(2,1)S(1)}, s32[8,768]{1,0:T(8,128)S(1)}, f32[16,16,512]{2,1,0:T(8,128)S(1)}, bf...) custom-call(s32[16,32]{1,0:T(8,128)} %bitcast.11, s32[32]{0:T(128)} %refs_1_.1, ...), custom_call_target="tpu_custom_call" | custom-call | flops 402653184 | bytes 25165824 | tf_op jit(solution)/shard_map/start/pallas_call | solution.py:280
  12.9 3.0 %collective-permute-start = (bf16[16,16,512]{2,1,0:T(8,128)(2,1)S(1)}, bf16[16,16,512]{2,1,0:T(8,128)(2,1)S(1)}, u32[]{:S(2)}, u32[]{:S(2)}) collective-permute-start(bf16[16,16,512]{2,1,0:T(8,128)(2,1)S(1)} %get-tuple-element.31), channel_id=1, source_target_pairs={{0,4},{1,9},{2,6},{3,11},{4,0},{5,13},{6,2},{7,15},{8,12},{9,1},{1... | collective-permute-start | bytes 786440 | tf_op jit(solution)/shard_map/ppermute | solution.py:256
  16.0 1.6 %collective-permute-start.3 = (bf16[16,16,512]{2,1,0:T(8,128)(2,1)S(1)}, bf16[16,16,512]{2,1,0:T(8,128)(2,1)S(1)}, u32[]{:S(2)}, u32[]{:S(2)}) collective-permute-start(bf16[16,16,512]{2,1,0:T(8,128)(2,1)S(1)} %get-tuple-element.34), channel_id=1, source_target_pairs={{0,8},{1,5},{2,10},{3,7},{4,12},{5,1},{6,14},{7,3},{8,0},{9,13},{1... | collective-permute-start | bytes 786440 | tf_op jit(solution)/shard_map/ppermute | solution.py:256
  17.6 5.0 %collective-permute-done = bf16[16,16,512]{2,1,0:T(8,128)(2,1)S(1)} collective-permute-done((bf16[16,16,512]{2,1,0:T(8,128)(2,1)S(1)}, bf16[16,16,512]{2,1,0:T(8,128)(2,1)S(1)}, u32[]{:S(2)}, u32[]{:S(2)}) %collective-permute-start) | collective-permute-done | bytes 262176 | tf_op jit(solution)/shard_map/ppermute | solution.py:256
  22.6 1.7 %collective-permute-start.1 = (bf16[8,16,512]{2,1,0:T(8,128)(2,1)S(1)}, bf16[8,16,512]{2,1,0:T(8,128)(2,1)S(1)}, u32[]{:S(2)}, u32[]{:S(2)}) collective-permute-start(bf16[8,16,512]{2,1,0:T(8,128)(2,1)S(1)} %get-tuple-element.70), channel_id=1, source_target_pairs={{0,8},{1,5},{2,10},{3,7},{4,12},{5,1},{6,14},{7,3},{8,0},{9,13},{1... | collective-permute-start | bytes 393224 | tf_op jit(solution)/shard_map/ppermute | solution.py:256
  24.4 1.7 %collective-permute-start.4 = (bf16[8,16,512]{2,1,0:T(8,128)(2,1)S(1)}, bf16[8,16,512]{2,1,0:T(8,128)(2,1)S(1)}, u32[]{:S(2)}, u32[]{:S(2)}) collective-permute-start(bf16[8,16,512]{2,1,0:T(8,128)(2,1)S(1)} %get-tuple-element.68), channel_id=1, source_target_pairs={{0,4},{1,9},{2,6},{3,11},{4,0},{5,13},{6,2},{7,15},{8,12},{9,1},{1... | collective-permute-start | bytes 393224 | tf_op jit(solution)/shard_map/ppermute | solution.py:256
  26.0 2.5 %collective-permute-done.1 = bf16[8,16,512]{2,1,0:T(8,128)(2,1)S(1)} collective-permute-done((bf16[8,16,512]{2,1,0:T(8,128)(2,1)S(1)}, bf16[8,16,512]{2,1,0:T(8,128)(2,1)S(1)}, u32[]{:S(2)}, u32[]{:S(2)}) %collective-permute-start.1) | collective-permute-done | bytes 131104 | tf_op jit(solution)/shard_map/ppermute | solution.py:256
  28.5 4.1 %collective-permute-start.2 = (bf16[4,16,512]{2,1,0:T(8,128)(2,1)S(1)}, bf16[4,16,512]{2,1,0:T(8,128)(2,1)S(1)}, u32[]{:S(2)}, u32[]{:S(2)}) collective-permute-start(bf16[4,16,512]{2,1,0:T(8,128)(2,1)S(1)} %get-tuple-element.86), channel_id=1, source_target_pairs={{0,16},{1,17},{2,18},{3,19},{4,20},{5,21},{6,22},{7,23},{8,24},{9,... | collective-permute-start | bytes 196616 | tf_op jit(solution)/shard_map/ppermute | solution.py:256
  32.7 0.1 collective-permute-start.5
  32.8 2.1 %collective-permute-done.2.refs_1_ = bf16[4,16,512]{2,1,0:T(8,128)(2,1)S(1)} collective-permute-done((bf16[4,16,512]{2,1,0:T(8,128)(2,1)S(1)}, bf16[4,16,512]{2,1,0:T(8,128)(2,1)S(1)}, u32[]{:S(2)}, u32[]{:S(2)}) %collective-permute-start.2) | collective-permute-done | bytes 65568 | tf_op jit(solution)/shard_map/ppermute | solution.py:256
  34.9 2.0 %early.3.sum_ref = f32[8,16,768]{2,1,0:T(8,128)S(1)} custom-call(s32[8,768]{1,0:T(8,128)S(1)} %get-tuple-element.29.code_ref, f32[4,1024]{1,0:T(4,128)S(1)} %copy-done, f32[4,16,512]{2,1,0:T(8,128)S(1)} %get-tuple-element.87.refs_0_, bf16[4,16,512]{2,1,0:T(8,128)(2,1)S(1)} %collective-permute-done.2.refs_1_, bf16[6144,1024]{1,0:T(8,128)(2,1)S(1)} %get-tuple-element.32.refs_2_), custom_call_target="tpu_custom_call" | custom-call | flops 100663296 | bytes 6291456 | tf_op jit(solution)/shard_map/early/pallas_call | solution.py:309
  36.9 1.0 collective-permute-done.5.refs_1_
  38.0 2.0 %step.9 = (bf16[16,16,512]{2,1,0:T(8,128)(2,1)S(1)}, bf16[4,64,768]{2,1,0:T(8,128)(2,1)S(1)}) custom-call(s32[8,768]{1,0:T(8,128)S(1)} %get-tuple-element.29.code_ref, f32[4,1024]{1,0:T(4,128)S(1)} %copy-done, f32[8,16,768]{2,1,0:T(8,128)S(1)} %early.3.sum_ref, f32[4,16,512]{2,1,0:T(8,128)S(1)} %get-tuple-element.85.refs_0_, ...), custom_call_target="tpu_custom_call" | custom-call | flops 100663296 | bytes 6291456 | tf_op jit(solution)/shard_map/step/pallas_call | solution.py:329
  39.9 1.4 %collective-permute-start.6 = (bf16[16,16,512]{2,1,0:T(8,128)(2,1)S(1)}, bf16[16,16,512]{2,1,0:T(8,128)(2,1)S(1)}, u32[]{:S(2)}, u32[]{:S(2)}) collective-permute-start(bf16[16,16,512]{2,1,0:T(8,128)(2,1)S(1)} %get-tuple-element.39), channel_id=1, source_target_pairs={{0,4},{1,9},{2,6},{3,11},{4,0},{5,13},{6,2},{7,15},{8,12},{9,1},{1... | collective-permute-start | bytes 786440 | tf_op jit(solution)/shard_map/ppermute | solution.py:256
  41.4 1.3 %step.10 = (bf16[16,16,512]{2,1,0:T(8,128)(2,1)S(1)}, bf16[2,64,768]{2,1,0:T(8,128)(2,1)S(1)}) custom-call(s32[8,768]{1,0:T(8,128)S(1)} %get-tuple-element.29.code_ref, f32[4,1024]{1,0:T(4,128)S(1)} %copy-done, f32[8,16,768]{2,1,0:T(8,128)S(1)} %early.3.sum_ref, f32[4,16,512]{2,1,0:T(8,128)S(1)} %get-tuple-element.85.refs_0_, ...), custom_call_target="tpu_custom_call" | custom-call | flops 100663296 | bytes 6291456 | tf_op jit(solution)/shard_map/step/pallas_call | solution.py:329
  42.8 1.9 %step.11 = (f32[16,16,512]{2,1,0:T(8,128)S(1)}, f32[16,16,512]{2,1,0:T(8,128)S(1)}) custom-call(s32[8,768]{1,0:T(8,128)S(1)} %get-tuple-element.29.code_ref, f32[4,1024]{1,0:T(4,128)S(1)} %copy-done, f32[8,16,768]{2,1,0:T(8,128)S(1)} %early.3.sum_ref, f32[4,16,512]{2,1,0:T(8,128)S(1)} %get-tuple-element.85.refs_0_, ...), custom_call_target="tpu_custom_call" | custom-call | flops 100663296 | bytes 6291456 | tf_op jit(solution)/shard_map/step/pallas_call | solution.py:329
  44.7 2.8 %collective-permute-done.6 = bf16[16,16,512]{2,1,0:T(8,128)(2,1)S(1)} collective-permute-done((bf16[16,16,512]{2,1,0:T(8,128)(2,1)S(1)}, bf16[16,16,512]{2,1,0:T(8,128)(2,1)S(1)}, u32[]{:S(2)}, u32[]{:S(2)}) %collective-permute-start.6) | collective-permute-done | bytes 262176 | tf_op jit(solution)/shard_map/ppermute | solution.py:256
  47.5 0.1 add_convert_fusion.5
  47.6 0.4 collective-permute-start.7
  48.0 1.5 %collective-permute-done.9 = bf16[16,16,512]{2,1,0:T(8,128)(2,1)S(1)} collective-permute-done((bf16[16,16,512]{2,1,0:T(8,128)(2,1)S(1)}, bf16[16,16,512]{2,1,0:T(8,128)(2,1)S(1)}, u32[]{:S(2)}, u32[]{:S(2)}) %collective-permute-start.9) | collective-permute-done | bytes 262176 | tf_op jit(solution)/shard_map/ppermute | solution.py:256
  49.5 0.1 add_convert_fusion.4
  49.5 2.5 %collective-permute-start.10 = (bf16[8,16,512]{2,1,0:T(8,128)(2,1)S(1)}, bf16[8,16,512]{2,1,0:T(8,128)(2,1)S(1)}, u32[]{:S(2)}, u32[]{:S(2)}) collective-permute-start(bf16[8,16,512]{2,1,0:T(8,128)(2,1)S(1)} %get-tuple-element.64), channel_id=1, source_target_pairs={{0,4},{1,9},{2,6},{3,11},{4,0},{5,13},{6,2},{7,15},{8,12},{9,1},{1... | collective-permute-start | bytes 393224 | tf_op jit(solution)/shard_map/ppermute | solution.py:256
  52.0 1.3 %collective-permute-done.7 = bf16[8,16,512]{2,1,0:T(8,128)(2,1)S(1)} collective-permute-done((bf16[8,16,512]{2,1,0:T(8,128)(2,1)S(1)}, bf16[8,16,512]{2,1,0:T(8,128)(2,1)S(1)}, u32[]{:S(2)}, u32[]{:S(2)}) %collective-permute-start.7) | collective-permute-done | bytes 131104 | tf_op jit(solution)/shard_map/ppermute | solution.py:256
  53.4 1.9 %collective-permute-start.8 = (bf16[4,16,512]{2,1,0:T(8,128)(2,1)S(1)}, bf16[4,16,512]{2,1,0:T(8,128)(2,1)S(1)}, u32[]{:S(2)}, u32[]{:S(2)}) collective-permute-start(bf16[4,16,512]{2,1,0:T(8,128)(2,1)S(1)} %get-tuple-element.82), channel_id=1, source_target_pairs={{0,16},{1,17},{2,18},{3,19},{4,20},{5,21},{6,22},{7,23},{8,24},{9,... | collective-permute-start | bytes 196616 | tf_op jit(solution)/shard_map/ppermute | solution.py:256
  55.3 2.2 %collective-permute-start.11 = (bf16[4,16,512]{2,1,0:T(8,128)(2,1)S(1)}, bf16[4,16,512]{2,1,0:T(8,128)(2,1)S(1)}, u32[]{:S(2)}, u32[]{:S(2)}) collective-permute-start(bf16[4,16,512]{2,1,0:T(8,128)(2,1)S(1)} %get-tuple-element.80), channel_id=1, source_target_pairs={{0,16},{1,17},{2,18},{3,19},{4,20},{5,21},{6,22},{7,23},{8,24},{9,... | collective-permute-start | bytes 196616 | tf_op jit(solution)/shard_map/ppermute | solution.py:256
  57.5 1.7 %collective-permute-done.8.refs_1_ = bf16[4,16,512]{2,1,0:T(8,128)(2,1)S(1)} collective-permute-done((bf16[4,16,512]{2,1,0:T(8,128)(2,1)S(1)}, bf16[4,16,512]{2,1,0:T(8,128)(2,1)S(1)}, u32[]{:S(2)}, u32[]{:S(2)}) %collective-permute-start.8) | collective-permute-done | bytes 65568 | tf_op jit(solution)/shard_map/ppermute | solution.py:256
  59.2 2.2 %early.4.sum_ref = f32[8,16,768]{2,1,0:T(8,128)S(1)} custom-call(s32[8,768]{1,0:T(8,128)S(1)} %get-tuple-element.29.code_ref, f32[4,1024]{1,0:T(4,128)S(1)} %copy-done, f32[4,16,512]{2,1,0:T(8,128)S(1)} %get-tuple-element.83.refs_0_, bf16[4,16,512]{2,1,0:T(8,128)(2,1)S(1)} %collective-permute-done.8.refs_1_, bf16[6144,1024]{1,0:T(8,128)(2,1)S(1)} %get-tuple-element.32.refs_2_), custom_call_target="tpu_custom_call" | custom-call | flops 100663296 | bytes 6291456 | tf_op jit(solution)/shard_map/early/pallas_call | solution.py:309
  61.4 2.0 %step.12 = (bf16[16,16,512]{2,1,0:T(8,128)(2,1)S(1)}, bf16[4,64,768]{2,1,0:T(8,128)(2,1)S(1)}) custom-call(s32[8,768]{1,0:T(8,128)S(1)} %get-tuple-element.29.code_ref, f32[4,1024]{1,0:T(4,128)S(1)} %copy-done, f32[8,16,768]{2,1,0:T(8,128)S(1)} %early.4.sum_ref, f32[4,16,512]{2,1,0:T(8,128)S(1)} %get-tuple-element.81.refs_0_, ...), custom_call_target="tpu_custom_call" | custom-call | flops 100663296 | bytes 6291456 | tf_op jit(solution)/shard_map/step/pallas_call | solution.py:329
  63.4 1.6 %collective-permute-start.12 = (bf16[16,16,512]{2,1,0:T(8,128)(2,1)S(1)}, bf16[16,16,512]{2,1,0:T(8,128)(2,1)S(1)}, u32[]{:S(2)}, u32[]{:S(2)}) collective-permute-start(bf16[16,16,512]{2,1,0:T(8,128)(2,1)S(1)} %get-tuple-element.45), channel_id=1, source_target_pairs={{0,4},{1,9},{2,6},{3,11},{4,0},{5,13},{6,2},{7,15},{8,12},{9,1},{1... | collective-permute-start | bytes 786440 | tf_op jit(solution)/shard_map/ppermute | solution.py:256
  65.0 1.3 %step.13 = (bf16[16,16,512]{2,1,0:T(8,128)(2,1)S(1)}, bf16[2,64,768]{2,1,0:T(8,128)(2,1)S(1)}) custom-call(s32[8,768]{1,0:T(8,128)S(1)} %get-tuple-element.29.code_ref, f32[4,1024]{1,0:T(4,128)S(1)} %copy-done, f32[8,16,768]{2,1,0:T(8,128)S(1)} %early.4.sum_ref, f32[4,16,512]{2,1,0:T(8,128)S(1)} %get-tuple-element.81.refs_0_, ...), custom_call_target="tpu_custom_call" | custom-call | flops 100663296 | bytes 6291456 | tf_op jit(solution)/shard_map/step/pallas_call | solution.py:329
  66.4 1.9 %step.14 = (f32[16,16,512]{2,1,0:T(8,128)S(1)}, f32[16,16,512]{2,1,0:T(8,128)S(1)}) custom-call(s32[8,768]{1,0:T(8,128)S(1)} %get-tuple-element.29.code_ref, f32[4,1024]{1,0:T(4,128)S(1)} %copy-done, f32[8,16,768]{2,1,0:T(8,128)S(1)} %early.4.sum_ref, f32[4,16,512]{2,1,0:T(8,128)S(1)} %get-tuple-element.81.refs_0_, ...), custom_call_target="tpu_custom_call" | custom-call | flops 100663296 | bytes 6291456 | tf_op jit(solution)/shard_map/step/pallas_call | solution.py:329
  68.3 1.5 %collective-permute-done.12 = bf16[16,16,512]{2,1,0:T(8,128)(2,1)S(1)} collective-permute-done((bf16[16,16,512]{2,1,0:T(8,128)(2,1)S(1)}, bf16[16,16,512]{2,1,0:T(8,128)(2,1)S(1)}, u32[]{:S(2)}, u32[]{:S(2)}) %collective-permute-start.12) | collective-permute-done | bytes 262176 | tf_op jit(solution)/shard_map/ppermute | solution.py:256
  69.8 0.1 add_convert_fusion.3
  69.9 0.6 collective-permute-start.13
  70.5 3.0 %collective-permute-done.15 = bf16[16,16,512]{2,1,0:T(8,128)(2,1)S(1)} collective-permute-done((bf16[16,16,512]{2,1,0:T(8,128)(2,1)S(1)}, bf16[16,16,512]{2,1,0:T(8,128)(2,1)S(1)}, u32[]{:S(2)}, u32[]{:S(2)}) %collective-permute-start.15) | collective-permute-done | bytes 262176 | tf_op jit(solution)/shard_map/ppermute | solution.py:256
  73.5 0.1 add_convert_fusion.2
  73.6 1.2 %collective-permute-start.16 = (bf16[8,16,512]{2,1,0:T(8,128)(2,1)S(1)}, bf16[8,16,512]{2,1,0:T(8,128)(2,1)S(1)}, u32[]{:S(2)}, u32[]{:S(2)}) collective-permute-start(bf16[8,16,512]{2,1,0:T(8,128)(2,1)S(1)} %get-tuple-element.60), channel_id=1, source_target_pairs={{0,4},{1,9},{2,6},{3,11},{4,0},{5,13},{6,2},{7,15},{8,12},{9,1},{1... | collective-permute-start | bytes 393224 | tf_op jit(solution)/shard_map/ppermute | solution.py:256
  74.8 0.1 collective-permute-done.13
  75.0 2.1 %collective-permute-start.14 = (bf16[4,16,512]{2,1,0:T(8,128)(2,1)S(1)}, bf16[4,16,512]{2,1,0:T(8,128)(2,1)S(1)}, u32[]{:S(2)}, u32[]{:S(2)}) collective-permute-start(bf16[4,16,512]{2,1,0:T(8,128)(2,1)S(1)} %get-tuple-element.78), channel_id=1, source_target_pairs={{0,16},{1,17},{2,18},{3,19},{4,20},{5,21},{6,22},{7,23},{8,24},{9,... | collective-permute-start | bytes 196616 | tf_op jit(solution)/shard_map/ppermute | solution.py:256
  77.1 1.5 %collective-permute-done.16 = bf16[8,16,512]{2,1,0:T(8,128)(2,1)S(1)} collective-permute-done((bf16[8,16,512]{2,1,0:T(8,128)(2,1)S(1)}, bf16[8,16,512]{2,1,0:T(8,128)(2,1)S(1)}, u32[]{:S(2)}, u32[]{:S(2)}) %collective-permute-start.16) | collective-permute-done | bytes 131104 | tf_op jit(solution)/shard_map/ppermute | solution.py:256
  78.7 1.8 %collective-permute-start.17 = (bf16[4,16,512]{2,1,0:T(8,128)(2,1)S(1)}, bf16[4,16,512]{2,1,0:T(8,128)(2,1)S(1)}, u32[]{:S(2)}, u32[]{:S(2)}) collective-permute-start(bf16[4,16,512]{2,1,0:T(8,128)(2,1)S(1)} %get-tuple-element.76), channel_id=1, source_target_pairs={{0,16},{1,17},{2,18},{3,19},{4,20},{5,21},{6,22},{7,23},{8,24},{9,... | collective-permute-start | bytes 196616 | tf_op jit(solution)/shard_map/ppermute | solution.py:256
  80.5 0.4 collective-permute-done.14.refs_1_
  80.9 2.0 %early.5.sum_ref = f32[8,16,768]{2,1,0:T(8,128)S(1)} custom-call(s32[8,768]{1,0:T(8,128)S(1)} %get-tuple-element.29.code_ref, f32[4,1024]{1,0:T(4,128)S(1)} %copy-done, f32[4,16,512]{2,1,0:T(8,128)S(1)} %get-tuple-element.79.refs_0_, bf16[4,16,512]{2,1,0:T(8,128)(2,1)S(1)} %collective-permute-done.14.refs_1_, bf16[6144,1024]{1,0:T(8,128)(2,1)S(1)} %get-tuple-element.32.refs_2_), custom_call_target="tpu_custom_call" | custom-call | flops 100663296 | bytes 6291456 | tf_op jit(solution)/shard_map/early/pallas_call | solution.py:309
  82.9 1.4 %collective-permute-done.17.refs_1_ = bf16[4,16,512]{2,1,0:T(8,128)(2,1)S(1)} collective-permute-done((bf16[4,16,512]{2,1,0:T(8,128)(2,1)S(1)}, bf16[4,16,512]{2,1,0:T(8,128)(2,1)S(1)}, u32[]{:S(2)}, u32[]{:S(2)}) %collective-permute-start.17) | collective-permute-done | bytes 65568 | tf_op jit(solution)/shard_map/ppermute | solution.py:256
  84.3 2.0 %step.15 = (bf16[16,16,512]{2,1,0:T(8,128)(2,1)S(1)}, bf16[4,64,768]{2,1,0:T(8,128)(2,1)S(1)}) custom-call(s32[8,768]{1,0:T(8,128)S(1)} %get-tuple-element.29.code_ref, f32[4,1024]{1,0:T(4,128)S(1)} %copy-done, f32[8,16,768]{2,1,0:T(8,128)S(1)} %early.5.sum_ref, f32[4,16,512]{2,1,0:T(8,128)S(1)} %get-tuple-element.77.refs_0_, ...), custom_call_target="tpu_custom_call" | custom-call | flops 100663296 | bytes 6291456 | tf_op jit(solution)/shard_map/step/pallas_call | solution.py:329
  86.2 1.2 %collective-permute-start.18 = (bf16[16,16,512]{2,1,0:T(8,128)(2,1)S(1)}, bf16[16,16,512]{2,1,0:T(8,128)(2,1)S(1)}, u32[]{:S(2)}, u32[]{:S(2)}) collective-permute-start(bf16[16,16,512]{2,1,0:T(8,128)(2,1)S(1)} %get-tuple-element.51), channel_id=1, source_target_pairs={{0,4},{1,9},{2,6},{3,11},{4,0},{5,13},{6,2},{7,15},{8,12},{9,1},{1... | collective-permute-start | bytes 786440 | tf_op jit(solution)/shard_map/ppermute | solution.py:256
  87.5 1.3 %step.16 = (bf16[16,16,512]{2,1,0:T(8,128)(2,1)S(1)}, bf16[2,64,768]{2,1,0:T(8,128)(2,1)S(1)}) custom-call(s32[8,768]{1,0:T(8,128)S(1)} %get-tuple-element.29.code_ref, f32[4,1024]{1,0:T(4,128)S(1)} %copy-done, f32[8,16,768]{2,1,0:T(8,128)S(1)} %early.5.sum_ref, f32[4,16,512]{2,1,0:T(8,128)S(1)} %get-tuple-element.77.refs_0_, ...), custom_call_target="tpu_custom_call" | custom-call | flops 100663296 | bytes 6291456 | tf_op jit(solution)/shard_map/step/pallas_call | solution.py:329
  88.9 1.9 %step.17 = (f32[16,16,512]{2,1,0:T(8,128)S(1)}, f32[16,16,512]{2,1,0:T(8,128)S(1)}) custom-call(s32[8,768]{1,0:T(8,128)S(1)} %get-tuple-element.29.code_ref, f32[4,1024]{1,0:T(4,128)S(1)} %copy-done, f32[8,16,768]{2,1,0:T(8,128)S(1)} %early.5.sum_ref, f32[4,16,512]{2,1,0:T(8,128)S(1)} %get-tuple-element.77.refs_0_, ...), custom_call_target="tpu_custom_call" | custom-call | flops 100663296 | bytes 6291456 | tf_op jit(solution)/shard_map/step/pallas_call | solution.py:329
  90.8 1.9 %collective-permute-done.18 = bf16[16,16,512]{2,1,0:T(8,128)(2,1)S(1)} collective-permute-done((bf16[16,16,512]{2,1,0:T(8,128)(2,1)S(1)}, bf16[16,16,512]{2,1,0:T(8,128)(2,1)S(1)}, u32[]{:S(2)}, u32[]{:S(2)}) %collective-permute-start.18) | collective-permute-done | bytes 262176 | tf_op jit(solution)/shard_map/ppermute | solution.py:256
  92.8 0.2 collective-permute-start.19
  92.9 2.3 %collective-permute-done.21 = bf16[16,16,512]{2,1,0:T(8,128)(2,1)S(1)} collective-permute-done((bf16[16,16,512]{2,1,0:T(8,128)(2,1)S(1)}, bf16[16,16,512]{2,1,0:T(8,128)(2,1)S(1)}, u32[]{:S(2)}, u32[]{:S(2)}) %collective-permute-start.21) | collective-permute-done | bytes 262176 | tf_op jit(solution)/shard_map/ppermute | solution.py:256
  95.3 0.9 collective-permute-start.22
  96.2 1.5 %collective-permute-done.19 = bf16[8,16,512]{2,1,0:T(8,128)(2,1)S(1)} collective-permute-done((bf16[8,16,512]{2,1,0:T(8,128)(2,1)S(1)}, bf16[8,16,512]{2,1,0:T(8,128)(2,1)S(1)}, u32[]{:S(2)}, u32[]{:S(2)}) %collective-permute-start.19) | collective-permute-done | bytes 131104 | tf_op jit(solution)/shard_map/ppermute | solution.py:256
  97.8 1.4 %collective-permute-start.20 = (bf16[4,16,512]{2,1,0:T(8,128)(2,1)S(1)}, bf16[4,16,512]{2,1,0:T(8,128)(2,1)S(1)}, u32[]{:S(2)}, u32[]{:S(2)}) collective-permute-start(bf16[4,16,512]{2,1,0:T(8,128)(2,1)S(1)} %get-tuple-element.74), channel_id=1, source_target_pairs={{0,16},{1,17},{2,18},{3,19},{4,20},{5,21},{6,22},{7,23},{8,24},{9,... | collective-permute-start | bytes 196616 | tf_op jit(solution)/shard_map/ppermute | solution.py:256
  99.3 1.1 collective-permute-done.22
  100.4 1.2 %collective-permute-start.23 = (bf16[4,16,512]{2,1,0:T(8,128)(2,1)S(1)}, bf16[4,16,512]{2,1,0:T(8,128)(2,1)S(1)}, u32[]{:S(2)}, u32[]{:S(2)}) collective-permute-start(bf16[4,16,512]{2,1,0:T(8,128)(2,1)S(1)} %get-tuple-element.72), channel_id=1, source_target_pairs={{0,16},{1,17},{2,18},{3,19},{4,20},{5,21},{6,22},{7,23},{8,24},{9,... | collective-permute-start | bytes 196616 | tf_op jit(solution)/shard_map/ppermute | solution.py:256
  101.6 1.7 %collective-permute-done.20.refs_1_ = bf16[4,16,512]{2,1,0:T(8,128)(2,1)S(1)} collective-permute-done((bf16[4,16,512]{2,1,0:T(8,128)(2,1)S(1)}, bf16[4,16,512]{2,1,0:T(8,128)(2,1)S(1)}, u32[]{:S(2)}, u32[]{:S(2)}) %collective-permute-start.20) | collective-permute-done | bytes 65568 | tf_op jit(solution)/shard_map/ppermute | solution.py:256
  103.3 2.4 %collective-permute-done.23.refs_3_ = bf16[4,16,512]{2,1,0:T(8,128)(2,1)S(1)} collective-permute-done((bf16[4,16,512]{2,1,0:T(8,128)(2,1)S(1)}, bf16[4,16,512]{2,1,0:T(8,128)(2,1)S(1)}, u32[]{:S(2)}, u32[]{:S(2)}) %collective-permute-start.23) | collective-permute-done | bytes 65568 | tf_op jit(solution)/shard_map/ppermute | solution.py:256
  105.8 0.8 finish.1
  106.5 1.5 %collective-permute-start.25 = (f32[4,1024]{1,0:T(4,128)S(1)}, f32[4,1024]{1,0:T(4,128)S(1)}, u32[]{:S(2)}, u32[]{:S(2)}) collective-permute-start(f32[4,1024]{1,0:T(4,128)S(1)} %get-tuple-element.55), channel_id=1, source_target_pairs={{0,2},{1,3},{2,0},{3,1},{4,6},{5,7},{6,4},{7,5},{8,10},{9,11},{10,... | collective-permute-start | bytes 49160 | tf_op jit(solution)/shard_map/ppermute | solution.py:436
  108.1 0.3 collective-permute-start.24
  108.4 1.4 %collective-permute-done.26 = f32[4,1024]{1,0:T(4,128)S(1)} collective-permute-done((f32[4,1024]{1,0:T(4,128)S(1)}, f32[4,1024]{1,0:T(4,128)S(1)}, u32[]{:S(2)}, u32[]{:S(2)}) %collective-permute-start.26) | collective-permute-done | bytes 16416 | tf_op jit(solution)/shard_map/ppermute | solution.py:436
  109.8 0.5 collective-permute-done.25
  110.3 0.6 add_multiply_fusion
  (28 shorter events, 0.9 us)
Async XLA Ops:
  0.6 16.9 %copy-start = (f32[4,1024]{1,0:T(4,128)S(1)}, f32[4,1024]{1,0:T(4,128)}, u32[]{:S(2)}) copy-start(f32[4,1024]{1,0:T(4,128)} %contrast_ref.25) | copy-start | bytes 49156
  0.6 27.8 %copy-start.2 = (f32[4,16,1024]{2,1,0:T(8,128)S(1)}, f32[4,16,1024]{2,1,0:T(8,128)}, u32[]{:S(2)}) copy-start(f32[4,16,1024]{2,1,0:T(8,128)} %refs_3_.1) | copy-start | bytes 786436
  12.9 9.6 %collective-permute-start = (bf16[16,16,512]{2,1,0:T(8,128)(2,1)S(1)}, bf16[16,16,512]{2,1,0:T(8,128)(2,1)S(1)}, u32[]{:S(2)}, u32[]{:S(2)}) collective-permute-start(bf16[16,16,512]{2,1,0:T(8,128)(2,1)S(1)} %get-tuple-element.31), channel_id=1, source_target_pairs={{0,4},{1,9},{2,6},{3,11},{4,0},{5,13},{6,2},{7,15},{8,12},{9,1},{1... | collective-permute-start | bytes 786440 | tf_op jit(solution)/shard_map/ppermute | solution.py:256
  16.0 8.3 %collective-permute-start.3 = (bf16[16,16,512]{2,1,0:T(8,128)(2,1)S(1)}, bf16[16,16,512]{2,1,0:T(8,128)(2,1)S(1)}, u32[]{:S(2)}, u32[]{:S(2)}) collective-permute-start(bf16[16,16,512]{2,1,0:T(8,128)(2,1)S(1)} %get-tuple-element.34), channel_id=1, source_target_pairs={{0,8},{1,5},{2,10},{3,7},{4,12},{5,1},{6,14},{7,3},{8,0},{9,13},{1... | collective-permute-start | bytes 786440 | tf_op jit(solution)/shard_map/ppermute | solution.py:256
  22.6 5.9 %collective-permute-start.1 = (bf16[8,16,512]{2,1,0:T(8,128)(2,1)S(1)}, bf16[8,16,512]{2,1,0:T(8,128)(2,1)S(1)}, u32[]{:S(2)}, u32[]{:S(2)}) collective-permute-start(bf16[8,16,512]{2,1,0:T(8,128)(2,1)S(1)} %get-tuple-element.70), channel_id=1, source_target_pairs={{0,8},{1,5},{2,10},{3,7},{4,12},{5,1},{6,14},{7,3},{8,0},{9,13},{1... | collective-permute-start | bytes 393224 | tf_op jit(solution)/shard_map/ppermute | solution.py:256
  24.4 8.3 %collective-permute-start.4 = (bf16[8,16,512]{2,1,0:T(8,128)(2,1)S(1)}, bf16[8,16,512]{2,1,0:T(8,128)(2,1)S(1)}, u32[]{:S(2)}, u32[]{:S(2)}) collective-permute-start(bf16[8,16,512]{2,1,0:T(8,128)(2,1)S(1)} %get-tuple-element.68), channel_id=1, source_target_pairs={{0,4},{1,9},{2,6},{3,11},{4,0},{5,13},{6,2},{7,15},{8,12},{9,1},{1... | collective-permute-start | bytes 393224 | tf_op jit(solution)/shard_map/ppermute | solution.py:256
  28.5 6.4 %collective-permute-start.2 = (bf16[4,16,512]{2,1,0:T(8,128)(2,1)S(1)}, bf16[4,16,512]{2,1,0:T(8,128)(2,1)S(1)}, u32[]{:S(2)}, u32[]{:S(2)}) collective-permute-start(bf16[4,16,512]{2,1,0:T(8,128)(2,1)S(1)} %get-tuple-element.86), channel_id=1, source_target_pairs={{0,16},{1,17},{2,18},{3,19},{4,20},{5,21},{6,22},{7,23},{8,24},{9,... | collective-permute-start | bytes 196616 | tf_op jit(solution)/shard_map/ppermute | solution.py:256
  32.7 5.3 %collective-permute-start.5 = (bf16[4,16,512]{2,1,0:T(8,128)(2,1)S(1)}, bf16[4,16,512]{2,1,0:T(8,128)(2,1)S(1)}, u32[]{:S(2)}, u32[]{:S(2)}) collective-permute-start(bf16[4,16,512]{2,1,0:T(8,128)(2,1)S(1)} %get-tuple-element.84), channel_id=1, source_target_pairs={{0,16},{1,17},{2,18},{3,19},{4,20},{5,21},{6,22},{7,23},{8,24},{9,... | collective-permute-start | bytes 196616 | tf_op jit(solution)/shard_map/ppermute | solution.py:256
  39.9 7.6 %collective-permute-start.6 = (bf16[16,16,512]{2,1,0:T(8,128)(2,1)S(1)}, bf16[16,16,512]{2,1,0:T(8,128)(2,1)S(1)}, u32[]{:S(2)}, u32[]{:S(2)}) collective-permute-start(bf16[16,16,512]{2,1,0:T(8,128)(2,1)S(1)} %get-tuple-element.39), channel_id=1, source_target_pairs={{0,4},{1,9},{2,6},{3,11},{4,0},{5,13},{6,2},{7,15},{8,12},{9,1},{1... | collective-permute-start | bytes 786440 | tf_op jit(solution)/shard_map/ppermute | solution.py:256
  42.7 6.8 %collective-permute-start.9 = (bf16[16,16,512]{2,1,0:T(8,128)(2,1)S(1)}, bf16[16,16,512]{2,1,0:T(8,128)(2,1)S(1)}, u32[]{:S(2)}, u32[]{:S(2)}) collective-permute-start(bf16[16,16,512]{2,1,0:T(8,128)(2,1)S(1)} %get-tuple-element.41), channel_id=1, source_target_pairs={{0,8},{1,5},{2,10},{3,7},{4,12},{5,1},{6,14},{7,3},{8,0},{9,13},{1... | collective-permute-start | bytes 786440 | tf_op jit(solution)/shard_map/ppermute | solution.py:256
  47.6 5.7 %collective-permute-start.7 = (bf16[8,16,512]{2,1,0:T(8,128)(2,1)S(1)}, bf16[8,16,512]{2,1,0:T(8,128)(2,1)S(1)}, u32[]{:S(2)}, u32[]{:S(2)}) collective-permute-start(bf16[8,16,512]{2,1,0:T(8,128)(2,1)S(1)} %get-tuple-element.66), channel_id=1, source_target_pairs={{0,8},{1,5},{2,10},{3,7},{4,12},{5,1},{6,14},{7,3},{8,0},{9,13},{1... | collective-permute-start | bytes 393224 | tf_op jit(solution)/shard_map/ppermute | solution.py:256
  49.5 5.7 %collective-permute-start.10 = (bf16[8,16,512]{2,1,0:T(8,128)(2,1)S(1)}, bf16[8,16,512]{2,1,0:T(8,128)(2,1)S(1)}, u32[]{:S(2)}, u32[]{:S(2)}) collective-permute-start(bf16[8,16,512]{2,1,0:T(8,128)(2,1)S(1)} %get-tuple-element.64), channel_id=1, source_target_pairs={{0,4},{1,9},{2,6},{3,11},{4,0},{5,13},{6,2},{7,15},{8,12},{9,1},{1... | collective-permute-start | bytes 393224 | tf_op jit(solution)/shard_map/ppermute | solution.py:256
  53.4 5.8 %collective-permute-start.8 = (bf16[4,16,512]{2,1,0:T(8,128)(2,1)S(1)}, bf16[4,16,512]{2,1,0:T(8,128)(2,1)S(1)}, u32[]{:S(2)}, u32[]{:S(2)}) collective-permute-start(bf16[4,16,512]{2,1,0:T(8,128)(2,1)S(1)} %get-tuple-element.82), channel_id=1, source_target_pairs={{0,16},{1,17},{2,18},{3,19},{4,20},{5,21},{6,22},{7,23},{8,24},{9,... | collective-permute-start | bytes 196616 | tf_op jit(solution)/shard_map/ppermute | solution.py:256
  55.3 6.1 %collective-permute-start.11 = (bf16[4,16,512]{2,1,0:T(8,128)(2,1)S(1)}, bf16[4,16,512]{2,1,0:T(8,128)(2,1)S(1)}, u32[]{:S(2)}, u32[]{:S(2)}) collective-permute-start(bf16[4,16,512]{2,1,0:T(8,128)(2,1)S(1)} %get-tuple-element.80), channel_id=1, source_target_pairs={{0,16},{1,17},{2,18},{3,19},{4,20},{5,21},{6,22},{7,23},{8,24},{9,... | collective-permute-start | bytes 196616 | tf_op jit(solution)/shard_map/ppermute | solution.py:256
  63.4 6.4 %collective-permute-start.12 = (bf16[16,16,512]{2,1,0:T(8,128)(2,1)S(1)}, bf16[16,16,512]{2,1,0:T(8,128)(2,1)S(1)}, u32[]{:S(2)}, u32[]{:S(2)}) collective-permute-start(bf16[16,16,512]{2,1,0:T(8,128)(2,1)S(1)} %get-tuple-element.45), channel_id=1, source_target_pairs={{0,4},{1,9},{2,6},{3,11},{4,0},{5,13},{6,2},{7,15},{8,12},{9,1},{1... | collective-permute-start | bytes 786440 | tf_op jit(solution)/shard_map/ppermute | solution.py:256
  66.4 7.1 %collective-permute-start.15 = (bf16[16,16,512]{2,1,0:T(8,128)(2,1)S(1)}, bf16[16,16,512]{2,1,0:T(8,128)(2,1)S(1)}, u32[]{:S(2)}, u32[]{:S(2)}) collective-permute-start(bf16[16,16,512]{2,1,0:T(8,128)(2,1)S(1)} %get-tuple-element.47), channel_id=1, source_target_pairs={{0,8},{1,5},{2,10},{3,7},{4,12},{5,1},{6,14},{7,3},{8,0},{9,13},{1... | collective-permute-start | bytes 786440 | tf_op jit(solution)/shard_map/ppermute | solution.py:256
  69.9 5.0 %collective-permute-start.13 = (bf16[8,16,512]{2,1,0:T(8,128)(2,1)S(1)}, bf16[8,16,512]{2,1,0:T(8,128)(2,1)S(1)}, u32[]{:S(2)}, u32[]{:S(2)}) collective-permute-start(bf16[8,16,512]{2,1,0:T(8,128)(2,1)S(1)} %get-tuple-element.62), channel_id=1, source_target_pairs={{0,8},{1,5},{2,10},{3,7},{4,12},{5,1},{6,14},{7,3},{8,0},{9,13},{1... | collective-permute-start | bytes 393224 | tf_op jit(solution)/shard_map/ppermute | solution.py:256
  73.6 5.0 %collective-permute-start.16 = (bf16[8,16,512]{2,1,0:T(8,128)(2,1)S(1)}, bf16[8,16,512]{2,1,0:T(8,128)(2,1)S(1)}, u32[]{:S(2)}, u32[]{:S(2)}) collective-permute-start(bf16[8,16,512]{2,1,0:T(8,128)(2,1)S(1)} %get-tuple-element.60), channel_id=1, source_target_pairs={{0,4},{1,9},{2,6},{3,11},{4,0},{5,13},{6,2},{7,15},{8,12},{9,1},{1... | collective-permute-start | bytes 393224 | tf_op jit(solution)/shard_map/ppermute | solution.py:256
  75.0 5.9 %collective-permute-start.14 = (bf16[4,16,512]{2,1,0:T(8,128)(2,1)S(1)}, bf16[4,16,512]{2,1,0:T(8,128)(2,1)S(1)}, u32[]{:S(2)}, u32[]{:S(2)}) collective-permute-start(bf16[4,16,512]{2,1,0:T(8,128)(2,1)S(1)} %get-tuple-element.78), channel_id=1, source_target_pairs={{0,16},{1,17},{2,18},{3,19},{4,20},{5,21},{6,22},{7,23},{8,24},{9,... | collective-permute-start | bytes 196616 | tf_op jit(solution)/shard_map/ppermute | solution.py:256
  78.7 5.6 %collective-permute-start.17 = (bf16[4,16,512]{2,1,0:T(8,128)(2,1)S(1)}, bf16[4,16,512]{2,1,0:T(8,128)(2,1)S(1)}, u32[]{:S(2)}, u32[]{:S(2)}) collective-permute-start(bf16[4,16,512]{2,1,0:T(8,128)(2,1)S(1)} %get-tuple-element.76), channel_id=1, source_target_pairs={{0,16},{1,17},{2,18},{3,19},{4,20},{5,21},{6,22},{7,23},{8,24},{9,... | collective-permute-start | bytes 196616 | tf_op jit(solution)/shard_map/ppermute | solution.py:256
  86.2 6.4 %collective-permute-start.18 = (bf16[16,16,512]{2,1,0:T(8,128)(2,1)S(1)}, bf16[16,16,512]{2,1,0:T(8,128)(2,1)S(1)}, u32[]{:S(2)}, u32[]{:S(2)}) collective-permute-start(bf16[16,16,512]{2,1,0:T(8,128)(2,1)S(1)} %get-tuple-element.51), channel_id=1, source_target_pairs={{0,4},{1,9},{2,6},{3,11},{4,0},{5,13},{6,2},{7,15},{8,12},{9,1},{1... | collective-permute-start | bytes 786440 | tf_op jit(solution)/shard_map/ppermute | solution.py:256
  88.8 6.4 %collective-permute-start.21 = (bf16[16,16,512]{2,1,0:T(8,128)(2,1)S(1)}, bf16[16,16,512]{2,1,0:T(8,128)(2,1)S(1)}, u32[]{:S(2)}, u32[]{:S(2)}) collective-permute-start(bf16[16,16,512]{2,1,0:T(8,128)(2,1)S(1)} %get-tuple-element.53), channel_id=1, source_target_pairs={{0,8},{1,5},{2,10},{3,7},{4,12},{5,1},{6,14},{7,3},{8,0},{9,13},{1... | collective-permute-start | bytes 786440 | tf_op jit(solution)/shard_map/ppermute | solution.py:256
  88.9 16.9 %copy-start.1 = (bf16[4,16,1024]{2,1,0:T(8,128)(2,1)S(1)}, bf16[4,16,1024]{2,1,0:T(8,128)(2,1)}, u32[]{:S(2)}) copy-start(bf16[4,16,1024]{2,1,0:T(8,128)(2,1)} %forward_ref.1) | copy-start | bytes 393220
  92.8 5.0 %collective-permute-start.19 = (bf16[8,16,512]{2,1,0:T(8,128)(2,1)S(1)}, bf16[8,16,512]{2,1,0:T(8,128)(2,1)S(1)}, u32[]{:S(2)}, u32[]{:S(2)}) collective-permute-start(bf16[8,16,512]{2,1,0:T(8,128)(2,1)S(1)} %get-tuple-element.58), channel_id=1, source_target_pairs={{0,8},{1,5},{2,10},{3,7},{4,12},{5,1},{6,14},{7,3},{8,0},{9,13},{1... | collective-permute-start | bytes 393224 | tf_op jit(solution)/shard_map/ppermute | solution.py:256
  95.3 5.0 %collective-permute-start.22 = (bf16[8,16,512]{2,1,0:T(8,128)(2,1)S(1)}, bf16[8,16,512]{2,1,0:T(8,128)(2,1)S(1)}, u32[]{:S(2)}, u32[]{:S(2)}) collective-permute-start(bf16[8,16,512]{2,1,0:T(8,128)(2,1)S(1)} %get-tuple-element.56), channel_id=1, source_target_pairs={{0,4},{1,9},{2,6},{3,11},{4,0},{5,13},{6,2},{7,15},{8,12},{9,1},{1... | collective-permute-start | bytes 393224 | tf_op jit(solution)/shard_map/ppermute | solution.py:256
  97.8 5.5 %collective-permute-start.20 = (bf16[4,16,512]{2,1,0:T(8,128)(2,1)S(1)}, bf16[4,16,512]{2,1,0:T(8,128)(2,1)S(1)}, u32[]{:S(2)}, u32[]{:S(2)}) collective-permute-start(bf16[4,16,512]{2,1,0:T(8,128)(2,1)S(1)} %get-tuple-element.74), channel_id=1, source_target_pairs={{0,16},{1,17},{2,18},{3,19},{4,20},{5,21},{6,22},{7,23},{8,24},{9,... | collective-permute-start | bytes 196616 | tf_op jit(solution)/shard_map/ppermute | solution.py:256
  100.4 5.4 %collective-permute-start.23 = (bf16[4,16,512]{2,1,0:T(8,128)(2,1)S(1)}, bf16[4,16,512]{2,1,0:T(8,128)(2,1)S(1)}, u32[]{:S(2)}, u32[]{:S(2)}) collective-permute-start(bf16[4,16,512]{2,1,0:T(8,128)(2,1)S(1)} %get-tuple-element.72), channel_id=1, source_target_pairs={{0,16},{1,17},{2,18},{3,19},{4,20},{5,21},{6,22},{7,23},{8,24},{9,... | collective-permute-start | bytes 196616 | tf_op jit(solution)/shard_map/ppermute | solution.py:256
  106.5 3.3 %collective-permute-start.26 = (f32[4,1024]{1,0:T(4,128)S(1)}, f32[4,1024]{1,0:T(4,128)S(1)}, u32[]{:S(2)}, u32[]{:S(2)}) collective-permute-start(f32[4,1024]{1,0:T(4,128)S(1)} %get-tuple-element.55), channel_id=1, source_target_pairs={{0,3},{1,2},{2,1},{3,0},{4,7},{5,6},{6,5},{7,4},{8,11},{9,10},{10,... | collective-permute-start | bytes 49160 | tf_op jit(solution)/shard_map/ppermute | solution.py:436
  106.5 3.8 %collective-permute-start.25 = (f32[4,1024]{1,0:T(4,128)S(1)}, f32[4,1024]{1,0:T(4,128)S(1)}, u32[]{:S(2)}, u32[]{:S(2)}) collective-permute-start(f32[4,1024]{1,0:T(4,128)S(1)} %get-tuple-element.55), channel_id=1, source_target_pairs={{0,2},{1,3},{2,0},{3,1},{4,6},{5,7},{6,4},{7,5},{8,10},{9,11},{10,... | collective-permute-start | bytes 49160 | tf_op jit(solution)/shard_map/ppermute | solution.py:436
  108.1 2.2 %collective-permute-start.24 = (f32[4,1024]{1,0:T(4,128)S(1)}, f32[4,1024]{1,0:T(4,128)S(1)}, u32[]{:S(2)}, u32[]{:S(2)}) collective-permute-start(f32[4,1024]{1,0:T(4,128)S(1)} %get-tuple-element.55), channel_id=1, source_target_pairs={{0,1},{1,0},{2,3},{3,2},{4,5},{5,4},{6,7},{7,6},{8,9},{9,8},{10,11... | collective-permute-start | bytes 49160 | tf_op jit(solution)/shard_map/ppermute | solution.py:436

commit v11 on v10

--- a/solution.py
+++ b/solution.py
@@ -11,7 +11,7 @@
 
 def parts_of(unknowns, peers):
     bits = list(range(peers.bit_length() - 1))
-    turned = bits[1:2] + bits[:1] + bits[2:]
+    turned = bits[1:] + bits[:1]
     width = unknowns // 2
     return [(0, width, bits), (width, width, turned)]
 

time: 111 us -> 117 us (1.054)
  waiting for transfers between devices: 38.6 us -> 45.6 us
    ppermute x24, waiting for transfers between devices: 36.7 us -> 43.8 us  [swap(): return lax.ppermute(x, ('rows', 'src'), pairs)]
where the time goes in v11:
time: 117 us
  waiting for transfers between devices  45.6 us (39%)
  Pallas kernels  34.8 us (30%)
  starting transfers between devices  34 us (29%)
  other arithmetic  1.58 us (1%)
    ppermute x24, waiting for transfers between devices, swap(): return lax.ppermute(x, ('rows', 'src'), pairs)  43.8 us
    ppermute x24, starting transfers between devices, swap(): return lax.ppermute(x, ('rows', 'src'), pairs)  32 us
    pallas_call x9, Pallas kernels, slot_sums(): pl.pallas_call(functools.partial(step_kernel, dims, parts[late], [*known]...  15.6 us
    pallas_call x1, Pallas kernels, slot_sums(): pl.pallas_call(functools.partial(start_kernel, (rows_dev, tiles_row, rank...  12.3 us
    pallas_call x3, Pallas kernels, slot_sums(): pl.pallas_call(functools.partial(early_kernel, dims, [parts[i] for i in e...  6.24 us
  transfers between devices with their start and end apart: 27, of which 22 were waited for; matrix products, arithmetic and copies ran while one was open for 1% of the time, Pallas kernels for 14%

profile of v11, /device:TPU:0, one launch (start us, length us, event | category | flops | bytes accessed | tf_op | source)
XLA Modules:
  0.0 116.9 jit_solution(3697575758586264617)
XLA Ops:
  0.7 12.3 %start.1 = (bf16[6144,1024]{1,0:T(8,128)(2,1)S(1)}, bf16[6144,1024]{1,0:T(8,128)(2,1)S(1)}, s32[8,768]{1,0:T(8,128)S(1)}, f32[16,16,512]{2,1,0:T(8,128)S(1)}, bf...) custom-call(s32[16,32]{1,0:T(8,128)} %bitcast.11, s32[32]{0:T(128)} %refs_1_.1, ...), custom_call_target="tpu_custom_call" | custom-call | flops 402653184 | bytes 25165824 | tf_op jit(solution)/shard_map/start/pallas_call | solution.py:280
  12.9 3.0 %collective-permute-start = (bf16[16,16,512]{2,1,0:T(8,128)(2,1)S(1)}, bf16[16,16,512]{2,1,0:T(8,128)(2,1)S(1)}, u32[]{:S(2)}, u32[]{:S(2)}) collective-permute-start(bf16[16,16,512]{2,1,0:T(8,128)(2,1)S(1)} %get-tuple-element.31), channel_id=1, source_target_pairs={{0,4},{1,9},{2,6},{3,11},{4,0},{5,13},{6,2},{7,15},{8,12},{9,1},{1... | collective-permute-start | bytes 786440 | tf_op jit(solution)/shard_map/ppermute | solution.py:256
  16.0 1.6 %collective-permute-start.3 = (bf16[16,16,512]{2,1,0:T(8,128)(2,1)S(1)}, bf16[16,16,512]{2,1,0:T(8,128)(2,1)S(1)}, u32[]{:S(2)}, u32[]{:S(2)}) collective-permute-start(bf16[16,16,512]{2,1,0:T(8,128)(2,1)S(1)} %get-tuple-element.34), channel_id=1, source_target_pairs={{0,8},{1,5},{2,10},{3,7},{4,12},{5,1},{6,14},{7,3},{8,0},{9,13},{1... | collective-permute-start | bytes 786440 | tf_op jit(solution)/shard_map/ppermute | solution.py:256
  17.6 5.0 %collective-permute-done = bf16[16,16,512]{2,1,0:T(8,128)(2,1)S(1)} collective-permute-done((bf16[16,16,512]{2,1,0:T(8,128)(2,1)S(1)}, bf16[16,16,512]{2,1,0:T(8,128)(2,1)S(1)}, u32[]{:S(2)}, u32[]{:S(2)}) %collective-permute-start) | collective-permute-done | bytes 262176 | tf_op jit(solution)/shard_map/ppermute | solution.py:256
  22.6 1.7 %collective-permute-start.1 = (bf16[8,16,512]{2,1,0:T(8,128)(2,1)S(1)}, bf16[8,16,512]{2,1,0:T(8,128)(2,1)S(1)}, u32[]{:S(2)}, u32[]{:S(2)}) collective-permute-start(bf16[8,16,512]{2,1,0:T(8,128)(2,1)S(1)} %get-tuple-element.70), channel_id=1, source_target_pairs={{0,8},{1,5},{2,10},{3,7},{4,12},{5,1},{6,14},{7,3},{8,0},{9,13},{1... | collective-permute-start | bytes 393224 | tf_op jit(solution)/shard_map/ppermute | solution.py:256
  24.4 2.7 %collective-permute-start.4 = (bf16[8,16,512]{2,1,0:T(8,128)(2,1)S(1)}, bf16[8,16,512]{2,1,0:T(8,128)(2,1)S(1)}, u32[]{:S(2)}, u32[]{:S(2)}) collective-permute-start(bf16[8,16,512]{2,1,0:T(8,128)(2,1)S(1)} %get-tuple-element.68), channel_id=1, source_target_pairs={{0,16},{1,17},{2,18},{3,19},{4,20},{5,21},{6,22},{7,23},{8,24},{9,... | collective-permute-start | bytes 393224 | tf_op jit(solution)/shard_map/ppermute | solution.py:256
  27.1 0.5 collective-permute-done.1
  27.7 4.3 %collective-permute-start.2 = (bf16[4,16,512]{2,1,0:T(8,128)(2,1)S(1)}, bf16[4,16,512]{2,1,0:T(8,128)(2,1)S(1)}, u32[]{:S(2)}, u32[]{:S(2)}) collective-permute-start(bf16[4,16,512]{2,1,0:T(8,128)(2,1)S(1)} %get-tuple-element.86), channel_id=1, source_target_pairs={{0,16},{1,17},{2,18},{3,19},{4,20},{5,21},{6,22},{7,23},{8,24},{9,... | collective-permute-start | bytes 196616 | tf_op jit(solution)/shard_map/ppermute | solution.py:256
  32.0 1.9 %collective-permute-done.4 = bf16[8,16,512]{2,1,0:T(8,128)(2,1)S(1)} collective-permute-done((bf16[8,16,512]{2,1,0:T(8,128)(2,1)S(1)}, bf16[8,16,512]{2,1,0:T(8,128)(2,1)S(1)}, u32[]{:S(2)}, u32[]{:S(2)}) %collective-permute-start.4) | collective-permute-done | bytes 131104 | tf_op jit(solution)/shard_map/ppermute | solution.py:256
  33.9 1.4 %collective-permute-start.5 = (bf16[4,16,512]{2,1,0:T(8,128)(2,1)S(1)}, bf16[4,16,512]{2,1,0:T(8,128)(2,1)S(1)}, u32[]{:S(2)}, u32[]{:S(2)}) collective-permute-start(bf16[4,16,512]{2,1,0:T(8,128)(2,1)S(1)} %get-tuple-element.84), channel_id=1, source_target_pairs={{0,4},{1,9},{2,6},{3,11},{4,0},{5,13},{6,2},{7,15},{8,12},{9,1},{1... | collective-permute-start | bytes 196616 | tf_op jit(solution)/shard_map/ppermute | solution.py:256
  35.3 0.1 collective-permute-done.2.refs_1_
  35.3 2.0 %early.3.sum_ref = f32[8,16,768]{2,1,0:T(8,128)S(1)} custom-call(s32[8,768]{1,0:T(8,128)S(1)} %get-tuple-element.29.code_ref, f32[4,1024]{1,0:T(4,128)S(1)} %copy-done, f32[4,16,512]{2,1,0:T(8,128)S(1)} %get-tuple-element.87.refs_0_, bf16[4,16,512]{2,1,0:T(8,128)(2,1)S(1)} %collective-permute-done.2.refs_1_, bf16[6144,1024]{1,0:T(8,128)(2,1)S(1)} %get-tuple-element.32.refs_2_), custom_call_target="tpu_custom_call" | custom-call | flops 100663296 | bytes 6291456 | tf_op jit(solution)/shard_map/early/pallas_call | solution.py:309
  37.4 0.9 collective-permute-done.5.refs_1_
  38.2 2.0 %step.9 = (bf16[16,16,512]{2,1,0:T(8,128)(2,1)S(1)}, bf16[4,64,768]{2,1,0:T(8,128)(2,1)S(1)}) custom-call(s32[8,768]{1,0:T(8,128)S(1)} %get-tuple-element.29.code_ref, f32[4,1024]{1,0:T(4,128)S(1)} %copy-done, f32[8,16,768]{2,1,0:T(8,128)S(1)} %early.3.sum_ref, f32[4,16,512]{2,1,0:T(8,128)S(1)} %get-tuple-element.85.refs_0_, ...), custom_call_target="tpu_custom_call" | custom-call | flops 100663296 | bytes 6291456 | tf_op jit(solution)/shard_map/step/pallas_call | solution.py:329
  40.2 1.4 %collective-permute-start.6 = (bf16[16,16,512]{2,1,0:T(8,128)(2,1)S(1)}, bf16[16,16,512]{2,1,0:T(8,128)(2,1)S(1)}, u32[]{:S(2)}, u32[]{:S(2)}) collective-permute-start(bf16[16,16,512]{2,1,0:T(8,128)(2,1)S(1)} %get-tuple-element.39), channel_id=1, source_target_pairs={{0,4},{1,9},{2,6},{3,11},{4,0},{5,13},{6,2},{7,15},{8,12},{9,1},{1... | collective-permute-start | bytes 786440 | tf_op jit(solution)/shard_map/ppermute | solution.py:256
  41.7 1.3 %step.10 = (bf16[16,16,512]{2,1,0:T(8,128)(2,1)S(1)}, bf16[2,64,768]{2,1,0:T(8,128)(2,1)S(1)}) custom-call(s32[8,768]{1,0:T(8,128)S(1)} %get-tuple-element.29.code_ref, f32[4,1024]{1,0:T(4,128)S(1)} %copy-done, f32[8,16,768]{2,1,0:T(8,128)S(1)} %early.3.sum_ref, f32[4,16,512]{2,1,0:T(8,128)S(1)} %get-tuple-element.85.refs_0_, ...), custom_call_target="tpu_custom_call" | custom-call | flops 100663296 | bytes 6291456 | tf_op jit(solution)/shard_map/step/pallas_call | solution.py:329
  43.0 0.3 collective-permute-start.9
  43.3 1.9 %step.11 = (f32[16,16,512]{2,1,0:T(8,128)S(1)}, f32[16,16,512]{2,1,0:T(8,128)S(1)}) custom-call(s32[8,768]{1,0:T(8,128)S(1)} %get-tuple-element.29.code_ref, f32[4,1024]{1,0:T(4,128)S(1)} %copy-done, f32[8,16,768]{2,1,0:T(8,128)S(1)} %early.3.sum_ref, f32[4,16,512]{2,1,0:T(8,128)S(1)} %get-tuple-element.85.refs_0_, ...), custom_call_target="tpu_custom_call" | custom-call | flops 100663296 | bytes 6291456 | tf_op jit(solution)/shard_map/step/pallas_call | solution.py:329
  45.2 4.0 %collective-permute-done.6 = bf16[16,16,512]{2,1,0:T(8,128)(2,1)S(1)} collective-permute-done((bf16[16,16,512]{2,1,0:T(8,128)(2,1)S(1)}, bf16[16,16,512]{2,1,0:T(8,128)(2,1)S(1)}, u32[]{:S(2)}, u32[]{:S(2)}) %collective-permute-start.6) | collective-permute-done | bytes 262176 | tf_op jit(solution)/shard_map/ppermute | solution.py:256
  49.2 0.1 add_convert_fusion.5
  49.3 0.2 collective-permute-start.7
  49.5 0.1 add_convert_fusion.4
  49.6 2.4 %collective-permute-start.10 = (bf16[8,16,512]{2,1,0:T(8,128)(2,1)S(1)}, bf16[8,16,512]{2,1,0:T(8,128)(2,1)S(1)}, u32[]{:S(2)}, u32[]{:S(2)}) collective-permute-start(bf16[8,16,512]{2,1,0:T(8,128)(2,1)S(1)} %get-tuple-element.64), channel_id=1, source_target_pairs={{0,16},{1,17},{2,18},{3,19},{4,20},{5,21},{6,22},{7,23},{8,24},{9,... | collective-permute-start | bytes 393224 | tf_op jit(solution)/shard_map/ppermute | solution.py:256
  52.0 3.1 %collective-permute-done.7 = bf16[8,16,512]{2,1,0:T(8,128)(2,1)S(1)} collective-permute-done((bf16[8,16,512]{2,1,0:T(8,128)(2,1)S(1)}, bf16[8,16,512]{2,1,0:T(8,128)(2,1)S(1)}, u32[]{:S(2)}, u32[]{:S(2)}) %collective-permute-start.7) | collective-permute-done | bytes 131104 | tf_op jit(solution)/shard_map/ppermute | solution.py:256
  55.1 1.7 %collective-permute-start.8 = (bf16[4,16,512]{2,1,0:T(8,128)(2,1)S(1)}, bf16[4,16,512]{2,1,0:T(8,128)(2,1)S(1)}, u32[]{:S(2)}, u32[]{:S(2)}) collective-permute-start(bf16[4,16,512]{2,1,0:T(8,128)(2,1)S(1)} %get-tuple-element.82), channel_id=1, source_target_pairs={{0,16},{1,17},{2,18},{3,19},{4,20},{5,21},{6,22},{7,23},{8,24},{9,... | collective-permute-start | bytes 196616 | tf_op jit(solution)/shard_map/ppermute | solution.py:256
  56.8 1.4 %collective-permute-done.10 = bf16[8,16,512]{2,1,0:T(8,128)(2,1)S(1)} collective-permute-done((bf16[8,16,512]{2,1,0:T(8,128)(2,1)S(1)}, bf16[8,16,512]{2,1,0:T(8,128)(2,1)S(1)}, u32[]{:S(2)}, u32[]{:S(2)}) %collective-permute-start.10) | collective-permute-done | bytes 131104 | tf_op jit(solution)/shard_map/ppermute | solution.py:256
  58.3 1.4 %collective-permute-start.11 = (bf16[4,16,512]{2,1,0:T(8,128)(2,1)S(1)}, bf16[4,16,512]{2,1,0:T(8,128)(2,1)S(1)}, u32[]{:S(2)}, u32[]{:S(2)}) collective-permute-start(bf16[4,16,512]{2,1,0:T(8,128)(2,1)S(1)} %get-tuple-element.80), channel_id=1, source_target_pairs={{0,4},{1,9},{2,6},{3,11},{4,0},{5,13},{6,2},{7,15},{8,12},{9,1},{1... | collective-permute-start | bytes 196616 | tf_op jit(solution)/shard_map/ppermute | solution.py:256
  59.7 1.4 %collective-permute-done.8.refs_1_ = bf16[4,16,512]{2,1,0:T(8,128)(2,1)S(1)} collective-permute-done((bf16[4,16,512]{2,1,0:T(8,128)(2,1)S(1)}, bf16[4,16,512]{2,1,0:T(8,128)(2,1)S(1)}, u32[]{:S(2)}, u32[]{:S(2)}) %collective-permute-start.8) | collective-permute-done | bytes 65568 | tf_op jit(solution)/shard_map/ppermute | solution.py:256
  61.1 2.2 %early.4.sum_ref = f32[8,16,768]{2,1,0:T(8,128)S(1)} custom-call(s32[8,768]{1,0:T(8,128)S(1)} %get-tuple-element.29.code_ref, f32[4,1024]{1,0:T(4,128)S(1)} %copy-done, f32[4,16,512]{2,1,0:T(8,128)S(1)} %get-tuple-element.83.refs_0_, bf16[4,16,512]{2,1,0:T(8,128)(2,1)S(1)} %collective-permute-done.8.refs_1_, bf16[6144,1024]{1,0:T(8,128)(2,1)S(1)} %get-tuple-element.32.refs_2_), custom_call_target="tpu_custom_call" | custom-call | flops 100663296 | bytes 6291456 | tf_op jit(solution)/shard_map/early/pallas_call | solution.py:309
  63.3 2.0 %step.12 = (bf16[16,16,512]{2,1,0:T(8,128)(2,1)S(1)}, bf16[4,64,768]{2,1,0:T(8,128)(2,1)S(1)}) custom-call(s32[8,768]{1,0:T(8,128)S(1)} %get-tuple-element.29.code_ref, f32[4,1024]{1,0:T(4,128)S(1)} %copy-done, f32[8,16,768]{2,1,0:T(8,128)S(1)} %early.4.sum_ref, f32[4,16,512]{2,1,0:T(8,128)S(1)} %get-tuple-element.81.refs_0_, ...), custom_call_target="tpu_custom_call" | custom-call | flops 100663296 | bytes 6291456 | tf_op jit(solution)/shard_map/step/pallas_call | solution.py:329
  65.2 1.9 %collective-permute-start.12 = (bf16[16,16,512]{2,1,0:T(8,128)(2,1)S(1)}, bf16[16,16,512]{2,1,0:T(8,128)(2,1)S(1)}, u32[]{:S(2)}, u32[]{:S(2)}) collective-permute-start(bf16[16,16,512]{2,1,0:T(8,128)(2,1)S(1)} %get-tuple-element.45), channel_id=1, source_target_pairs={{0,4},{1,9},{2,6},{3,11},{4,0},{5,13},{6,2},{7,15},{8,12},{9,1},{1... | collective-permute-start | bytes 786440 | tf_op jit(solution)/shard_map/ppermute | solution.py:256
  67.2 1.3 %step.13 = (bf16[16,16,512]{2,1,0:T(8,128)(2,1)S(1)}, bf16[2,64,768]{2,1,0:T(8,128)(2,1)S(1)}) custom-call(s32[8,768]{1,0:T(8,128)S(1)} %get-tuple-element.29.code_ref, f32[4,1024]{1,0:T(4,128)S(1)} %copy-done, f32[8,16,768]{2,1,0:T(8,128)S(1)} %early.4.sum_ref, f32[4,16,512]{2,1,0:T(8,128)S(1)} %get-tuple-element.81.refs_0_, ...), custom_call_target="tpu_custom_call" | custom-call | flops 100663296 | bytes 6291456 | tf_op jit(solution)/shard_map/step/pallas_call | solution.py:329
  68.6 1.9 %step.14 = (f32[16,16,512]{2,1,0:T(8,128)S(1)}, f32[16,16,512]{2,1,0:T(8,128)S(1)}) custom-call(s32[8,768]{1,0:T(8,128)S(1)} %get-tuple-element.29.code_ref, f32[4,1024]{1,0:T(4,128)S(1)} %copy-done, f32[8,16,768]{2,1,0:T(8,128)S(1)} %early.4.sum_ref, f32[4,16,512]{2,1,0:T(8,128)S(1)} %get-tuple-element.81.refs_0_, ...), custom_call_target="tpu_custom_call" | custom-call | flops 100663296 | bytes 6291456 | tf_op jit(solution)/shard_map/step/pallas_call | solution.py:329
  70.5 2.6 %collective-permute-done.12 = bf16[16,16,512]{2,1,0:T(8,128)(2,1)S(1)} collective-permute-done((bf16[16,16,512]{2,1,0:T(8,128)(2,1)S(1)}, bf16[16,16,512]{2,1,0:T(8,128)(2,1)S(1)}, u32[]{:S(2)}, u32[]{:S(2)}) %collective-permute-start.12) | collective-permute-done | bytes 262176 | tf_op jit(solution)/shard_map/ppermute | solution.py:256
  73.1 0.1 add_convert_fusion.3
  73.2 1.1 collective-permute-start.13
  74.3 2.5 %collective-permute-done.15 = bf16[16,16,512]{2,1,0:T(8,128)(2,1)S(1)} collective-permute-done((bf16[16,16,512]{2,1,0:T(8,128)(2,1)S(1)}, bf16[16,16,512]{2,1,0:T(8,128)(2,1)S(1)}, u32[]{:S(2)}, u32[]{:S(2)}) %collective-permute-start.15) | collective-permute-done | bytes 262176 | tf_op jit(solution)/shard_map/ppermute | solution.py:256
  76.8 0.1 add_convert_fusion.2
  76.9 2.0 %collective-permute-done.13 = bf16[8,16,512]{2,1,0:T(8,128)(2,1)S(1)} collective-permute-done((bf16[8,16,512]{2,1,0:T(8,128)(2,1)S(1)}, bf16[8,16,512]{2,1,0:T(8,128)(2,1)S(1)}, u32[]{:S(2)}, u32[]{:S(2)}) %collective-permute-start.13) | collective-permute-done | bytes 131104 | tf_op jit(solution)/shard_map/ppermute | solution.py:256
  79.0 1.2 %collective-permute-start.14 = (bf16[4,16,512]{2,1,0:T(8,128)(2,1)S(1)}, bf16[4,16,512]{2,1,0:T(8,128)(2,1)S(1)}, u32[]{:S(2)}, u32[]{:S(2)}) collective-permute-start(bf16[4,16,512]{2,1,0:T(8,128)(2,1)S(1)} %get-tuple-element.78), channel_id=1, source_target_pairs={{0,16},{1,17},{2,18},{3,19},{4,20},{5,21},{6,22},{7,23},{8,24},{9,... | collective-permute-start | bytes 196616 | tf_op jit(solution)/shard_map/ppermute | solution.py:256
  80.1 2.6 %collective-permute-done.16 = bf16[8,16,512]{2,1,0:T(8,128)(2,1)S(1)} collective-permute-done((bf16[8,16,512]{2,1,0:T(8,128)(2,1)S(1)}, bf16[8,16,512]{2,1,0:T(8,128)(2,1)S(1)}, u32[]{:S(2)}, u32[]{:S(2)}) %collective-permute-start.16) | collective-permute-done | bytes 131104 | tf_op jit(solution)/shard_map/ppermute | solution.py:256
  82.8 1.2 %collective-permute-start.17 = (bf16[4,16,512]{2,1,0:T(8,128)(2,1)S(1)}, bf16[4,16,512]{2,1,0:T(8,128)(2,1)S(1)}, u32[]{:S(2)}, u32[]{:S(2)}) collective-permute-start(bf16[4,16,512]{2,1,0:T(8,128)(2,1)S(1)} %get-tuple-element.76), channel_id=1, source_target_pairs={{0,4},{1,9},{2,6},{3,11},{4,0},{5,13},{6,2},{7,15},{8,12},{9,1},{1... | collective-permute-start | bytes 196616 | tf_op jit(solution)/shard_map/ppermute | solution.py:256
  84.0 0.8 collective-permute-done.14.refs_1_
  84.9 2.0 %early.5.sum_ref = f32[8,16,768]{2,1,0:T(8,128)S(1)} custom-call(s32[8,768]{1,0:T(8,128)S(1)} %get-tuple-element.29.code_ref, f32[4,1024]{1,0:T(4,128)S(1)} %copy-done, f32[4,16,512]{2,1,0:T(8,128)S(1)} %get-tuple-element.79.refs_0_, bf16[4,16,512]{2,1,0:T(8,128)(2,1)S(1)} %collective-permute-done.14.refs_1_, bf16[6144,1024]{1,0:T(8,128)(2,1)S(1)} %get-tuple-element.32.refs_2_), custom_call_target="tpu_custom_call" | custom-call | flops 100663296 | bytes 6291456 | tf_op jit(solution)/shard_map/early/pallas_call | solution.py:309
  86.9 1.0 collective-permute-done.17.refs_1_
  87.9 2.0 %step.15 = (bf16[16,16,512]{2,1,0:T(8,128)(2,1)S(1)}, bf16[4,64,768]{2,1,0:T(8,128)(2,1)S(1)}) custom-call(s32[8,768]{1,0:T(8,128)S(1)} %get-tuple-element.29.code_ref, f32[4,1024]{1,0:T(4,128)S(1)} %copy-done, f32[8,16,768]{2,1,0:T(8,128)S(1)} %early.5.sum_ref, f32[4,16,512]{2,1,0:T(8,128)S(1)} %get-tuple-element.77.refs_0_, ...), custom_call_target="tpu_custom_call" | custom-call | flops 100663296 | bytes 6291456 | tf_op jit(solution)/shard_map/step/pallas_call | solution.py:329
  89.9 0.9 collective-permute-start.18
  90.7 1.3 %step.16 = (bf16[16,16,512]{2,1,0:T(8,128)(2,1)S(1)}, bf16[2,64,768]{2,1,0:T(8,128)(2,1)S(1)}) custom-call(s32[8,768]{1,0:T(8,128)S(1)} %get-tuple-element.29.code_ref, f32[4,1024]{1,0:T(4,128)S(1)} %copy-done, f32[8,16,768]{2,1,0:T(8,128)S(1)} %early.5.sum_ref, f32[4,16,512]{2,1,0:T(8,128)S(1)} %get-tuple-element.77.refs_0_, ...), custom_call_target="tpu_custom_call" | custom-call | flops 100663296 | bytes 6291456 | tf_op jit(solution)/shard_map/step/pallas_call | solution.py:329
  92.0 0.8 collective-permute-start.21
  92.9 1.9 %step.17 = (f32[16,16,512]{2,1,0:T(8,128)S(1)}, f32[16,16,512]{2,1,0:T(8,128)S(1)}) custom-call(s32[8,768]{1,0:T(8,128)S(1)} %get-tuple-element.29.code_ref, f32[4,1024]{1,0:T(4,128)S(1)} %copy-done, f32[8,16,768]{2,1,0:T(8,128)S(1)} %early.5.sum_ref, f32[4,16,512]{2,1,0:T(8,128)S(1)} %get-tuple-element.77.refs_0_, ...), custom_call_target="tpu_custom_call" | custom-call | flops 100663296 | bytes 6291456 | tf_op jit(solution)/shard_map/step/pallas_call | solution.py:329
  94.8 1.5 %collective-permute-done.18 = bf16[16,16,512]{2,1,0:T(8,128)(2,1)S(1)} collective-permute-done((bf16[16,16,512]{2,1,0:T(8,128)(2,1)S(1)}, bf16[16,16,512]{2,1,0:T(8,128)(2,1)S(1)}, u32[]{:S(2)}, u32[]{:S(2)}) %collective-permute-start.18) | collective-permute-done | bytes 262176 | tf_op jit(solution)/shard_map/ppermute | solution.py:256
  96.3 0.1 add_convert_fusion.1
  96.5 3.5 %collective-permute-done.21 = bf16[16,16,512]{2,1,0:T(8,128)(2,1)S(1)} collective-permute-done((bf16[16,16,512]{2,1,0:T(8,128)(2,1)S(1)}, bf16[16,16,512]{2,1,0:T(8,128)(2,1)S(1)}, u32[]{:S(2)}, u32[]{:S(2)}) %collective-permute-start.21) | collective-permute-done | bytes 262176 | tf_op jit(solution)/shard_map/ppermute | solution.py:256
  100.1 1.3 %collective-permute-done.19 = bf16[8,16,512]{2,1,0:T(8,128)(2,1)S(1)} collective-permute-done((bf16[8,16,512]{2,1,0:T(8,128)(2,1)S(1)}, bf16[8,16,512]{2,1,0:T(8,128)(2,1)S(1)}, u32[]{:S(2)}, u32[]{:S(2)}) %collective-permute-start.19) | collective-permute-done | bytes 131104 | tf_op jit(solution)/shard_map/ppermute | solution.py:256
  101.5 1.7 %collective-permute-start.20 = (bf16[4,16,512]{2,1,0:T(8,128)(2,1)S(1)}, bf16[4,16,512]{2,1,0:T(8,128)(2,1)S(1)}, u32[]{:S(2)}, u32[]{:S(2)}) collective-permute-start(bf16[4,16,512]{2,1,0:T(8,128)(2,1)S(1)} %get-tuple-element.74), channel_id=1, source_target_pairs={{0,16},{1,17},{2,18},{3,19},{4,20},{5,21},{6,22},{7,23},{8,24},{9,... | collective-permute-start | bytes 196616 | tf_op jit(solution)/shard_map/ppermute | solution.py:256
  103.2 4.1 %collective-permute-done.22 = bf16[8,16,512]{2,1,0:T(8,128)(2,1)S(1)} collective-permute-done((bf16[8,16,512]{2,1,0:T(8,128)(2,1)S(1)}, bf16[8,16,512]{2,1,0:T(8,128)(2,1)S(1)}, u32[]{:S(2)}, u32[]{:S(2)}) %collective-permute-start.22) | collective-permute-done | bytes 131104 | tf_op jit(solution)/shard_map/ppermute | solution.py:256
  107.4 0.7 collective-permute-start.23
  108.1 3.6 %collective-permute-done.23.refs_3_ = bf16[4,16,512]{2,1,0:T(8,128)(2,1)S(1)} collective-permute-done((bf16[4,16,512]{2,1,0:T(8,128)(2,1)S(1)}, bf16[4,16,512]{2,1,0:T(8,128)(2,1)S(1)}, u32[]{:S(2)}, u32[]{:S(2)}) %collective-permute-start.23) | collective-permute-done | bytes 65568 | tf_op jit(solution)/shard_map/ppermute | solution.py:256
  111.7 0.8 finish.1
  112.5 1.9 %collective-permute-start.25 = (f32[4,1024]{1,0:T(4,128)S(1)}, f32[4,1024]{1,0:T(4,128)S(1)}, u32[]{:S(2)}, u32[]{:S(2)}) collective-permute-start(f32[4,1024]{1,0:T(4,128)S(1)} %get-tuple-element.55), channel_id=1, source_target_pairs={{0,2},{1,3},{2,0},{3,1},{4,6},{5,7},{6,4},{7,5},{8,10},{9,11},{10,... | collective-permute-start | bytes 49160 | tf_op jit(solution)/shard_map/ppermute | solution.py:436
  114.3 0.1 collective-permute-start.24
  114.4 1.2 %collective-permute-done.26 = f32[4,1024]{1,0:T(4,128)S(1)} collective-permute-done((f32[4,1024]{1,0:T(4,128)S(1)}, f32[4,1024]{1,0:T(4,128)S(1)}, u32[]{:S(2)}, u32[]{:S(2)}) %collective-permute-start.26) | collective-permute-done | bytes 16416 | tf_op jit(solution)/shard_map/ppermute | solution.py:436
  115.6 0.6 collective-permute-done.25
  116.2 0.6 add_multiply_fusion
  (28 shorter events, 0.9 us)
Async XLA Ops:
  0.6 16.9 %copy-start = (f32[4,1024]{1,0:T(4,128)S(1)}, f32[4,1024]{1,0:T(4,128)}, u32[]{:S(2)}) copy-start(f32[4,1024]{1,0:T(4,128)} %contrast_ref.25) | copy-start | bytes 49156
  0.6 27.0 %copy-start.2 = (f32[4,16,1024]{2,1,0:T(8,128)S(1)}, f32[4,16,1024]{2,1,0:T(8,128)}, u32[]{:S(2)}) copy-start(f32[4,16,1024]{2,1,0:T(8,128)} %refs_3_.1) | copy-start | bytes 786436
  12.9 9.6 %collective-permute-start = (bf16[16,16,512]{2,1,0:T(8,128)(2,1)S(1)}, bf16[16,16,512]{2,1,0:T(8,128)(2,1)S(1)}, u32[]{:S(2)}, u32[]{:S(2)}) collective-permute-start(bf16[16,16,512]{2,1,0:T(8,128)(2,1)S(1)} %get-tuple-element.31), channel_id=1, source_target_pairs={{0,4},{1,9},{2,6},{3,11},{4,0},{5,13},{6,2},{7,15},{8,12},{9,1},{1... | collective-permute-start | bytes 786440 | tf_op jit(solution)/shard_map/ppermute | solution.py:256
  16.0 8.3 %collective-permute-start.3 = (bf16[16,16,512]{2,1,0:T(8,128)(2,1)S(1)}, bf16[16,16,512]{2,1,0:T(8,128)(2,1)S(1)}, u32[]{:S(2)}, u32[]{:S(2)}) collective-permute-start(bf16[16,16,512]{2,1,0:T(8,128)(2,1)S(1)} %get-tuple-element.34), channel_id=1, source_target_pairs={{0,8},{1,5},{2,10},{3,7},{4,12},{5,1},{6,14},{7,3},{8,0},{9,13},{1... | collective-permute-start | bytes 786440 | tf_op jit(solution)/shard_map/ppermute | solution.py:256
  22.6 5.1 %collective-permute-start.1 = (bf16[8,16,512]{2,1,0:T(8,128)(2,1)S(1)}, bf16[8,16,512]{2,1,0:T(8,128)(2,1)S(1)}, u32[]{:S(2)}, u32[]{:S(2)}) collective-permute-start(bf16[8,16,512]{2,1,0:T(8,128)(2,1)S(1)} %get-tuple-element.70), channel_id=1, source_target_pairs={{0,8},{1,5},{2,10},{3,7},{4,12},{5,1},{6,14},{7,3},{8,0},{9,13},{1... | collective-permute-start | bytes 393224 | tf_op jit(solution)/shard_map/ppermute | solution.py:256
  24.4 9.5 %collective-permute-start.4 = (bf16[8,16,512]{2,1,0:T(8,128)(2,1)S(1)}, bf16[8,16,512]{2,1,0:T(8,128)(2,1)S(1)}, u32[]{:S(2)}, u32[]{:S(2)}) collective-permute-start(bf16[8,16,512]{2,1,0:T(8,128)(2,1)S(1)} %get-tuple-element.68), channel_id=1, source_target_pairs={{0,16},{1,17},{2,18},{3,19},{4,20},{5,21},{6,22},{7,23},{8,24},{9,... | collective-permute-start | bytes 393224 | tf_op jit(solution)/shard_map/ppermute | solution.py:256
  27.7 7.6 %collective-permute-start.2 = (bf16[4,16,512]{2,1,0:T(8,128)(2,1)S(1)}, bf16[4,16,512]{2,1,0:T(8,128)(2,1)S(1)}, u32[]{:S(2)}, u32[]{:S(2)}) collective-permute-start(bf16[4,16,512]{2,1,0:T(8,128)(2,1)S(1)} %get-tuple-element.86), channel_id=1, source_target_pairs={{0,16},{1,17},{2,18},{3,19},{4,20},{5,21},{6,22},{7,23},{8,24},{9,... | collective-permute-start | bytes 196616 | tf_op jit(solution)/shard_map/ppermute | solution.py:256
  33.9 4.3 %collective-permute-start.5 = (bf16[4,16,512]{2,1,0:T(8,128)(2,1)S(1)}, bf16[4,16,512]{2,1,0:T(8,128)(2,1)S(1)}, u32[]{:S(2)}, u32[]{:S(2)}) collective-permute-start(bf16[4,16,512]{2,1,0:T(8,128)(2,1)S(1)} %get-tuple-element.84), channel_id=1, source_target_pairs={{0,4},{1,9},{2,6},{3,11},{4,0},{5,13},{6,2},{7,15},{8,12},{9,1},{1... | collective-permute-start | bytes 196616 | tf_op jit(solution)/shard_map/ppermute | solution.py:256
  40.2 9.0 %collective-permute-start.6 = (bf16[16,16,512]{2,1,0:T(8,128)(2,1)S(1)}, bf16[16,16,512]{2,1,0:T(8,128)(2,1)S(1)}, u32[]{:S(2)}, u32[]{:S(2)}) collective-permute-start(bf16[16,16,512]{2,1,0:T(8,128)(2,1)S(1)} %get-tuple-element.39), channel_id=1, source_target_pairs={{0,4},{1,9},{2,6},{3,11},{4,0},{5,13},{6,2},{7,15},{8,12},{9,1},{1... | collective-permute-start | bytes 786440 | tf_op jit(solution)/shard_map/ppermute | solution.py:256
  43.0 6.5 %collective-permute-start.9 = (bf16[16,16,512]{2,1,0:T(8,128)(2,1)S(1)}, bf16[16,16,512]{2,1,0:T(8,128)(2,1)S(1)}, u32[]{:S(2)}, u32[]{:S(2)}) collective-permute-start(bf16[16,16,512]{2,1,0:T(8,128)(2,1)S(1)} %get-tuple-element.41), channel_id=1, source_target_pairs={{0,8},{1,5},{2,10},{3,7},{4,12},{5,1},{6,14},{7,3},{8,0},{9,13},{1... | collective-permute-start | bytes 786440 | tf_op jit(solution)/shard_map/ppermute | solution.py:256
  49.3 5.8 %collective-permute-start.7 = (bf16[8,16,512]{2,1,0:T(8,128)(2,1)S(1)}, bf16[8,16,512]{2,1,0:T(8,128)(2,1)S(1)}, u32[]{:S(2)}, u32[]{:S(2)}) collective-permute-start(bf16[8,16,512]{2,1,0:T(8,128)(2,1)S(1)} %get-tuple-element.66), channel_id=1, source_target_pairs={{0,8},{1,5},{2,10},{3,7},{4,12},{5,1},{6,14},{7,3},{8,0},{9,13},{1... | collective-permute-start | bytes 393224 | tf_op jit(solution)/shard_map/ppermute | solution.py:256
  49.6 8.7 %collective-permute-start.10 = (bf16[8,16,512]{2,1,0:T(8,128)(2,1)S(1)}, bf16[8,16,512]{2,1,0:T(8,128)(2,1)S(1)}, u32[]{:S(2)}, u32[]{:S(2)}) collective-permute-start(bf16[8,16,512]{2,1,0:T(8,128)(2,1)S(1)} %get-tuple-element.64), channel_id=1, source_target_pairs={{0,16},{1,17},{2,18},{3,19},{4,20},{5,21},{6,22},{7,23},{8,24},{9,... | collective-permute-start | bytes 393224 | tf_op jit(solution)/shard_map/ppermute | solution.py:256
  55.1 5.9 %collective-permute-start.8 = (bf16[4,16,512]{2,1,0:T(8,128)(2,1)S(1)}, bf16[4,16,512]{2,1,0:T(8,128)(2,1)S(1)}, u32[]{:S(2)}, u32[]{:S(2)}) collective-permute-start(bf16[4,16,512]{2,1,0:T(8,128)(2,1)S(1)} %get-tuple-element.82), channel_id=1, source_target_pairs={{0,16},{1,17},{2,18},{3,19},{4,20},{5,21},{6,22},{7,23},{8,24},{9,... | collective-permute-start | bytes 196616 | tf_op jit(solution)/shard_map/ppermute | solution.py:256
  58.3 5.0 %collective-permute-start.11 = (bf16[4,16,512]{2,1,0:T(8,128)(2,1)S(1)}, bf16[4,16,512]{2,1,0:T(8,128)(2,1)S(1)}, u32[]{:S(2)}, u32[]{:S(2)}) collective-permute-start(bf16[4,16,512]{2,1,0:T(8,128)(2,1)S(1)} %get-tuple-element.80), channel_id=1, source_target_pairs={{0,4},{1,9},{2,6},{3,11},{4,0},{5,13},{6,2},{7,15},{8,12},{9,1},{1... | collective-permute-start | bytes 196616 | tf_op jit(solution)/shard_map/ppermute | solution.py:256
  65.2 7.8 %collective-permute-start.12 = (bf16[16,16,512]{2,1,0:T(8,128)(2,1)S(1)}, bf16[16,16,512]{2,1,0:T(8,128)(2,1)S(1)}, u32[]{:S(2)}, u32[]{:S(2)}) collective-permute-start(bf16[16,16,512]{2,1,0:T(8,128)(2,1)S(1)} %get-tuple-element.45), channel_id=1, source_target_pairs={{0,4},{1,9},{2,6},{3,11},{4,0},{5,13},{6,2},{7,15},{8,12},{9,1},{1... | collective-permute-start | bytes 786440 | tf_op jit(solution)/shard_map/ppermute | solution.py:256
  68.5 8.3 %collective-permute-start.15 = (bf16[16,16,512]{2,1,0:T(8,128)(2,1)S(1)}, bf16[16,16,512]{2,1,0:T(8,128)(2,1)S(1)}, u32[]{:S(2)}, u32[]{:S(2)}) collective-permute-start(bf16[16,16,512]{2,1,0:T(8,128)(2,1)S(1)} %get-tuple-element.47), channel_id=1, source_target_pairs={{0,8},{1,5},{2,10},{3,7},{4,12},{5,1},{6,14},{7,3},{8,0},{9,13},{1... | collective-permute-start | bytes 786440 | tf_op jit(solution)/shard_map/ppermute | solution.py:256
  73.2 5.7 %collective-permute-start.13 = (bf16[8,16,512]{2,1,0:T(8,128)(2,1)S(1)}, bf16[8,16,512]{2,1,0:T(8,128)(2,1)S(1)}, u32[]{:S(2)}, u32[]{:S(2)}) collective-permute-start(bf16[8,16,512]{2,1,0:T(8,128)(2,1)S(1)} %get-tuple-element.62), channel_id=1, source_target_pairs={{0,8},{1,5},{2,10},{3,7},{4,12},{5,1},{6,14},{7,3},{8,0},{9,13},{1... | collective-permute-start | bytes 393224 | tf_op jit(solution)/shard_map/ppermute | solution.py:256
  76.9 5.9 %collective-permute-start.16 = (bf16[8,16,512]{2,1,0:T(8,128)(2,1)S(1)}, bf16[8,16,512]{2,1,0:T(8,128)(2,1)S(1)}, u32[]{:S(2)}, u32[]{:S(2)}) collective-permute-start(bf16[8,16,512]{2,1,0:T(8,128)(2,1)S(1)} %get-tuple-element.60), channel_id=1, source_target_pairs={{0,16},{1,17},{2,18},{3,19},{4,20},{5,21},{6,22},{7,23},{8,24},{9,... | collective-permute-start | bytes 393224 | tf_op jit(solution)/shard_map/ppermute | solution.py:256
  79.0 5.9 %collective-permute-start.14 = (bf16[4,16,512]{2,1,0:T(8,128)(2,1)S(1)}, bf16[4,16,512]{2,1,0:T(8,128)(2,1)S(1)}, u32[]{:S(2)}, u32[]{:S(2)}) collective-permute-start(bf16[4,16,512]{2,1,0:T(8,128)(2,1)S(1)} %get-tuple-element.78), channel_id=1, source_target_pairs={{0,16},{1,17},{2,18},{3,19},{4,20},{5,21},{6,22},{7,23},{8,24},{9,... | collective-permute-start | bytes 196616 | tf_op jit(solution)/shard_map/ppermute | solution.py:256
  82.8 5.0 %collective-permute-start.17 = (bf16[4,16,512]{2,1,0:T(8,128)(2,1)S(1)}, bf16[4,16,512]{2,1,0:T(8,128)(2,1)S(1)}, u32[]{:S(2)}, u32[]{:S(2)}) collective-permute-start(bf16[4,16,512]{2,1,0:T(8,128)(2,1)S(1)} %get-tuple-element.76), channel_id=1, source_target_pairs={{0,4},{1,9},{2,6},{3,11},{4,0},{5,13},{6,2},{7,15},{8,12},{9,1},{1... | collective-permute-start | bytes 196616 | tf_op jit(solution)/shard_map/ppermute | solution.py:256
  89.9 6.4 %collective-permute-start.18 = (bf16[16,16,512]{2,1,0:T(8,128)(2,1)S(1)}, bf16[16,16,512]{2,1,0:T(8,128)(2,1)S(1)}, u32[]{:S(2)}, u32[]{:S(2)}) collective-permute-start(bf16[16,16,512]{2,1,0:T(8,128)(2,1)S(1)} %get-tuple-element.51), channel_id=1, source_target_pairs={{0,4},{1,9},{2,6},{3,11},{4,0},{5,13},{6,2},{7,15},{8,12},{9,1},{1... | collective-permute-start | bytes 786440 | tf_op jit(solution)/shard_map/ppermute | solution.py:256
  92.0 7.9 %collective-permute-start.21 = (bf16[16,16,512]{2,1,0:T(8,128)(2,1)S(1)}, bf16[16,16,512]{2,1,0:T(8,128)(2,1)S(1)}, u32[]{:S(2)}, u32[]{:S(2)}) collective-permute-start(bf16[16,16,512]{2,1,0:T(8,128)(2,1)S(1)} %get-tuple-element.53), channel_id=1, source_target_pairs={{0,8},{1,5},{2,10},{3,7},{4,12},{5,1},{6,14},{7,3},{8,0},{9,13},{1... | collective-permute-start | bytes 786440 | tf_op jit(solution)/shard_map/ppermute | solution.py:256
  92.9 18.8 %copy-start.1 = (bf16[4,16,1024]{2,1,0:T(8,128)(2,1)S(1)}, bf16[4,16,1024]{2,1,0:T(8,128)(2,1)}, u32[]{:S(2)}) copy-start(bf16[4,16,1024]{2,1,0:T(8,128)(2,1)} %forward_ref.1) | copy-start | bytes 393220
  96.4 5.0 %collective-permute-start.19 = (bf16[8,16,512]{2,1,0:T(8,128)(2,1)S(1)}, bf16[8,16,512]{2,1,0:T(8,128)(2,1)S(1)}, u32[]{:S(2)}, u32[]{:S(2)}) collective-permute-start(bf16[8,16,512]{2,1,0:T(8,128)(2,1)S(1)} %get-tuple-element.58), channel_id=1, source_target_pairs={{0,8},{1,5},{2,10},{3,7},{4,12},{5,1},{6,14},{7,3},{8,0},{9,13},{1... | collective-permute-start | bytes 393224 | tf_op jit(solution)/shard_map/ppermute | solution.py:256
  100.1 7.2 %collective-permute-start.22 = (bf16[8,16,512]{2,1,0:T(8,128)(2,1)S(1)}, bf16[8,16,512]{2,1,0:T(8,128)(2,1)S(1)}, u32[]{:S(2)}, u32[]{:S(2)}) collective-permute-start(bf16[8,16,512]{2,1,0:T(8,128)(2,1)S(1)} %get-tuple-element.56), channel_id=1, source_target_pairs={{0,16},{1,17},{2,18},{3,19},{4,20},{5,21},{6,22},{7,23},{8,24},{9,... | collective-permute-start | bytes 393224 | tf_op jit(solution)/shard_map/ppermute | solution.py:256
  101.5 6.6 %collective-permute-start.20 = (bf16[4,16,512]{2,1,0:T(8,128)(2,1)S(1)}, bf16[4,16,512]{2,1,0:T(8,128)(2,1)S(1)}, u32[]{:S(2)}, u32[]{:S(2)}) collective-permute-start(bf16[4,16,512]{2,1,0:T(8,128)(2,1)S(1)} %get-tuple-element.74), channel_id=1, source_target_pairs={{0,16},{1,17},{2,18},{3,19},{4,20},{5,21},{6,22},{7,23},{8,24},{9,... | collective-permute-start | bytes 196616 | tf_op jit(solution)/shard_map/ppermute | solution.py:256
  107.4 4.3 %collective-permute-start.23 = (bf16[4,16,512]{2,1,0:T(8,128)(2,1)S(1)}, bf16[4,16,512]{2,1,0:T(8,128)(2,1)S(1)}, u32[]{:S(2)}, u32[]{:S(2)}) collective-permute-start(bf16[4,16,512]{2,1,0:T(8,128)(2,1)S(1)} %get-tuple-element.72), channel_id=1, source_target_pairs={{0,4},{1,9},{2,6},{3,11},{4,0},{5,13},{6,2},{7,15},{8,12},{9,1},{1... | collective-permute-start | bytes 196616 | tf_op jit(solution)/shard_map/ppermute | solution.py:256
  112.5 3.2 %collective-permute-start.26 = (f32[4,1024]{1,0:T(4,128)S(1)}, f32[4,1024]{1,0:T(4,128)S(1)}, u32[]{:S(2)}, u32[]{:S(2)}) collective-permute-start(f32[4,1024]{1,0:T(4,128)S(1)} %get-tuple-element.55), channel_id=1, source_target_pairs={{0,3},{1,2},{2,1},{3,0},{4,7},{5,6},{6,5},{7,4},{8,11},{9,10},{10,... | collective-permute-start | bytes 49160 | tf_op jit(solution)/shard_map/ppermute | solution.py:436
  112.5 3.8 %collective-permute-start.25 = (f32[4,1024]{1,0:T(4,128)S(1)}, f32[4,1024]{1,0:T(4,128)S(1)}, u32[]{:S(2)}, u32[]{:S(2)}) collective-permute-start(f32[4,1024]{1,0:T(4,128)S(1)} %get-tuple-element.55), channel_id=1, source_target_pairs={{0,2},{1,3},{2,0},{3,1},{4,6},{5,7},{6,4},{7,5},{8,10},{9,11},{10,... | collective-permute-start | bytes 49160 | tf_op jit(solution)/shard_map/ppermute | solution.py:436
  114.3 1.9 %collective-permute-start.24 = (f32[4,1024]{1,0:T(4,128)S(1)}, f32[4,1024]{1,0:T(4,128)S(1)}, u32[]{:S(2)}, u32[]{:S(2)}) collective-permute-start(f32[4,1024]{1,0:T(4,128)S(1)} %get-tuple-element.55), channel_id=1, source_target_pairs={{0,1},{1,0},{2,3},{3,2},{4,5},{5,4},{6,7},{7,6},{8,9},{9,8},{10,11... | collective-permute-start | bytes 49160 | tf_op jit(solution)/shard_map/ppermute | solution.py:436
